TPU v7x, 32 devices: a whole 2x2x4 slice. The times are simulated.
32 devices in a mesh: dp: 4 (over z), label: 8 (over y, x, core).
Axes of the slice: x: 2, y: 2, z: 4, core: 2. Of those that a mesh axis runs over, the one named last changes fastest.
Arguments:
- enc: bfloat16 [32768, 768], P(('dp', 'label')), may hold values from -6 to 6
- proj: bfloat16 [768, 768], replicated, may hold values from -0.21875 to 0.21875
- head_weight: bfloat16 [1024, 768], P('label'), may hold values from -0.21875 to 0.21875
- shortlist: int32 [256, 4], P(('dp', 'label')), may hold values from 0 to 7, all different within a row; in each aligned block of 8 rows (0 to 7, 8 to 15, ...) at most 8 rows name the same one
- positives: int32 [32768, 8], P(('dp', 'label')), may hold values from 0 to 511
- weight_num: int32 [1024], P('label'), may hold values from 1 to 16
- weight_den: int32 [1024], P('label'), may hold values from 1 to 16
Outputs:
- grad_enc: float32 [32768, 768], P(('dp', 'label'))
- grad_proj: float32 [768, 768], replicated
- grad_head: float32 [1024, 768], P('label', 'dp')
Inputs may be any that keep to these rules, and one draw needn't show every extreme that they name: `shortlist`: each row names 4 different clusters; among the rows of one device no cluster is named by more than 8 rows, and in every draw some cluster is named by exactly 8 rows of some device; every cluster is named somewhere.
All inputs are finite; a program needn't handle non-finite values.
Results may differ from a plain program's by a relative error of at most 0.005.
Values may be sent and summed in bfloat16 or wider, within the bound.
No kernel may reach another device: no remote copies, remote signals or barrier semaphores. Data moves between devices by JAX's collectives and lax.ppermute only.
A program may use at most 128 MiB of HBM per device.

v0:
```python
import jax
import jax.numpy as jnp
from jax import lax
from jax.sharding import PartitionSpec as P


def contract(left, right, left_dim, right_dim):
    return lax.dot_general(
        left, right, (((left_dim,), (right_dim,)), ((), ())), preferred_element_type=jnp.float32
    )


def cluster_grads(hidden_rows, cluster_rows, cluster_scale, wanted, keeping):
    cluster_size = cluster_rows.shape[-2]
    sample_block = hidden_rows.shape[1]
    label_iota = jnp.arange(cluster_size, dtype=jnp.int32)
    logits = jnp.einsum(
        "msd,ld->msl", hidden_rows, cluster_rows, preferred_element_type=jnp.float32
    )
    target = jnp.zeros(logits.shape, jnp.bool_)
    for column in range(wanted.shape[2]):
        target = target | (wanted[:, :, column, None] == label_iota)
    scaled = cluster_scale * (jax.nn.sigmoid(logits) - target.astype(jnp.float32)) / sample_block
    grad_logits = (scaled * keeping[:, None, None]).astype(jnp.bfloat16)
    grad_part = jnp.einsum(
        "msl,ld->msd", grad_logits, cluster_rows, preferred_element_type=jnp.float32
    ).astype(jnp.bfloat16)
    grad_cluster = jnp.einsum(
        "msl,msd->ld", grad_logits, hidden_rows, preferred_element_type=jnp.float32
    )
    return (grad_part, grad_cluster)


def shards(enc, proj, head_weight, shortlist, positives, weight_num, weight_den):
    owners = lax.axis_size("label")
    block_count, beam_width = shortlist.shape
    samples, model_width = enc.shape
    sample_block = samples // block_count
    cluster_size = head_weight.shape[0]
    positive_count = positives.shape[1]
    pair_count = block_count * beam_width
    hidden = jnp.dot(enc, proj, preferred_element_type=jnp.float32).astype(jnp.bfloat16)
    hidden_blocks = hidden.reshape(block_count, sample_block, model_width)
    wanted_blocks = positives.reshape(block_count, sample_block, positive_count)
    capacity = max(2, 2 * pair_count // owners)
    slot_count = owners * capacity
    pair_owner = shortlist.reshape(pair_count)
    pair_iota = jnp.arange(pair_count, dtype=jnp.int32)
    earlier = (pair_owner[:, None] == pair_owner[None, :]) & (
        pair_iota[None, :] < pair_iota[:, None]
    )
    pair_rank = jnp.sum(earlier.astype(jnp.int32), axis=1)
    pair_slot = pair_owner * capacity + pair_rank
    slot_iota = jnp.arange(slot_count, dtype=jnp.int32)
    placed = pair_slot[None, :] == slot_iota[:, None]
    occupied = jnp.any(placed, axis=1).astype(jnp.int32)
    source_pair = jnp.sum(jnp.where(placed, pair_iota[None, :], 0), axis=1)
    source_block = source_pair // beam_width
    source_slot = source_pair % beam_width
    send_rows = jnp.take(hidden_blocks, source_block, axis=0)
    send_wanted = (
        jnp.take(wanted_blocks, source_block, axis=0) - (source_slot * cluster_size)[:, None, None]
    )
    recv_rows, recv_wanted, recv_occupied = (
        lax.all_to_all(send_rows, "label", split_axis=0, concat_axis=0, tiled=True),
        lax.all_to_all(send_wanted, "label", split_axis=0, concat_axis=0, tiled=True),
        lax.all_to_all(occupied, "label", split_axis=0, concat_axis=0, tiled=True),
    )
    cluster_scale = weight_num.astype(jnp.float32) / weight_den.astype(jnp.float32)
    grad_part, weight_part = cluster_grads(
        recv_rows, head_weight, cluster_scale, recv_wanted, recv_occupied.astype(jnp.float32)
    )
    returned = lax.all_to_all(grad_part, "label", split_axis=0, concat_axis=0, tiled=True)
    block_pick = jnp.sum(
        placed.reshape(slot_count, block_count, beam_width).astype(jnp.int32), axis=2
    ).T.astype(jnp.bfloat16)
    grad_hidden = jnp.einsum(
        "bm,msd->bsd", block_pick, returned, preferred_element_type=jnp.float32
    )
    grad_hidden = grad_hidden.reshape(samples, model_width).astype(jnp.bfloat16)
    grad_enc = contract(grad_hidden, proj, 1, 1)
    grad_proj = lax.psum(contract(enc, grad_hidden, 0, 0), ("dp", "label"))
    grad_head = lax.psum_scatter(weight_part, "dp", scatter_dimension=1, tiled=True)
    return (grad_enc, grad_proj, grad_head)


def solution(mesh):
    placed = (
        P(("dp", "label"), None),
        P(),
        P("label", None),
        P(("dp", "label"), None),
        P(("dp", "label"), None),
        P("label"),
        P("label"),
    )
    return jax.shard_map(
        shards,
        mesh=mesh,
        in_specs=placed,
        out_specs=(P(("dp", "label"), None), P(), P("label", "dp")),
        check_vma=False,
    )
```

profile of v0, /device:TPU:0, one launch (start us, length us, event | category | flops | bytes accessed | tf_op | source)
XLA Modules:
  0.0 542.1 jit_solution(7851949984037380171)
XLA Ops:
  8.0 0.9 copy.28
  9.3 0.7 reshape.137
  9.9 5.2 all-to-all-start.2
  15.3 1.4 gather_fusion.1
  16.6 2.7 convolution_convert_fusion.1
  19.3 0.9 select_subtract_fusion
  20.2 7.1 %gather_fusion = bf16[64,128,768]{2,1,0:T(8,128)(2,1)} fusion(bf16[8,128,768]{2,1,0:T(8,128)(2,1)S(1)} %bitcast.46, s32[1024]{0:T(1024)S(1)} %pad_clamp_fusion), kind=kCustom, calls=%fused_computation | custom fusion | bytes 25166080 | tf_op jit(solution)/shard_map/jit(_take)/gather | solution.py:60
  27.3 4.2 all-to-all-start.1
  31.5 10.9 %broadcast_select_fusion = bf16[64,128,768]{2,1,0:T(8,128)(2,1)} fusion(bf16[64,128,768]{2,1,0:T(8,128)(2,1)} %gather_fusion, pred[64]{0:T(512)(128)(4,1)S(1)} %compare_and_fusion), kind=kLoop, calls=%fused_computation.4 | loop fusion | flops 6291456 | bytes 25165888 | tf_op jit(solution)/shard_map/jit(_take)/select_n | solution.py:60
  42.4 5.7 %all-to-all-start = ((bf16[64,128,768]{2,1,0:T(8,128)(2,1)}), bf16[64,128,768]{2,1,0:T(8,128)(2,1)}, u32[]{:S(2)}, u32[]{:S(2)}) async-start(bf16[64,128,768]{2,1,0:T(8,128)(2,1)} %broadcast_select_fusion), calls=%async_computation | async-start | bytes 25165824 | tf_op jit(solution)/shard_map/all_to_all | solution.py:65
  48.4 138.7 %all-to-all-done = bf16[64,128,768]{2,1,0:T(8,128)(2,1)} async-done(((bf16[64,128,768]{2,1,0:T(8,128)(2,1)}), bf16[64,128,768]{2,1,0:T(8,128)(2,1)}, u32[]{:S(2)}, u32[]{:S(2)}) %all-to-all-start) | async-done | bytes 12582944 | tf_op jit(solution)/shard_map/all_to_all | solution.py:65
  187.0 12.7 %multiply_convert_fusion = bf16[64,128,128]{2,1,0:T(8,128)(2,1)} fusion(bf16[64,128,768]{2,1,0:T(8,128)(2,1)} %all-to-all-done, f32[64]{0:T(128)S(1)} %mul.57, s32[64,128]{1,0:T(8,128)S(1)} %bitcast.50, s32[64,128]{1,0:T(8,128)S(1)} %bitcast.51, s32[64,128]{1,0:T(8,128)S(1)} %bitcast.52, s32[64,128]{1,0:T(8,128)S(1)} %bitcast.53, ...), kind=kOutput, calls=%fused_computation.6 | convolution fusion | flops 1634729984 | bytes 15139584 | tf_op jit(solution)/shard_map/msd,ld->msl/dot_general | solution.py:17
  199.7 6.3 %convolution_convert_fusion = bf16[64,128,768]{2,0,1:T(8,128)(2,1)S(1)} fusion(bf16[64,128,128]{2,1,0:T(8,128)(2,1)} %multiply_convert_fusion, bf16[128,768]{1,0:T(8,128)(2,1)S(1)} %copy-done.1), kind=kOutput, calls=%fused_computation.5 | convolution fusion | flops 1616904192 | bytes 14876672 | tf_op jit(solution)/shard_map/msl,ld->msd/dot_general | solution.py:25
  206.0 22.9 %copy.33 = bf16[64,128,768]{2,1,0:T(8,128)(2,1)} copy(bf16[64,128,768]{2,0,1:T(8,128)(2,1)S(1)} %convolution_convert_fusion) | data formatting | bytes 25165824 | tf_op jit(solution)/shard_map/convert_element_type | solution.py:27
  228.9 5.4 all-to-all-start.3
  234.3 0.3 all-reduce.2.cloned.1.call-start
  234.9 138.5 %all-to-all-done.3 = bf16[64,128,768]{2,1,0:T(8,128)(2,1)} async-done(((bf16[64,128,768]{2,1,0:T(8,128)(2,1)}), bf16[64,128,768]{2,1,0:T(8,128)(2,1)}, u32[]{:S(2)}, u32[]{:S(2)}) %all-to-all-start.3) | async-done | bytes 12582944 | tf_op jit(solution)/shard_map/all_to_all | solution.py:73
  373.3 18.0 %fusion.10 = bf16[8,128,768]{2,0,1:T(8,128)(2,1)S(1)} fusion(bf16[64,128,768]{2,1,0:T(8,128)(2,1)} %all-to-all-done.3, s32[64,8]{0,1:T(8,128)S(1)} %convert_reduce_fusion), kind=kOutput, calls=%fused_computation.24 | convolution fusion | flops 101450240 | bytes 14157824 | tf_op jit(solution)/shard_map/bm,msd->bsd/dot_general | solution.py:77
  391.4 0.3 copy.35
  391.7 2.8 convolution_bitcast_fusion
  394.6 11.2 %convolution_bitcast_fusion.1 = f32[128,768]{0,1:T(8,128)} fusion(bf16[64,128,128]{2,1,0:T(8,128)(2,1)} %multiply_convert_fusion, bf16[64,128,768]{2,1,0:T(8,128)(2,1)} %all-to-all-done), kind=kOutput, calls=%fused_computation.26 | convolution fusion | flops 1610612736 | bytes 15073280 | tf_op jit(solution)/shard_map/msl,msd->ld/dot_general | solution.py:28
  405.8 4.4 fusion.22
  410.1 121.5 %all-reduce.2.cloned.1.call-done = f32[768,768]{0,1:T(8,128)} async-done(((f32[768,768]{0,1:T(8,128)}), f32[768,768]{0,1:T(8,128)}) %all-reduce.2.cloned.1.call-update) | async-done | bytes 2359312 | tf_op jit(solution)/shard_map/psum | solution.py:82
  531.6 3.0 copy.37
  (32 shorter events, 1.1 us)
Async XLA Ops:
  8.0 8.6 %copy-start = (bf16[1024,768]{1,0:T(8,128)(2,1)S(1)}, bf16[1024,768]{1,0:T(8,128)(2,1)}, u32[]{:S(2)}) copy-start(bf16[1024,768]{1,0:T(8,128)(2,1)} %param.7) | copy-start | bytes 4718596
  9.9 17.3 %all-to-all-start.2 = ((s32[8,8,1]{1,2,0:T(1,128)}), s32[8,8,1]{1,2,0:T(1,128)S(1)}, u32[]{:S(2)}, u32[]{:S(2)}) async-start(s32[8,8,1]{1,2,0:T(1,128)} %bitcast.14), calls=%async_computation.2 | async-start | bytes 8192 | tf_op jit(solution)/shard_map/all_to_all | solution.py:67
  27.3 15.1 %all-to-all-start.1 = ((s32[64,128,8]{1,2,0:T(8,128)}), s32[64,128,8]{1,2,0:T(8,128)S(1)}, u32[]{:S(2)}, u32[]{:S(2)}) async-start(s32[64,128,8]{1,2,0:T(8,128)} %select_subtract_fusion), calls=%async_computation.1 | async-start | bytes 524288 | tf_op jit(solution)/shard_map/all_to_all | solution.py:66
  42.4 5.7 %copy-start.2 = (s32[128]{0:T(128)S(1)}, s32[128]{0:T(128)}, u32[]{:S(2)}) copy-start(s32[128]{0:T(128)} %param.13) | copy-start | bytes 1540
  42.4 5.7 %copy-start.3 = (s32[128]{0:T(128)S(1)}, s32[128]{0:T(128)}, u32[]{:S(2)}) copy-start(s32[128]{0:T(128)} %param.12) | copy-start | bytes 1540
  42.4 144.7 %copy-start.1 = (bf16[128,768]{1,0:T(8,128)(2,1)S(1)}, bf16[128,768]{1,0:T(8,128)(2,1)}, u32[]{:S(2)}) copy-start(bf16[128,768]{1,0:T(8,128)(2,1)} %param.9) | copy-start | bytes 589828
  42.4 144.6 %all-to-all-start = ((bf16[64,128,768]{2,1,0:T(8,128)(2,1)}), bf16[64,128,768]{2,1,0:T(8,128)(2,1)}, u32[]{:S(2)}, u32[]{:S(2)}) async-start(bf16[64,128,768]{2,1,0:T(8,128)(2,1)} %broadcast_select_fusion), calls=%async_computation | async-start | bytes 25165824 | tf_op jit(solution)/shard_map/all_to_all | solution.py:65
  228.9 144.4 %all-to-all-start.3 = ((bf16[64,128,768]{2,1,0:T(8,128)(2,1)}), bf16[64,128,768]{2,1,0:T(8,128)(2,1)}, u32[]{:S(2)}, u32[]{:S(2)}) async-start(bf16[64,128,768]{2,1,0:T(8,128)(2,1)} %copy.33), calls=%async_computation.3 | async-start | bytes 25165824 | tf_op jit(solution)/shard_map/all_to_all | solution.py:73
  234.3 297.3 %all-reduce.2.cloned.1.call-start = ((), (), s32[]{:S(2)}) async-start(), calls=%async_computation.5 | async-start | bytes 4718592 | tf_op jit(solution)/shard_map/psum | solution.py:82
  394.5 140.1 %reduce-scatter.2.cloned.1.call-start = ((), (), s32[]{:S(2)}) async-start(), calls=%async_computation.6 | async-start | bytes 491520 | tf_op jit(solution)/shard_map/reduce_scatter | solution.py:83
Sparse Core Ops, SparseCore 0:
  394.7 136.9 all-reduce.1
Sparse Core Ops, SparseCore 1:
  405.9 20.6 reduce-scatter.1
where the time goes:
time: 543 us; the launch traced here: 542 us
  waiting for transfers between devices  399 us (73%)
  matrix products  58 us (11%)
  local copies, waits for them, and re-layouts  36.7 us (7%)
  starting transfers between devices  20.7 us (4%)
  between operations  15.6 us (3%)
  other arithmetic  12.3 us (2%)
    all_to_all x1, waiting for transfers between devices, shards(): lax.all_to_all(send_rows, 'label', split_axis=0, concat_axis=0, tiled=True)  139 us
    all_to_all x1, waiting for transfers between devices, shards(): lax.all_to_all(grad_part, 'label', split_axis=0, concat_axis=0, tiled=True)  138 us
    psum x1, waiting for transfers between devices, shards(): grad_proj = lax.psum(contract(enc, grad_hidden, 0, 0), ('dp', 'label'))  121 us
    convert_element_type x1, local copies, waits for them, and re-layouts, cluster_grads(): grad_part = jnp.einsum('msl,ld->msd', grad_logits, cluster_rows, preferre...  22.9 us
    dot_general x1, matrix products, shards(): jnp.einsum('bm,msd->bsd', block_pick, returned, preferred_element_type=jn...  18 us
    dot_general x1, matrix products, cluster_grads(): jnp.einsum('msd,ld->msl', hidden_rows, cluster_rows, preferred_element_ty...  12.7 us
    dot_general x1, matrix products, cluster_grads(): jnp.einsum('msl,msd->ld', grad_logits, hidden_rows, preferred_element_typ...  11.2 us
    select_n x2, other arithmetic, shards(): send_rows = jnp.take(hidden_blocks, source_block, axis=0)  10.9 us
  transfers between devices with their start and end apart: 6, of which 3 were waited for; matrix products, arithmetic and copies ran while one was open for 8% of the time, Pallas kernels for 0%

commit v1 on v0

v1 whole, which is shorter than its diff:
```python
import functools

import jax
import jax.numpy as jnp
from jax import lax
from jax.experimental import pallas as pl
from jax.experimental.pallas import tpu as pltpu
from jax.sharding import PartitionSpec as P

BF16 = jnp.bfloat16
F32 = jnp.float32
VMEM = pl.BlockSpec(memory_space=pltpu.VMEM)
SMEM = pl.BlockSpec(memory_space=pltpu.SMEM)
TAIL = 16
NN = (((1,), (0,)), ((), ()))
NT = (((1,), (1,)), ((), ()))
TN = (((0,), (0,)), ((), ()))


def dot(left, right, dims):
    return lax.dot_general(left, right, dims, preferred_element_type=F32)


def swap(value, axis, distance):
    size = lax.axis_size(axis)
    return lax.ppermute(value, axis, [(i, i ^ distance) for i in range(size)])


def call(kernel, outs, args, scalars=(), scratch=(), flops=0, nbytes=0):
    return pl.pallas_call(
        kernel,
        out_shape=outs,
        in_specs=[SMEM] * len(scalars) + [VMEM] * len(args),
        out_specs=[VMEM] * len(outs),
        scratch_shapes=list(scratch),
        compiler_params=pltpu.CompilerParams(vmem_limit_bytes=40 * 1024 * 1024),
        cost_estimate=pl.CostEstimate(flops=flops, bytes_accessed=nbytes, transcendentals=0),
    )(*scalars, *args)


def slot_of(relative, owners):
    return (relative >> 1) + (relative & 1) * (owners // 2)


def score_kernel(owners, beam, block, size, slots_ref, hidden_ref, wanted_ref, enc_t_ref, *refs):
    payloads, refs = refs[:owners], refs[owners:]
    grads_ref, weights_ref, refs = refs[0], refs[1], refs[2:]
    sent = refs[: owners // 2]
    scale_ref, logits_ref = refs[owners // 2 :]
    samples = hidden_ref.shape[0]
    for relative in range(owners):
        slot = slot_of(relative, owners)
        rows = pl.ds(slot * size, size)
        weights_ref[rows, :] = payloads[relative][:size, :]
        tail = payloads[relative][size : size + TAIL, :size].astype(F32)
        ratio = tail[0:1, :] / tail[1:2, :]
        scale_ref[rows, :] = jnp.broadcast_to(ratio, (block, size)).T / block
    grads_ref[...] = jnp.zeros_like(grads_ref)
    label_iota = lax.broadcasted_iota(jnp.int32, (size, block), 0)
    tile = min(2 * block, samples)
    for start in range(0, samples, tile):
        logits_ref[...] = dot(weights_ref[...], hidden_ref[start : start + tile, :], NT)
        for low in range(start, start + tile, block):
            for beam_slot in range(beam):
                slot = slots_ref[(low // block) * beam + beam_slot]
                rows = pl.ds(pl.multiple_of(slot * size, size), size)
                logits = logits_ref[rows, low - start : low - start + block]
                labels = label_iota + beam_slot * size
                target = labels == wanted_ref[0:1, low : low + block]
                for column in range(1, wanted_ref.shape[0]):
                    target = target | (labels == wanted_ref[column : column + 1, low : low + block])
                share = jax.nn.sigmoid(logits) - jnp.where(target, 1.0, 0.0)
                grads_ref[rows, low : low + block] = (scale_ref[rows, :] * share).astype(BF16)
    half = owners // 2 * size
    outer = dot(enc_t_ref[...], grads_ref[half:, :], NT)
    for j in range(owners // 2):
        sent[j][...] = outer[:, j * size : (j + 1) * size].astype(BF16)


def keep_kernel(owners, size, enc_t_ref, grads_ref, *kept):
    outer = dot(enc_t_ref[...], grads_ref[: owners // 2 * size, :], NT)
    for j in range(owners // 2):
        kept[j][...] = outer[:, j * size : (j + 1) * size]


def enc_kernel(grads_ref, weights_ref, proj_ref, out_ref):
    grad_hidden = dot(grads_ref[...], weights_ref[...], TN).astype(BF16)
    out_ref[...] = dot(grad_hidden, proj_ref[...], NT)


def plane_kernel(planes, z_ref, own_ref, *refs):
    recv, refs = refs[: len(refs) - planes - 1], refs[len(refs) - planes - 1 :]
    kept, sent, total_ref = refs[0], refs[1:planes], refs[planes]
    total = own_ref[...]
    for ref in recv:
        total = total + ref[...].astype(F32)
    total_ref[...] = total
    depth = kept.shape[0]
    z = z_ref[0]
    kept[...] = total_ref[pl.ds(pl.multiple_of(z * depth, depth), depth), :]
    for q in range(1, planes):
        start = pl.multiple_of((z ^ q) * depth, depth)
        sent[q - 1][...] = total_ref[pl.ds(start, depth), :].astype(BF16)


def head_kernel(planes, z_ref, *refs):
    parts, refs = refs[:planes], refs[planes:]
    proj_ref, whole_ref, out_ref = refs
    depth = parts[0].shape[0]
    z = z_ref[0]
    for q in range(planes):
        start = pl.multiple_of((z ^ q) * depth, depth)
        whole_ref[pl.ds(start, depth), :] = parts[q][...]
    out_ref[...] = dot(whole_ref[...], proj_ref[...], TN)


def proj_kernel(owners, size, me_ref, *refs):
    parts, refs = refs[:owners], refs[owners:]
    weights_ref, out_ref, outer_ref, rows_ref = refs
    me = me_ref[0]
    for relative in range(owners):
        start = pl.multiple_of((me ^ relative) * size, size)
        slot = slot_of(relative, owners)
        outer_ref[:, pl.ds(start, size)] = parts[relative][...]
        rows_ref[pl.ds(start, size), :] = weights_ref[slot * size : (slot + 1) * size, :]
    out_ref[...] = dot(outer_ref[...], rows_ref[...], NN)


def shards(enc, proj, head_weight, shortlist, positives, weight_num, weight_den):
    owners, planes = lax.axis_size("label"), lax.axis_size("dp")
    me, z = lax.axis_index("label"), lax.axis_index("dp")
    me_s = jnp.reshape(me, (1,)).astype(jnp.int32)
    z_s = jnp.reshape(z, (1,)).astype(jnp.int32)
    blocks, beam = shortlist.shape
    samples, width = enc.shape
    block = samples // blocks
    size = head_weight.shape[0]
    labels = owners * size
    chips = range(2, owners, 2)

    tail = jnp.zeros((TAIL, width), BF16)
    tail = tail.at[0, :size].set(weight_num.astype(BF16)).at[1, :size].set(weight_den.astype(BF16))
    payload = jnp.concatenate([head_weight, tail], axis=0)
    got = {0: payload, 1: swap(payload, "label", 1)}
    for relative in chips:
        got[relative] = swap(payload, "label", relative)
    for relative in chips:
        got[relative + 1] = swap(got[relative], "label", 1)

    hidden = dot(enc, proj, NN).astype(BF16)
    enc_t = enc.T
    wanted = positives.T
    slots = slot_of(jnp.bitwise_xor(shortlist, me), owners).astype(jnp.int32).reshape(-1)

    piece = jax.ShapeDtypeStruct((width, size), BF16)
    piece_f32 = jax.ShapeDtypeStruct((width, size), F32)
    grads, weights, *sent = call(
        functools.partial(score_kernel, owners, beam, block, size),
        [jax.ShapeDtypeStruct((labels, samples), BF16), jax.ShapeDtypeStruct((labels, width), BF16)]
        + [piece] * (owners // 2),
        [hidden, wanted, enc_t] + [got[relative] for relative in range(owners)],
        scalars=[slots],
        scratch=[pltpu.VMEM((labels, block), F32), pltpu.VMEM((labels, min(2 * block, samples)), F32)],
        flops=4 * samples * labels * width,
        nbytes=12_000_000,
    )
    from_core = [swap(value, "label", 1) for value in sent]
    kept = call(
        functools.partial(keep_kernel, owners, size),
        [piece_f32] * (owners // 2),
        [enc_t, grads],
        flops=samples * labels * width,
        nbytes=4_000_000,
    )
    grad_enc = pl.pallas_call(
        enc_kernel,
        grid=(max(1, samples // 256),),
        out_shape=jax.ShapeDtypeStruct((samples, width), F32),
        in_specs=[
            pl.BlockSpec((labels, min(256, samples)), lambda i: (0, i)),
            pl.BlockSpec((labels, width), lambda i: (0, 0)),
            pl.BlockSpec((width, width), lambda i: (0, 0)),
        ],
        out_specs=pl.BlockSpec((min(256, samples), width), lambda i: (i, 0)),
        compiler_params=pltpu.CompilerParams(vmem_limit_bytes=40 * 1024 * 1024),
        cost_estimate=pl.CostEstimate(
            flops=2 * samples * width * (labels + width), bytes_accessed=9_000_000, transcendentals=0
        ),
    )(grads, weights, proj)

    pairs = [a + b.astype(F32) for a, b in zip(kept, from_core)]
    from_chips = [swap(pairs[p // 2].astype(BF16), "label", p) for p in chips]
    depth = width // planes
    part = jax.ShapeDtypeStruct((depth, size), BF16)
    own, *sent = call(
        functools.partial(plane_kernel, planes),
        [jax.ShapeDtypeStruct((depth, size), F32)] + [part] * (planes - 1),
        [pairs[0]] + from_chips,
        scalars=[z_s],
        scratch=[pltpu.VMEM((width, size), F32)],
        nbytes=2_000_000,
    )
    total = own
    for q in range(1, planes):
        total = total + swap(sent[q - 1], "dp", q).astype(F32)
    total = total.astype(BF16)
    parts = [total] + [swap(total, "dp", q) for q in range(1, planes)]
    proj_slice = lax.dynamic_slice_in_dim(proj, z * depth, depth, 1)
    whole, grad_head = call(
        functools.partial(head_kernel, planes),
        [piece, jax.ShapeDtypeStruct((size, depth), F32)],
        parts + [proj_slice],
        scalars=[z_s],
        flops=2 * size * width * depth,
        nbytes=1_000_000,
    )
    have = {0: whole, 1: swap(whole, "label", 1)}
    for relative in chips:
        have[relative] = swap(whole, "label", relative)
    for relative in chips:
        have[relative + 1] = swap(have[relative], "label", 1)
    (grad_proj,) = call(
        functools.partial(proj_kernel, owners, size),
        [jax.ShapeDtypeStruct((width, width), F32)],
        [have[relative] for relative in range(owners)] + [weights],
        scalars=[me_s],
        scratch=[pltpu.VMEM((width, labels), BF16), pltpu.VMEM((labels, width), BF16)],
        flops=2 * labels * width * width,
        nbytes=6_000_000,
    )
    return (grad_enc, grad_proj, grad_head)


def solution(mesh):
    placed = (
        P(("dp", "label"), None),
        P(),
        P("label", None),
        P(("dp", "label"), None),
        P(("dp", "label"), None),
        P("label"),
        P("label"),
    )
    return jax.shard_map(
        shards,
        mesh=mesh,
        in_specs=placed,
        out_specs=(P(("dp", "label"), None), P(), P("label", "dp")),
        check_vma=False,
    )
```

time: 543 us -> 93 us (0.17)
  waiting for transfers between devices: 399 us -> 29.9 us
  matrix products: 58 us -> 2.79 us
  local copies, waits for them, and re-layouts: 36.7 us -> 14.8 us
  Pallas kernels: 0 us -> 17.5 us
  between operations: 15.6 us -> 0.85 us
  other arithmetic: 12.3 us -> 3.98 us
    all_to_all x4 -> x0, waiting for transfers between devices: 277 us -> none  [the longest x1 139 us: shards(): lax.all_to_all(send_rows, 'label', split_axis=0, concat_axis=0, tiled=True)]
    psum x1 -> x0, waiting for transfers between devices: 121 us -> none  [shards(): grad_proj = lax.psum(contract(enc, grad_hidden, 0, 0), ('dp', 'label'))]
    dot_general x7 -> x1, matrix products: 58 us -> 2.79 us  [dot(): return lax.dot_general(left, right, dims, preferred_element_type=F32)]
    ppermute x0 -> x27, waiting for transfers between devices: none -> 29.9 us  [swap(): return lax.ppermute(value, axis, [(i, i ^ distance) for i in range(size)])]
    convert_element_type x3 -> x0, local copies, waits for them, and re-layouts: 23.9 us -> none  [the longest x1 22.9 us: cluster_grads(): grad_part = jnp.einsum('msl,ld->msd', grad_logits, cluster_rows, preferre...]
    ppermute x0 -> x27, starting transfers between devices: none -> 22.7 us  [swap(): return lax.ppermute(value, axis, [(i, i ^ distance) for i in range(size)])]
    all_to_all x4 -> x0, starting transfers between devices: 20.4 us -> none  [the longest x1 5.66 us: shards(): lax.all_to_all(send_rows, 'label', split_axis=0, concat_axis=0, tiled=True)]
    pallas_call x0 -> x6, Pallas kernels: none -> 17.5 us  [the longest x5 12.3 us: call(): pl.pallas_call(kernel, out_shape=outs, in_specs=[SMEM] * len(scalars) + [...]
  transfers between devices with their start and end apart: 6 -> 27, of which waited for: 3 -> 11; matrix products, arithmetic and copies ran while one was open for 8% -> 8% of each run, Pallas kernels for 0% -> 7%
where the time goes in v1:
time: 93 us; the launch traced here: 92.5 us
  waiting for transfers between devices  29.9 us (32%)
  starting transfers between devices  22.7 us (24%)
  Pallas kernels  17.5 us (19%)
  local copies, waits for them, and re-layouts  14.8 us (16%)
  other arithmetic  3.98 us (4%)
  matrix products  2.79 us (3%)
    ppermute x27, waiting for transfers between devices, swap(): return lax.ppermute(value, axis, [(i, i ^ distance) for i in range(size)])  29.9 us
    ppermute x27, starting transfers between devices, swap(): return lax.ppermute(value, axis, [(i, i ^ distance) for i in range(size)])  22.7 us
    unnamed x28, local copies, waits for them, and re-layouts  14.3 us
    pallas_call x5, Pallas kernels, call(): pl.pallas_call(kernel, out_shape=outs, in_specs=[SMEM] * len(scalars) + [...  12.3 us
    pallas_call x1, Pallas kernels, shards(): pl.pallas_call(enc_kernel, grid=(max(1, samples // 256),), out_shape=jax....  5.24 us
    dot_general x1, matrix products, dot(): return lax.dot_general(left, right, dims, preferred_element_type=F32)  2.79 us
  transfers between devices with their start and end apart: 27, of which 11 were waited for; matrix products, arithmetic and copies ran while one was open for 8% of the time, Pallas kernels for 7%

profile of v1, /device:TPU:0, one launch (start us, length us, event | category | flops | bytes accessed | tf_op | source)
XLA Modules:
  0.0 92.5 jit_solution(17215715895281376758)
XLA Ops:
  3.1 3.0 %collective-permute-start.1 = (bf16[144,768]{1,0:T(8,128)(2,1)S(1)}, bf16[144,768]{1,0:T(8,128)(2,1)S(1)}, u32[]{:S(2)}, u32[]{:S(2)}) collective-permute-start(bf16[144,768]{1,0:T(8,128)(2,1)S(1)} %pad_maximum_fusion.refs_0_), channel_id=1, source_target_pairs={{0,2},{1,3},{2,0},{3,1},{4,6},{5,7},{6,4},{7,5},{8,10},{9,11},{10,... | collective-permute-start | bytes 663560 | tf_op jit(solution)/shard_map/ppermute | solution.py:26
  6.1 1.5 %collective-permute-start.3 = (bf16[144,768]{1,0:T(8,128)(2,1)S(1)}, bf16[144,768]{1,0:T(8,128)(2,1)S(1)}, u32[]{:S(2)}, u32[]{:S(2)}) collective-permute-start(bf16[144,768]{1,0:T(8,128)(2,1)S(1)} %pad_maximum_fusion.refs_0_), channel_id=1, source_target_pairs={{0,4},{1,5},{2,6},{3,7},{4,0},{5,1},{6,2},{7,3},{8,12},{9,13},{10,... | collective-permute-start | bytes 663560 | tf_op jit(solution)/shard_map/ppermute | solution.py:26
  8.5 1.8 %copy.14 = bf16[1024,768]{0,1:T(8,128)(2,1)S(1)} copy(bf16[1024,768]{1,0:T(8,128)(2,1)} %param.11) | data formatting | bytes 3145728 | tf_op args[0]
  10.3 2.0 %collective-permute-done.1.refs_2_ = bf16[144,768]{1,0:T(8,128)(2,1)S(1)} collective-permute-done((bf16[144,768]{1,0:T(8,128)(2,1)S(1)}, bf16[144,768]{1,0:T(8,128)(2,1)S(1)}, u32[]{:S(2)}, u32[]{:S(2)}) %collective-permute-start.1) | collective-permute-done | bytes 221216 | tf_op jit(solution)/shard_map/ppermute | solution.py:26
  12.3 5.4 %collective-permute-done.3.refs_4_ = bf16[144,768]{1,0:T(8,128)(2,1)S(1)} collective-permute-done((bf16[144,768]{1,0:T(8,128)(2,1)S(1)}, bf16[144,768]{1,0:T(8,128)(2,1)S(1)}, u32[]{:S(2)}, u32[]{:S(2)}) %collective-permute-start.3) | collective-permute-done | bytes 221216 | tf_op jit(solution)/shard_map/ppermute | solution.py:26
  18.2 2.8 %convolution_convert_fusion.hidden_ref = bf16[1024,768]{1,0:T(8,128)(2,1)S(1)} fusion(bf16[1024,768]{1,0:T(8,128)(2,1)} %param.11, bf16[768,768]{1,0:T(8,128)(2,1)S(1)} %copy-done.7), kind=kOutput, calls=%fused_computation | convolution fusion | flops 1208745984 | bytes 4325376 | tf_op jit(solution)/shard_map/dot_general | solution.py:21
  21.1 6.6 %shard_map.94 = (bf16[1024,1024]{1,0:T(8,128)(2,1)S(1)}, bf16[1024,768]{1,0:T(8,128)(2,1)S(1)}, bf16[768,128]{1,0:T(8,128)(2,1)S(1)}, bf16[768,128]{1,0:T(8,128)...) custom-call(s32[32]{0:T(128)S(1)} %reshape.74.slots_ref, ...), custom_call_target="tpu_custom_call" | custom-call | flops 3221225472 | bytes 12000000 | tf_op jit(solution)/shard_map/pallas_call | solution.py:30
  33.2 1.6 %copy-done.1 = bf16[1024,1024]{1,0:T(8,128)(2,1)S(1)} copy-done((bf16[1024,1024]{1,0:T(8,128)(2,1)S(1)}, bf16[1024,1024]{1,0:T(8,128)(2,1)}, u32[]{:S(2)}) %copy-start.1) | copy-done | bytes 2097176
  35.9 1.6 %collective-permute-start.13 = (bf16[768,128]{1,0:T(8,128)(2,1)S(1)}, bf16[768,128]{1,0:T(8,128)(2,1)S(1)}, u32[]{:S(2)}, u32[]{:S(2)}) collective-permute-start(bf16[768,128]{1,0:T(8,128)(2,1)S(1)} %add_convert_fusion), channel_id=1, source_target_pairs={{0,6},{1,7},{2,4},{3,5},{4,2},{5,3},{6,0},{7,1},{8,14},{9,15},{10,... | collective-permute-start | bytes 589832 | tf_op jit(solution)/shard_map/ppermute | solution.py:26
  39.7 4.9 %collective-permute-done.13.refs_2_ = bf16[768,128]{1,0:T(8,128)(2,1)S(1)} collective-permute-done((bf16[768,128]{1,0:T(8,128)(2,1)S(1)}, bf16[768,128]{1,0:T(8,128)(2,1)S(1)}, u32[]{:S(2)}, u32[]{:S(2)}) %collective-permute-start.13) | collective-permute-done | bytes 196640 | tf_op jit(solution)/shard_map/ppermute | solution.py:26
  44.6 3.2 %collective-permute-done.11.refs_1_ = bf16[768,128]{1,0:T(8,128)(2,1)S(1)} collective-permute-done((bf16[768,128]{1,0:T(8,128)(2,1)S(1)}, bf16[768,128]{1,0:T(8,128)(2,1)S(1)}, u32[]{:S(2)}, u32[]{:S(2)}) %collective-permute-start.11) | collective-permute-done | bytes 196640 | tf_op jit(solution)/shard_map/ppermute | solution.py:26
  48.1 1.6 %collective-permute-start.14 = (bf16[192,128]{1,0:T(8,128)(2,1)S(1)}, bf16[192,128]{1,0:T(8,128)(2,1)}, u32[]{:S(2)}, u32[]{:S(2)}) collective-permute-start(bf16[192,128]{1,0:T(8,128)(2,1)S(1)} %get-tuple-element.54), channel_id=1, source_target_pairs={{0,8},{8,0},{16,24},{24,16},{1,9},{9,1},{17,25},{25,17},{2,10},{10... | collective-permute-start | bytes 147464 | tf_op jit(solution)/shard_map/ppermute | solution.py:26
  49.8 2.6 %collective-permute-start.15 = (bf16[192,128]{1,0:T(8,128)(2,1)S(1)}, bf16[192,128]{1,0:T(8,128)(2,1)}, u32[]{:S(2)}, u32[]{:S(2)}) collective-permute-start(bf16[192,128]{1,0:T(8,128)(2,1)S(1)} %get-tuple-element.55), channel_id=1, source_target_pairs={{0,16},{8,24},{16,0},{24,8},{1,17},{9,25},{17,1},{25,9},{2,18},{10... | collective-permute-start | bytes 147464 | tf_op jit(solution)/shard_map/ppermute | solution.py:26
  52.6 3.3 %collective-permute-done.15 = bf16[192,128]{1,0:T(8,128)(2,1)} collective-permute-done((bf16[192,128]{1,0:T(8,128)(2,1)S(1)}, bf16[192,128]{1,0:T(8,128)(2,1)}, u32[]{:S(2)}, u32[]{:S(2)}) %collective-permute-start.15) | collective-permute-done | bytes 49184 | tf_op jit(solution)/shard_map/ppermute | solution.py:26
  55.9 2.5 %collective-permute-done.16 = bf16[192,128]{1,0:T(8,128)(2,1)} collective-permute-done((bf16[192,128]{1,0:T(8,128)(2,1)S(1)}, bf16[192,128]{1,0:T(8,128)(2,1)}, u32[]{:S(2)}, u32[]{:S(2)}) %collective-permute-start.16) | collective-permute-done | bytes 49184 | tf_op jit(solution)/shard_map/ppermute | solution.py:26
  60.6 3.0 %collective-permute-start.19 = (bf16[192,128]{1,0:T(8,128)(2,1)S(1)}, bf16[192,128]{1,0:T(8,128)(2,1)S(1)}, u32[]{:S(2)}, u32[]{:S(2)}) collective-permute-start(bf16[192,128]{1,0:T(8,128)(2,1)S(1)} %add_convert_fusion.3.refs_0_), channel_id=1, source_target_pairs={{0,24},{8,16},{16,8},{24,0},{1,25},{9,17},{17,9},{25,1},{2,26},{10... | collective-permute-start | bytes 147464 | tf_op jit(solution)/shard_map/ppermute | solution.py:26
  64.4 2.1 %collective-permute-done.19.refs_3_ = bf16[192,128]{1,0:T(8,128)(2,1)S(1)} collective-permute-done((bf16[192,128]{1,0:T(8,128)(2,1)S(1)}, bf16[192,128]{1,0:T(8,128)(2,1)S(1)}, u32[]{:S(2)}, u32[]{:S(2)}) %collective-permute-start.19) | collective-permute-done | bytes 49184 | tf_op jit(solution)/shard_map/ppermute | solution.py:26
  69.5 1.4 %collective-permute-start.25 = (bf16[768,128]{1,0:T(8,128)(2,1)S(1)}, bf16[768,128]{1,0:T(8,128)(2,1)S(1)}, u32[]{:S(2)}, u32[]{:S(2)}) collective-permute-start(bf16[768,128]{1,0:T(8,128)(2,1)S(1)} %get-tuple-element.57.refs_0_), channel_id=1, source_target_pairs={{0,6},{1,7},{2,4},{3,5},{4,2},{5,3},{6,0},{7,1},{8,14},{9,15},{10,... | collective-permute-start | bytes 589832 | tf_op jit(solution)/shard_map/ppermute | solution.py:26
  71.0 2.7 %collective-permute-done.21.refs_2_ = bf16[768,128]{1,0:T(8,128)(2,1)S(1)} collective-permute-done((bf16[768,128]{1,0:T(8,128)(2,1)S(1)}, bf16[768,128]{1,0:T(8,128)(2,1)S(1)}, u32[]{:S(2)}, u32[]{:S(2)}) %collective-permute-start.21) | collective-permute-done | bytes 196640 | tf_op jit(solution)/shard_map/ppermute | solution.py:26
  73.7 3.1 %collective-permute-done.23.refs_4_ = bf16[768,128]{1,0:T(8,128)(2,1)S(1)} collective-permute-done((bf16[768,128]{1,0:T(8,128)(2,1)S(1)}, bf16[768,128]{1,0:T(8,128)(2,1)S(1)}, u32[]{:S(2)}, u32[]{:S(2)}) %collective-permute-start.23) | collective-permute-done | bytes 196640 | tf_op jit(solution)/shard_map/ppermute | solution.py:26
  77.3 1.4 %copy-done.4 = bf16[1024,768]{1,0:T(8,128)(2,1)S(1)} copy-done((bf16[1024,768]{1,0:T(8,128)(2,1)S(1)}, bf16[1024,768]{1,0:T(8,128)(2,1)}, u32[]{:S(2)}) %copy-start.4) | copy-done | bytes 1572888
  79.9 5.2 %shard_map.95 = f32[1024,768]{1,0:T(8,128)} custom-call(bf16[1024,1024]{1,0:T(8,128)(2,1)S(1)} %copy-done.2, bf16[1024,768]{1,0:T(8,128)(2,1)S(1)} %copy-done.4, bf16[768,768]{1,0:T(8,128)(2,1)S(1)} %copy-done.8), custom_call_target="tpu_custom_call" | custom-call | flops 2818572288 | bytes 9000000 | tf_op jit(solution)/shard_map/pallas_call | solution.py:175
  85.2 1.6 %copy.15 = f32[128,192]{0,1:T(8,128)} copy(f32[128,192]{1,0:T(8,128)} %copy-done.6) | data formatting | bytes 196608
  88.3 4.2 %shard_map.99 = f32[768,768]{1,0:T(8,128)} custom-call(s32[1]{0:T(128)} %bitcast.4.me_ref, bf16[768,128]{1,0:T(8,128)(2,1)S(1)} %get-tuple-element.57.refs_0_, bf16[768,128]{1,0:T(8,128)(2,1)S(1)} %collective-permute-done.20.refs_1_, bf16[768,128]{1,0:T(8,128)(2,1)S(1)} %collective-permute-done.21.refs_2_, ...), custom_call_target="tpu_custom_call" | custom-call | flops 1207959552 | bytes 6000000 | tf_op jit(solution)/shard_map/pallas_call | solution.py:30
  (79 shorter events, 22.4 us)
Async XLA Ops:
  3.1 9.3 %collective-permute-start.1 = (bf16[144,768]{1,0:T(8,128)(2,1)S(1)}, bf16[144,768]{1,0:T(8,128)(2,1)S(1)}, u32[]{:S(2)}, u32[]{:S(2)}) collective-permute-start(bf16[144,768]{1,0:T(8,128)(2,1)S(1)} %pad_maximum_fusion.refs_0_), channel_id=1, source_target_pairs={{0,2},{1,3},{2,0},{3,1},{4,6},{5,7},{6,4},{7,5},{8,10},{9,11},{10,... | collective-permute-start | bytes 663560 | tf_op jit(solution)/shard_map/ppermute | solution.py:26
  6.1 11.6 %collective-permute-start.3 = (bf16[144,768]{1,0:T(8,128)(2,1)S(1)}, bf16[144,768]{1,0:T(8,128)(2,1)S(1)}, u32[]{:S(2)}, u32[]{:S(2)}) collective-permute-start(bf16[144,768]{1,0:T(8,128)(2,1)S(1)} %pad_maximum_fusion.refs_0_), channel_id=1, source_target_pairs={{0,4},{1,5},{2,6},{3,7},{4,0},{5,1},{6,2},{7,3},{8,12},{9,13},{10,... | collective-permute-start | bytes 663560 | tf_op jit(solution)/shard_map/ppermute | solution.py:26
  7.6 10.1 %collective-permute-start.5 = (bf16[144,768]{1,0:T(8,128)(2,1)S(1)}, bf16[144,768]{1,0:T(8,128)(2,1)}, u32[]{:S(2)}, u32[]{:S(2)}) collective-permute-start(bf16[144,768]{1,0:T(8,128)(2,1)S(1)} %pad_maximum_fusion.refs_0_), channel_id=1, source_target_pairs={{0,6},{1,7},{2,4},{3,5},{4,2},{5,3},{6,0},{7,1},{8,14},{9,15},{10,... | collective-permute-start | bytes 663560 | tf_op jit(solution)/shard_map/ppermute | solution.py:26
  7.6 13.4 %collective-permute-start = (bf16[144,768]{1,0:T(8,128)(2,1)S(1)}, bf16[144,768]{1,0:T(8,128)(2,1)}, u32[]{:S(2)}, u32[]{:S(2)}) collective-permute-start(bf16[144,768]{1,0:T(8,128)(2,1)S(1)} %pad_maximum_fusion.refs_0_), channel_id=1, source_target_pairs={{0,1},{1,0},{2,3},{3,2},{4,5},{5,4},{6,7},{7,6},{8,9},{9,8},{10,11... | collective-permute-start | bytes 663560 | tf_op jit(solution)/shard_map/ppermute | solution.py:26
  12.3 8.7 %collective-permute-start.2 = (bf16[144,768]{1,0:T(8,128)(2,1)S(1)}, bf16[144,768]{1,0:T(8,128)(2,1)S(1)}, u32[]{:S(2)}, u32[]{:S(2)}) collective-permute-start(bf16[144,768]{1,0:T(8,128)(2,1)S(1)} %collective-permute-done.1.refs_2_), channel_id=1, source_target_pairs={{0,1},{1,0},{2,3},{3,2},{4,5},{5,4},{6,7},{7,6},{8,9},{9,8},{10,11... | collective-permute-start | bytes 663560 | tf_op jit(solution)/shard_map/ppermute | solution.py:26
  32.2 5.2 %collective-permute-start.10 = (bf16[768,128]{1,0:T(8,128)(2,1)}, bf16[768,128]{1,0:T(8,128)(2,1)S(1)}, u32[]{:S(2)}, u32[]{:S(2)}) collective-permute-start(bf16[768,128]{1,0:T(8,128)(2,1)} %copy-done.11), channel_id=1, source_target_pairs={{0,1},{1,0},{2,3},{3,2},{4,5},{5,4},{6,7},{7,6},{8,9},{9,8},{10,11... | collective-permute-start | bytes 589832 | tf_op jit(solution)/shard_map/ppermute | solution.py:26
  32.7 5.7 %collective-permute-start.8 = (bf16[768,128]{1,0:T(8,128)(2,1)}, bf16[768,128]{1,0:T(8,128)(2,1)S(1)}, u32[]{:S(2)}, u32[]{:S(2)}) collective-permute-start(bf16[768,128]{1,0:T(8,128)(2,1)} %copy-done.10), channel_id=1, source_target_pairs={{0,1},{1,0},{2,3},{3,2},{4,5},{5,4},{6,7},{7,6},{8,9},{9,8},{10,11... | collective-permute-start | bytes 589832 | tf_op jit(solution)/shard_map/ppermute | solution.py:26
  32.7 6.9 %collective-permute-start.7 = (bf16[768,128]{1,0:T(8,128)(2,1)}, bf16[768,128]{1,0:T(8,128)(2,1)S(1)}, u32[]{:S(2)}, u32[]{:S(2)}) collective-permute-start(bf16[768,128]{1,0:T(8,128)(2,1)} %copy-done.9), channel_id=1, source_target_pairs={{0,1},{1,0},{2,3},{3,2},{4,5},{5,4},{6,7},{7,6},{8,9},{9,8},{10,11... | collective-permute-start | bytes 589832 | tf_op jit(solution)/shard_map/ppermute | solution.py:26
  35.9 8.8 %collective-permute-start.13 = (bf16[768,128]{1,0:T(8,128)(2,1)S(1)}, bf16[768,128]{1,0:T(8,128)(2,1)S(1)}, u32[]{:S(2)}, u32[]{:S(2)}) collective-permute-start(bf16[768,128]{1,0:T(8,128)(2,1)S(1)} %add_convert_fusion), channel_id=1, source_target_pairs={{0,6},{1,7},{2,4},{3,5},{4,2},{5,3},{6,0},{7,1},{8,14},{9,15},{10,... | collective-permute-start | bytes 589832 | tf_op jit(solution)/shard_map/ppermute | solution.py:26
  37.5 10.4 %collective-permute-start.11 = (bf16[768,128]{1,0:T(8,128)(2,1)S(1)}, bf16[768,128]{1,0:T(8,128)(2,1)S(1)}, u32[]{:S(2)}, u32[]{:S(2)}) collective-permute-start(bf16[768,128]{1,0:T(8,128)(2,1)S(1)} %add_convert_fusion.1), channel_id=1, source_target_pairs={{0,4},{1,5},{2,6},{3,7},{4,0},{5,1},{6,2},{7,3},{8,12},{9,13},{10,... | collective-permute-start | bytes 589832 | tf_op jit(solution)/shard_map/ppermute | solution.py:26
  38.4 9.6 %collective-permute-start.9 = (bf16[768,128]{1,0:T(8,128)(2,1)S(1)}, bf16[768,128]{1,0:T(8,128)(2,1)S(1)}, u32[]{:S(2)}, u32[]{:S(2)}) collective-permute-start(bf16[768,128]{1,0:T(8,128)(2,1)S(1)} %add_convert_fusion.2), channel_id=1, source_target_pairs={{0,2},{1,3},{2,0},{3,1},{4,6},{5,7},{6,4},{7,5},{8,10},{9,11},{10,... | collective-permute-start | bytes 589832 | tf_op jit(solution)/shard_map/ppermute | solution.py:26
  48.1 4.5 %collective-permute-start.14 = (bf16[192,128]{1,0:T(8,128)(2,1)S(1)}, bf16[192,128]{1,0:T(8,128)(2,1)}, u32[]{:S(2)}, u32[]{:S(2)}) collective-permute-start(bf16[192,128]{1,0:T(8,128)(2,1)S(1)} %get-tuple-element.54), channel_id=1, source_target_pairs={{0,8},{8,0},{16,24},{24,16},{1,9},{9,1},{17,25},{25,17},{2,10},{10... | collective-permute-start | bytes 147464 | tf_op jit(solution)/shard_map/ppermute | solution.py:26
  49.8 6.1 %collective-permute-start.15 = (bf16[192,128]{1,0:T(8,128)(2,1)S(1)}, bf16[192,128]{1,0:T(8,128)(2,1)}, u32[]{:S(2)}, u32[]{:S(2)}) collective-permute-start(bf16[192,128]{1,0:T(8,128)(2,1)S(1)} %get-tuple-element.55), channel_id=1, source_target_pairs={{0,16},{8,24},{16,0},{24,8},{1,17},{9,25},{17,1},{25,9},{2,18},{10... | collective-permute-start | bytes 147464 | tf_op jit(solution)/shard_map/ppermute | solution.py:26
  52.3 6.0 %collective-permute-start.16 = (bf16[192,128]{1,0:T(8,128)(2,1)S(1)}, bf16[192,128]{1,0:T(8,128)(2,1)}, u32[]{:S(2)}, u32[]{:S(2)}) collective-permute-start(bf16[192,128]{1,0:T(8,128)(2,1)S(1)} %get-tuple-element.56), channel_id=1, source_target_pairs={{0,24},{8,16},{16,8},{24,0},{1,25},{9,17},{17,9},{25,1},{2,26},{10... | collective-permute-start | bytes 147464 | tf_op jit(solution)/shard_map/ppermute | solution.py:26
  59.2 4.6 %collective-permute-start.17 = (bf16[192,128]{1,0:T(8,128)(2,1)S(1)}, bf16[192,128]{1,0:T(8,128)(2,1)S(1)}, u32[]{:S(2)}, u32[]{:S(2)}) collective-permute-start(bf16[192,128]{1,0:T(8,128)(2,1)S(1)} %add_convert_fusion.3.refs_0_), channel_id=1, source_target_pairs={{0,8},{8,0},{16,24},{24,16},{1,9},{9,1},{17,25},{25,17},{2,10},{10... | collective-permute-start | bytes 147464 | tf_op jit(solution)/shard_map/ppermute | solution.py:26
  59.3 5.1 %collective-permute-start.18 = (bf16[192,128]{1,0:T(8,128)(2,1)S(1)}, bf16[192,128]{1,0:T(8,128)(2,1)S(1)}, u32[]{:S(2)}, u32[]{:S(2)}) collective-permute-start(bf16[192,128]{1,0:T(8,128)(2,1)S(1)} %add_convert_fusion.3.refs_0_), channel_id=1, source_target_pairs={{0,16},{8,24},{16,0},{24,8},{1,17},{9,25},{17,1},{25,9},{2,18},{10... | collective-permute-start | bytes 147464 | tf_op jit(solution)/shard_map/ppermute | solution.py:26
  60.6 5.9 %collective-permute-start.19 = (bf16[192,128]{1,0:T(8,128)(2,1)S(1)}, bf16[192,128]{1,0:T(8,128)(2,1)S(1)}, u32[]{:S(2)}, u32[]{:S(2)}) collective-permute-start(bf16[192,128]{1,0:T(8,128)(2,1)S(1)} %add_convert_fusion.3.refs_0_), channel_id=1, source_target_pairs={{0,24},{8,16},{16,8},{24,0},{1,25},{9,17},{17,9},{25,1},{2,26},{10... | collective-permute-start | bytes 147464 | tf_op jit(solution)/shard_map/ppermute | solution.py:26
  67.5 6.2 %collective-permute-start.21 = (bf16[768,128]{1,0:T(8,128)(2,1)S(1)}, bf16[768,128]{1,0:T(8,128)(2,1)S(1)}, u32[]{:S(2)}, u32[]{:S(2)}) collective-permute-start(bf16[768,128]{1,0:T(8,128)(2,1)S(1)} %get-tuple-element.57.refs_0_), channel_id=1, source_target_pairs={{0,2},{1,3},{2,0},{3,1},{4,6},{5,7},{6,4},{7,5},{8,10},{9,11},{10,... | collective-permute-start | bytes 589832 | tf_op jit(solution)/shard_map/ppermute | solution.py:26
  68.8 7.9 %collective-permute-start.23 = (bf16[768,128]{1,0:T(8,128)(2,1)S(1)}, bf16[768,128]{1,0:T(8,128)(2,1)S(1)}, u32[]{:S(2)}, u32[]{:S(2)}) collective-permute-start(bf16[768,128]{1,0:T(8,128)(2,1)S(1)} %get-tuple-element.57.refs_0_), channel_id=1, source_target_pairs={{0,4},{1,5},{2,6},{3,7},{4,0},{5,1},{6,2},{7,3},{8,12},{9,13},{10,... | collective-permute-start | bytes 589832 | tf_op jit(solution)/shard_map/ppermute | solution.py:26
  69.5 7.2 %collective-permute-start.25 = (bf16[768,128]{1,0:T(8,128)(2,1)S(1)}, bf16[768,128]{1,0:T(8,128)(2,1)S(1)}, u32[]{:S(2)}, u32[]{:S(2)}) collective-permute-start(bf16[768,128]{1,0:T(8,128)(2,1)S(1)} %get-tuple-element.57.refs_0_), channel_id=1, source_target_pairs={{0,6},{1,7},{2,4},{3,5},{4,2},{5,3},{6,0},{7,1},{8,14},{9,15},{10,... | collective-permute-start | bytes 589832 | tf_op jit(solution)/shard_map/ppermute | solution.py:26
  71.0 15.9 %collective-permute-start.20 = (bf16[768,128]{1,0:T(8,128)(2,1)S(1)}, bf16[768,128]{1,0:T(8,128)(2,1)S(1)}, u32[]{:S(2)}, u32[]{:S(2)}) collective-permute-start(bf16[768,128]{1,0:T(8,128)(2,1)S(1)} %get-tuple-element.57.refs_0_), channel_id=1, source_target_pairs={{0,1},{1,0},{2,3},{3,2},{4,5},{5,4},{6,7},{7,6},{8,9},{9,8},{10,11... | collective-permute-start | bytes 589832 | tf_op jit(solution)/shard_map/ppermute | solution.py:26
  73.7 13.2 %collective-permute-start.22 = (bf16[768,128]{1,0:T(8,128)(2,1)S(1)}, bf16[768,128]{1,0:T(8,128)(2,1)S(1)}, u32[]{:S(2)}, u32[]{:S(2)}) collective-permute-start(bf16[768,128]{1,0:T(8,128)(2,1)S(1)} %collective-permute-done.21.refs_2_), channel_id=1, source_target_pairs={{0,1},{1,0},{2,3},{3,2},{4,5},{5,4},{6,7},{7,6},{8,9},{9,8},{10,11... | collective-permute-start | bytes 589832 | tf_op jit(solution)/shard_map/ppermute | solution.py:26
  76.7 10.1 %collective-permute-start.24 = (bf16[768,128]{1,0:T(8,128)(2,1)S(1)}, bf16[768,128]{1,0:T(8,128)(2,1)S(1)}, u32[]{:S(2)}, u32[]{:S(2)}) collective-permute-start(bf16[768,128]{1,0:T(8,128)(2,1)S(1)} %collective-permute-done.23.refs_4_), channel_id=1, source_target_pairs={{0,1},{1,0},{2,3},{3,2},{4,5},{5,4},{6,7},{7,6},{8,9},{9,8},{10,11... | collective-permute-start | bytes 589832 | tf_op jit(solution)/shard_map/ppermute | solution.py:26
  76.8 10.1 %collective-permute-start.26 = (bf16[768,128]{1,0:T(8,128)(2,1)S(1)}, bf16[768,128]{1,0:T(8,128)(2,1)}, u32[]{:S(2)}, u32[]{:S(2)}) collective-permute-start(bf16[768,128]{1,0:T(8,128)(2,1)S(1)} %collective-permute-done.25.refs_6_), channel_id=1, source_target_pairs={{0,1},{1,0},{2,3},{3,2},{4,5},{5,4},{6,7},{7,6},{8,9},{9,8},{10,11... | collective-permute-start | bytes 589832 | tf_op jit(solution)/shard_map/ppermute | solution.py:26
  (16 other events, 79.3 us)

commit v2 on v1

v2 whole, which is shorter than its diff:
```python
import functools

import jax
import jax.numpy as jnp
from jax import lax
from jax.experimental import pallas as pl
from jax.experimental.pallas import tpu as pltpu
from jax.sharding import PartitionSpec as P

BF16 = jnp.bfloat16
F32 = jnp.float32
VMEM = pl.BlockSpec(memory_space=pltpu.VMEM)
SMEM = pl.BlockSpec(memory_space=pltpu.SMEM)
TAIL = 16
MIB = 1024 * 1024
NN = (((1,), (0,)), ((), ()))
NT = (((1,), (1,)), ((), ()))
TN = (((0,), (0,)), ((), ()))


def dot(left, right, dims):
    return lax.dot_general(left, right, dims, preferred_element_type=F32)


def shape(dims, dtype):
    return jax.ShapeDtypeStruct(dims, dtype)


def call(kernel, outs, args, scalars=(), scratch=(), vmem=8, flops=0, nbytes=0):
    return pl.pallas_call(
        kernel,
        out_shape=outs,
        in_specs=[SMEM] * len(scalars) + [VMEM] * len(args),
        out_specs=[VMEM] * len(outs),
        scratch_shapes=list(scratch),
        compiler_params=pltpu.CompilerParams(vmem_limit_bytes=vmem * MIB),
        cost_estimate=pl.CostEstimate(flops=flops, bytes_accessed=nbytes, transcendentals=0),
    )(*scalars, *args)


def stage_distance(owner, stage, stages):
    forward, backward = 2 << stage, 2 << (stages - 1 - stage)
    return forward + (owner & 1) * (backward - forward)


def chip_swap(value, stage, stages):
    owners = lax.axis_size("label")
    return lax.ppermute(
        value, "label", [(i, i ^ stage_distance(i, stage, stages)) for i in range(owners)]
    )


def core_swap(value):
    owners = lax.axis_size("label")
    return lax.ppermute(value, "label", [(i, i ^ 1) for i in range(owners)])


def plane_swap(value, distance):
    planes = lax.axis_size("dp")
    return lax.ppermute(value, "dp", [(i, i ^ distance) for i in range(planes)])


def slot_of_cluster(cluster, me, stages):
    offset = cluster ^ me
    side = me ^ (offset & 1)
    chips = sum(
        (jnp.where((offset & stage_distance(side, stage, stages)) != 0, 1, 0) << stage)
        for stage in range(stages)
    )
    return chips + (offset & 1) * (1 << stages)


def cluster_of_slot(slot, me, stages):
    side = me ^ (slot >> stages)
    return side ^ sum(
        ((slot >> stage) & 1) * stage_distance(side, stage, stages) for stage in range(stages)
    )


def payload_kernel(num_ref, den_ref, rows_ref, out_ref):
    size, width = rows_ref.shape
    out_ref[:size, :] = rows_ref[...]
    row = lax.broadcasted_iota(jnp.int32, (TAIL, size), 0)
    both = jnp.where(row == 0, num_ref[...], den_ref[...])
    out_ref[size:, :size] = both.astype(F32).astype(BF16)
    out_ref[size:, size:] = jnp.zeros((TAIL, width - size), BF16)


def score_kernel(owners, beam, block, size, slots_ref, hidden_ref, wanted_ref, enc_t_ref, *refs):
    payloads, refs = refs[:owners], refs[owners:]
    grads_ref, weights_ref, first_ref, second_ref, scale_ref, logits_ref = refs
    samples = hidden_ref.shape[0]
    for slot in range(owners):
        rows = pl.ds(slot * size, size)
        weights_ref[rows, :] = payloads[slot][:size, :]
        tail = payloads[slot][size : size + TAIL, :size].astype(F32)
        ratio = tail[0:1, :] / tail[1:2, :]
        scale_ref[rows, :] = jnp.broadcast_to(ratio, (block, size)).T / block
    grads_ref[...] = jnp.zeros_like(grads_ref)
    label_iota = lax.broadcasted_iota(jnp.int32, (size, block), 0)
    tile = min(2 * block, samples)
    for start in range(0, samples, tile):
        logits_ref[...] = dot(weights_ref[...], hidden_ref[start : start + tile, :], NT)
        for low in range(start, start + tile, block):
            for beam_slot in range(beam):
                slot = slots_ref[(low // block) * beam + beam_slot]
                rows = pl.ds(pl.multiple_of(slot * size, size), size)
                logits = logits_ref[rows, low - start : low - start + block]
                labels = label_iota + beam_slot * size
                target = labels == wanted_ref[0:1, low : low + block]
                for column in range(1, wanted_ref.shape[0]):
                    target = target | (labels == wanted_ref[column : column + 1, low : low + block])
                share = jax.nn.sigmoid(logits) - jnp.where(target, 1.0, 0.0)
                grads_ref[rows, low : low + block] = (scale_ref[rows, :] * share).astype(BF16)
    half = owners // 2
    outer = dot(enc_t_ref[...], grads_ref[half * size :, :], NT)
    for slot in range(half):
        part = outer[:, slot * size : (slot + 1) * size].astype(BF16)
        if slot % 2:
            first_ref[slot // 2] = part
        else:
            second_ref[slot // 2] = part


def keep_kernel(owners, size, enc_t_ref, grads_ref, *kept):
    outer = dot(enc_t_ref[...], grads_ref[: owners // 2 * size, :], NT)
    for slot in range(owners // 2):
        kept[slot][...] = outer[:, slot * size : (slot + 1) * size]


def hidden_kernel(grads_ref, weights_ref, out_ref):
    out_ref[...] = dot(grads_ref[...], weights_ref[...], TN).astype(BF16)


def enc_kernel(grad_hidden_ref, proj_ref, out_ref):
    out_ref[...] = dot(grad_hidden_ref[...], proj_ref[...], NT)


def head_kernel(count, z_ref, *refs):
    parts, (proj_ref, out_ref) = refs[:count], refs[count:]
    depth = parts[0].shape[0]
    total = jnp.zeros(out_ref.shape, F32)
    for r in range(count):
        start = pl.multiple_of((z_ref[0] ^ r) * depth, depth)
        total = total + dot(proj_ref[pl.ds(start, depth), :], parts[r][...], TN)
    out_ref[...] = total


def proj_kernel(owners, size, count, me_ref, z_ref, *refs):
    parts, refs = refs[: owners * count], refs[owners * count :]
    weights_ref, out_ref, outer_ref, rows_ref = refs
    stages = owners.bit_length() - 2
    depth = parts[0].shape[0]
    for slot in range(owners):
        cluster = cluster_of_slot(slot, me_ref[0], stages)
        start = pl.multiple_of(cluster * size, size)
        rows_ref[pl.ds(start, size), :] = weights_ref[slot * size : (slot + 1) * size, :]
        for r in range(count):
            outer_ref[r * depth : (r + 1) * depth, pl.ds(start, size)] = parts[slot * count + r][...]
    for r in range(count):
        start = pl.multiple_of((z_ref[0] ^ r) * depth, depth)
        rows = outer_ref[r * depth : (r + 1) * depth, :]
        out_ref[pl.ds(start, depth), :] = dot(rows, rows_ref[...], NN)


def shards(enc, proj, head_weight, shortlist, positives, weight_num, weight_den):
    owners, planes = lax.axis_size("label"), lax.axis_size("dp")
    stages = owners.bit_length() - 2
    chips = 1 << stages
    row_blocks = max(1, planes // 2)
    me = lax.axis_index("label").astype(jnp.int32)
    z = lax.axis_index("dp").astype(jnp.int32)
    z_low = z & (row_blocks - 1)
    blocks, beam = shortlist.shape
    samples, width = enc.shape
    block = samples // blocks
    size = head_weight.shape[0]
    labels = owners * size
    depth = width // row_blocks
    me_s, z_s = me.reshape(1), z_low.reshape(1)

    (payload,) = call(
        payload_kernel,
        [shape((size + TAIL, width), BF16)],
        [weight_num.reshape(1, size), weight_den.reshape(1, size), head_weight],
        nbytes=400_000,
    )
    got = {0: payload}
    for stage in reversed(range(stages)):
        for slot in list(got):
            got[slot | (1 << stage)] = chip_swap(got[slot], stage, stages)
    hidden = dot(enc, proj, NN).astype(BF16)
    enc_blocks = enc.T.reshape(row_blocks, depth, samples)
    enc_t = jnp.concatenate(
        [lax.dynamic_index_in_dim(enc_blocks, z_low ^ r, 0, False) for r in range(row_blocks)], axis=0
    )
    for slot in range(chips):
        got[slot + chips] = core_swap(got[slot])
    slots = slot_of_cluster(shortlist, me, stages).astype(jnp.int32).reshape(-1)

    group = shape((chips // 2, width, size), BF16)
    grads, weights, send_first, send_second = call(
        functools.partial(score_kernel, owners, beam, block, size),
        [shape((labels, samples), BF16), shape((labels, width), BF16), group, group],
        [hidden, positives.T, enc_t] + [got[slot] for slot in range(owners)],
        scalars=[slots],
        scratch=[pltpu.VMEM((labels, block), F32), pltpu.VMEM((labels, min(2 * block, samples)), F32)],
        vmem=16,
        flops=4 * samples * labels * width,
        nbytes=12_000_000,
    )
    from_core = [core_swap(send_first), core_swap(send_second)]
    kept = call(
        functools.partial(keep_kernel, owners, size),
        [shape((width, size), F32)] * chips,
        [enc_t, grads],
        flops=samples * labels * width,
        nbytes=4_000_000,
    )
    sums = {}
    for slot in sorted(range(chips), key=lambda s: -(s & 1)):
        sums[slot] = kept[slot] + from_core[1 - slot % 2][slot // 2].astype(F32)
    for stage in range(stages):
        bit = 1 << stage
        moving = sorted((s for s in sums if s & bit), key=lambda s: -s)
        for slot in moving:
            if len(moving) > 1 or row_blocks == 1:
                recv = chip_swap(sums[slot].astype(BF16), stage, stages).astype(F32)
            else:
                cut = width // 2
                upper = chip_swap(sums[slot][cut:].astype(BF16), stage, stages)
                lower = chip_swap(sums[slot][:cut].astype(BF16), stage, stages)
                recv = jnp.concatenate([lower, upper], axis=0).astype(F32)
            sums[slot ^ bit] = sums[slot ^ bit] + recv
            del sums[slot]
    total = sums[0]
    (grad_hidden,) = call(
        hidden_kernel,
        [shape((samples, width), BF16)],
        [grads, weights],
        vmem=16,
        flops=2 * samples * width * labels,
        nbytes=5_000_000,
    )
    tile = min(256, samples)
    grad_enc = pl.pallas_call(
        enc_kernel,
        grid=(samples // tile,),
        out_shape=shape((samples, width), F32),
        in_specs=[
            pl.BlockSpec((tile, width), lambda i: (i, 0)),
            pl.BlockSpec((width, width), lambda i: (0, 0)),
        ],
        out_specs=pl.BlockSpec((tile, width), lambda i: (i, 0)),
        compiler_params=pltpu.CompilerParams(vmem_limit_bytes=12 * MIB),
        cost_estimate=pl.CostEstimate(
            flops=2 * samples * width * width, bytes_accessed=6_000_000, transcendentals=0
        ),
    )(grad_hidden, proj)

    span = row_blocks
    while span > 1:
        cut = span // 2 * depth
        total = total[:cut] + plane_swap(total[cut:].astype(BF16), span // 2).astype(F32)
        span //= 2
    total = total.astype(BF16)
    if planes > 1:
        other = plane_swap(total, planes // 2)
        total = (total.astype(F32) + other.astype(F32)).astype(BF16)
    parts = {0: total}
    span = 1
    while span < row_blocks:
        for r in range(span):
            parts[r + span] = plane_swap(parts[r], span)
        span *= 2

    proj_slice = lax.dynamic_slice_in_dim(proj, z * (width // planes), width // planes, 1)
    (grad_head,) = call(
        functools.partial(head_kernel, row_blocks),
        [shape((width // planes, size), F32)],
        [parts[r] for r in range(row_blocks)] + [proj_slice],
        scalars=[z_s],
        flops=2 * size * width * width // planes,
        nbytes=1_000_000,
    )
    have = {(0, r): parts[r] for r in range(row_blocks)}
    for r in range(row_blocks):
        for stage in reversed(range(stages)):
            for slot in [s for s, at in list(have) if at == r]:
                have[slot | (1 << stage), r] = chip_swap(have[slot, r], stage, stages)
        for slot in range(chips):
            have[slot + chips, r] = core_swap(have[slot, r])
    (grad_proj,) = call(
        functools.partial(proj_kernel, owners, size, row_blocks),
        [shape((width, width), F32)],
        [have[slot, r] for slot in range(owners) for r in range(row_blocks)] + [weights],
        scalars=[me_s, z_s],
        scratch=[pltpu.VMEM((width, labels), BF16), pltpu.VMEM((labels, width), BF16)],
        vmem=20,
        flops=2 * labels * width * width,
        nbytes=6_000_000,
    )
    return (grad_enc, grad_proj, grad_head.T)


def solution(mesh):
    placed = (
        P(("dp", "label"), None),
        P(),
        P("label", None),
        P(("dp", "label"), None),
        P(("dp", "label"), None),
        P("label"),
        P("label"),
    )
    return jax.shard_map(
        shards,
        mesh=mesh,
        in_specs=placed,
        out_specs=(P(("dp", "label"), None), P(), P("label", "dp")),
        check_vma=False,
    )
```

time: 93 us -> 82.4 us (0.89)
  waiting for transfers between devices: 29.9 us -> 22 us
  other arithmetic: 3.98 us -> 1.94 us
  Pallas kernels: 17.5 us -> 15.9 us
  matrix products: 2.79 us -> 4.06 us
    ppermute x27 -> x30, waiting for transfers between devices: 29.9 us -> 22 us  [the longest x13 14.1 us: chip_swap(): lax.ppermute(value, 'label', [(i, i ^ stage_distance(i, stage, stages)) f...]
    unnamed x28 -> x50, local copies, waits for them, and re-layouts: 14.3 us -> 10.2 us
    reshape x1 -> x2, local copies, waits for them, and re-layouts: 0.08 us -> 2.75 us  [the longest x1 2.67 us: shards(): enc_blocks = enc.T.reshape(row_blocks, depth, samples)]
    pallas_call x1, Pallas kernels: 5.24 us -> 3.28 us  [shards(): pl.pallas_call(enc_kernel, grid=(samples // tile,), out_shape=shape((samp...]
    squeeze x0 -> x1, local copies, waits for them, and re-layouts: none -> 1.3 us  [shards(): lax.dynamic_index_in_dim(enc_blocks, z_low ^ r, 0, False)]
    dot_general x1, matrix products: 2.79 us -> 4.06 us  [dot(): return lax.dot_general(left, right, dims, preferred_element_type=F32)]
    another operation x2 -> x1, other arithmetic: 1.32 us -> 0.07 us
    pallas_call x5 -> x6, Pallas kernels: 12.3 us -> 12.6 us  [call(): pl.pallas_call(kernel, out_shape=outs, in_specs=[SMEM] * len(scalars) + [...]
  transfers between devices with their start and end apart: 27 -> 30, of which waited for: 11 -> 10; matrix products, arithmetic and copies ran while one was open for 8% -> 12% of each run, Pallas kernels for 7% -> 9%
where the time goes in v2:
time: 82.4 us; the launch traced here: 81.8 us
  starting transfers between devices  22.6 us (27%)
  waiting for transfers between devices  22 us (27%)
  Pallas kernels  15.9 us (19%)
  local copies, waits for them, and re-layouts  14.5 us (18%)
  matrix products  4.06 us (5%)
  other arithmetic  1.94 us (2%)
  between operations  0.92 us (1%)
    ppermute x13, waiting for transfers between devices, chip_swap(): lax.ppermute(value, 'label', [(i, i ^ stage_distance(i, stage, stages)) f...  14.1 us
    ppermute x13, starting transfers between devices, chip_swap(): lax.ppermute(value, 'label', [(i, i ^ stage_distance(i, stage, stages)) f...  14.1 us
    pallas_call x6, Pallas kernels, call(): pl.pallas_call(kernel, out_shape=outs, in_specs=[SMEM] * len(scalars) + [...  12.6 us
    unnamed x50, local copies, waits for them, and re-layouts  10.2 us
    ppermute x3, waiting for transfers between devices, plane_swap(): return lax.ppermute(value, 'dp', [(i, i ^ distance) for i in range(planes)])  7.59 us
    ppermute x3, starting transfers between devices, plane_swap(): return lax.ppermute(value, 'dp', [(i, i ^ distance) for i in range(planes)])  6.05 us
    dot_general x1, matrix products, dot(): return lax.dot_general(left, right, dims, preferred_element_type=F32)  4.06 us
    pallas_call x1, Pallas kernels, shards(): pl.pallas_call(enc_kernel, grid=(samples // tile,), out_shape=shape((samp...  3.28 us
  transfers between devices with their start and end apart: 30, of which 10 were waited for; matrix products, arithmetic and copies ran while one was open for 12% of the time, Pallas kernels for 9%

profile of v2, /device:TPU:0, one launch (start us, length us, event | category | flops | bytes accessed | tf_op | source)
XLA Modules:
  0.0 81.8 jit_solution(13542397420761309856)
XLA Ops:
  2.9 3.0 %collective-permute-start.1 = (bf16[144,768]{1,0:T(8,128)(2,1)S(1)}, bf16[144,768]{1,0:T(8,128)(2,1)S(1)}, u32[]{:S(2)}, u32[]{:S(2)}) collective-permute-start(bf16[144,768]{1,0:T(8,128)(2,1)S(1)} %shard_map.94.refs_0_), channel_id=1, source_target_pairs={{0,4},{1,3},{2,6},{3,1},{4,0},{5,7},{6,2},{7,5},{8,12},{9,11},{10,... | collective-permute-start | bytes 663560 | tf_op jit(solution)/shard_map/ppermute | solution.py:48
  5.9 1.5 %collective-permute-start = (bf16[144,768]{1,0:T(8,128)(2,1)S(1)}, bf16[144,768]{1,0:T(8,128)(2,1)S(1)}, u32[]{:S(2)}, u32[]{:S(2)}) collective-permute-start(bf16[144,768]{1,0:T(8,128)(2,1)S(1)} %shard_map.94.refs_0_), channel_id=1, source_target_pairs={{0,2},{1,5},{2,0},{3,7},{4,6},{5,1},{6,4},{7,3},{8,10},{9,13},{10,... | collective-permute-start | bytes 663560 | tf_op jit(solution)/shard_map/ppermute | solution.py:48
  7.4 2.7 %copy.16 = bf16[768,1024]{1,0:T(8,128)(2,1)} copy(bf16[768,1024]{0,1:T(8,128)(2,1)} %bitcast.38) | data formatting | bytes 3145728 | tf_op jit(solution)/shard_map/reshape | solution.py:193
  10.1 4.1 %convolution_convert_fusion.hidden_ref = bf16[1024,768]{1,0:T(8,128)(2,1)} fusion(bf16[1024,768]{1,0:T(8,128)(2,1)} %param.7, bf16[768,768]{1,0:T(8,128)(2,1)S(1)} %copy-done), kind=kOutput, calls=%fused_computation | convolution fusion | flops 1208745984 | bytes 4325376 | tf_op jit(solution)/shard_map/dot_general | solution.py:22
  15.3 4.8 %collective-permute-done.2.refs_3_ = bf16[144,768]{1,0:T(8,128)(2,1)S(1)} collective-permute-done((bf16[144,768]{1,0:T(8,128)(2,1)S(1)}, bf16[144,768]{1,0:T(8,128)(2,1)S(1)}, u32[]{:S(2)}, u32[]{:S(2)}) %collective-permute-start.2) | collective-permute-done | bytes 221216 | tf_op jit(solution)/shard_map/ppermute | solution.py:48
  20.1 1.3 %dynamic-slice_bitcast_fusion.1 = (bf16[384,1024]{1,0:T(8,128)(2,1)}, bf16[384,1024]{1,0:T(8,128)(2,1)}) fusion(bf16[2,384,1024]{2,1,0:T(8,128)(2,1)S(1)} %bitcast.37, s32[]{:T(128)S(6)} %select_n.19, s32[]{:T(128)S(6)} %select_n.20), kind=kLoop, calls=%fused_computation.3 | loop fusion | bytes 3145736 | tf_op jit(solution)/shard_map/jit(dynamic_index_in_dim)/squeeze | solution.py:195
  21.6 1.6 %pad_maximum_fusion.enc_t_ref = bf16[768,1024]{1,0:T(8,128)(2,1)S(1)} fusion(bf16[384,1024]{1,0:T(8,128)(2,1)} %get-tuple-element.20, bf16[384,1024]{1,0:T(8,128)(2,1)} %get-tuple-element.19), kind=kLoop, calls=%fused_computation.1 | loop fusion | flops 3145728 | bytes 3145728 | tf_op jit(solution)/shard_map/concatenate | solution.py:194
  29.8 5.4 %shard_map.95 = (bf16[1024,1024]{1,0:T(8,128)(2,1)S(1)}, bf16[1024,768]{1,0:T(8,128)(2,1)S(1)}, bf16[2,768,128]{2,1,0:T(8,128)(2,1)S(1)}, bf16[2,768,128]{2,1,0:T(8,128)(2,1)S(1)}) custom-call(s32[32]{0:T(128)S(1)} %reshape.32.slots_ref, bf16[1024,768]{1,0:T(8,128)(2,1)S(1)} %copy-done.22, s32[8,1024]{1,0:T(8,128)S(1)} %bitcast.36, ...), custom_call_target="tpu_custom_call" | custom-call | flops 3221225472 | bytes 12000000 | tf_op jit(solution)/shard_map/pallas_call | solution.py:30
  37.8 1.5 %collective-permute-start.9 = (bf16[768,128]{1,0:T(8,128)(2,1)S(1)}, bf16[768,128]{1,0:T(8,128)(2,1)S(1)}, u32[]{:S(2)}, u32[]{:S(2)}) collective-permute-start(bf16[768,128]{1,0:T(8,128)(2,1)S(1)} %get-tuple-element.22), channel_id=1, source_target_pairs={{0,2},{1,5},{2,0},{3,7},{4,6},{5,1},{6,4},{7,3},{8,10},{9,13},{10,... | collective-permute-start | bytes 589832 | tf_op jit(solution)/shard_map/ppermute | solution.py:48
  39.3 3.6 %collective-permute-done.10 = bf16[768,128]{1,0:T(8,128)(2,1)S(1)} collective-permute-done((bf16[768,128]{1,0:T(8,128)(2,1)S(1)}, bf16[768,128]{1,0:T(8,128)(2,1)S(1)}, u32[]{:S(2)}, u32[]{:S(2)}) %collective-permute-start.10) | collective-permute-done | bytes 196640 | tf_op jit(solution)/shard_map/ppermute | solution.py:48
  43.6 1.5 %collective-permute-start.12 = (bf16[384,128]{1,0:T(8,128)(2,1)S(1)}, bf16[384,128]{1,0:T(8,128)(2,1)S(1)}, u32[]{:S(2)}, u32[]{:S(2)}) collective-permute-start(bf16[384,128]{1,0:T(8,128)(2,1)S(1)} %get-tuple-element.24), channel_id=1, source_target_pairs={{0,4},{1,3},{2,6},{3,1},{4,0},{5,7},{6,2},{7,5},{8,12},{9,11},{10,... | collective-permute-start | bytes 294920 | tf_op jit(solution)/shard_map/ppermute | solution.py:48
  45.1 2.6 %collective-permute-done.11 = bf16[384,128]{1,0:T(8,128)(2,1)S(1)} collective-permute-done((bf16[384,128]{1,0:T(8,128)(2,1)S(1)}, bf16[384,128]{1,0:T(8,128)(2,1)S(1)}, u32[]{:S(2)}, u32[]{:S(2)}) %collective-permute-start.11) | collective-permute-done | bytes 98336 | tf_op jit(solution)/shard_map/ppermute | solution.py:48
  48.9 1.6 %collective-permute-start.13 = (bf16[384,128]{1,0:T(8,128)(2,1)S(1)}, bf16[384,128]{1,0:T(8,128)(2,1)S(1)}, u32[]{:S(2)}, u32[]{:S(2)}) collective-permute-start(bf16[384,128]{1,0:T(8,128)(2,1)S(1)} %slice.59), channel_id=1, source_target_pairs={{0,8},{8,0},{16,24},{24,16},{1,9},{9,1},{17,25},{25,17},{2,10},{10... | collective-permute-start | bytes 294920 | tf_op jit(solution)/shard_map/ppermute | solution.py:60
  50.5 3.0 %collective-permute-done.13 = bf16[384,128]{1,0:T(8,128)(2,1)S(1)} collective-permute-done((bf16[384,128]{1,0:T(8,128)(2,1)S(1)}, bf16[384,128]{1,0:T(8,128)(2,1)S(1)}, u32[]{:S(2)}, u32[]{:S(2)}) %collective-permute-start.13) | collective-permute-done | bytes 98336 | tf_op jit(solution)/shard_map/ppermute | solution.py:60
  53.6 2.7 %collective-permute-start.14 = (bf16[384,128]{1,0:T(8,128)(2,1)S(1)}, bf16[384,128]{1,0:T(8,128)(2,1)S(1)}, u32[]{:S(2)}, u32[]{:S(2)}) collective-permute-start(bf16[384,128]{1,0:T(8,128)(2,1)S(1)} %fusion.6), channel_id=1, source_target_pairs={{0,16},{8,24},{16,0},{24,8},{1,17},{9,25},{17,1},{25,9},{2,18},{10... | collective-permute-start | bytes 294920 | tf_op jit(solution)/shard_map/ppermute | solution.py:60
  56.3 3.0 %collective-permute-done.14 = bf16[384,128]{1,0:T(8,128)(2,1)S(1)} collective-permute-done((bf16[384,128]{1,0:T(8,128)(2,1)S(1)}, bf16[384,128]{1,0:T(8,128)(2,1)S(1)}, u32[]{:S(2)}, u32[]{:S(2)}) %collective-permute-start.14) | collective-permute-done | bytes 98336 | tf_op jit(solution)/shard_map/ppermute | solution.py:60
  59.3 1.8 %collective-permute-start.15 = (bf16[384,128]{1,0:T(8,128)(2,1)S(1)}, bf16[384,128]{1,0:T(8,128)(2,1)S(1)}, u32[]{:S(2)}, u32[]{:S(2)}) collective-permute-start(bf16[384,128]{1,0:T(8,128)(2,1)S(1)} %add_convert_fusion.refs_0_), channel_id=1, source_target_pairs={{0,8},{8,0},{16,24},{24,16},{1,9},{9,1},{17,25},{25,17},{2,10},{10... | collective-permute-start | bytes 294920 | tf_op jit(solution)/shard_map/ppermute | solution.py:60
  62.4 1.6 %collective-permute-done.15.refs_1_ = bf16[384,128]{1,0:T(8,128)(2,1)S(1)} collective-permute-done((bf16[384,128]{1,0:T(8,128)(2,1)S(1)}, bf16[384,128]{1,0:T(8,128)(2,1)S(1)}, u32[]{:S(2)}, u32[]{:S(2)}) %collective-permute-start.15) | collective-permute-done | bytes 98336 | tf_op jit(solution)/shard_map/ppermute | solution.py:60
  64.0 2.1 %collective-permute-start.19 = (bf16[384,128]{1,0:T(8,128)(2,1)S(1)}, bf16[384,128]{1,0:T(8,128)(2,1)S(1)}, u32[]{:S(2)}, u32[]{:S(2)}) collective-permute-start(bf16[384,128]{1,0:T(8,128)(2,1)S(1)} %collective-permute-done.15.refs_1_), channel_id=1, source_target_pairs={{0,4},{1,3},{2,6},{3,1},{4,0},{5,7},{6,2},{7,5},{8,12},{9,11},{10,... | collective-permute-start | bytes 294920 | tf_op jit(solution)/shard_map/ppermute | solution.py:48
  66.4 1.2 %collective-permute-done.16.refs_2_ = bf16[384,128]{1,0:T(8,128)(2,1)S(1)} collective-permute-done((bf16[384,128]{1,0:T(8,128)(2,1)S(1)}, bf16[384,128]{1,0:T(8,128)(2,1)S(1)}, u32[]{:S(2)}, u32[]{:S(2)}) %collective-permute-start.16) | collective-permute-done | bytes 98336 | tf_op jit(solution)/shard_map/ppermute | solution.py:48
  69.7 1.4 %copy-done.2 = bf16[1024,768]{1,0:T(8,128)(2,1)S(1)} copy-done((bf16[1024,768]{1,0:T(8,128)(2,1)S(1)}, bf16[1024,768]{1,0:T(8,128)(2,1)}, u32[]{:S(2)}) %copy-start.2) | copy-done | bytes 1572888
  71.1 1.9 %shard_map.96.grad_hidden_ref = bf16[1024,768]{1,0:T(8,128)(2,1)S(1)} custom-call(bf16[1024,1024]{1,0:T(8,128)(2,1)S(1)} %get-tuple-element.11.grads_ref, bf16[1024,768]{1,0:T(8,128)(2,1)S(1)} %copy-done.2), custom_call_target="tpu_custom_call" | custom-call | flops 1610612736 | bytes 5000000 | tf_op jit(solution)/shard_map/pallas_call | solution.py:30
  74.2 3.3 %shard_map.97 = f32[1024,768]{1,0:T(8,128)} custom-call(bf16[1024,768]{1,0:T(8,128)(2,1)S(1)} %shard_map.96.grad_hidden_ref, bf16[768,768]{1,0:T(8,128)(2,1)S(1)} %copy-done), custom_call_target="tpu_custom_call" | custom-call | flops 1207959552 | bytes 6000000 | tf_op jit(solution)/shard_map/pallas_call | solution.py:246
  78.4 3.4 %shard_map.99 = f32[768,768]{1,0:T(8,128)} custom-call(s32[1]{0:T(128)} %bitcast.6.me_ref, s32[1]{0:T(128)} %bitcast.7.z_ref, bf16[384,128]{1,0:T(8,128)(2,1)S(1)} %add_convert_fusion.refs_0_, bf16[384,128]{1,0:T(8,128)(2,1)S(1)} %collective-permute-done.15.refs_1_, bf16[384,128]{1,0:T(8,128)(2,1)S(1)} %collective-permute-done.16.refs_2_, ...), custom_call_target="tpu_custom_call" | custom-call | flops 1207959552 | bytes 6000000 | tf_op jit(solution)/shard_map/pallas_call | solution.py:30
  (108 shorter events, 20.4 us)
Async XLA Ops:
  2.9 11.3 %collective-permute-start.1 = (bf16[144,768]{1,0:T(8,128)(2,1)S(1)}, bf16[144,768]{1,0:T(8,128)(2,1)S(1)}, u32[]{:S(2)}, u32[]{:S(2)}) collective-permute-start(bf16[144,768]{1,0:T(8,128)(2,1)S(1)} %shard_map.94.refs_0_), channel_id=1, source_target_pairs={{0,4},{1,3},{2,6},{3,1},{4,0},{5,7},{6,2},{7,5},{8,12},{9,11},{10,... | collective-permute-start | bytes 663560 | tf_op jit(solution)/shard_map/ppermute | solution.py:48
  5.9 9.1 %collective-permute-start = (bf16[144,768]{1,0:T(8,128)(2,1)S(1)}, bf16[144,768]{1,0:T(8,128)(2,1)S(1)}, u32[]{:S(2)}, u32[]{:S(2)}) collective-permute-start(bf16[144,768]{1,0:T(8,128)(2,1)S(1)} %shard_map.94.refs_0_), channel_id=1, source_target_pairs={{0,2},{1,5},{2,0},{3,7},{4,6},{5,1},{6,4},{7,3},{8,10},{9,13},{10,... | collective-permute-start | bytes 663560 | tf_op jit(solution)/shard_map/ppermute | solution.py:48
  7.4 15.9 %collective-permute-start.3 = (bf16[144,768]{1,0:T(8,128)(2,1)S(1)}, bf16[144,768]{1,0:T(8,128)(2,1)S(1)}, u32[]{:S(2)}, u32[]{:S(2)}) collective-permute-start(bf16[144,768]{1,0:T(8,128)(2,1)S(1)} %shard_map.94.refs_0_), channel_id=1, source_target_pairs={{0,1},{1,0},{2,3},{3,2},{4,5},{5,4},{6,7},{7,6},{8,9},{9,8},{10,11... | collective-permute-start | bytes 663560 | tf_op jit(solution)/shard_map/ppermute | solution.py:55
  14.2 5.9 %collective-permute-start.2 = (bf16[144,768]{1,0:T(8,128)(2,1)S(1)}, bf16[144,768]{1,0:T(8,128)(2,1)S(1)}, u32[]{:S(2)}, u32[]{:S(2)}) collective-permute-start(bf16[144,768]{1,0:T(8,128)(2,1)S(1)} %collective-permute-done.1.refs_2_), channel_id=1, source_target_pairs={{0,2},{1,5},{2,0},{3,7},{4,6},{5,1},{6,4},{7,3},{8,10},{9,13},{10,... | collective-permute-start | bytes 663560 | tf_op jit(solution)/shard_map/ppermute | solution.py:48
  14.7 9.3 %collective-permute-start.5 = (bf16[144,768]{1,0:T(8,128)(2,1)S(1)}, bf16[144,768]{1,0:T(8,128)(2,1)S(1)}, u32[]{:S(2)}, u32[]{:S(2)}) collective-permute-start(bf16[144,768]{1,0:T(8,128)(2,1)S(1)} %collective-permute-done.1.refs_2_), channel_id=1, source_target_pairs={{0,1},{1,0},{2,3},{3,2},{4,5},{5,4},{6,7},{7,6},{8,9},{9,8},{10,11... | collective-permute-start | bytes 663560 | tf_op jit(solution)/shard_map/ppermute | solution.py:55
  15.0 9.7 %collective-permute-start.4 = (bf16[144,768]{1,0:T(8,128)(2,1)S(1)}, bf16[144,768]{1,0:T(8,128)(2,1)S(1)}, u32[]{:S(2)}, u32[]{:S(2)}) collective-permute-start(bf16[144,768]{1,0:T(8,128)(2,1)S(1)} %collective-permute-done.refs_1_), channel_id=1, source_target_pairs={{0,1},{1,0},{2,3},{3,2},{4,5},{5,4},{6,7},{7,6},{8,9},{9,8},{10,11... | collective-permute-start | bytes 663560 | tf_op jit(solution)/shard_map/ppermute | solution.py:55
  20.1 5.3 %collective-permute-start.6 = (bf16[144,768]{1,0:T(8,128)(2,1)S(1)}, bf16[144,768]{1,0:T(8,128)(2,1)S(1)}, u32[]{:S(2)}, u32[]{:S(2)}) collective-permute-start(bf16[144,768]{1,0:T(8,128)(2,1)S(1)} %collective-permute-done.2.refs_3_), channel_id=1, source_target_pairs={{0,1},{1,0},{2,3},{3,2},{4,5},{5,4},{6,7},{7,6},{8,9},{9,8},{10,11... | collective-permute-start | bytes 663560 | tf_op jit(solution)/shard_map/ppermute | solution.py:55
  37.2 5.7 %collective-permute-start.10 = (bf16[768,128]{1,0:T(8,128)(2,1)S(1)}, bf16[768,128]{1,0:T(8,128)(2,1)S(1)}, u32[]{:S(2)}, u32[]{:S(2)}) collective-permute-start(bf16[768,128]{1,0:T(8,128)(2,1)S(1)} %get-tuple-element.21), channel_id=1, source_target_pairs={{0,2},{1,5},{2,0},{3,7},{4,6},{5,1},{6,4},{7,3},{8,10},{9,13},{10,... | collective-permute-start | bytes 589832 | tf_op jit(solution)/shard_map/ppermute | solution.py:48
  37.8 7.3 %collective-permute-start.9 = (bf16[768,128]{1,0:T(8,128)(2,1)S(1)}, bf16[768,128]{1,0:T(8,128)(2,1)S(1)}, u32[]{:S(2)}, u32[]{:S(2)}) collective-permute-start(bf16[768,128]{1,0:T(8,128)(2,1)S(1)} %get-tuple-element.22), channel_id=1, source_target_pairs={{0,2},{1,5},{2,0},{3,7},{4,6},{5,1},{6,4},{7,3},{8,10},{9,13},{10,... | collective-permute-start | bytes 589832 | tf_op jit(solution)/shard_map/ppermute | solution.py:48
  43.6 5.2 %collective-permute-start.12 = (bf16[384,128]{1,0:T(8,128)(2,1)S(1)}, bf16[384,128]{1,0:T(8,128)(2,1)S(1)}, u32[]{:S(2)}, u32[]{:S(2)}) collective-permute-start(bf16[384,128]{1,0:T(8,128)(2,1)S(1)} %get-tuple-element.24), channel_id=1, source_target_pairs={{0,4},{1,3},{2,6},{3,1},{4,0},{5,7},{6,2},{7,5},{8,12},{9,11},{10,... | collective-permute-start | bytes 294920 | tf_op jit(solution)/shard_map/ppermute | solution.py:48
  53.6 5.7 %collective-permute-start.14 = (bf16[384,128]{1,0:T(8,128)(2,1)S(1)}, bf16[384,128]{1,0:T(8,128)(2,1)S(1)}, u32[]{:S(2)}, u32[]{:S(2)}) collective-permute-start(bf16[384,128]{1,0:T(8,128)(2,1)S(1)} %fusion.6), channel_id=1, source_target_pairs={{0,16},{8,24},{16,0},{24,8},{1,17},{9,25},{17,1},{25,9},{2,18},{10... | collective-permute-start | bytes 294920 | tf_op jit(solution)/shard_map/ppermute | solution.py:60
  61.0 5.2 %collective-permute-start.18 = (bf16[384,128]{1,0:T(8,128)(2,1)S(1)}, bf16[384,128]{1,0:T(8,128)(2,1)S(1)}, u32[]{:S(2)}, u32[]{:S(2)}) collective-permute-start(bf16[384,128]{1,0:T(8,128)(2,1)S(1)} %add_convert_fusion.refs_0_), channel_id=1, source_target_pairs={{0,4},{1,3},{2,6},{3,1},{4,0},{5,7},{6,2},{7,5},{8,12},{9,11},{10,... | collective-permute-start | bytes 294920 | tf_op jit(solution)/shard_map/ppermute | solution.py:48
  61.9 5.7 %collective-permute-start.16 = (bf16[384,128]{1,0:T(8,128)(2,1)S(1)}, bf16[384,128]{1,0:T(8,128)(2,1)S(1)}, u32[]{:S(2)}, u32[]{:S(2)}) collective-permute-start(bf16[384,128]{1,0:T(8,128)(2,1)S(1)} %add_convert_fusion.refs_0_), channel_id=1, source_target_pairs={{0,2},{1,5},{2,0},{3,7},{4,6},{5,1},{6,4},{7,3},{8,10},{9,13},{10,... | collective-permute-start | bytes 294920 | tf_op jit(solution)/shard_map/ppermute | solution.py:48
  62.4 6.0 %collective-permute-start.22 = (bf16[384,128]{1,0:T(8,128)(2,1)S(1)}, bf16[384,128]{1,0:T(8,128)(2,1)S(1)}, u32[]{:S(2)}, u32[]{:S(2)}) collective-permute-start(bf16[384,128]{1,0:T(8,128)(2,1)S(1)} %add_convert_fusion.refs_0_), channel_id=1, source_target_pairs={{0,1},{1,0},{2,3},{3,2},{4,5},{5,4},{6,7},{7,6},{8,9},{9,8},{10,11... | collective-permute-start | bytes 294920 | tf_op jit(solution)/shard_map/ppermute | solution.py:55
  64.0 5.2 %collective-permute-start.19 = (bf16[384,128]{1,0:T(8,128)(2,1)S(1)}, bf16[384,128]{1,0:T(8,128)(2,1)S(1)}, u32[]{:S(2)}, u32[]{:S(2)}) collective-permute-start(bf16[384,128]{1,0:T(8,128)(2,1)S(1)} %collective-permute-done.15.refs_1_), channel_id=1, source_target_pairs={{0,4},{1,3},{2,6},{3,1},{4,0},{5,7},{6,2},{7,5},{8,12},{9,11},{10,... | collective-permute-start | bytes 294920 | tf_op jit(solution)/shard_map/ppermute | solution.py:48
  66.2 6.8 %collective-permute-start.17 = (bf16[384,128]{1,0:T(8,128)(2,1)S(1)}, bf16[384,128]{1,0:T(8,128)(2,1)S(1)}, u32[]{:S(2)}, u32[]{:S(2)}) collective-permute-start(bf16[384,128]{1,0:T(8,128)(2,1)S(1)} %collective-permute-done.15.refs_1_), channel_id=1, source_target_pairs={{0,2},{1,5},{2,0},{3,7},{4,6},{5,1},{6,4},{7,3},{8,10},{9,13},{10,... | collective-permute-start | bytes 294920 | tf_op jit(solution)/shard_map/ppermute | solution.py:48
  66.3 7.3 %collective-permute-start.23 = (bf16[384,128]{1,0:T(8,128)(2,1)S(1)}, bf16[384,128]{1,0:T(8,128)(2,1)S(1)}, u32[]{:S(2)}, u32[]{:S(2)}) collective-permute-start(bf16[384,128]{1,0:T(8,128)(2,1)S(1)} %collective-permute-done.15.refs_1_), channel_id=1, source_target_pairs={{0,1},{1,0},{2,3},{3,2},{4,5},{5,4},{6,7},{7,6},{8,9},{9,8},{10,11... | collective-permute-start | bytes 294920 | tf_op jit(solution)/shard_map/ppermute | solution.py:55
  67.6 5.5 %collective-permute-start.20 = (bf16[384,128]{1,0:T(8,128)(2,1)S(1)}, bf16[384,128]{1,0:T(8,128)(2,1)S(1)}, u32[]{:S(2)}, u32[]{:S(2)}) collective-permute-start(bf16[384,128]{1,0:T(8,128)(2,1)S(1)} %collective-permute-done.18.refs_4_), channel_id=1, source_target_pairs={{0,2},{1,5},{2,0},{3,7},{4,6},{5,1},{6,4},{7,3},{8,10},{9,13},{10,... | collective-permute-start | bytes 294920 | tf_op jit(solution)/shard_map/ppermute | solution.py:48
  68.4 5.3 %collective-permute-start.24 = (bf16[384,128]{1,0:T(8,128)(2,1)S(1)}, bf16[384,128]{1,0:T(8,128)(2,1)S(1)}, u32[]{:S(2)}, u32[]{:S(2)}) collective-permute-start(bf16[384,128]{1,0:T(8,128)(2,1)S(1)} %collective-permute-done.16.refs_2_), channel_id=1, source_target_pairs={{0,1},{1,0},{2,3},{3,2},{4,5},{5,4},{6,7},{7,6},{8,9},{9,8},{10,11... | collective-permute-start | bytes 294920 | tf_op jit(solution)/shard_map/ppermute | solution.py:55
  69.1 5.0 %collective-permute-start.21 = (bf16[384,128]{1,0:T(8,128)(2,1)S(1)}, bf16[384,128]{1,0:T(8,128)(2,1)S(1)}, u32[]{:S(2)}, u32[]{:S(2)}) collective-permute-start(bf16[384,128]{1,0:T(8,128)(2,1)S(1)} %collective-permute-done.19.refs_5_), channel_id=1, source_target_pairs={{0,2},{1,5},{2,0},{3,7},{4,6},{5,1},{6,4},{7,3},{8,10},{9,13},{10,... | collective-permute-start | bytes 294920 | tf_op jit(solution)/shard_map/ppermute | solution.py:48
  73.0 5.4 %collective-permute-start.26 = (bf16[384,128]{1,0:T(8,128)(2,1)S(1)}, bf16[384,128]{1,0:T(8,128)(2,1)S(1)}, u32[]{:S(2)}, u32[]{:S(2)}) collective-permute-start(bf16[384,128]{1,0:T(8,128)(2,1)S(1)} %collective-permute-done.18.refs_4_), channel_id=1, source_target_pairs={{0,1},{1,0},{2,3},{3,2},{4,5},{5,4},{6,7},{7,6},{8,9},{9,8},{10,11... | collective-permute-start | bytes 294920 | tf_op jit(solution)/shard_map/ppermute | solution.py:55
  73.1 5.3 %collective-permute-start.27 = (bf16[384,128]{1,0:T(8,128)(2,1)S(1)}, bf16[384,128]{1,0:T(8,128)(2,1)S(1)}, u32[]{:S(2)}, u32[]{:S(2)}) collective-permute-start(bf16[384,128]{1,0:T(8,128)(2,1)S(1)} %collective-permute-done.19.refs_5_), channel_id=1, source_target_pairs={{0,1},{1,0},{2,3},{3,2},{4,5},{5,4},{6,7},{7,6},{8,9},{9,8},{10,11... | collective-permute-start | bytes 294920 | tf_op jit(solution)/shard_map/ppermute | solution.py:55
  73.6 4.8 %collective-permute-start.25 = (bf16[384,128]{1,0:T(8,128)(2,1)S(1)}, bf16[384,128]{1,0:T(8,128)(2,1)S(1)}, u32[]{:S(2)}, u32[]{:S(2)}) collective-permute-start(bf16[384,128]{1,0:T(8,128)(2,1)S(1)} %collective-permute-done.17.refs_3_), channel_id=1, source_target_pairs={{0,1},{1,0},{2,3},{3,2},{4,5},{5,4},{6,7},{7,6},{8,9},{9,8},{10,11... | collective-permute-start | bytes 294920 | tf_op jit(solution)/shard_map/ppermute | solution.py:55
  73.7 4.7 %collective-permute-start.28 = (bf16[384,128]{1,0:T(8,128)(2,1)S(1)}, bf16[384,128]{1,0:T(8,128)(2,1)S(1)}, u32[]{:S(2)}, u32[]{:S(2)}) collective-permute-start(bf16[384,128]{1,0:T(8,128)(2,1)S(1)} %collective-permute-done.20.refs_6_), channel_id=1, source_target_pairs={{0,1},{1,0},{2,3},{3,2},{4,5},{5,4},{6,7},{7,6},{8,9},{9,8},{10,11... | collective-permute-start | bytes 294920 | tf_op jit(solution)/shard_map/ppermute | solution.py:55
  (31 other events, 94.4 us)

commit v3 on v2

v3 whole, which is shorter than its diff:
```python
import functools

import jax
import jax.numpy as jnp
from jax import lax
from jax.experimental import pallas as pl
from jax.experimental.pallas import tpu as pltpu
from jax.sharding import PartitionSpec as P

BF16 = jnp.bfloat16
F32 = jnp.float32
VMEM = pl.BlockSpec(memory_space=pltpu.VMEM)
SMEM = pl.BlockSpec(memory_space=pltpu.SMEM)
ANY = pl.BlockSpec(memory_space=pl.ANY)
MIB = 1024 * 1024
NN = (((1,), (0,)), ((), ()))
NT = (((1,), (1,)), ((), ()))
TN = (((0,), (0,)), ((), ()))


def dot(left, right, dims):
    return lax.dot_general(left, right, dims, preferred_element_type=F32)


def shape(dims, dtype):
    return jax.ShapeDtypeStruct(dims, dtype)


def call(kernel, outs, args, scalars=(), after=(), scratch=(), vmem=8, flops=0, nbytes=0):
    return pl.pallas_call(
        kernel,
        out_shape=outs,
        in_specs=[SMEM] * len(scalars) + [VMEM] * len(args) + [ANY] * len(after),
        out_specs=[VMEM] * len(outs),
        scratch_shapes=list(scratch),
        compiler_params=pltpu.CompilerParams(vmem_limit_bytes=vmem * MIB),
        cost_estimate=pl.CostEstimate(flops=flops, bytes_accessed=nbytes, transcendentals=0),
    )(*scalars, *args, *after)


def gate(value, after):
    return pl.pallas_call(
        lambda value_ref, after_ref, out_ref: None,
        out_shape=shape(value.shape, value.dtype),
        in_specs=[ANY, ANY],
        out_specs=ANY,
        input_output_aliases={0: 0},
    )(value, after)


def distance_of(slot, chips):
    return 2 * (slot % chips) + slot // chips


def slot_of(cluster, me, chips):
    distance = cluster ^ me
    return (distance >> 1) + (distance & 1) * chips


def swap(value, axis, distance):
    size = lax.axis_size(axis)
    return lax.ppermute(value, axis, [(i, i ^ distance) for i in range(size)])


def inputs_kernel(enc_ref, proj_ref, hidden_ref, enc_t_ref):
    samples = enc_ref.shape[0]
    tile = min(256, samples)
    for start in range(0, samples, tile):
        rows = enc_ref[start : start + tile, :]
        enc_t_ref[:, start : start + tile] = rows.T
        hidden_ref[start : start + tile, :] = dot(rows, proj_ref[...], NN).astype(BF16)


def outer_rows(enc_t_ref, grads, z, count):
    depth = enc_t_ref.shape[0] // count
    for r in range(count):
        start = pl.multiple_of((z ^ r) * depth, depth)
        yield r * depth, depth, dot(enc_t_ref[pl.ds(start, depth), :], grads, NT)


def score_kernel(owners, beam, block, count, slots_ref, me_ref, z_ref, hidden_ref, wanted_ref, enc_t_ref, ratio_ref, *refs):
    pieces, refs = refs[:owners], refs[owners:]
    grads_ref, weights_ref, first_ref, second_ref, scale_ref, logits_ref = refs
    samples = hidden_ref.shape[0]
    size = pieces[0].shape[0]
    chips = owners // 2
    for slot in range(owners):
        rows = pl.ds(slot * size, size)
        weights_ref[rows, :] = pieces[slot][...]
        ratio = ratio_ref[pl.ds(me_ref[0] ^ distance_of(slot, chips), 1), :]
        scale_ref[rows, :] = jnp.broadcast_to(ratio, (block, size)).T / block
    grads_ref[...] = jnp.zeros_like(grads_ref)
    label_iota = lax.broadcasted_iota(jnp.int32, (size, block), 0)
    tile = min(2 * block, samples)
    for start in range(0, samples, tile):
        logits_ref[...] = dot(weights_ref[...], hidden_ref[start : start + tile, :], NT)
        for low in range(start, start + tile, block):
            for beam_slot in range(beam):
                slot = slots_ref[(low // block) * beam + beam_slot]
                rows = pl.ds(pl.multiple_of(slot * size, size), size)
                logits = logits_ref[rows, low - start : low - start + block]
                labels = label_iota + beam_slot * size
                target = labels == wanted_ref[0:1, low : low + block]
                for column in range(1, wanted_ref.shape[0]):
                    target = target | (labels == wanted_ref[column : column + 1, low : low + block])
                share = jax.nn.sigmoid(logits) - jnp.where(target, 1.0, 0.0)
                grads_ref[rows, low : low + block] = (scale_ref[rows, :] * share).astype(BF16)
    for low, depth, outer in outer_rows(enc_t_ref, grads_ref[chips * size :, :], z_ref[0], count):
        for slot in range(chips):
            part = outer[:, slot * size : (slot + 1) * size].astype(BF16)
            out_ref = first_ref if slot % 2 else second_ref
            out_ref[slot // 2, low : low + depth, :] = part


def keep_kernel(count, z_ref, enc_t_ref, grads_ref, *kept):
    size = kept[0].shape[1]
    for low, depth, outer in outer_rows(enc_t_ref, grads_ref[: len(kept) * size, :], z_ref[0], count):
        for slot, ref in enumerate(kept):
            ref[low : low + depth, :] = outer[:, slot * size : (slot + 1) * size]


def hidden_kernel(owners, me_ref, grads_ref, weights_ref, after_ref, out_ref, rows_ref):
    size = weights_ref.shape[0] // owners
    for slot in range(owners):
        start = pl.multiple_of((me_ref[0] ^ distance_of(slot, owners // 2)) * size, size)
        rows_ref[pl.ds(start, size), :] = weights_ref[slot * size : (slot + 1) * size, :]
    out_ref[...] = dot(grads_ref[...], weights_ref[...], TN).astype(BF16)


def enc_kernel(grad_hidden_ref, proj_ref, out_ref, done_ref):
    out_ref[...] = dot(grad_hidden_ref[...], proj_ref[...], NT)
    done_ref[...] = jnp.zeros_like(done_ref)


def combine_kernel(own_ref, *refs):
    *received, after_ref, kept_ref, sent_ref = refs
    cut = kept_ref.shape[0]
    for rows, out_ref in ((slice(cut, None), sent_ref), (slice(0, cut), kept_ref)):
        total = own_ref[rows, :]
        for ref in received:
            total = total + ref[rows, :].astype(F32)
        out_ref[...] = total.astype(out_ref.dtype)


def proj_kernel(owners, count, me_ref, z_ref, *refs):
    parts, refs = refs[: owners * count], refs[owners * count :]
    rows_ref, slice_ref, out_ref, head_ref, outer_ref = refs
    depth, size = parts[0].shape
    for slot in range(owners):
        start = pl.multiple_of((me_ref[0] ^ distance_of(slot, owners // 2)) * size, size)
        for r in range(count):
            outer_ref[r * depth : (r + 1) * depth, pl.ds(start, size)] = parts[slot * count + r][...]
    head = jnp.zeros(head_ref.shape, F32)
    for r in range(count):
        start = pl.multiple_of((z_ref[0] ^ r) * depth, depth)
        rows = outer_ref[r * depth : (r + 1) * depth, :]
        out_ref[pl.ds(start, depth), :] = dot(rows, rows_ref[...], NN)
        head = head + dot(slice_ref[pl.ds(start, depth), :], parts[r][...], TN)
    head_ref[...] = head


def shards(enc, proj, head_weight, shortlist, positives, weight_num, weight_den):
    owners, planes = lax.axis_size("label"), lax.axis_size("dp")
    chips = owners // 2
    row_blocks = max(1, planes // 2)
    me = lax.axis_index("label").astype(jnp.int32)
    z = lax.axis_index("dp").astype(jnp.int32)
    z_low = z & (row_blocks - 1)
    blocks, beam = shortlist.shape
    samples, width = enc.shape
    block = samples // blocks
    size = head_weight.shape[0]
    labels = owners * size
    depth = width // row_blocks
    me_s, z_s = me.reshape(1), z_low.reshape(1)

    got = {0: head_weight}
    for slot in range(1, chips):
        got[slot] = swap(head_weight, "label", distance_of(slot, chips))
    ratio = weight_num.astype(F32) / weight_den.astype(F32)
    ratio = lax.all_gather(ratio, "label", axis=0, tiled=True).reshape(owners, size)
    hidden, enc_t = call(
        inputs_kernel,
        [shape((samples, width), BF16), shape((width, samples), BF16)],
        [enc, proj],
        flops=2 * samples * width * width,
        nbytes=6_000_000,
    )
    for slot in range(1, chips):
        got[slot] = gate(got[slot], hidden)
    for slot in range(chips):
        got[slot + chips] = swap(got[slot], "label", 1)
    slots = slot_of(shortlist, me, chips).astype(jnp.int32).reshape(-1)

    group = shape((chips // 2, width, size), BF16)
    grads, weights, send_first, send_second = call(
        functools.partial(score_kernel, owners, beam, block, row_blocks),
        [shape((labels, samples), BF16), shape((labels, width), BF16), group, group],
        [hidden, positives.T, enc_t, ratio] + [got[slot] for slot in range(owners)],
        scalars=[slots, me_s, z_s],
        scratch=[pltpu.VMEM((labels, block), F32), pltpu.VMEM((labels, min(2 * block, samples)), F32)],
        vmem=16,
        flops=4 * samples * labels * width,
        nbytes=12_000_000,
    )
    from_core = [swap(send_first, "label", 1), swap(send_second, "label", 1)]
    kept = call(
        functools.partial(keep_kernel, row_blocks),
        [shape((width, size), F32)] * chips,
        [enc_t, grads],
        scalars=[z_s],
        flops=samples * labels * width,
        nbytes=4_000_000,
    )
    received, moved = [], None
    for slot in sorted(range(1, chips), key=lambda s: (-(s & 1), -s)):
        moved = (kept[slot] + from_core[1 - slot % 2][slot // 2].astype(F32)).astype(BF16)
        received.append(swap(moved, "label", distance_of(slot, chips)))
    own = kept[0] + from_core[1][0].astype(F32)
    grad_hidden, rows = call(
        functools.partial(hidden_kernel, owners),
        [shape((samples, width), BF16), shape((labels, width), BF16)],
        [grads, weights],
        scalars=[me_s],
        after=[moved],
        vmem=16,
        flops=2 * samples * width * labels,
        nbytes=5_000_000,
    )
    tile = min(256, samples)
    grad_enc, enc_done = pl.pallas_call(
        enc_kernel,
        grid=(samples // tile,),
        out_shape=[shape((samples, width), F32), shape((8, 128), F32)],
        in_specs=[
            pl.BlockSpec((tile, width), lambda i: (i, 0)),
            pl.BlockSpec((width, width), lambda i: (0, 0)),
        ],
        out_specs=[
            pl.BlockSpec((tile, width), lambda i: (i, 0)),
            pl.BlockSpec((8, 128), lambda i: (0, 0)),
        ],
        compiler_params=pltpu.CompilerParams(vmem_limit_bytes=12 * MIB),
        cost_estimate=pl.CostEstimate(
            flops=2 * samples * width * width, bytes_accessed=6_000_000, transcendentals=0
        ),
    )(grad_hidden, proj)

    if row_blocks > 1:
        cut = width // 2
        total, upper = call(
            combine_kernel,
            [shape((cut, size), F32), shape((cut, size), BF16)],
            [own] + received,
            after=[enc_done],
            nbytes=2_000_000,
        )
        span = row_blocks // 2
        total = total + swap(upper, "dp", span).astype(F32)
        while span > 1:
            cut = span // 2 * depth
            total = total[:cut] + swap(total[cut:].astype(BF16), "dp", span // 2).astype(F32)
            span //= 2
    else:
        total = own
        for value in received:
            total = total + value.astype(F32)
    total = total.astype(BF16)
    if planes > 1:
        other = swap(total, "dp", planes // 2)
        total = (total.astype(F32) + other.astype(F32)).astype(BF16)
    parts = {0: total}
    span = 1
    while span < row_blocks:
        for r in range(span):
            parts[r + span] = swap(parts[r], "dp", span)
        span *= 2
    have = {(0, r): parts[r] for r in range(row_blocks)}
    for r in range(row_blocks):
        for slot in range(1, chips):
            have[slot, r] = swap(parts[r], "label", distance_of(slot, chips))
        for slot in range(chips):
            have[slot + chips, r] = swap(have[slot, r], "label", 1)
    proj_slice = lax.dynamic_slice_in_dim(proj, z * (width // planes), width // planes, 1)
    grad_proj, grad_head = call(
        functools.partial(proj_kernel, owners, row_blocks),
        [shape((width, width), F32), shape((width // planes, size), F32)],
        [have[slot, r] for slot in range(owners) for r in range(row_blocks)] + [rows, proj_slice],
        scalars=[me_s, z_s],
        scratch=[pltpu.VMEM((width, labels), BF16)],
        vmem=16,
        flops=2 * labels * width * width,
        nbytes=6_000_000,
    )
    return (grad_enc, grad_proj, grad_head.T)


def solution(mesh):
    placed = (
        P(("dp", "label"), None),
        P(),
        P("label", None),
        P(("dp", "label"), None),
        P(("dp", "label"), None),
        P("label"),
        P("label"),
    )
    return jax.shard_map(
        shards,
        mesh=mesh,
        in_specs=placed,
        out_specs=(P(("dp", "label"), None), P(), P("label", "dp")),
        check_vma=False,
    )
```

time: 82.4 us -> 80.4 us (0.976)
  blocking collectives: 0 us -> 8.76 us
  matrix products: 4.06 us -> 0 us
  waiting for transfers between devices: 22 us -> 18.3 us
  local copies, waits for them, and re-layouts: 14.5 us -> 11.1 us
  Pallas kernels: 15.9 us -> 17 us
  other arithmetic: 1.94 us -> 0.91 us
    all_gather x0 -> x1, blocking collectives: none -> 8.76 us  [shards(): lax.all_gather(ratio, 'label', axis=0, tiled=True).reshape(owners, size)]
    dot_general x1 -> x0, matrix products: 4.06 us -> none  [dot(): return lax.dot_general(left, right, dims, preferred_element_type=F32)]
    ppermute x30 -> x29, waiting for transfers between devices: 22 us -> 18.3 us  [swap(): return lax.ppermute(value, axis, [(i, i ^ distance) for i in range(size)])]
    reshape x2 -> x1, local copies, waits for them, and re-layouts: 2.75 us -> 0.08 us  [shards(): slots = slot_of(shortlist, me, chips).astype(jnp.int32).reshape(-1)]
    concatenate x1 -> x0, other arithmetic: 1.64 us -> none  [shards(): jnp.concatenate([lax.dynamic_index_in_dim(enc_blocks, z_low ^ r, 0, False...]
    squeeze x1 -> x0, local copies, waits for them, and re-layouts: 1.3 us -> none  [shards(): lax.dynamic_index_in_dim(enc_blocks, z_low ^ r, 0, False)]
    pallas_call x6, Pallas kernels: 12.6 us -> 13.7 us  [call(): pl.pallas_call(kernel, out_shape=outs, in_specs=[SMEM] * len(scalars) + [...]
    unnamed x50 -> x34, local copies, waits for them, and re-layouts: 10.2 us -> 10.8 us
  transfers between devices with their start and end apart: 30 -> 29, of which waited for: 10 -> 15; matrix products, arithmetic and copies ran while one was open for 12% -> 2% of each run, Pallas kernels for 9% -> 10%
where the time goes in v3:
time: 80.4 us; the launch traced here: 80 us
  starting transfers between devices  23.1 us (29%)
  waiting for transfers between devices  18.3 us (23%)
  Pallas kernels  17 us (21%)
  local copies, waits for them, and re-layouts  11.1 us (14%)
  blocking collectives  8.76 us (11%)
  other arithmetic  0.91 us (1%)
  between operations  0.81 us (1%)
    ppermute x29, starting transfers between devices, swap(): return lax.ppermute(value, axis, [(i, i ^ distance) for i in range(size)])  23.1 us
    ppermute x29, waiting for transfers between devices, swap(): return lax.ppermute(value, axis, [(i, i ^ distance) for i in range(size)])  18.3 us
    pallas_call x6, Pallas kernels, call(): pl.pallas_call(kernel, out_shape=outs, in_specs=[SMEM] * len(scalars) + [...  13.7 us
    unnamed x34, local copies, waits for them, and re-layouts  10.8 us
    all_gather x1, blocking collectives, shards(): lax.all_gather(ratio, 'label', axis=0, tiled=True).reshape(owners, size)  8.76 us
    pallas_call x1, Pallas kernels, shards(): pl.pallas_call(enc_kernel, grid=(samples // tile,), out_shape=[shape((sam...  3.3 us
  transfers between devices with their start and end apart: 29, of which 15 were waited for; matrix products, arithmetic and copies ran while one was open for 2% of the time, Pallas kernels for 10%

profile of v3, /device:TPU:0, one launch (start us, length us, event | category | flops | bytes accessed | tf_op | source)
XLA Modules:
  0.0 80.0 jit_solution(16142644481333246176)
XLA Ops:
  0.6 3.0 %collective-permute-start = (bf16[128,768]{1,0:T(8,128)(2,1)}, bf16[128,768]{1,0:T(8,128)(2,1)S(1)}, u32[]{:S(2)}, u32[]{:S(2)}) collective-permute-start(bf16[128,768]{1,0:T(8,128)(2,1)} %refs_0_.1), channel_id=1, source_target_pairs={{0,2},{1,3},{2,0},{3,1},{4,6},{5,7},{6,4},{7,5},{8,10},{9,11},{10,... | collective-permute-start | bytes 589832 | tf_op jit(solution)/shard_map/ppermute | solution.py:62
  3.6 1.5 %collective-permute-start.1 = (bf16[128,768]{1,0:T(8,128)(2,1)}, bf16[128,768]{1,0:T(8,128)(2,1)S(1)}, u32[]{:S(2)}, u32[]{:S(2)}) collective-permute-start(bf16[128,768]{1,0:T(8,128)(2,1)} %refs_0_.1), channel_id=1, source_target_pairs={{0,4},{1,5},{2,6},{3,7},{4,0},{5,1},{6,2},{7,3},{8,12},{9,13},{10,... | collective-permute-start | bytes 589832 | tf_op jit(solution)/shard_map/ppermute | solution.py:62
  6.0 1.3 %copy-done.8 = bf16[768,768]{1,0:T(8,128)(2,1)S(1)} copy-done((bf16[768,768]{1,0:T(8,128)(2,1)S(1)}, bf16[768,768]{1,0:T(8,128)(2,1)}, u32[]{:S(2)}) %copy-start.8) | copy-done | bytes 1179672
  7.3 1.4 %copy-done.10 = bf16[1024,768]{1,0:T(8,128)(2,1)S(1)} copy-done((bf16[1024,768]{1,0:T(8,128)(2,1)S(1)}, bf16[1024,768]{1,0:T(8,128)(2,1)}, u32[]{:S(2)}) %copy-start.10) | copy-done | bytes 1572888
  8.7 1.4 %shard_map.94 = (bf16[1024,768]{1,0:T(8,128)(2,1)S(1)}, bf16[768,1024]{1,0:T(8,128)(2,1)S(1)}) custom-call(bf16[1024,768]{1,0:T(8,128)(2,1)S(1)} %copy-done.10, bf16[768,768]{1,0:T(8,128)(2,1)S(1)} %copy-done.8), custom_call_target="tpu_custom_call" | custom-call | flops 1207959552 | bytes 6000000 | tf_op jit(solution)/shard_map/pallas_call | solution.py:30
  12.5 1.9 %collective-permute-done.1.value_ref = bf16[128,768]{1,0:T(8,128)(2,1)S(1)} collective-permute-done((bf16[128,768]{1,0:T(8,128)(2,1)}, bf16[128,768]{1,0:T(8,128)(2,1)S(1)}, u32[]{:S(2)}, u32[]{:S(2)}) %collective-permute-start.1) | collective-permute-done | bytes 196640 | tf_op jit(solution)/shard_map/ppermute | solution.py:62
  16.3 8.8 %all-gather = f32[8,1,128]{2,1,0:T(1,128)S(1)} all-gather(f32[1,1,128]{2,1,0:T(1,128)S(1)} %fusion.3), channel_id=1, replica_groups=mesh['dp'=4,'label'=8] {'label'}, dimensions={0}, use_global_device_ids=true | all-gather | bytes 4608 | tf_op jit(solution)/shard_map/all_gather | solution.py:181
  28.6 6.0 %shard_map.98 = (bf16[1024,1024]{1,0:T(8,128)(2,1)S(1)}, bf16[1024,768]{1,0:T(8,128)(2,1)S(1)}, bf16[2,768,128]{2,1,0:T(8,128)(2,1)S(1)}, bf16[2,768,128]{2,1,0:T(8,128)(2,1)S(1)}) custom-call(s32[32]{0:T(128)S(1)} %reshape.27.slots_ref, s32[1]{0:T(128)} %bitcast.me_ref, s32[1]{0:T(128)} %bitcast.1.z_ref, bf16[1024,768]{1,0:T(8,128)(2,1)S(1)} %copy-done.1, ...), custom_call_target="tpu_custom_call" | custom-call | flops 3221225472 | bytes 12000000 | tf_op jit(solution)/shard_map/pallas_call | solution.py:30
  36.5 1.5 %collective-permute-start.9 = (bf16[768,128]{1,0:T(8,128)(2,1)S(1)}, bf16[768,128]{1,0:T(8,128)(2,1)S(1)}, u32[]{:S(2)}, u32[]{:S(2)}) collective-permute-start(bf16[768,128]{1,0:T(8,128)(2,1)S(1)} %get-tuple-element.40), channel_id=1, source_target_pairs={{0,6},{1,7},{2,4},{3,5},{4,2},{5,3},{6,0},{7,1},{8,14},{9,15},{10,... | collective-permute-start | bytes 589832 | tf_op jit(solution)/shard_map/ppermute | solution.py:62
  38.6 1.6 %collective-permute-start.11 = (bf16[768,128]{1,0:T(8,128)(2,1)S(1)}, bf16[768,128]{1,0:T(8,128)(2,1)S(1)}, u32[]{:S(2)}, u32[]{:S(2)}) collective-permute-start(bf16[768,128]{1,0:T(8,128)(2,1)S(1)} %get-tuple-element.42.after_ref), channel_id=1, source_target_pairs={{0,4},{1,5},{2,6},{3,7},{4,0},{5,1},{6,2},{7,3},{8,12},{9,13},{10,... | collective-permute-start | bytes 589832 | tf_op jit(solution)/shard_map/ppermute | solution.py:62
  40.2 1.9 %shard_map.100 = (bf16[1024,768]{1,0:T(8,128)(2,1)S(1)}, bf16[1024,768]{1,0:T(8,128)(2,1)S(1)}) custom-call(s32[1]{0:T(128)} %bitcast.me_ref, bf16[1024,1024]{1,0:T(8,128)(2,1)S(1)} %get-tuple-element.23.grads_ref, bf16[1024,768]{1,0:T(8,128)(2,1)S(1)} %get-tuple-element.24.weights_ref, bf16[768,128]{1,0:T(8,128)(2,1)S(1)} %get-tuple-element.42.after_ref), custom_call_target="tpu_custom_call" | custom-call | flops 1610612736 | bytes 5000000 | tf_op jit(solution)/shard_map/pallas_call | solution.py:30
  42.2 3.3 %shard_map.101 = (f32[1024,768]{1,0:T(8,128)}, f32[8,128]{1,0:T(8,128)S(1)}) custom-call(bf16[1024,768]{1,0:T(8,128)(2,1)S(1)} %get-tuple-element.27.grad_hidden_ref, bf16[768,768]{1,0:T(8,128)(2,1)S(1)} %copy-done.9), custom_call_target="tpu_custom_call" | custom-call | flops 1207959552 | bytes 6000000 | tf_op jit(solution)/shard_map/pallas_call | solution.py:231
  45.5 2.5 %collective-permute-done.10.refs_1_ = bf16[768,128]{1,0:T(8,128)(2,1)S(1)} collective-permute-done((bf16[768,128]{1,0:T(8,128)(2,1)S(1)}, bf16[768,128]{1,0:T(8,128)(2,1)S(1)}, u32[]{:S(2)}, u32[]{:S(2)}) %collective-permute-start.10) | collective-permute-done | bytes 196640 | tf_op jit(solution)/shard_map/ppermute | solution.py:62
  48.9 1.6 %collective-permute-start.12 = (bf16[384,128]{1,0:T(8,128)(2,1)S(1)}, bf16[384,128]{1,0:T(8,128)(2,1)S(1)}, u32[]{:S(2)}, u32[]{:S(2)}) collective-permute-start(bf16[384,128]{1,0:T(8,128)(2,1)S(1)} %get-tuple-element.35), channel_id=1, source_target_pairs={{0,8},{8,0},{16,24},{24,16},{1,9},{9,1},{17,25},{25,17},{2,10},{10... | collective-permute-start | bytes 294920 | tf_op jit(solution)/shard_map/ppermute | solution.py:62
  50.5 3.1 %collective-permute-done.12 = bf16[384,128]{1,0:T(8,128)(2,1)S(1)} collective-permute-done((bf16[384,128]{1,0:T(8,128)(2,1)S(1)}, bf16[384,128]{1,0:T(8,128)(2,1)S(1)}, u32[]{:S(2)}, u32[]{:S(2)}) %collective-permute-start.12) | collective-permute-done | bytes 98336 | tf_op jit(solution)/shard_map/ppermute | solution.py:62
  53.7 2.7 %collective-permute-start.13 = (bf16[384,128]{1,0:T(8,128)(2,1)S(1)}, bf16[384,128]{1,0:T(8,128)(2,1)S(1)}, u32[]{:S(2)}, u32[]{:S(2)}) collective-permute-start(bf16[384,128]{1,0:T(8,128)(2,1)S(1)} %add_convert_fusion.1), channel_id=1, source_target_pairs={{0,16},{8,24},{16,0},{24,8},{1,17},{9,25},{17,1},{25,9},{2,18},{10... | collective-permute-start | bytes 294920 | tf_op jit(solution)/shard_map/ppermute | solution.py:62
  56.4 4.4 %collective-permute-done.13 = bf16[384,128]{1,0:T(8,128)(2,1)S(1)} collective-permute-done((bf16[384,128]{1,0:T(8,128)(2,1)S(1)}, bf16[384,128]{1,0:T(8,128)(2,1)S(1)}, u32[]{:S(2)}, u32[]{:S(2)}) %collective-permute-start.13) | collective-permute-done | bytes 98336 | tf_op jit(solution)/shard_map/ppermute | solution.py:62
  61.9 1.6 %collective-permute-start.17 = (bf16[384,128]{1,0:T(8,128)(2,1)S(1)}, bf16[384,128]{1,0:T(8,128)(2,1)S(1)}, u32[]{:S(2)}, u32[]{:S(2)}) collective-permute-start(bf16[384,128]{1,0:T(8,128)(2,1)S(1)} %add_convert_fusion.refs_0_), channel_id=1, source_target_pairs={{0,4},{1,5},{2,6},{3,7},{4,0},{5,1},{6,2},{7,3},{8,12},{9,13},{10,... | collective-permute-start | bytes 294920 | tf_op jit(solution)/shard_map/ppermute | solution.py:62
  63.4 1.5 %collective-permute-start.19 = (bf16[384,128]{1,0:T(8,128)(2,1)S(1)}, bf16[384,128]{1,0:T(8,128)(2,1)S(1)}, u32[]{:S(2)}, u32[]{:S(2)}) collective-permute-start(bf16[384,128]{1,0:T(8,128)(2,1)S(1)} %add_convert_fusion.refs_0_), channel_id=1, source_target_pairs={{0,6},{1,7},{2,4},{3,5},{4,2},{5,3},{6,0},{7,1},{8,14},{9,15},{10,... | collective-permute-start | bytes 294920 | tf_op jit(solution)/shard_map/ppermute | solution.py:62
  66.0 1.5 %collective-permute-start.18 = (bf16[384,128]{1,0:T(8,128)(2,1)S(1)}, bf16[384,128]{1,0:T(8,128)(2,1)S(1)}, u32[]{:S(2)}, u32[]{:S(2)}) collective-permute-start(bf16[384,128]{1,0:T(8,128)(2,1)S(1)} %collective-permute-done.14.refs_1_), channel_id=1, source_target_pairs={{0,4},{1,5},{2,6},{3,7},{4,0},{5,1},{6,2},{7,3},{8,12},{9,13},{10,... | collective-permute-start | bytes 294920 | tf_op jit(solution)/shard_map/ppermute | solution.py:62
  67.5 1.5 %collective-permute-start.20 = (bf16[384,128]{1,0:T(8,128)(2,1)S(1)}, bf16[384,128]{1,0:T(8,128)(2,1)S(1)}, u32[]{:S(2)}, u32[]{:S(2)}) collective-permute-start(bf16[384,128]{1,0:T(8,128)(2,1)S(1)} %collective-permute-done.14.refs_1_), channel_id=1, source_target_pairs={{0,6},{1,7},{2,4},{3,5},{4,2},{5,3},{6,0},{7,1},{8,14},{9,15},{10,... | collective-permute-start | bytes 294920 | tf_op jit(solution)/shard_map/ppermute | solution.py:62
  70.9 2.4 %collective-permute-done.18.refs_5_ = bf16[384,128]{1,0:T(8,128)(2,1)S(1)} collective-permute-done((bf16[384,128]{1,0:T(8,128)(2,1)S(1)}, bf16[384,128]{1,0:T(8,128)(2,1)S(1)}, u32[]{:S(2)}, u32[]{:S(2)}) %collective-permute-start.18) | collective-permute-done | bytes 98336 | tf_op jit(solution)/shard_map/ppermute | solution.py:62
  75.3 1.4 %copy-done.14 = bf16[1024,768]{1,0:T(8,128)(2,1)S(1)} copy-done((bf16[1024,768]{1,0:T(8,128)(2,1)S(1)}, bf16[1024,768]{1,0:T(8,128)(2,1)}, u32[]{:S(2)}) %copy-start.14) | copy-done | bytes 1572888
  76.7 3.3 %shard_map.103 = (f32[768,768]{1,0:T(8,128)}, f32[192,128]{1,0:T(8,128)}) custom-call(s32[1]{0:T(128)} %bitcast.me_ref, s32[1]{0:T(128)} %bitcast.1.z_ref, bf16[384,128]{1,0:T(8,128)(2,1)S(1)} %add_convert_fusion.refs_0_, bf16[384,128]{1,0:T(8,128)(2,1)S(1)} %collective-permute-done.14.refs_1_, bf16[384,128]{1,0:T(8,128)(2,1)S(1)} %collective-permute-done.15.refs_2_, ...), custom_call_target="tpu_custom_call" | custom-call | flops 1207959552 | bytes 6000000 | tf_op jit(solution)/shard_map/pallas_call | solution.py:30
  (88 shorter events, 18.2 us)
Async XLA Ops:
  0.6 10.7 %collective-permute-start = (bf16[128,768]{1,0:T(8,128)(2,1)}, bf16[128,768]{1,0:T(8,128)(2,1)S(1)}, u32[]{:S(2)}, u32[]{:S(2)}) collective-permute-start(bf16[128,768]{1,0:T(8,128)(2,1)} %refs_0_.1), channel_id=1, source_target_pairs={{0,2},{1,3},{2,0},{3,1},{4,6},{5,7},{6,4},{7,5},{8,10},{9,11},{10,... | collective-permute-start | bytes 589832 | tf_op jit(solution)/shard_map/ppermute | solution.py:62
  3.6 10.8 %collective-permute-start.1 = (bf16[128,768]{1,0:T(8,128)(2,1)}, bf16[128,768]{1,0:T(8,128)(2,1)S(1)}, u32[]{:S(2)}, u32[]{:S(2)}) collective-permute-start(bf16[128,768]{1,0:T(8,128)(2,1)} %refs_0_.1), channel_id=1, source_target_pairs={{0,4},{1,5},{2,6},{3,7},{4,0},{5,1},{6,2},{7,3},{8,12},{9,13},{10,... | collective-permute-start | bytes 589832 | tf_op jit(solution)/shard_map/ppermute | solution.py:62
  5.2 9.9 %collective-permute-start.2 = (bf16[128,768]{1,0:T(8,128)(2,1)}, bf16[128,768]{1,0:T(8,128)(2,1)S(1)}, u32[]{:S(2)}, u32[]{:S(2)}) collective-permute-start(bf16[128,768]{1,0:T(8,128)(2,1)} %refs_0_.1), channel_id=1, source_target_pairs={{0,6},{1,7},{2,4},{3,5},{4,2},{5,3},{6,0},{7,1},{8,14},{9,15},{10,... | collective-permute-start | bytes 589832 | tf_op jit(solution)/shard_map/ppermute | solution.py:62
  5.2 19.9 %collective-permute-start.3 = (bf16[128,768]{1,0:T(8,128)(2,1)}, bf16[128,768]{1,0:T(8,128)(2,1)}, u32[]{:S(2)}, u32[]{:S(2)}) collective-permute-start(bf16[128,768]{1,0:T(8,128)(2,1)} %refs_0_.1), channel_id=1, source_target_pairs={{0,1},{1,0},{2,3},{3,2},{4,5},{5,4},{6,7},{7,6},{8,9},{9,8},{10,11... | collective-permute-start | bytes 589832 | tf_op jit(solution)/shard_map/ppermute | solution.py:62
  12.0 13.1 %collective-permute-start.4 = (bf16[128,768]{1,0:T(8,128)(2,1)}, bf16[128,768]{1,0:T(8,128)(2,1)}, u32[]{:S(2)}, u32[]{:S(2)}) collective-permute-start(bf16[128,768]{1,0:T(8,128)(2,1)} %shard_map.95.refs_1_), channel_id=1, source_target_pairs={{0,1},{1,0},{2,3},{3,2},{4,5},{5,4},{6,7},{7,6},{8,9},{9,8},{10,11... | collective-permute-start | bytes 589832 | tf_op jit(solution)/shard_map/ppermute | solution.py:62
  15.1 10.0 %collective-permute-start.5 = (bf16[128,768]{1,0:T(8,128)(2,1)}, bf16[128,768]{1,0:T(8,128)(2,1)}, u32[]{:S(2)}, u32[]{:S(2)}) collective-permute-start(bf16[128,768]{1,0:T(8,128)(2,1)} %shard_map.96.refs_2_), channel_id=1, source_target_pairs={{0,1},{1,0},{2,3},{3,2},{4,5},{5,4},{6,7},{7,6},{8,9},{9,8},{10,11... | collective-permute-start | bytes 589832 | tf_op jit(solution)/shard_map/ppermute | solution.py:62
  15.8 9.3 %collective-permute-start.6 = (bf16[128,768]{1,0:T(8,128)(2,1)}, bf16[128,768]{1,0:T(8,128)(2,1)S(1)}, u32[]{:S(2)}, u32[]{:S(2)}) collective-permute-start(bf16[128,768]{1,0:T(8,128)(2,1)} %shard_map.97.refs_3_), channel_id=1, source_target_pairs={{0,1},{1,0},{2,3},{3,2},{4,5},{5,4},{6,7},{7,6},{8,9},{9,8},{10,11... | collective-permute-start | bytes 589832 | tf_op jit(solution)/shard_map/ppermute | solution.py:62
  35.0 3.6 %collective-permute-start.7 = (bf16[2,768,128]{2,1,0:T(8,128)(2,1)S(1)}, bf16[2,768,128]{2,1,0:T(8,128)(2,1)S(1)}, u32[]{:S(2)}, u32[]{:S(2)}) collective-permute-start(bf16[2,768,128]{2,1,0:T(8,128)(2,1)S(1)} %get-tuple-element.26), channel_id=1, source_target_pairs={{0,1},{1,0},{2,3},{3,2},{4,5},{5,4},{6,7},{7,6},{8,9},{9,8},{10,11... | collective-permute-start | bytes 1179656 | tf_op jit(solution)/shard_map/ppermute | solution.py:62
  36.5 9.0 %collective-permute-start.9 = (bf16[768,128]{1,0:T(8,128)(2,1)S(1)}, bf16[768,128]{1,0:T(8,128)(2,1)S(1)}, u32[]{:S(2)}, u32[]{:S(2)}) collective-permute-start(bf16[768,128]{1,0:T(8,128)(2,1)S(1)} %get-tuple-element.40), channel_id=1, source_target_pairs={{0,6},{1,7},{2,4},{3,5},{4,2},{5,3},{6,0},{7,1},{8,14},{9,15},{10,... | collective-permute-start | bytes 589832 | tf_op jit(solution)/shard_map/ppermute | solution.py:62
  38.0 9.9 %collective-permute-start.10 = (bf16[768,128]{1,0:T(8,128)(2,1)S(1)}, bf16[768,128]{1,0:T(8,128)(2,1)S(1)}, u32[]{:S(2)}, u32[]{:S(2)}) collective-permute-start(bf16[768,128]{1,0:T(8,128)(2,1)S(1)} %get-tuple-element.39), channel_id=1, source_target_pairs={{0,2},{1,3},{2,0},{3,1},{4,6},{5,7},{6,4},{7,5},{8,10},{9,11},{10,... | collective-permute-start | bytes 589832 | tf_op jit(solution)/shard_map/ppermute | solution.py:62
  38.6 10.2 %collective-permute-start.11 = (bf16[768,128]{1,0:T(8,128)(2,1)S(1)}, bf16[768,128]{1,0:T(8,128)(2,1)S(1)}, u32[]{:S(2)}, u32[]{:S(2)}) collective-permute-start(bf16[768,128]{1,0:T(8,128)(2,1)S(1)} %get-tuple-element.42.after_ref), channel_id=1, source_target_pairs={{0,4},{1,5},{2,6},{3,7},{4,0},{5,1},{6,2},{7,3},{8,12},{9,13},{10,... | collective-permute-start | bytes 589832 | tf_op jit(solution)/shard_map/ppermute | solution.py:62
  48.9 4.8 %collective-permute-start.12 = (bf16[384,128]{1,0:T(8,128)(2,1)S(1)}, bf16[384,128]{1,0:T(8,128)(2,1)S(1)}, u32[]{:S(2)}, u32[]{:S(2)}) collective-permute-start(bf16[384,128]{1,0:T(8,128)(2,1)S(1)} %get-tuple-element.35), channel_id=1, source_target_pairs={{0,8},{8,0},{16,24},{24,16},{1,9},{9,1},{17,25},{25,17},{2,10},{10... | collective-permute-start | bytes 294920 | tf_op jit(solution)/shard_map/ppermute | solution.py:62
  53.7 7.0 %collective-permute-start.13 = (bf16[384,128]{1,0:T(8,128)(2,1)S(1)}, bf16[384,128]{1,0:T(8,128)(2,1)S(1)}, u32[]{:S(2)}, u32[]{:S(2)}) collective-permute-start(bf16[384,128]{1,0:T(8,128)(2,1)S(1)} %add_convert_fusion.1), channel_id=1, source_target_pairs={{0,16},{8,24},{16,0},{24,8},{1,17},{9,25},{17,1},{25,9},{2,18},{10... | collective-permute-start | bytes 294920 | tf_op jit(solution)/shard_map/ppermute | solution.py:62
  60.8 4.7 %collective-permute-start.14 = (bf16[384,128]{1,0:T(8,128)(2,1)S(1)}, bf16[384,128]{1,0:T(8,128)(2,1)S(1)}, u32[]{:S(2)}, u32[]{:S(2)}) collective-permute-start(bf16[384,128]{1,0:T(8,128)(2,1)S(1)} %add_convert_fusion.refs_0_), channel_id=1, source_target_pairs={{0,8},{8,0},{16,24},{24,16},{1,9},{9,1},{17,25},{25,17},{2,10},{10... | collective-permute-start | bytes 294920 | tf_op jit(solution)/shard_map/ppermute | solution.py:62
  61.4 4.6 %collective-permute-start.15 = (bf16[384,128]{1,0:T(8,128)(2,1)S(1)}, bf16[384,128]{1,0:T(8,128)(2,1)S(1)}, u32[]{:S(2)}, u32[]{:S(2)}) collective-permute-start(bf16[384,128]{1,0:T(8,128)(2,1)S(1)} %add_convert_fusion.refs_0_), channel_id=1, source_target_pairs={{0,2},{1,3},{2,0},{3,1},{4,6},{5,7},{6,4},{7,5},{8,10},{9,11},{10,... | collective-permute-start | bytes 294920 | tf_op jit(solution)/shard_map/ppermute | solution.py:62
  61.9 5.6 %collective-permute-start.17 = (bf16[384,128]{1,0:T(8,128)(2,1)S(1)}, bf16[384,128]{1,0:T(8,128)(2,1)S(1)}, u32[]{:S(2)}, u32[]{:S(2)}) collective-permute-start(bf16[384,128]{1,0:T(8,128)(2,1)S(1)} %add_convert_fusion.refs_0_), channel_id=1, source_target_pairs={{0,4},{1,5},{2,6},{3,7},{4,0},{5,1},{6,2},{7,3},{8,12},{9,13},{10,... | collective-permute-start | bytes 294920 | tf_op jit(solution)/shard_map/ppermute | solution.py:62
  63.4 6.5 %collective-permute-start.19 = (bf16[384,128]{1,0:T(8,128)(2,1)S(1)}, bf16[384,128]{1,0:T(8,128)(2,1)S(1)}, u32[]{:S(2)}, u32[]{:S(2)}) collective-permute-start(bf16[384,128]{1,0:T(8,128)(2,1)S(1)} %add_convert_fusion.refs_0_), channel_id=1, source_target_pairs={{0,6},{1,7},{2,4},{3,5},{4,2},{5,3},{6,0},{7,1},{8,14},{9,15},{10,... | collective-permute-start | bytes 294920 | tf_op jit(solution)/shard_map/ppermute | solution.py:62
  64.9 5.0 %collective-permute-start.21 = (bf16[384,128]{1,0:T(8,128)(2,1)S(1)}, bf16[384,128]{1,0:T(8,128)(2,1)S(1)}, u32[]{:S(2)}, u32[]{:S(2)}) collective-permute-start(bf16[384,128]{1,0:T(8,128)(2,1)S(1)} %add_convert_fusion.refs_0_), channel_id=1, source_target_pairs={{0,1},{1,0},{2,3},{3,2},{4,5},{5,4},{6,7},{7,6},{8,9},{9,8},{10,11... | collective-permute-start | bytes 294920 | tf_op jit(solution)/shard_map/ppermute | solution.py:62
  65.5 5.4 %collective-permute-start.16 = (bf16[384,128]{1,0:T(8,128)(2,1)S(1)}, bf16[384,128]{1,0:T(8,128)(2,1)S(1)}, u32[]{:S(2)}, u32[]{:S(2)}) collective-permute-start(bf16[384,128]{1,0:T(8,128)(2,1)S(1)} %collective-permute-done.14.refs_1_), channel_id=1, source_target_pairs={{0,2},{1,3},{2,0},{3,1},{4,6},{5,7},{6,4},{7,5},{8,10},{9,11},{10,... | collective-permute-start | bytes 294920 | tf_op jit(solution)/shard_map/ppermute | solution.py:62
  66.0 7.3 %collective-permute-start.18 = (bf16[384,128]{1,0:T(8,128)(2,1)S(1)}, bf16[384,128]{1,0:T(8,128)(2,1)S(1)}, u32[]{:S(2)}, u32[]{:S(2)}) collective-permute-start(bf16[384,128]{1,0:T(8,128)(2,1)S(1)} %collective-permute-done.14.refs_1_), channel_id=1, source_target_pairs={{0,4},{1,5},{2,6},{3,7},{4,0},{5,1},{6,2},{7,3},{8,12},{9,13},{10,... | collective-permute-start | bytes 294920 | tf_op jit(solution)/shard_map/ppermute | solution.py:62
  67.5 5.8 %collective-permute-start.20 = (bf16[384,128]{1,0:T(8,128)(2,1)S(1)}, bf16[384,128]{1,0:T(8,128)(2,1)S(1)}, u32[]{:S(2)}, u32[]{:S(2)}) collective-permute-start(bf16[384,128]{1,0:T(8,128)(2,1)S(1)} %collective-permute-done.14.refs_1_), channel_id=1, source_target_pairs={{0,6},{1,7},{2,4},{3,5},{4,2},{5,3},{6,0},{7,1},{8,14},{9,15},{10,... | collective-permute-start | bytes 294920 | tf_op jit(solution)/shard_map/ppermute | solution.py:62
  69.9 3.9 %collective-permute-start.22 = (bf16[384,128]{1,0:T(8,128)(2,1)S(1)}, bf16[384,128]{1,0:T(8,128)(2,1)S(1)}, u32[]{:S(2)}, u32[]{:S(2)}) collective-permute-start(bf16[384,128]{1,0:T(8,128)(2,1)S(1)} %collective-permute-done.14.refs_1_), channel_id=1, source_target_pairs={{0,1},{1,0},{2,3},{3,2},{4,5},{5,4},{6,7},{7,6},{8,9},{9,8},{10,11... | collective-permute-start | bytes 294920 | tf_op jit(solution)/shard_map/ppermute | solution.py:62
  70.0 3.9 %collective-permute-start.23 = (bf16[384,128]{1,0:T(8,128)(2,1)S(1)}, bf16[384,128]{1,0:T(8,128)(2,1)S(1)}, u32[]{:S(2)}, u32[]{:S(2)}) collective-permute-start(bf16[384,128]{1,0:T(8,128)(2,1)S(1)} %collective-permute-done.15.refs_2_), channel_id=1, source_target_pairs={{0,1},{1,0},{2,3},{3,2},{4,5},{5,4},{6,7},{7,6},{8,9},{9,8},{10,11... | collective-permute-start | bytes 294920 | tf_op jit(solution)/shard_map/ppermute | solution.py:62
  70.9 3.6 %collective-permute-start.25 = (bf16[384,128]{1,0:T(8,128)(2,1)S(1)}, bf16[384,128]{1,0:T(8,128)(2,1)S(1)}, u32[]{:S(2)}, u32[]{:S(2)}) collective-permute-start(bf16[384,128]{1,0:T(8,128)(2,1)S(1)} %collective-permute-done.17.refs_4_), channel_id=1, source_target_pairs={{0,1},{1,0},{2,3},{3,2},{4,5},{5,4},{6,7},{7,6},{8,9},{9,8},{10,11... | collective-permute-start | bytes 294920 | tf_op jit(solution)/shard_map/ppermute | solution.py:62
  (22 other events, 55.1 us)

commit v4 on v3

v4 whole, which is shorter than its diff:
```python
import functools

import jax
import jax.numpy as jnp
from jax import lax
from jax.experimental import pallas as pl
from jax.experimental.pallas import tpu as pltpu
from jax.sharding import PartitionSpec as P

BF16 = jnp.bfloat16
F32 = jnp.float32
VMEM = pl.BlockSpec(memory_space=pltpu.VMEM)
SMEM = pl.BlockSpec(memory_space=pltpu.SMEM)
ANY = pl.BlockSpec(memory_space=pl.ANY)
MIB = 1024 * 1024
TAIL = 16
NN = (((1,), (0,)), ((), ()))
NT = (((1,), (1,)), ((), ()))
TN = (((0,), (0,)), ((), ()))


def dot(left, right, dims):
    return lax.dot_general(left, right, dims, preferred_element_type=F32)


def shape(dims, dtype):
    return jax.ShapeDtypeStruct(dims, dtype)


def call(kernel, outs, args, scalars=(), after=(), scratch=(), vmem=8, flops=0, nbytes=0):
    return pl.pallas_call(
        kernel,
        out_shape=outs,
        in_specs=[SMEM] * len(scalars) + [VMEM] * len(args) + [ANY] * len(after),
        out_specs=[VMEM] * len(outs),
        scratch_shapes=list(scratch),
        compiler_params=pltpu.CompilerParams(vmem_limit_bytes=vmem * MIB),
        cost_estimate=pl.CostEstimate(flops=flops, bytes_accessed=nbytes, transcendentals=0),
    )(*scalars, *args, *after)


def gate(value, *after):
    return pl.pallas_call(
        lambda value_ref, *refs: None,
        out_shape=shape(value.shape, value.dtype),
        in_specs=[ANY] * (1 + len(after)),
        out_specs=ANY,
        input_output_aliases={0: 0},
        compiler_params=pltpu.CompilerParams(vmem_limit_bytes=MIB),
    )(value, *after)


def swap(value, axis, distance):
    size = lax.axis_size(axis)
    return lax.ppermute(value, axis, [(i, i ^ distance) for i in range(size)])


def payload_kernel(num_hbm, den_hbm, rows_hbm, out_ref, num_ref, den_ref, sems):
    size, width = rows_hbm.shape
    copies = [
        pltpu.make_async_copy(num_hbm, num_ref, sems.at[0]),
        pltpu.make_async_copy(den_hbm, den_ref, sems.at[1]),
        pltpu.make_async_copy(rows_hbm, out_ref.at[pl.ds(0, size), :], sems.at[2]),
    ]
    for copy in copies:
        copy.start()
    out_ref[size:, size:] = jnp.zeros((TAIL, width - size), BF16)
    copies[0].wait()
    copies[1].wait()
    row = lax.broadcasted_iota(jnp.int32, (TAIL, size), 0)
    both = jnp.where(row == 0, num_ref[...], den_ref[...])
    out_ref[size:, :size] = both.astype(F32).astype(BF16)
    copies[2].wait()


def inputs_kernel(enc_ref, proj_ref, hidden_ref, enc_t_ref):
    samples = enc_ref.shape[0]
    tile = min(256, samples)
    for start in range(0, samples, tile):
        rows = enc_ref[start : start + tile, :]
        enc_t_ref[:, start : start + tile] = rows.T
        hidden_ref[start : start + tile, :] = dot(rows, proj_ref[...], NN).astype(BF16)


def score_kernel(group, beam, block, count, list_ref, me_ref, z_ref, hidden_ref, wanted_ref, enc_t_ref, *refs):
    payloads, refs = refs[:2], refs[-8:]
    grads_ref, kept_ref, sent_ref, weights_ref, scale_ref, logits_ref = refs[-6:]
    samples = hidden_ref.shape[0]
    size = payloads[0].shape[0] - TAIL
    for core in range(2):
        rows = pl.ds(core * size, size)
        weights_ref[rows, :] = payloads[core][:size, :]
        tail = payloads[core][size:, :size].astype(F32)
        ratio = tail[0:1, :] / tail[1:2, :]
        scale_ref[rows, :] = jnp.broadcast_to(ratio, (block, size)).T / block
    logits_ref[...] = dot(weights_ref[...], hidden_ref[...], NT)
    grads_ref[...] = jnp.zeros_like(grads_ref)
    label_iota = lax.broadcasted_iota(jnp.int32, (size, block), 0)

    def one_block(at, carried):
        low = pl.multiple_of(at * block, block)
        for core in range(2):
            cluster = me_ref[0] ^ (2 * group + core)
            place = jnp.int32(-1)
            for beam_slot in range(beam):
                place = jnp.where(list_ref[at * beam + beam_slot] == cluster, beam_slot, place)

            @pl.when(place >= 0)
            def _():
                rows = slice(core * size, (core + 1) * size)
                labels = label_iota + place * size
                target = labels == wanted_ref[0:1, pl.ds(low, block)]
                for column in range(1, wanted_ref.shape[0]):
                    target = target | (labels == wanted_ref[column : column + 1, pl.ds(low, block)])
                share = jax.nn.sigmoid(logits_ref[rows, pl.ds(low, block)]) - jnp.where(target, 1.0, 0.0)
                grads_ref[rows, pl.ds(low, block)] = (scale_ref[rows, :] * share).astype(BF16)

        return carried

    lax.fori_loop(0, samples // block, one_block, 0)
    depth = enc_t_ref.shape[0] // count
    for r in range(count):
        start = pl.multiple_of((z_ref[0] ^ r) * depth, depth)
        outer = dot(enc_t_ref[pl.ds(start, depth), :], grads_ref[...], NT)
        kept_ref[r * depth : (r + 1) * depth, :] = outer[:, :size]
        sent_ref[r * depth : (r + 1) * depth, :] = outer[:, size:].astype(BF16)


def hidden_kernel(owners, me_ref, *refs):
    chips = owners // 2
    grads, payloads, refs = refs[:chips], refs[chips : chips + owners], refs[chips + owners :]
    out_ref, rows_ref, weights_ref = refs[-3:]
    size = payloads[0].shape[0] - TAIL
    for slot in range(owners):
        piece = payloads[slot][:size, :]
        start = pl.multiple_of((me_ref[0] ^ slot) * size, size)
        rows_ref[pl.ds(start, size), :] = piece
        weights_ref[slot * size : (slot + 1) * size, :] = piece
    samples = out_ref.shape[0]
    tile = min(256, samples)
    for low in range(0, samples, tile):
        total = jnp.zeros((tile, out_ref.shape[1]), F32)
        for group in range(chips):
            rows = weights_ref[2 * group * size : 2 * (group + 1) * size, :]
            total = total + dot(grads[group][:, low : low + tile], rows, TN)
        out_ref[low : low + tile, :] = total.astype(BF16)


def enc_kernel(grad_hidden_ref, proj_ref, after_ref, out_ref, done_ref):
    out_ref[...] = dot(grad_hidden_ref[...], proj_ref[...], NT)
    done_ref[...] = jnp.zeros_like(done_ref)


def combine_kernel(own_ref, *refs):
    *received, after_ref, kept_ref, sent_ref = refs
    cut = kept_ref.shape[0]
    for rows, out_ref in ((slice(cut, None), sent_ref), (slice(0, cut), kept_ref)):
        total = own_ref[rows, :]
        for ref in received:
            total = total + ref[rows, :].astype(F32)
        out_ref[...] = total.astype(out_ref.dtype)


def head_kernel(count, z_ref, *refs):
    parts, (slice_ref, whole_ref, head_ref) = refs[:count], refs[count:]
    depth = parts[0].shape[0]
    head = jnp.zeros(head_ref.shape, F32)
    for r in range(count):
        whole_ref[r * depth : (r + 1) * depth, :] = parts[r][...]
        start = pl.multiple_of((z_ref[0] ^ r) * depth, depth)
        head = head + dot(slice_ref[pl.ds(start, depth), :], parts[r][...], TN)
    head_ref[...] = head


def fetch_kernel(rows_any, after_ref, out_ref, sem):
    copy = pltpu.make_async_copy(rows_any, out_ref, sem)
    copy.start()
    copy.wait()


def proj_kernel(count, me_ref, z_ref, *refs):
    *parts, rows_ref, out_ref, outer_ref = refs
    width, size = parts[0].shape
    for distance, part in enumerate(parts):
        start = pl.multiple_of((me_ref[0] ^ distance) * size, size)
        outer_ref[:, pl.ds(start, size)] = part[...]
    depth = width // count
    for r in range(count):
        start = pl.multiple_of((z_ref[0] ^ r) * depth, depth)
        out_ref[pl.ds(start, depth), :] = dot(outer_ref[r * depth : (r + 1) * depth, :], rows_ref[...], NN)


def shards(enc, proj, head_weight, shortlist, positives, weight_num, weight_den):
    owners, planes = lax.axis_size("label"), lax.axis_size("dp")
    chips = owners // 2
    near = [g for g in range(1, chips) if g & (g - 1) == 0]
    far = [g for g in range(1, chips) if g & (g - 1) != 0]
    row_blocks = max(1, planes // 2)
    me = lax.axis_index("label").astype(jnp.int32)
    z = lax.axis_index("dp").astype(jnp.int32)
    z_low = z & (row_blocks - 1)
    blocks, beam = shortlist.shape
    samples, width = enc.shape
    block = samples // blocks
    size = head_weight.shape[0]
    labels = owners * size
    depth = width // row_blocks
    me_s, z_s = me.reshape(1), z_low.reshape(1)
    listed = shortlist.astype(jnp.int32).reshape(-1)

    (payload,) = pl.pallas_call(
        payload_kernel,
        out_shape=[shape((size + TAIL, width), BF16)],
        in_specs=[ANY] * 3,
        out_specs=[VMEM],
        scratch_shapes=[pltpu.VMEM((1, size), jnp.int32)] * 2 + [pltpu.SemaphoreType.DMA((3,))],
        compiler_params=pltpu.CompilerParams(vmem_limit_bytes=56 * MIB),
    )(weight_num.reshape(1, size), weight_den.reshape(1, size), head_weight)
    got = {0: payload}
    for g in near:
        got[2 * g] = swap(payload, "label", 2 * g)
    got[1] = swap(payload, "label", 1)
    hidden, enc_t = call(
        inputs_kernel,
        [shape((samples, width), BF16), shape((width, samples), BF16)],
        [enc, proj],
        flops=2 * samples * width * width,
        nbytes=6_000_000,
    )
    late = gate(payload, hidden) if far else payload
    for g in far:
        got[2 * g] = swap(late, "label", 2 * g)
    for g in near + far:
        got[2 * g] = gate(got[2 * g], hidden)
        got[2 * g + 1] = swap(got[2 * g], "label", 1)

    grads, kept, from_core, moved, received = {}, {}, {}, {}, {}
    order = [0] + near + far
    wanted = positives.T
    for at, g in enumerate(order):
        if at == 0:
            after = [got[2 * n] for n in near]
        else:
            after = [grads[order[at - 1]]]
            if at + 1 < len(order):
                after.append(got[2 * order[at + 1]])
            if at >= 3:
                after.append(moved[order[at - 2]])
        grads[g], kept[g], sent = call(
            functools.partial(score_kernel, g, beam, block, row_blocks),
            [shape((2 * size, samples), BF16), shape((width, size), F32), shape((width, size), BF16)],
            [hidden, wanted, enc_t, got[2 * g], got[2 * g + 1]],
            scalars=[listed, me_s, z_s],
            after=after,
            scratch=[
                pltpu.VMEM((2 * size, width), BF16),
                pltpu.VMEM((2 * size, block), F32),
                pltpu.VMEM((2 * size, samples), F32),
            ],
            flops=8 * samples * size * width,
            nbytes=5_000_000,
        )
        from_core[g] = swap(sent, "label", 1)
        if g:
            moved[g] = (kept[g] + from_core[g].astype(F32)).astype(BF16)
            received[g] = swap(moved[g], "label", 2 * g)
    own = kept[0] + from_core[0].astype(F32)
    received = [received[g] for g in near + far]

    grad_hidden, rows = call(
        functools.partial(hidden_kernel, owners),
        [shape((samples, width), BF16), shape((labels, width), BF16)],
        [grads[g] for g in range(chips)] + [got[d] for d in range(owners)],
        scalars=[me_s],
        after=[moved[g] for g in near + far],
        scratch=[pltpu.VMEM((labels, width), BF16)],
        vmem=12,
        flops=2 * samples * width * labels,
        nbytes=5_000_000,
    )
    tile = min(256, samples)

    def grad_enc_after(value):
        return pl.pallas_call(
            enc_kernel,
            grid=(samples // tile,),
            out_shape=[shape((samples, width), F32), shape((8, 128), F32)],
            in_specs=[
                pl.BlockSpec((tile, width), lambda i: (i, 0)),
                pl.BlockSpec((width, width), lambda i: (0, 0)),
                ANY,
            ],
            out_specs=[
                pl.BlockSpec((tile, width), lambda i: (i, 0)),
                pl.BlockSpec((8, 128), lambda i: (0, 0)),
            ],
            compiler_params=pltpu.CompilerParams(vmem_limit_bytes=12 * MIB),
            cost_estimate=pl.CostEstimate(
                flops=2 * samples * width * width, bytes_accessed=6_000_000, transcendentals=0
            ),
        )(grad_hidden, proj, value)

    if row_blocks > 1:
        cut = width // 2
        total, upper = call(
            combine_kernel,
            [shape((cut, size), F32), shape((cut, size), BF16)],
            [own] + received,
            after=[grad_hidden],
            nbytes=2_000_000,
        )
        span = row_blocks // 2
        grad_enc, enc_done = grad_enc_after(upper)
        total = total + gate(swap(upper, "dp", span), enc_done).astype(F32)
        while span > 1:
            cut = span // 2 * depth
            total = total[:cut] + swap(total[cut:].astype(BF16), "dp", span // 2).astype(F32)
            span //= 2
    else:
        total = own
        for value in received:
            total = total + value.astype(F32)
        grad_enc, enc_done = grad_enc_after(total)
    total = total.astype(BF16)
    if planes > 1:
        other = swap(total, "dp", planes // 2)
        total = (total.astype(F32) + other.astype(F32)).astype(BF16)
    parts = {0: total}
    span = 1
    while span < row_blocks:
        for r in range(span):
            parts[r + span] = swap(parts[r], "dp", span)
        span *= 2
    proj_slice = lax.dynamic_slice_in_dim(proj, z * (width // planes), width // planes, 1)
    whole, grad_head = call(
        functools.partial(head_kernel, row_blocks),
        [shape((width, size), BF16), shape((width // planes, size), F32)],
        [parts[r] for r in range(row_blocks)] + [proj_slice],
        scalars=[z_s],
        flops=2 * size * width * width // planes,
        nbytes=1_000_000,
    )
    (rows,) = pl.pallas_call(
        fetch_kernel,
        out_shape=[shape((labels, width), BF16)],
        in_specs=[ANY, ANY],
        out_specs=[VMEM],
        scratch_shapes=[pltpu.SemaphoreType.DMA],
        compiler_params=pltpu.CompilerParams(vmem_limit_bytes=2 * MIB),
        cost_estimate=pl.CostEstimate(flops=0, bytes_accessed=3_000_000, transcendentals=0),
    )(rows, whole)
    have = {0: whole}
    for g in near + far:
        have[2 * g] = swap(whole, "label", 2 * g)
    if near:
        have[2 * near[0]] = gate(have[2 * near[0]], rows)
    for distance in list(have):
        have[distance + 1] = swap(have[distance], "label", 1)
    (grad_proj,) = call(
        functools.partial(proj_kernel, row_blocks),
        [shape((width, width), F32)],
        [have[distance] for distance in range(owners)] + [rows],
        scalars=[me_s, z_s],
        scratch=[pltpu.VMEM((width, labels), BF16)],
        vmem=16,
        flops=2 * labels * width * width,
        nbytes=6_000_000,
    )
    return (grad_enc, grad_proj, grad_head.T)


def solution(mesh):
    placed = (
        P(("dp", "label"), None),
        P(),
        P("label", None),
        P(("dp", "label"), None),
        P(("dp", "label"), None),
        P("label"),
        P("label"),
    )
    return jax.shard_map(
        shards,
        mesh=mesh,
        in_specs=placed,
        out_specs=(P(("dp", "label"), None), P(), P("label", "dp")),
        check_vma=False,
    )
```

time: 80.4 us -> 73.5 us (0.914)
  blocking collectives: 8.76 us -> 0 us
  Pallas kernels: 17 us -> 25.3 us
  local copies, waits for them, and re-layouts: 11.1 us -> 4.68 us
  waiting for transfers between devices: 18.3 us -> 20.8 us
  starting transfers between devices: 23.1 us -> 21.3 us
    all_gather x1 -> x0, blocking collectives: 8.76 us -> none  [shards(): lax.all_gather(ratio, 'label', axis=0, tiled=True).reshape(owners, size)]
    pallas_call x6 -> x9, Pallas kernels: 13.7 us -> 20.2 us  [call(): pl.pallas_call(kernel, out_shape=outs, in_specs=[SMEM] * len(scalars) + [...]
    unnamed x34 -> x16, local copies, waits for them, and re-layouts: 10.8 us -> 4.41 us
    ppermute x29 -> x24, waiting for transfers between devices: 18.3 us -> 20.8 us  [swap(): return lax.ppermute(value, axis, [(i, i ^ distance) for i in range(size)])]
    ppermute x29 -> x24, starting transfers between devices: 23.1 us -> 21.3 us  [swap(): return lax.ppermute(value, axis, [(i, i ^ distance) for i in range(size)])]
    pallas_call x4 -> x9, Pallas kernels: 3.3 us -> 5.08 us  [the longest x1 3.29 us: grad_enc_after(): pl.pallas_call(enc_kernel, grid=(samples // tile,), out_shape=[shape((sam...]
  transfers between devices with their start and end apart: 29 -> 24, of which waited for: 15 -> 8; matrix products, arithmetic and copies ran while one was open for 2% -> 2% of each run, Pallas kernels for 10% -> 26%
where the time goes in v4:
time: 73.5 us; the launch traced here: 73.1 us
  Pallas kernels  25.3 us (34%)
  starting transfers between devices  21.3 us (29%)
  waiting for transfers between devices  20.8 us (28%)
  local copies, waits for them, and re-layouts  4.68 us (6%)
  between operations  0.8 us (1%)
    ppermute x24, starting transfers between devices, swap(): return lax.ppermute(value, axis, [(i, i ^ distance) for i in range(size)])  21.3 us
    ppermute x24, waiting for transfers between devices, swap(): return lax.ppermute(value, axis, [(i, i ^ distance) for i in range(size)])  20.8 us
    pallas_call x9, Pallas kernels, call(): pl.pallas_call(kernel, out_shape=outs, in_specs=[SMEM] * len(scalars) + [...  20.2 us
    unnamed x16, local copies, waits for them, and re-layouts  4.41 us
    pallas_call x1, Pallas kernels, grad_enc_after(): pl.pallas_call(enc_kernel, grid=(samples // tile,), out_shape=[shape((sam...  3.29 us
    pallas_call x1, Pallas kernels, shards(): pl.pallas_call(payload_kernel, out_shape=[shape((size + TAIL, width), BF1...  1.67 us
  transfers between devices with their start and end apart: 24, of which 8 were waited for; matrix products, arithmetic and copies ran while one was open for 2% of the time, Pallas kernels for 26%

profile of v4, /device:TPU:0, one launch (start us, length us, event | category | flops | bytes accessed | tf_op | source)
XLA Modules:
  0.0 73.1 jit_solution(14572172663783640505)
XLA Ops:
  0.6 1.7 %shard_map.95.refs_0_.refs_4_ = bf16[144,768]{1,0:T(8,128)(2,1)} custom-call(s32[1,128]{1,0:T(1,128)} %bitcast.10, s32[1,128]{1,0:T(1,128)} %bitcast.11, bf16[128,768]{1,0:T(8,128)(2,1)} %rows_hbm.1), custom_call_target="tpu_custom_call" | custom-call | tf_op jit(solution)/shard_map/pallas_call | solution.py:211
  2.3 3.0 %collective-permute-start.1 = (bf16[144,768]{1,0:T(8,128)(2,1)}, bf16[144,768]{1,0:T(8,128)(2,1)}, u32[]{:S(2)}, u32[]{:S(2)}) collective-permute-start(bf16[144,768]{1,0:T(8,128)(2,1)} %shard_map.95.refs_0_.refs_4_), channel_id=1, source_target_pairs={{0,2},{1,3},{2,0},{3,1},{4,6},{5,7},{6,4},{7,5},{8,10},{9,11},{10,... | collective-permute-start | bytes 663560 | tf_op jit(solution)/shard_map/ppermute | solution.py:55
  5.3 1.5 %collective-permute-start.2 = (bf16[144,768]{1,0:T(8,128)(2,1)}, bf16[144,768]{1,0:T(8,128)(2,1)S(1)}, u32[]{:S(2)}, u32[]{:S(2)}) collective-permute-start(bf16[144,768]{1,0:T(8,128)(2,1)} %shard_map.95.refs_0_.refs_4_), channel_id=1, source_target_pairs={{0,4},{1,5},{2,6},{3,7},{4,0},{5,1},{6,2},{7,3},{8,12},{9,13},{10,... | collective-permute-start | bytes 663560 | tf_op jit(solution)/shard_map/ppermute | solution.py:55
  6.8 1.3 %copy-done.3 = bf16[768,768]{1,0:T(8,128)(2,1)S(1)} copy-done((bf16[768,768]{1,0:T(8,128)(2,1)S(1)}, bf16[768,768]{1,0:T(8,128)(2,1)}, u32[]{:S(2)}) %copy-start.3) | copy-done | bytes 1179672
  8.1 1.4 %copy-done.5 = bf16[1024,768]{1,0:T(8,128)(2,1)S(1)} copy-done((bf16[1024,768]{1,0:T(8,128)(2,1)S(1)}, bf16[1024,768]{1,0:T(8,128)(2,1)}, u32[]{:S(2)}) %copy-start.5) | copy-done | bytes 1572888
  9.5 1.4 %shard_map.94 = (bf16[1024,768]{1,0:T(8,128)(2,1)S(1)}, bf16[768,1024]{1,0:T(8,128)(2,1)S(1)}) custom-call(bf16[1024,768]{1,0:T(8,128)(2,1)S(1)} %copy-done.5, bf16[768,768]{1,0:T(8,128)(2,1)S(1)} %copy-done.3), custom_call_target="tpu_custom_call" | custom-call | flops 1207959552 | bytes 6000000 | tf_op jit(solution)/shard_map/pallas_call | solution.py:31
  12.6 1.9 %collective-permute-start.5 = (bf16[144,768]{1,0:T(8,128)(2,1)}, bf16[144,768]{1,0:T(8,128)(2,1)}, u32[]{:S(2)}, u32[]{:S(2)}) collective-permute-start(bf16[144,768]{1,0:T(8,128)(2,1)} %shard_map.100), channel_id=1, source_target_pairs={{0,6},{1,7},{2,4},{3,5},{4,2},{5,3},{6,0},{7,1},{8,14},{9,15},{10,... | collective-permute-start | bytes 663560 | tf_op jit(solution)/shard_map/ppermute | solution.py:55
  15.6 3.2 %shard_map.98 = (bf16[256,1024]{1,0:T(8,128)(2,1)S(1)}, f32[768,128]{1,0:T(8,128)S(1)}, bf16[768,128]{1,0:T(8,128)(2,1)S(1)}) custom-call(s32[32]{0:T(128)S(1)} %reshape.22.list_ref, s32[1]{0:T(128)} %bitcast.me_ref, s32[1]{0:T(128)} %bitcast.1.z_ref, bf16[1024,768]{1,0:T(8,128)(2,1)S(1)} %get-tuple-element.25.refs_0_.hidden_ref, s32[8,1024]{1,0:T(8,128)S(1)} %bitcast.6, ...), custom_call_target="tpu_custom_call" | custom-call | flops 805306368 | bytes 5000000 | tf_op jit(solution)/shard_map/pallas_call | solution.py:31
  18.8 2.8 %shard_map.99 = (bf16[256,1024]{1,0:T(8,128)(2,1)S(1)}, f32[768,128]{1,0:T(8,128)S(1)}, bf16[768,128]{1,0:T(8,128)(2,1)S(1)}) custom-call(s32[32]{0:T(128)S(1)} %reshape.22.list_ref, s32[1]{0:T(128)} %bitcast.me_ref, s32[1]{0:T(128)} %bitcast.1.z_ref, bf16[1024,768]{1,0:T(8,128)(2,1)S(1)} %get-tuple-element.25.refs_0_.hidden_ref, s32[8,1024]{1,0:T(8,128)S(1)} %bitcast.7, ...), custom_call_target="tpu_custom_call" | custom-call | flops 805306368 | bytes 5000000 | tf_op jit(solution)/shard_map/pallas_call | solution.py:31
  22.4 2.6 %shard_map.102 = (bf16[256,1024]{1,0:T(8,128)(2,1)S(1)}, f32[768,128]{1,0:T(8,128)S(1)}, bf16[768,128]{1,0:T(8,128)(2,1)S(1)}) custom-call(s32[32]{0:T(128)S(1)} %reshape.22.list_ref, s32[1]{0:T(128)} %bitcast.me_ref, s32[1]{0:T(128)} %bitcast.1.z_ref, bf16[1024,768]{1,0:T(8,128)(2,1)S(1)} %get-tuple-element.25.refs_0_.hidden_ref, s32[8,1024]{1,0:T(8,128)S(1)} %bitcast.8, ...), custom_call_target="tpu_custom_call" | custom-call | flops 805306368 | bytes 5000000 | tf_op jit(solution)/shard_map/pallas_call | solution.py:31
  25.7 2.6 %shard_map.103 = (bf16[256,1024]{1,0:T(8,128)(2,1)S(1)}, f32[768,128]{1,0:T(8,128)S(1)}, bf16[768,128]{1,0:T(8,128)(2,1)S(1)}) custom-call(s32[32]{0:T(128)S(1)} %reshape.22.list_ref, s32[1]{0:T(128)} %bitcast.me_ref, s32[1]{0:T(128)} %bitcast.1.z_ref, bf16[1024,768]{1,0:T(8,128)(2,1)S(1)} %get-tuple-element.25.refs_0_.hidden_ref, s32[8,1024]{1,0:T(8,128)S(1)} %bitcast.9, ...), custom_call_target="tpu_custom_call" | custom-call | flops 805306368 | bytes 5000000 | tf_op jit(solution)/shard_map/pallas_call | solution.py:31
  28.6 1.7 %collective-permute-start.12 = (bf16[768,128]{1,0:T(8,128)(2,1)S(1)}, bf16[768,128]{1,0:T(8,128)(2,1)S(1)}, u32[]{:S(2)}, u32[]{:S(2)}) collective-permute-start(bf16[768,128]{1,0:T(8,128)(2,1)S(1)} %add_convert_fusion.1.refs_13_), channel_id=1, source_target_pairs={{0,4},{1,5},{2,6},{3,7},{4,0},{5,1},{6,2},{7,3},{8,12},{9,13},{10,... | collective-permute-start | bytes 589832 | tf_op jit(solution)/shard_map/ppermute | solution.py:55
  30.4 1.9 %collective-permute-start.13 = (bf16[768,128]{1,0:T(8,128)(2,1)S(1)}, bf16[768,128]{1,0:T(8,128)(2,1)S(1)}, u32[]{:S(2)}, u32[]{:S(2)}) collective-permute-start(bf16[768,128]{1,0:T(8,128)(2,1)S(1)} %add_convert_fusion.refs_14_), channel_id=1, source_target_pairs={{0,6},{1,7},{2,4},{3,5},{4,2},{5,3},{6,0},{7,1},{8,14},{9,15},{10,... | collective-permute-start | bytes 589832 | tf_op jit(solution)/shard_map/ppermute | solution.py:55
  32.3 3.2 %shard_map.104 = (bf16[1024,768]{1,0:T(8,128)(2,1)S(1)}, bf16[1024,768]{1,0:T(8,128)(2,1)S(1)}) custom-call(s32[1]{0:T(128)} %bitcast.me_ref, bf16[256,1024]{1,0:T(8,128)(2,1)S(1)} %get-tuple-element.27.refs_2_.refs_0_, bf16[256,1024]{1,0:T(8,128)(2,1)S(1)} %get-tuple-element.28.refs_2_.refs_1_, bf16[256,1024]{1,0:T(8,128)(2,1)S(1)} %get-tuple-element.29.refs_2_, ...), custom_call_target="tpu_custom_call" | custom-call | flops 1610612736 | bytes 5000000 | tf_op jit(solution)/shard_map/pallas_call | solution.py:31
  35.6 4.5 %collective-permute-done.12.refs_1_ = bf16[768,128]{1,0:T(8,128)(2,1)S(1)} collective-permute-done((bf16[768,128]{1,0:T(8,128)(2,1)S(1)}, bf16[768,128]{1,0:T(8,128)(2,1)S(1)}, u32[]{:S(2)}, u32[]{:S(2)}) %collective-permute-start.12) | collective-permute-done | bytes 196640 | tf_op jit(solution)/shard_map/ppermute | solution.py:55
  40.2 1.6 %collective-permute-start.14 = (bf16[384,128]{1,0:T(8,128)(2,1)S(1)}, bf16[384,128]{1,0:T(8,128)(2,1)S(1)}, u32[]{:S(2)}, u32[]{:S(2)}) collective-permute-start(bf16[384,128]{1,0:T(8,128)(2,1)S(1)} %get-tuple-element.40.after_ref), channel_id=1, source_target_pairs={{0,8},{8,0},{16,24},{24,16},{1,9},{9,1},{17,25},{25,17},{2,10},{10... | collective-permute-start | bytes 294920 | tf_op jit(solution)/shard_map/ppermute | solution.py:55
  41.8 3.3 %shard_map.106 = (f32[1024,768]{1,0:T(8,128)}, f32[8,128]{1,0:T(8,128)S(1)}) custom-call(bf16[1024,768]{1,0:T(8,128)(2,1)S(1)} %get-tuple-element.37.refs_3_.grad_hidden_ref, bf16[768,768]{1,0:T(8,128)(2,1)S(1)} %copy-done.4, bf16[384,128]{1,0:T(8,128)(2,1)S(1)} %get-tuple-element.40.after_ref), custom_call_target="tpu_custom_call" | custom-call | flops 1207959552 | bytes 6000000 | tf_op jit(solution)/shard_map/pallas_call | solution.py:284
  45.1 2.7 %collective-permute-start.15 = (bf16[384,128]{1,0:T(8,128)(2,1)S(1)}, bf16[384,128]{1,0:T(8,128)(2,1)S(1)}, u32[]{:S(2)}, u32[]{:S(2)}) collective-permute-start(bf16[384,128]{1,0:T(8,128)(2,1)S(1)} %add_convert_fusion.4), channel_id=1, source_target_pairs={{0,16},{8,24},{16,0},{24,8},{1,17},{9,25},{17,1},{25,9},{2,18},{10... | collective-permute-start | bytes 294920 | tf_op jit(solution)/shard_map/ppermute | solution.py:55
  47.8 4.3 %collective-permute-done.15 = bf16[384,128]{1,0:T(8,128)(2,1)S(1)} collective-permute-done((bf16[384,128]{1,0:T(8,128)(2,1)S(1)}, bf16[384,128]{1,0:T(8,128)(2,1)S(1)}, u32[]{:S(2)}, u32[]{:S(2)}) %collective-permute-start.15) | collective-permute-done | bytes 98336 | tf_op jit(solution)/shard_map/ppermute | solution.py:55
  52.6 4.3 %collective-permute-done.16.refs_1_ = bf16[384,128]{1,0:T(8,128)(2,1)S(1)} collective-permute-done((bf16[384,128]{1,0:T(8,128)(2,1)S(1)}, bf16[384,128]{1,0:T(8,128)(2,1)S(1)}, u32[]{:S(2)}, u32[]{:S(2)}) %collective-permute-start.16) | collective-permute-done | bytes 98336 | tf_op jit(solution)/shard_map/ppermute | solution.py:55
  57.8 2.3 %collective-permute-start.18 = (bf16[768,128]{1,0:T(8,128)(2,1)S(1)}, bf16[768,128]{1,0:T(8,128)(2,1)S(1)}, u32[]{:S(2)}, u32[]{:S(2)}) collective-permute-start(bf16[768,128]{1,0:T(8,128)(2,1)S(1)} %get-tuple-element.44.after_ref.refs_0_), channel_id=1, source_target_pairs={{0,2},{1,3},{2,0},{3,1},{4,6},{5,7},{6,4},{7,5},{8,10},{9,11},{10,... | collective-permute-start | bytes 589832 | tf_op jit(solution)/shard_map/ppermute | solution.py:55
  61.6 3.4 %collective-permute-done.18.value_ref = bf16[768,128]{1,0:T(8,128)(2,1)S(1)} collective-permute-done((bf16[768,128]{1,0:T(8,128)(2,1)S(1)}, bf16[768,128]{1,0:T(8,128)(2,1)S(1)}, u32[]{:S(2)}, u32[]{:S(2)}) %collective-permute-start.18) | collective-permute-done | bytes 196640 | tf_op jit(solution)/shard_map/ppermute | solution.py:55
  65.0 3.0 %collective-permute-done.20.refs_4_ = bf16[768,128]{1,0:T(8,128)(2,1)S(1)} collective-permute-done((bf16[768,128]{1,0:T(8,128)(2,1)S(1)}, bf16[768,128]{1,0:T(8,128)(2,1)S(1)}, u32[]{:S(2)}, u32[]{:S(2)}) %collective-permute-start.20) | collective-permute-done | bytes 196640 | tf_op jit(solution)/shard_map/ppermute | solution.py:55
  69.8 3.3 %shard_map.111 = f32[768,768]{1,0:T(8,128)} custom-call(s32[1]{0:T(128)} %bitcast.me_ref, s32[1]{0:T(128)} %bitcast.1.z_ref, bf16[768,128]{1,0:T(8,128)(2,1)S(1)} %get-tuple-element.44.after_ref.refs_0_, bf16[768,128]{1,0:T(8,128)(2,1)S(1)} %collective-permute-done.17.refs_1_, bf16[768,128]{1,0:T(8,128)(2,1)S(1)} %shard_map.110.refs_2_, ...), custom_call_target="tpu_custom_call" | custom-call | flops 1207959552 | bytes 6000000 | tf_op jit(solution)/shard_map/pallas_call | solution.py:31
  (66 shorter events, 9.4 us)
Async XLA Ops:
  2.3 8.7 %collective-permute-start.1 = (bf16[144,768]{1,0:T(8,128)(2,1)}, bf16[144,768]{1,0:T(8,128)(2,1)}, u32[]{:S(2)}, u32[]{:S(2)}) collective-permute-start(bf16[144,768]{1,0:T(8,128)(2,1)} %shard_map.95.refs_0_.refs_4_), channel_id=1, source_target_pairs={{0,2},{1,3},{2,0},{3,1},{4,6},{5,7},{6,4},{7,5},{8,10},{9,11},{10,... | collective-permute-start | bytes 663560 | tf_op jit(solution)/shard_map/ppermute | solution.py:55
  5.3 9.3 %collective-permute-start.2 = (bf16[144,768]{1,0:T(8,128)(2,1)}, bf16[144,768]{1,0:T(8,128)(2,1)S(1)}, u32[]{:S(2)}, u32[]{:S(2)}) collective-permute-start(bf16[144,768]{1,0:T(8,128)(2,1)} %shard_map.95.refs_0_.refs_4_), channel_id=1, source_target_pairs={{0,4},{1,5},{2,6},{3,7},{4,0},{5,1},{6,2},{7,3},{8,12},{9,13},{10,... | collective-permute-start | bytes 663560 | tf_op jit(solution)/shard_map/ppermute | solution.py:55
  6.8 8.1 %collective-permute-start = (bf16[144,768]{1,0:T(8,128)(2,1)}, bf16[144,768]{1,0:T(8,128)(2,1)}, u32[]{:S(2)}, u32[]{:S(2)}) collective-permute-start(bf16[144,768]{1,0:T(8,128)(2,1)} %shard_map.95.refs_0_.refs_4_), channel_id=1, source_target_pairs={{0,1},{1,0},{2,3},{3,2},{4,5},{5,4},{6,7},{7,6},{8,9},{9,8},{10,11... | collective-permute-start | bytes 663560 | tf_op jit(solution)/shard_map/ppermute | solution.py:55
  11.1 7.7 %collective-permute-start.3 = (bf16[144,768]{1,0:T(8,128)(2,1)}, bf16[144,768]{1,0:T(8,128)(2,1)}, u32[]{:S(2)}, u32[]{:S(2)}) collective-permute-start(bf16[144,768]{1,0:T(8,128)(2,1)} %shard_map.96.refs_2_.refs_0_.refs_6_), channel_id=1, source_target_pairs={{0,1},{1,0},{2,3},{3,2},{4,5},{5,4},{6,7},{7,6},{8,9},{9,8},{10,11... | collective-permute-start | bytes 663560 | tf_op jit(solution)/shard_map/ppermute | solution.py:55
  12.6 9.3 %collective-permute-start.5 = (bf16[144,768]{1,0:T(8,128)(2,1)}, bf16[144,768]{1,0:T(8,128)(2,1)}, u32[]{:S(2)}, u32[]{:S(2)}) collective-permute-start(bf16[144,768]{1,0:T(8,128)(2,1)} %shard_map.100), channel_id=1, source_target_pairs={{0,6},{1,7},{2,4},{3,5},{4,2},{5,3},{6,0},{7,1},{8,14},{9,15},{10,... | collective-permute-start | bytes 663560 | tf_op jit(solution)/shard_map/ppermute | solution.py:55
  14.6 7.7 %collective-permute-start.4 = (bf16[144,768]{1,0:T(8,128)(2,1)S(1)}, bf16[144,768]{1,0:T(8,128)(2,1)S(1)}, u32[]{:S(2)}, u32[]{:S(2)}) collective-permute-start(bf16[144,768]{1,0:T(8,128)(2,1)S(1)} %shard_map.97.refs_3_.refs_0_.refs_8_), channel_id=1, source_target_pairs={{0,1},{1,0},{2,3},{3,2},{4,5},{5,4},{6,7},{7,6},{8,9},{9,8},{10,11... | collective-permute-start | bytes 663560 | tf_op jit(solution)/shard_map/ppermute | solution.py:55
  21.6 3.8 %collective-permute-start.7 = (bf16[768,128]{1,0:T(8,128)(2,1)S(1)}, bf16[768,128]{1,0:T(8,128)(2,1)S(1)}, u32[]{:S(2)}, u32[]{:S(2)}) collective-permute-start(bf16[768,128]{1,0:T(8,128)(2,1)S(1)} %get-tuple-element.31), channel_id=1, source_target_pairs={{0,1},{1,0},{2,3},{3,2},{4,5},{5,4},{6,7},{7,6},{8,9},{9,8},{10,11... | collective-permute-start | bytes 589832 | tf_op jit(solution)/shard_map/ppermute | solution.py:55
  21.9 3.8 %collective-permute-start.6 = (bf16[144,768]{1,0:T(8,128)(2,1)}, bf16[144,768]{1,0:T(8,128)(2,1)S(1)}, u32[]{:S(2)}, u32[]{:S(2)}) collective-permute-start(bf16[144,768]{1,0:T(8,128)(2,1)} %shard_map.101.refs_3_.refs_0_.refs_10_), channel_id=1, source_target_pairs={{0,1},{1,0},{2,3},{3,2},{4,5},{5,4},{6,7},{7,6},{8,9},{9,8},{10,11... | collective-permute-start | bytes 663560 | tf_op jit(solution)/shard_map/ppermute | solution.py:55
  22.2 10.1 %collective-permute-start.10 = (bf16[768,128]{1,0:T(8,128)(2,1)S(1)}, bf16[768,128]{1,0:T(8,128)(2,1)S(1)}, u32[]{:S(2)}, u32[]{:S(2)}) collective-permute-start(bf16[768,128]{1,0:T(8,128)(2,1)S(1)} %get-tuple-element.39), channel_id=1, source_target_pairs={{0,1},{1,0},{2,3},{3,2},{4,5},{5,4},{6,7},{7,6},{8,9},{9,8},{10,11... | collective-permute-start | bytes 589832 | tf_op jit(solution)/shard_map/ppermute | solution.py:55
  25.0 3.6 %collective-permute-start.8 = (bf16[768,128]{1,0:T(8,128)(2,1)S(1)}, bf16[768,128]{1,0:T(8,128)(2,1)S(1)}, u32[]{:S(2)}, u32[]{:S(2)}) collective-permute-start(bf16[768,128]{1,0:T(8,128)(2,1)S(1)} %get-tuple-element.34), channel_id=1, source_target_pairs={{0,1},{1,0},{2,3},{3,2},{4,5},{5,4},{6,7},{7,6},{8,9},{9,8},{10,11... | collective-permute-start | bytes 589832 | tf_op jit(solution)/shard_map/ppermute | solution.py:55
  25.4 14.6 %collective-permute-start.11 = (bf16[768,128]{1,0:T(8,128)(2,1)S(1)}, bf16[768,128]{1,0:T(8,128)(2,1)S(1)}, u32[]{:S(2)}, u32[]{:S(2)}) collective-permute-start(bf16[768,128]{1,0:T(8,128)(2,1)S(1)} %add_convert_fusion.2.refs_3_.refs_12_), channel_id=1, source_target_pairs={{0,2},{1,3},{2,0},{3,1},{4,6},{5,7},{6,4},{7,5},{8,10},{9,11},{10,... | collective-permute-start | bytes 589832 | tf_op jit(solution)/shard_map/ppermute | solution.py:55
  28.3 2.0 %collective-permute-start.9 = (bf16[768,128]{1,0:T(8,128)(2,1)S(1)}, bf16[768,128]{1,0:T(8,128)(2,1)S(1)}, u32[]{:S(2)}, u32[]{:S(2)}) collective-permute-start(bf16[768,128]{1,0:T(8,128)(2,1)S(1)} %get-tuple-element.36), channel_id=1, source_target_pairs={{0,1},{1,0},{2,3},{3,2},{4,5},{5,4},{6,7},{7,6},{8,9},{9,8},{10,11... | collective-permute-start | bytes 589832 | tf_op jit(solution)/shard_map/ppermute | solution.py:55
  28.6 11.4 %collective-permute-start.12 = (bf16[768,128]{1,0:T(8,128)(2,1)S(1)}, bf16[768,128]{1,0:T(8,128)(2,1)S(1)}, u32[]{:S(2)}, u32[]{:S(2)}) collective-permute-start(bf16[768,128]{1,0:T(8,128)(2,1)S(1)} %add_convert_fusion.1.refs_13_), channel_id=1, source_target_pairs={{0,4},{1,5},{2,6},{3,7},{4,0},{5,1},{6,2},{7,3},{8,12},{9,13},{10,... | collective-permute-start | bytes 589832 | tf_op jit(solution)/shard_map/ppermute | solution.py:55
  30.4 9.7 %collective-permute-start.13 = (bf16[768,128]{1,0:T(8,128)(2,1)S(1)}, bf16[768,128]{1,0:T(8,128)(2,1)S(1)}, u32[]{:S(2)}, u32[]{:S(2)}) collective-permute-start(bf16[768,128]{1,0:T(8,128)(2,1)S(1)} %add_convert_fusion.refs_14_), channel_id=1, source_target_pairs={{0,6},{1,7},{2,4},{3,5},{4,2},{5,3},{6,0},{7,1},{8,14},{9,15},{10,... | collective-permute-start | bytes 589832 | tf_op jit(solution)/shard_map/ppermute | solution.py:55
  40.2 4.9 %collective-permute-start.14 = (bf16[384,128]{1,0:T(8,128)(2,1)S(1)}, bf16[384,128]{1,0:T(8,128)(2,1)S(1)}, u32[]{:S(2)}, u32[]{:S(2)}) collective-permute-start(bf16[384,128]{1,0:T(8,128)(2,1)S(1)} %get-tuple-element.40.after_ref), channel_id=1, source_target_pairs={{0,8},{8,0},{16,24},{24,16},{1,9},{9,1},{17,25},{25,17},{2,10},{10... | collective-permute-start | bytes 294920 | tf_op jit(solution)/shard_map/ppermute | solution.py:55
  45.1 7.0 %collective-permute-start.15 = (bf16[384,128]{1,0:T(8,128)(2,1)S(1)}, bf16[384,128]{1,0:T(8,128)(2,1)S(1)}, u32[]{:S(2)}, u32[]{:S(2)}) collective-permute-start(bf16[384,128]{1,0:T(8,128)(2,1)S(1)} %add_convert_fusion.4), channel_id=1, source_target_pairs={{0,16},{8,24},{16,0},{24,8},{1,17},{9,25},{17,1},{25,9},{2,18},{10... | collective-permute-start | bytes 294920 | tf_op jit(solution)/shard_map/ppermute | solution.py:55
  52.2 4.7 %collective-permute-start.16 = (bf16[384,128]{1,0:T(8,128)(2,1)S(1)}, bf16[384,128]{1,0:T(8,128)(2,1)S(1)}, u32[]{:S(2)}, u32[]{:S(2)}) collective-permute-start(bf16[384,128]{1,0:T(8,128)(2,1)S(1)} %add_convert_fusion.3.refs_0_), channel_id=1, source_target_pairs={{0,8},{8,0},{16,24},{24,16},{1,9},{9,1},{17,25},{25,17},{2,10},{10... | collective-permute-start | bytes 294920 | tf_op jit(solution)/shard_map/ppermute | solution.py:55
  57.8 7.2 %collective-permute-start.18 = (bf16[768,128]{1,0:T(8,128)(2,1)S(1)}, bf16[768,128]{1,0:T(8,128)(2,1)S(1)}, u32[]{:S(2)}, u32[]{:S(2)}) collective-permute-start(bf16[768,128]{1,0:T(8,128)(2,1)S(1)} %get-tuple-element.44.after_ref.refs_0_), channel_id=1, source_target_pairs={{0,2},{1,3},{2,0},{3,1},{4,6},{5,7},{6,4},{7,5},{8,10},{9,11},{10,... | collective-permute-start | bytes 589832 | tf_op jit(solution)/shard_map/ppermute | solution.py:55
  60.0 8.0 %collective-permute-start.20 = (bf16[768,128]{1,0:T(8,128)(2,1)S(1)}, bf16[768,128]{1,0:T(8,128)(2,1)S(1)}, u32[]{:S(2)}, u32[]{:S(2)}) collective-permute-start(bf16[768,128]{1,0:T(8,128)(2,1)S(1)} %get-tuple-element.44.after_ref.refs_0_), channel_id=1, source_target_pairs={{0,4},{1,5},{2,6},{3,7},{4,0},{5,1},{6,2},{7,3},{8,12},{9,13},{10,... | collective-permute-start | bytes 589832 | tf_op jit(solution)/shard_map/ppermute | solution.py:55
  60.7 7.4 %collective-permute-start.22 = (bf16[768,128]{1,0:T(8,128)(2,1)S(1)}, bf16[768,128]{1,0:T(8,128)(2,1)S(1)}, u32[]{:S(2)}, u32[]{:S(2)}) collective-permute-start(bf16[768,128]{1,0:T(8,128)(2,1)S(1)} %get-tuple-element.44.after_ref.refs_0_), channel_id=1, source_target_pairs={{0,6},{1,7},{2,4},{3,5},{4,2},{5,3},{6,0},{7,1},{8,14},{9,15},{10,... | collective-permute-start | bytes 589832 | tf_op jit(solution)/shard_map/ppermute | solution.py:55
  61.5 7.1 %collective-permute-start.17 = (bf16[768,128]{1,0:T(8,128)(2,1)S(1)}, bf16[768,128]{1,0:T(8,128)(2,1)S(1)}, u32[]{:S(2)}, u32[]{:S(2)}) collective-permute-start(bf16[768,128]{1,0:T(8,128)(2,1)S(1)} %get-tuple-element.44.after_ref.refs_0_), channel_id=1, source_target_pairs={{0,1},{1,0},{2,3},{3,2},{4,5},{5,4},{6,7},{7,6},{8,9},{9,8},{10,11... | collective-permute-start | bytes 589832 | tf_op jit(solution)/shard_map/ppermute | solution.py:55
  65.0 3.5 %collective-permute-start.19 = (bf16[768,128]{1,0:T(8,128)(2,1)S(1)}, bf16[768,128]{1,0:T(8,128)(2,1)S(1)}, u32[]{:S(2)}, u32[]{:S(2)}) collective-permute-start(bf16[768,128]{1,0:T(8,128)(2,1)S(1)} %shard_map.110.refs_2_), channel_id=1, source_target_pairs={{0,1},{1,0},{2,3},{3,2},{4,5},{5,4},{6,7},{7,6},{8,9},{9,8},{10,11... | collective-permute-start | bytes 589832 | tf_op jit(solution)/shard_map/ppermute | solution.py:55
  68.0 1.4 %collective-permute-start.21 = (bf16[768,128]{1,0:T(8,128)(2,1)S(1)}, bf16[768,128]{1,0:T(8,128)(2,1)S(1)}, u32[]{:S(2)}, u32[]{:S(2)}) collective-permute-start(bf16[768,128]{1,0:T(8,128)(2,1)S(1)} %collective-permute-done.20.refs_4_), channel_id=1, source_target_pairs={{0,1},{1,0},{2,3},{3,2},{4,5},{5,4},{6,7},{7,6},{8,9},{9,8},{10,11... | collective-permute-start | bytes 589832 | tf_op jit(solution)/shard_map/ppermute | solution.py:55
  68.1 1.7 %collective-permute-start.23 = (bf16[768,128]{1,0:T(8,128)(2,1)S(1)}, bf16[768,128]{1,0:T(8,128)(2,1)S(1)}, u32[]{:S(2)}, u32[]{:S(2)}) collective-permute-start(bf16[768,128]{1,0:T(8,128)(2,1)S(1)} %collective-permute-done.22.refs_6_), channel_id=1, source_target_pairs={{0,1},{1,0},{2,3},{3,2},{4,5},{5,4},{6,7},{7,6},{8,9},{9,8},{10,11... | collective-permute-start | bytes 589832 | tf_op jit(solution)/shard_map/ppermute | solution.py:55
  (7 other events, 16.5 us)

commit v5 on v4

--- a/solution.py
+++ b/solution.py
@@ -55,13 +55,17 @@
     return lax.ppermute(value, axis, [(i, i ^ distance) for i in range(size)])
 
 
-def payload_kernel(num_hbm, den_hbm, rows_hbm, out_ref, num_ref, den_ref, sems):
+def payload_kernel(num_hbm, den_hbm, rows_hbm, enc_hbm, proj_hbm, wanted_hbm, out_ref, enc_ref, proj_ref, wanted_ref, num_ref, den_ref, sems):
     size, width = rows_hbm.shape
-    copies = [
-        pltpu.make_async_copy(num_hbm, num_ref, sems.at[0]),
-        pltpu.make_async_copy(den_hbm, den_ref, sems.at[1]),
-        pltpu.make_async_copy(rows_hbm, out_ref.at[pl.ds(0, size), :], sems.at[2]),
+    pairs = [
+        (num_hbm, num_ref),
+        (den_hbm, den_ref),
+        (rows_hbm, out_ref.at[pl.ds(0, size), :]),
+        (wanted_hbm, wanted_ref),
+        (proj_hbm, proj_ref),
+        (enc_hbm, enc_ref),
     ]
+    copies = [pltpu.make_async_copy(a, b, sems.at[i]) for i, (a, b) in enumerate(pairs)]
     for copy in copies:
         copy.start()
     out_ref[size:, size:] = jnp.zeros((TAIL, width - size), BF16)
@@ -70,19 +74,37 @@
     row = lax.broadcasted_iota(jnp.int32, (TAIL, size), 0)
     both = jnp.where(row == 0, num_ref[...], den_ref[...])
     out_ref[size:, :size] = both.astype(F32).astype(BF16)
-    copies[2].wait()
-
-
-def inputs_kernel(enc_ref, proj_ref, hidden_ref, enc_t_ref):
+    for copy in copies[2:]:
+        copy.wait()
+
+
+def inputs_kernel(beam, block, enc_ref, proj_ref, wanted_ref, hidden_ref, enc_t_ref, target_ref):
     samples = enc_ref.shape[0]
+    size = target_ref.shape[0] // beam
+    label_iota = lax.broadcasted_iota(jnp.int32, (size, block), 0)
     tile = min(256, samples)
     for start in range(0, samples, tile):
         rows = enc_ref[start : start + tile, :]
         enc_t_ref[:, start : start + tile] = rows.T
         hidden_ref[start : start + tile, :] = dot(rows, proj_ref[...], NN).astype(BF16)
-
-
-def score_kernel(group, beam, block, count, list_ref, me_ref, z_ref, hidden_ref, wanted_ref, enc_t_ref, *refs):
+        for low in range(start, start + tile, block):
+            for place in range(beam):
+                labels = label_iota + place * size
+                target = labels == wanted_ref[0:1, low : low + block]
+                for column in range(1, wanted_ref.shape[0]):
+                    target = target | (labels == wanted_ref[column : column + 1, low : low + block])
+                target_ref[place * size : (place + 1) * size, low : low + block] = jnp.where(
+                    target, 1.0, 0.0
+                ).astype(BF16)
+
+
+def logistic(value):
+    bottom = 1.0 + jnp.exp(-jnp.maximum(value, -80.0))
+    guess = pl.reciprocal(bottom, approx=True)
+    return guess * (2.0 - bottom * guess)
+
+
+def score_kernel(group, block, count, list_ref, me_ref, z_ref, hidden_ref, target_ref, enc_t_ref, *refs):
     payloads, refs = refs[:2], refs[-8:]
     grads_ref, kept_ref, sent_ref, weights_ref, scale_ref, logits_ref = refs[-6:]
     samples = hidden_ref.shape[0]
@@ -95,35 +117,31 @@
         scale_ref[rows, :] = jnp.broadcast_to(ratio, (block, size)).T / block
     logits_ref[...] = dot(weights_ref[...], hidden_ref[...], NT)
     grads_ref[...] = jnp.zeros_like(grads_ref)
-    label_iota = lax.broadcasted_iota(jnp.int32, (size, block), 0)
 
     def one_block(at, carried):
         low = pl.multiple_of(at * block, block)
         for core in range(2):
             cluster = me_ref[0] ^ (2 * group + core)
             place = jnp.int32(-1)
-            for beam_slot in range(beam):
-                place = jnp.where(list_ref[at * beam + beam_slot] == cluster, beam_slot, place)
+            for beam_slot in range(list_ref.shape[0]):
+                place = jnp.where(list_ref[beam_slot, at] == cluster, beam_slot, place)
 
             @pl.when(place >= 0)
             def _():
                 rows = slice(core * size, (core + 1) * size)
-                labels = label_iota + place * size
-                target = labels == wanted_ref[0:1, pl.ds(low, block)]
-                for column in range(1, wanted_ref.shape[0]):
-                    target = target | (labels == wanted_ref[column : column + 1, pl.ds(low, block)])
-                share = jax.nn.sigmoid(logits_ref[rows, pl.ds(low, block)]) - jnp.where(target, 1.0, 0.0)
+                target = target_ref[pl.ds(pl.multiple_of(place * size, size), size), pl.ds(low, block)]
+                share = logistic(logits_ref[rows, pl.ds(low, block)]) - target.astype(F32)
                 grads_ref[rows, pl.ds(low, block)] = (scale_ref[rows, :] * share).astype(BF16)
 
         return carried
 
     lax.fori_loop(0, samples // block, one_block, 0)
+    outer = dot(enc_t_ref[...], grads_ref[...], NT)
     depth = enc_t_ref.shape[0] // count
     for r in range(count):
-        start = pl.multiple_of((z_ref[0] ^ r) * depth, depth)
-        outer = dot(enc_t_ref[pl.ds(start, depth), :], grads_ref[...], NT)
-        kept_ref[r * depth : (r + 1) * depth, :] = outer[:, :size]
-        sent_ref[r * depth : (r + 1) * depth, :] = outer[:, size:].astype(BF16)
+        rows = pl.ds(pl.multiple_of((z_ref[0] ^ r) * depth, depth), depth)
+        kept_ref[rows, :] = outer[r * depth : (r + 1) * depth, :size]
+        sent_ref[rows, :] = outer[r * depth : (r + 1) * depth, size:].astype(BF16)
 
 
 def hidden_kernel(owners, me_ref, *refs):
@@ -161,33 +179,45 @@
         out_ref[...] = total.astype(out_ref.dtype)
 
 
-def head_kernel(count, z_ref, *refs):
-    parts, (slice_ref, whole_ref, head_ref) = refs[:count], refs[count:]
+def whole_kernel(*refs):
+    *parts, whole_ref = refs
     depth = parts[0].shape[0]
+    for r, part in enumerate(parts):
+        whole_ref[r * depth : (r + 1) * depth, :] = part[...]
+
+
+def head_kernel(count, z_ref, rows_any, whole_ref, slice_ref, rows_ref, head_ref, sem):
+    copy = pltpu.make_async_copy(rows_any, rows_ref, sem)
+    copy.start()
+    depth = whole_ref.shape[0] // count
     head = jnp.zeros(head_ref.shape, F32)
     for r in range(count):
-        whole_ref[r * depth : (r + 1) * depth, :] = parts[r][...]
         start = pl.multiple_of((z_ref[0] ^ r) * depth, depth)
-        head = head + dot(slice_ref[pl.ds(start, depth), :], parts[r][...], TN)
+        head = head + dot(slice_ref[pl.ds(start, depth), :], whole_ref[r * depth : (r + 1) * depth, :], TN)
     head_ref[...] = head
-
-
-def fetch_kernel(rows_any, after_ref, out_ref, sem):
-    copy = pltpu.make_async_copy(rows_any, out_ref, sem)
-    copy.start()
     copy.wait()
 
 
-def proj_kernel(count, me_ref, z_ref, *refs):
-    *parts, rows_ref, out_ref, outer_ref = refs
+def proj_kernel(count, cuts, me_ref, z_ref, *refs):
+    *parts, rows_ref, out_hbm, outer_ref, done_ref, sems = refs
     width, size = parts[0].shape
     for distance, part in enumerate(parts):
         start = pl.multiple_of((me_ref[0] ^ distance) * size, size)
         outer_ref[:, pl.ds(start, size)] = part[...]
-    depth = width // count
+    depth, height = width // count, width // count // cuts
+    copies = []
     for r in range(count):
-        start = pl.multiple_of((z_ref[0] ^ r) * depth, depth)
-        out_ref[pl.ds(start, depth), :] = dot(outer_ref[r * depth : (r + 1) * depth, :], rows_ref[...], NN)
+        for cut in range(cuts):
+            low = r * depth + cut * height
+            start = pl.multiple_of((z_ref[0] ^ r) * depth + cut * height, height)
+            done_ref[low : low + height, :] = dot(outer_ref[low : low + height, :], rows_ref[...], NN)
+            copy = pltpu.make_async_copy(
+                done_ref.at[pl.ds(low, height), :], out_hbm.at[pl.ds(start, height), :], sems.at[len(copies)]
+            )
+            copy.start()
+            copies.append(copy)
+    for copy in copies:
+        copy.wait()
 
 
 def shards(enc, proj, head_weight, shortlist, positives, weight_num, weight_den):
@@ -206,50 +236,48 @@
     labels = owners * size
     depth = width // row_blocks
     me_s, z_s = me.reshape(1), z_low.reshape(1)
-    listed = shortlist.astype(jnp.int32).reshape(-1)
-
-    (payload,) = pl.pallas_call(
+    listed = shortlist.astype(jnp.int32).T
+
+    payload, enc_near, proj_near, wanted = pl.pallas_call(
         payload_kernel,
-        out_shape=[shape((size + TAIL, width), BF16)],
-        in_specs=[ANY] * 3,
-        out_specs=[VMEM],
-        scratch_shapes=[pltpu.VMEM((1, size), jnp.int32)] * 2 + [pltpu.SemaphoreType.DMA((3,))],
-        compiler_params=pltpu.CompilerParams(vmem_limit_bytes=56 * MIB),
-    )(weight_num.reshape(1, size), weight_den.reshape(1, size), head_weight)
+        out_shape=[
+            shape((size + TAIL, width), BF16),
+            shape((samples, width), BF16),
+            shape((width, width), BF16),
+            shape((positives.shape[1], samples), jnp.int32),
+        ],
+        in_specs=[ANY] * 6,
+        out_specs=[VMEM] * 4,
+        scratch_shapes=[pltpu.VMEM((1, size), jnp.int32)] * 2 + [pltpu.SemaphoreType.DMA((6,))],
+        compiler_params=pltpu.CompilerParams(vmem_limit_bytes=48 * MIB),
+    )(weight_num.reshape(1, size), weight_den.reshape(1, size), head_weight, enc, proj, positives.T)
     got = {0: payload}
-    for g in near:
+    for g in far + near:
         got[2 * g] = swap(payload, "label", 2 * g)
     got[1] = swap(payload, "label", 1)
-    hidden, enc_t = call(
-        inputs_kernel,
-        [shape((samples, width), BF16), shape((width, samples), BF16)],
-        [enc, proj],
+    hidden, enc_t, target = call(
+        functools.partial(inputs_kernel, beam, block),
+        [shape((samples, width), BF16), shape((width, samples), BF16), shape((beam * size, samples), BF16)],
+        [enc_near, proj_near, wanted],
         flops=2 * samples * width * width,
         nbytes=6_000_000,
     )
-    late = gate(payload, hidden) if far else payload
-    for g in far:
-        got[2 * g] = swap(late, "label", 2 * g)
-    for g in near + far:
-        got[2 * g] = gate(got[2 * g], hidden)
-        got[2 * g + 1] = swap(got[2 * g], "label", 1)
-
     grads, kept, from_core, moved, received = {}, {}, {}, {}, {}
-    order = [0] + near + far
-    wanted = positives.T
+    order = [0] + far + near
     for at, g in enumerate(order):
-        if at == 0:
-            after = [got[2 * n] for n in near]
-        else:
-            after = [grads[order[at - 1]]]
-            if at + 1 < len(order):
-                after.append(got[2 * order[at + 1]])
-            if at >= 3:
-                after.append(moved[order[at - 2]])
+        if at + 1 < len(order):
+            ahead = order[at + 1]
+            got[2 * ahead] = gate(got[2 * ahead], hidden if at < 2 else grads[order[at - 2]])
+            got[2 * ahead + 1] = swap(got[2 * ahead], "label", 1)
+        after = [] if at == 0 else [grads[order[at - 1]]]
+        if at + 1 < len(order) and at > 0:
+            after.append(got[2 * order[at + 1]])
+        if at >= 3:
+            after.append(moved[order[at - 2]])
         grads[g], kept[g], sent = call(
-            functools.partial(score_kernel, g, beam, block, row_blocks),
+            functools.partial(score_kernel, g, block, row_blocks),
             [shape((2 * size, samples), BF16), shape((width, size), F32), shape((width, size), BF16)],
-            [hidden, wanted, enc_t, got[2 * g], got[2 * g + 1]],
+            [hidden, target, enc_t, got[2 * g], got[2 * g + 1]],
             scalars=[listed, me_s, z_s],
             after=after,
             scratch=[
@@ -265,14 +293,14 @@
             moved[g] = (kept[g] + from_core[g].astype(F32)).astype(BF16)
             received[g] = swap(moved[g], "label", 2 * g)
     own = kept[0] + from_core[0].astype(F32)
-    received = [received[g] for g in near + far]
+    received = [received[g] for g in far + near]
 
     grad_hidden, rows = call(
         functools.partial(hidden_kernel, owners),
         [shape((samples, width), BF16), shape((labels, width), BF16)],
         [grads[g] for g in range(chips)] + [got[d] for d in range(owners)],
         scalars=[me_s],
-        after=[moved[g] for g in near + far],
+        after=[moved[g] for g in far + near],
         scratch=[pltpu.VMEM((labels, width), BF16)],
         vmem=12,
         flops=2 * samples * width * labels,
@@ -310,8 +338,7 @@
             nbytes=2_000_000,
         )
         span = row_blocks // 2
-        grad_enc, enc_done = grad_enc_after(upper)
-        total = total + gate(swap(upper, "dp", span), enc_done).astype(F32)
+        total = total + swap(upper, "dp", span).astype(F32)
         while span > 1:
             cut = span // 2 * depth
             total = total[:cut] + swap(total[cut:].astype(BF16), "dp", span // 2).astype(F32)
@@ -320,10 +347,10 @@
         total = own
         for value in received:
             total = total + value.astype(F32)
-        grad_enc, enc_done = grad_enc_after(total)
     total = total.astype(BF16)
+    grad_enc, enc_done = grad_enc_after(total)
     if planes > 1:
-        other = swap(total, "dp", planes // 2)
+        other = gate(swap(total, "dp", planes // 2), enc_done)
         total = (total.astype(F32) + other.astype(F32)).astype(BF16)
     parts = {0: total}
     span = 1
@@ -332,40 +359,39 @@
             parts[r + span] = swap(parts[r], "dp", span)
         span *= 2
     proj_slice = lax.dynamic_slice_in_dim(proj, z * (width // planes), width // planes, 1)
-    whole, grad_head = call(
+    (whole,) = call(whole_kernel, [shape((width, size), BF16)], [parts[r] for r in range(row_blocks)], vmem=2)
+    rows, grad_head = pl.pallas_call(
         functools.partial(head_kernel, row_blocks),
-        [shape((width, size), BF16), shape((width // planes, size), F32)],
-        [parts[r] for r in range(row_blocks)] + [proj_slice],
-        scalars=[z_s],
-        flops=2 * size * width * width // planes,
-        nbytes=1_000_000,
-    )
-    (rows,) = pl.pallas_call(
-        fetch_kernel,
-        out_shape=[shape((labels, width), BF16)],
-        in_specs=[ANY, ANY],
-        out_specs=[VMEM],
+        out_shape=[shape((labels, width), BF16), shape((width // planes, size), F32)],
+        in_specs=[SMEM, ANY, VMEM, VMEM],
+        out_specs=[VMEM, VMEM],
         scratch_shapes=[pltpu.SemaphoreType.DMA],
-        compiler_params=pltpu.CompilerParams(vmem_limit_bytes=2 * MIB),
-        cost_estimate=pl.CostEstimate(flops=0, bytes_accessed=3_000_000, transcendentals=0),
-    )(rows, whole)
+        compiler_params=pltpu.CompilerParams(vmem_limit_bytes=4 * MIB),
+        cost_estimate=pl.CostEstimate(
+            flops=2 * size * width * width // planes, bytes_accessed=3_000_000, transcendentals=0
+        ),
+    )(z_s, rows, whole, proj_slice)
     have = {0: whole}
     for g in near + far:
-        have[2 * g] = swap(whole, "label", 2 * g)
-    if near:
-        have[2 * near[0]] = gate(have[2 * near[0]], rows)
+        have[2 * g] = gate(swap(whole, "label", 2 * g), rows)
     for distance in list(have):
         have[distance + 1] = swap(have[distance], "label", 1)
-    (grad_proj,) = call(
-        functools.partial(proj_kernel, row_blocks),
-        [shape((width, width), F32)],
-        [have[distance] for distance in range(owners)] + [rows],
-        scalars=[me_s, z_s],
-        scratch=[pltpu.VMEM((width, labels), BF16)],
-        vmem=16,
-        flops=2 * labels * width * width,
-        nbytes=6_000_000,
-    )
+    cuts = 2
+    grad_proj = pl.pallas_call(
+        functools.partial(proj_kernel, row_blocks, cuts),
+        out_shape=shape((width, width), F32),
+        in_specs=[SMEM] * 2 + [VMEM] * (owners + 1),
+        out_specs=ANY,
+        scratch_shapes=[
+            pltpu.VMEM((width, labels), BF16),
+            pltpu.VMEM((width, width), F32),
+            pltpu.SemaphoreType.DMA((row_blocks * cuts,)),
+        ],
+        compiler_params=pltpu.CompilerParams(vmem_limit_bytes=16 * MIB),
+        cost_estimate=pl.CostEstimate(
+            flops=2 * labels * width * width, bytes_accessed=6_000_000, transcendentals=0
+        ),
+    )(me_s, z_s, *[have[distance] for distance in range(owners)], rows)
     return (grad_enc, grad_proj, grad_head.T)
 
 

time: 73.5 us -> 74.2 us (level)
  local copies, waits for them, and re-layouts: 4.68 us -> 6.82 us
  waiting for transfers between devices: 20.8 us -> 19.1 us
    pallas_call x1 -> x2, Pallas kernels: 0.12 us -> 3.86 us  [the longest x1 2.81 us: shards(): pl.pallas_call(functools.partial(proj_kernel, row_blocks, cuts), out_shap...]
    pallas_call x9 -> x8, Pallas kernels: 20.2 us -> 16.5 us  [call(): pl.pallas_call(kernel, out_shape=outs, in_specs=[SMEM] * len(scalars) + [...]
    unnamed x16 -> x20, local copies, waits for them, and re-layouts: 4.41 us -> 6.64 us
    ppermute x24, waiting for transfers between devices: 20.8 us -> 19.1 us  [swap(): return lax.ppermute(value, axis, [(i, i ^ distance) for i in range(size)])]
  transfers between devices with their start and end apart: 24 -> 24, of which waited for: 8 -> 11; matrix products, arithmetic and copies ran while one was open for 2% -> 0% of each run, Pallas kernels for 26% -> 28%
where the time goes in v5:
time: 74.2 us; the launch traced here: 73.7 us
  Pallas kernels  25.1 us (34%)
  starting transfers between devices  21.6 us (29%)
  waiting for transfers between devices  19.1 us (26%)
  local copies, waits for them, and re-layouts  6.82 us (9%)
  between operations  0.84 us (1%)
    ppermute x24, starting transfers between devices, swap(): return lax.ppermute(value, axis, [(i, i ^ distance) for i in range(size)])  21.6 us
    ppermute x24, waiting for transfers between devices, swap(): return lax.ppermute(value, axis, [(i, i ^ distance) for i in range(size)])  19.1 us
    pallas_call x8, Pallas kernels, call(): pl.pallas_call(kernel, out_shape=outs, in_specs=[SMEM] * len(scalars) + [...  16.5 us
    unnamed x20, local copies, waits for them, and re-layouts  6.64 us
    pallas_call x1, Pallas kernels, grad_enc_after(): pl.pallas_call(enc_kernel, grid=(samples // tile,), out_shape=[shape((sam...  3.28 us
    pallas_call x1, Pallas kernels, shards(): pl.pallas_call(functools.partial(proj_kernel, row_blocks, cuts), out_shap...  2.81 us
  transfers between devices with their start and end apart: 24, of which 11 were waited for; matrix products, arithmetic and copies ran while one was open for 0% of the time, Pallas kernels for 28%

profile of v5, /device:TPU:0, one launch (start us, length us, event | category | flops | bytes accessed | tf_op | source)
XLA Modules:
  0.0 73.7 jit_solution(7243102824404635229)
XLA Ops:
  1.9 1.4 %copy-done.4 = bf16[1024,768]{1,0:T(8,128)(2,1)S(1)} copy-done((bf16[1024,768]{1,0:T(8,128)(2,1)S(1)}, bf16[1024,768]{1,0:T(8,128)(2,1)}, u32[]{:S(2)}) %copy-start.4) | copy-done | bytes 1572888
  6.3 1.4 %shard_map.94 = (bf16[144,768]{1,0:T(8,128)(2,1)}, bf16[1024,768]{1,0:T(8,128)(2,1)S(1)}, bf16[768,768]{1,0:T(8,128)(2,1)S(1)}, s32[8,1024]{1,0:T(8,128)S(1)}) custom-call(s32[1,128]{1,0:T(1,128)S(1)} %bitcast.12, s32[1,128]{1,0:T(1,128)S(1)} %bitcast.13, bf16[128,768]{1,0:T(8,128)(2,1)S(1)} %copy-done.5, bf16[1024,768]{1,0:T(8,128)(2,1)S(1)} %copy-done.4, ...), custom_call_target="tpu_custom_call" | custom-call | tf_op jit(solution)/shard_map/pallas_call | solution.py:241
  7.7 4.0 %collective-permute-start.3 = (bf16[144,768]{1,0:T(8,128)(2,1)}, bf16[144,768]{1,0:T(8,128)(2,1)}, u32[]{:S(2)}, u32[]{:S(2)}) collective-permute-start(bf16[144,768]{1,0:T(8,128)(2,1)} %get-tuple-element.36.refs_0_.refs_4_), channel_id=1, source_target_pairs={{0,6},{1,7},{2,4},{3,5},{4,2},{5,3},{6,0},{7,1},{8,14},{9,15},{10,... | collective-permute-start | bytes 663560 | tf_op jit(solution)/shard_map/ppermute | solution.py:55
  12.2 2.5 %shard_map.95 = (bf16[1024,768]{1,0:T(8,128)(2,1)S(1)}, bf16[768,1024]{1,0:T(8,128)(2,1)S(1)}, bf16[512,1024]{1,0:T(8,128)(2,1)S(1)}) custom-call(bf16[1024,768]{1,0:T(8,128)(2,1)S(1)} %get-tuple-element.30.enc_ref, bf16[768,768]{1,0:T(8,128)(2,1)S(1)} %get-tuple-element.31.proj_ref, s32[8,1024]{1,0:T(8,128)S(1)} %get-tuple-element.32.wanted_ref), custom_call_target="tpu_custom_call" | custom-call | flops 1207959552 | bytes 6000000 | tf_op jit(solution)/shard_map/pallas_call | solution.py:31
  15.7 2.6 %collective-permute-done.3.value_ref = bf16[144,768]{1,0:T(8,128)(2,1)} collective-permute-done((bf16[144,768]{1,0:T(8,128)(2,1)}, bf16[144,768]{1,0:T(8,128)(2,1)}, u32[]{:S(2)}, u32[]{:S(2)}) %collective-permute-start.3) | collective-permute-done | bytes 221216 | tf_op jit(solution)/shard_map/ppermute | solution.py:55
  18.2 2.0 %collective-permute-start.5 = (bf16[144,768]{1,0:T(8,128)(2,1)}, bf16[144,768]{1,0:T(8,128)(2,1)S(1)}, u32[]{:S(2)}, u32[]{:S(2)}) collective-permute-start(bf16[144,768]{1,0:T(8,128)(2,1)} %get-tuple-element.36.refs_0_.refs_4_), channel_id=1, source_target_pairs={{0,4},{1,5},{2,6},{3,7},{4,0},{5,1},{6,2},{7,3},{8,12},{9,13},{10,... | collective-permute-start | bytes 663560 | tf_op jit(solution)/shard_map/ppermute | solution.py:55
  20.3 2.1 %collective-permute-done.1.value_ref = bf16[144,768]{1,0:T(8,128)(2,1)} collective-permute-done((bf16[144,768]{1,0:T(8,128)(2,1)}, bf16[144,768]{1,0:T(8,128)(2,1)}, u32[]{:S(2)}, u32[]{:S(2)}) %collective-permute-start.1) | collective-permute-done | bytes 221216 | tf_op jit(solution)/shard_map/ppermute | solution.py:55
  22.4 3.0 %shard_map.96 = (bf16[256,1024]{1,0:T(8,128)(2,1)S(1)}, f32[768,128]{1,0:T(8,128)S(1)}, bf16[768,128]{1,0:T(8,128)(2,1)S(1)}) custom-call(s32[4,8]{1,0:T(4,128)S(1)} %bitcast.8, s32[1]{0:T(128)} %bitcast.me_ref, s32[1]{0:T(128)} %bitcast.2.z_ref, bf16[1024,768]{1,0:T(8,128)(2,1)S(1)} %get-tuple-element.33.hidden_ref.refs_0_, ...), custom_call_target="tpu_custom_call" | custom-call | flops 805306368 | bytes 5000000 | tf_op jit(solution)/shard_map/pallas_call | solution.py:31
  25.4 2.7 %shard_map.99 = (bf16[256,1024]{1,0:T(8,128)(2,1)S(1)}, f32[768,128]{1,0:T(8,128)S(1)}, bf16[768,128]{1,0:T(8,128)(2,1)S(1)}) custom-call(s32[4,8]{1,0:T(4,128)S(1)} %bitcast.9, s32[1]{0:T(128)} %bitcast.me_ref, s32[1]{0:T(128)} %bitcast.2.z_ref, bf16[1024,768]{1,0:T(8,128)(2,1)S(1)} %get-tuple-element.33.hidden_ref.refs_0_, ...), custom_call_target="tpu_custom_call" | custom-call | flops 805306368 | bytes 5000000 | tf_op jit(solution)/shard_map/pallas_call | solution.py:31
  29.3 2.7 %shard_map.101 = (bf16[256,1024]{1,0:T(8,128)(2,1)S(1)}, f32[768,128]{1,0:T(8,128)S(1)}, bf16[768,128]{1,0:T(8,128)(2,1)S(1)}) custom-call(s32[4,8]{1,0:T(4,128)S(1)} %bitcast.10, s32[1]{0:T(128)} %bitcast.me_ref, s32[1]{0:T(128)} %bitcast.2.z_ref, bf16[1024,768]{1,0:T(8,128)(2,1)S(1)} %get-tuple-element.33.hidden_ref.refs_0_, ...), custom_call_target="tpu_custom_call" | custom-call | flops 805306368 | bytes 5000000 | tf_op jit(solution)/shard_map/pallas_call | solution.py:31
  32.2 1.5 %collective-permute-start.11 = (bf16[768,128]{1,0:T(8,128)(2,1)S(1)}, bf16[768,128]{1,0:T(8,128)(2,1)S(1)}, u32[]{:S(2)}, u32[]{:S(2)}) collective-permute-start(bf16[768,128]{1,0:T(8,128)(2,1)S(1)} %add_convert_fusion.2.refs_3_.refs_12_), channel_id=1, source_target_pairs={{0,6},{1,7},{2,4},{3,5},{4,2},{5,3},{6,0},{7,1},{8,14},{9,15},{10,... | collective-permute-start | bytes 589832 | tf_op jit(solution)/shard_map/ppermute | solution.py:55
  33.7 2.3 %shard_map.102 = (bf16[256,1024]{1,0:T(8,128)(2,1)S(1)}, f32[768,128]{1,0:T(8,128)S(1)}, bf16[768,128]{1,0:T(8,128)(2,1)S(1)}) custom-call(s32[4,8]{1,0:T(4,128)S(1)} %bitcast.11, s32[1]{0:T(128)} %bitcast.me_ref, s32[1]{0:T(128)} %bitcast.2.z_ref, bf16[1024,768]{1,0:T(8,128)(2,1)S(1)} %get-tuple-element.33.hidden_ref.refs_0_, ...), custom_call_target="tpu_custom_call" | custom-call | flops 805306368 | bytes 5000000 | tf_op jit(solution)/shard_map/pallas_call | solution.py:31
  37.5 1.8 %collective-permute-start.13 = (bf16[768,128]{1,0:T(8,128)(2,1)S(1)}, bf16[768,128]{1,0:T(8,128)(2,1)S(1)}, u32[]{:S(2)}, u32[]{:S(2)}) collective-permute-start(bf16[768,128]{1,0:T(8,128)(2,1)S(1)} %add_convert_fusion.refs_14_), channel_id=1, source_target_pairs={{0,4},{1,5},{2,6},{3,7},{4,0},{5,1},{6,2},{7,3},{8,12},{9,13},{10,... | collective-permute-start | bytes 589832 | tf_op jit(solution)/shard_map/ppermute | solution.py:55
  39.3 3.3 %shard_map.103 = (bf16[1024,768]{1,0:T(8,128)(2,1)S(1)}, bf16[1024,768]{1,0:T(8,128)(2,1)S(1)}) custom-call(s32[1]{0:T(128)} %bitcast.me_ref, bf16[256,1024]{1,0:T(8,128)(2,1)S(1)} %get-tuple-element.37.refs_2_.refs_0_, bf16[256,1024]{1,0:T(8,128)(2,1)S(1)} %get-tuple-element.39.refs_2_.refs_1_, bf16[256,1024]{1,0:T(8,128)(2,1)S(1)} %get-tuple-element.42.refs_2_, ...), custom_call_target="tpu_custom_call" | custom-call | flops 1610612736 | bytes 5000000 | tf_op jit(solution)/shard_map/pallas_call | solution.py:31
  44.8 1.6 %collective-permute-start.14 = (bf16[384,128]{1,0:T(8,128)(2,1)S(1)}, bf16[384,128]{1,0:T(8,128)(2,1)S(1)}, u32[]{:S(2)}, u32[]{:S(2)}) collective-permute-start(bf16[384,128]{1,0:T(8,128)(2,1)S(1)} %get-tuple-element.51), channel_id=1, source_target_pairs={{0,8},{8,0},{16,24},{24,16},{1,9},{9,1},{17,25},{25,17},{2,10},{10... | collective-permute-start | bytes 294920 | tf_op jit(solution)/shard_map/ppermute | solution.py:55
  46.3 3.1 %collective-permute-done.14 = bf16[384,128]{1,0:T(8,128)(2,1)S(1)} collective-permute-done((bf16[384,128]{1,0:T(8,128)(2,1)S(1)}, bf16[384,128]{1,0:T(8,128)(2,1)S(1)}, u32[]{:S(2)}, u32[]{:S(2)}) %collective-permute-start.14) | collective-permute-done | bytes 98336 | tf_op jit(solution)/shard_map/ppermute | solution.py:55
  49.5 2.6 %collective-permute-start.15 = (bf16[384,128]{1,0:T(8,128)(2,1)S(1)}, bf16[384,128]{1,0:T(8,128)(2,1)S(1)}, u32[]{:S(2)}, u32[]{:S(2)}) collective-permute-start(bf16[384,128]{1,0:T(8,128)(2,1)S(1)} %add_convert_fusion.4.after_ref), channel_id=1, source_target_pairs={{0,16},{8,24},{16,0},{24,8},{1,17},{9,25},{17,1},{25,9},{2,18},{10... | collective-permute-start | bytes 294920 | tf_op jit(solution)/shard_map/ppermute | solution.py:55
  52.1 3.3 %shard_map.105 = (f32[1024,768]{1,0:T(8,128)}, f32[8,128]{1,0:T(8,128)S(1)}) custom-call(bf16[1024,768]{1,0:T(8,128)(2,1)S(1)} %get-tuple-element.47.refs_3_.grad_hidden_ref, bf16[768,768]{1,0:T(8,128)(2,1)S(1)} %copy-done.3, bf16[384,128]{1,0:T(8,128)(2,1)S(1)} %add_convert_fusion.4.after_ref), custom_call_target="tpu_custom_call" | custom-call | flops 1207959552 | bytes 6000000 | tf_op jit(solution)/shard_map/pallas_call | solution.py:312
  55.4 1.6 %collective-permute-start.16 = (bf16[384,128]{1,0:T(8,128)(2,1)S(1)}, bf16[384,128]{1,0:T(8,128)(2,1)S(1)}, u32[]{:S(2)}, u32[]{:S(2)}) collective-permute-start(bf16[384,128]{1,0:T(8,128)(2,1)S(1)} %add_convert_fusion.3.refs_0_), channel_id=1, source_target_pairs={{0,8},{8,0},{16,24},{24,16},{1,9},{9,1},{17,25},{25,17},{2,10},{10... | collective-permute-start | bytes 294920 | tf_op jit(solution)/shard_map/ppermute | solution.py:55
  57.0 3.1 %collective-permute-done.16.refs_1_ = bf16[384,128]{1,0:T(8,128)(2,1)S(1)} collective-permute-done((bf16[384,128]{1,0:T(8,128)(2,1)S(1)}, bf16[384,128]{1,0:T(8,128)(2,1)S(1)}, u32[]{:S(2)}, u32[]{:S(2)}) %collective-permute-start.16) | collective-permute-done | bytes 98336 | tf_op jit(solution)/shard_map/ppermute | solution.py:55
  60.1 2.0 %collective-permute-start.22 = (bf16[768,128]{1,0:T(8,128)(2,1)S(1)}, bf16[768,128]{1,0:T(8,128)(2,1)S(1)}, u32[]{:S(2)}, u32[]{:S(2)}) collective-permute-start(bf16[768,128]{1,0:T(8,128)(2,1)S(1)} %shard_map.107.whole_ref.refs_0_), channel_id=1, source_target_pairs={{0,6},{1,7},{2,4},{3,5},{4,2},{5,3},{6,0},{7,1},{8,14},{9,15},{10,... | collective-permute-start | bytes 589832 | tf_op jit(solution)/shard_map/ppermute | solution.py:55
  65.0 2.1 %collective-permute-done.22.value_ref = bf16[768,128]{1,0:T(8,128)(2,1)S(1)} collective-permute-done((bf16[768,128]{1,0:T(8,128)(2,1)S(1)}, bf16[768,128]{1,0:T(8,128)(2,1)S(1)}, u32[]{:S(2)}, u32[]{:S(2)}) %collective-permute-start.22) | collective-permute-done | bytes 196640 | tf_op jit(solution)/shard_map/ppermute | solution.py:55
  67.1 2.0 %collective-permute-done.20.value_ref = bf16[768,128]{1,0:T(8,128)(2,1)S(1)} collective-permute-done((bf16[768,128]{1,0:T(8,128)(2,1)S(1)}, bf16[768,128]{1,0:T(8,128)(2,1)S(1)}, u32[]{:S(2)}, u32[]{:S(2)}) %collective-permute-start.20) | collective-permute-done | bytes 196640 | tf_op jit(solution)/shard_map/ppermute | solution.py:55
  70.8 2.8 %shard_map.112 = f32[768,768]{1,0:T(8,128)} custom-call(s32[1]{0:T(128)} %bitcast.me_ref, s32[1]{0:T(128)} %bitcast.2.z_ref, bf16[768,128]{1,0:T(8,128)(2,1)S(1)} %shard_map.107.whole_ref.refs_0_, bf16[768,128]{1,0:T(8,128)(2,1)S(1)} %collective-permute-done.17.refs_1_, bf16[768,128]{1,0:T(8,128)(2,1)S(1)} %shard_map.109.refs_2_, ...), custom_call_target="tpu_custom_call" | custom-call | flops 1207959552 | bytes 6000000 | tf_op jit(solution)/shard_map/pallas_call | solution.py:380
  (70 shorter events, 15.4 us)
Async XLA Ops:
  7.7 10.5 %collective-permute-start.3 = (bf16[144,768]{1,0:T(8,128)(2,1)}, bf16[144,768]{1,0:T(8,128)(2,1)}, u32[]{:S(2)}, u32[]{:S(2)}) collective-permute-start(bf16[144,768]{1,0:T(8,128)(2,1)} %get-tuple-element.36.refs_0_.refs_4_), channel_id=1, source_target_pairs={{0,6},{1,7},{2,4},{3,5},{4,2},{5,3},{6,0},{7,1},{8,14},{9,15},{10,... | collective-permute-start | bytes 663560 | tf_op jit(solution)/shard_map/ppermute | solution.py:55
  11.7 10.7 %collective-permute-start = (bf16[144,768]{1,0:T(8,128)(2,1)}, bf16[144,768]{1,0:T(8,128)(2,1)}, u32[]{:S(2)}, u32[]{:S(2)}) collective-permute-start(bf16[144,768]{1,0:T(8,128)(2,1)} %get-tuple-element.36.refs_0_.refs_4_), channel_id=1, source_target_pairs={{0,1},{1,0},{2,3},{3,2},{4,5},{5,4},{6,7},{7,6},{8,9},{9,8},{10,11... | collective-permute-start | bytes 663560 | tf_op jit(solution)/shard_map/ppermute | solution.py:55
  11.7 10.7 %collective-permute-start.1 = (bf16[144,768]{1,0:T(8,128)(2,1)}, bf16[144,768]{1,0:T(8,128)(2,1)}, u32[]{:S(2)}, u32[]{:S(2)}) collective-permute-start(bf16[144,768]{1,0:T(8,128)(2,1)} %get-tuple-element.36.refs_0_.refs_4_), channel_id=1, source_target_pairs={{0,2},{1,3},{2,0},{3,1},{4,6},{5,7},{6,4},{7,5},{8,10},{9,11},{10,... | collective-permute-start | bytes 663560 | tf_op jit(solution)/shard_map/ppermute | solution.py:55
  18.2 7.2 %collective-permute-start.4 = (bf16[144,768]{1,0:T(8,128)(2,1)}, bf16[144,768]{1,0:T(8,128)(2,1)}, u32[]{:S(2)}, u32[]{:S(2)}) collective-permute-start(bf16[144,768]{1,0:T(8,128)(2,1)} %shard_map.98.refs_0_.refs_10_), channel_id=1, source_target_pairs={{0,1},{1,0},{2,3},{3,2},{4,5},{5,4},{6,7},{7,6},{8,9},{9,8},{10,11... | collective-permute-start | bytes 663560 | tf_op jit(solution)/shard_map/ppermute | solution.py:55
  18.2 10.6 %collective-permute-start.5 = (bf16[144,768]{1,0:T(8,128)(2,1)}, bf16[144,768]{1,0:T(8,128)(2,1)S(1)}, u32[]{:S(2)}, u32[]{:S(2)}) collective-permute-start(bf16[144,768]{1,0:T(8,128)(2,1)} %get-tuple-element.36.refs_0_.refs_4_), channel_id=1, source_target_pairs={{0,4},{1,5},{2,6},{3,7},{4,0},{5,1},{6,2},{7,3},{8,12},{9,13},{10,... | collective-permute-start | bytes 663560 | tf_op jit(solution)/shard_map/ppermute | solution.py:55
  22.4 6.9 %collective-permute-start.2 = (bf16[144,768]{1,0:T(8,128)(2,1)}, bf16[144,768]{1,0:T(8,128)(2,1)S(1)}, u32[]{:S(2)}, u32[]{:S(2)}) collective-permute-start(bf16[144,768]{1,0:T(8,128)(2,1)} %shard_map.97.refs_3_.refs_0_.refs_6_), channel_id=1, source_target_pairs={{0,1},{1,0},{2,3},{3,2},{4,5},{5,4},{6,7},{7,6},{8,9},{9,8},{10,11... | collective-permute-start | bytes 663560 | tf_op jit(solution)/shard_map/ppermute | solution.py:55
  28.1 4.0 %collective-permute-start.7 = (bf16[768,128]{1,0:T(8,128)(2,1)S(1)}, bf16[768,128]{1,0:T(8,128)(2,1)S(1)}, u32[]{:S(2)}, u32[]{:S(2)}) collective-permute-start(bf16[768,128]{1,0:T(8,128)(2,1)S(1)} %get-tuple-element.41), channel_id=1, source_target_pairs={{0,1},{1,0},{2,3},{3,2},{4,5},{5,4},{6,7},{7,6},{8,9},{9,8},{10,11... | collective-permute-start | bytes 589832 | tf_op jit(solution)/shard_map/ppermute | solution.py:55
  28.8 4.9 %collective-permute-start.6 = (bf16[144,768]{1,0:T(8,128)(2,1)S(1)}, bf16[144,768]{1,0:T(8,128)(2,1)S(1)}, u32[]{:S(2)}, u32[]{:S(2)}) collective-permute-start(bf16[144,768]{1,0:T(8,128)(2,1)S(1)} %shard_map.100.refs_3_.refs_0_.refs_8_), channel_id=1, source_target_pairs={{0,1},{1,0},{2,3},{3,2},{4,5},{5,4},{6,7},{7,6},{8,9},{9,8},{10,11... | collective-permute-start | bytes 663560 | tf_op jit(solution)/shard_map/ppermute | solution.py:55
  28.9 10.4 %collective-permute-start.10 = (bf16[768,128]{1,0:T(8,128)(2,1)S(1)}, bf16[768,128]{1,0:T(8,128)(2,1)S(1)}, u32[]{:S(2)}, u32[]{:S(2)}) collective-permute-start(bf16[768,128]{1,0:T(8,128)(2,1)S(1)} %get-tuple-element.49), channel_id=1, source_target_pairs={{0,1},{1,0},{2,3},{3,2},{4,5},{5,4},{6,7},{7,6},{8,9},{9,8},{10,11... | collective-permute-start | bytes 589832 | tf_op jit(solution)/shard_map/ppermute | solution.py:55
  32.0 4.0 %collective-permute-start.8 = (bf16[768,128]{1,0:T(8,128)(2,1)S(1)}, bf16[768,128]{1,0:T(8,128)(2,1)S(1)}, u32[]{:S(2)}, u32[]{:S(2)}) collective-permute-start(bf16[768,128]{1,0:T(8,128)(2,1)S(1)} %get-tuple-element.44), channel_id=1, source_target_pairs={{0,1},{1,0},{2,3},{3,2},{4,5},{5,4},{6,7},{7,6},{8,9},{9,8},{10,11... | collective-permute-start | bytes 589832 | tf_op jit(solution)/shard_map/ppermute | solution.py:55
  32.2 11.2 %collective-permute-start.11 = (bf16[768,128]{1,0:T(8,128)(2,1)S(1)}, bf16[768,128]{1,0:T(8,128)(2,1)S(1)}, u32[]{:S(2)}, u32[]{:S(2)}) collective-permute-start(bf16[768,128]{1,0:T(8,128)(2,1)S(1)} %add_convert_fusion.2.refs_3_.refs_12_), channel_id=1, source_target_pairs={{0,6},{1,7},{2,4},{3,5},{4,2},{5,3},{6,0},{7,1},{8,14},{9,15},{10,... | collective-permute-start | bytes 589832 | tf_op jit(solution)/shard_map/ppermute | solution.py:55
  35.9 1.5 %collective-permute-start.9 = (bf16[768,128]{1,0:T(8,128)(2,1)S(1)}, bf16[768,128]{1,0:T(8,128)(2,1)S(1)}, u32[]{:S(2)}, u32[]{:S(2)}) collective-permute-start(bf16[768,128]{1,0:T(8,128)(2,1)S(1)} %get-tuple-element.46), channel_id=1, source_target_pairs={{0,1},{1,0},{2,3},{3,2},{4,5},{5,4},{6,7},{7,6},{8,9},{9,8},{10,11... | collective-permute-start | bytes 589832 | tf_op jit(solution)/shard_map/ppermute | solution.py:55
  36.1 7.3 %collective-permute-start.12 = (bf16[768,128]{1,0:T(8,128)(2,1)S(1)}, bf16[768,128]{1,0:T(8,128)(2,1)S(1)}, u32[]{:S(2)}, u32[]{:S(2)}) collective-permute-start(bf16[768,128]{1,0:T(8,128)(2,1)S(1)} %add_convert_fusion.1.refs_13_), channel_id=1, source_target_pairs={{0,2},{1,3},{2,0},{3,1},{4,6},{5,7},{6,4},{7,5},{8,10},{9,11},{10,... | collective-permute-start | bytes 589832 | tf_op jit(solution)/shard_map/ppermute | solution.py:55
  37.5 7.2 %collective-permute-start.13 = (bf16[768,128]{1,0:T(8,128)(2,1)S(1)}, bf16[768,128]{1,0:T(8,128)(2,1)S(1)}, u32[]{:S(2)}, u32[]{:S(2)}) collective-permute-start(bf16[768,128]{1,0:T(8,128)(2,1)S(1)} %add_convert_fusion.refs_14_), channel_id=1, source_target_pairs={{0,4},{1,5},{2,6},{3,7},{4,0},{5,1},{6,2},{7,3},{8,12},{9,13},{10,... | collective-permute-start | bytes 589832 | tf_op jit(solution)/shard_map/ppermute | solution.py:55
  44.8 4.7 %collective-permute-start.14 = (bf16[384,128]{1,0:T(8,128)(2,1)S(1)}, bf16[384,128]{1,0:T(8,128)(2,1)S(1)}, u32[]{:S(2)}, u32[]{:S(2)}) collective-permute-start(bf16[384,128]{1,0:T(8,128)(2,1)S(1)} %get-tuple-element.51), channel_id=1, source_target_pairs={{0,8},{8,0},{16,24},{24,16},{1,9},{9,1},{17,25},{25,17},{2,10},{10... | collective-permute-start | bytes 294920 | tf_op jit(solution)/shard_map/ppermute | solution.py:55
  49.5 5.9 %collective-permute-start.15 = (bf16[384,128]{1,0:T(8,128)(2,1)S(1)}, bf16[384,128]{1,0:T(8,128)(2,1)S(1)}, u32[]{:S(2)}, u32[]{:S(2)}) collective-permute-start(bf16[384,128]{1,0:T(8,128)(2,1)S(1)} %add_convert_fusion.4.after_ref), channel_id=1, source_target_pairs={{0,16},{8,24},{16,0},{24,8},{1,17},{9,25},{17,1},{25,9},{2,18},{10... | collective-permute-start | bytes 294920 | tf_op jit(solution)/shard_map/ppermute | solution.py:55
  55.4 4.7 %collective-permute-start.16 = (bf16[384,128]{1,0:T(8,128)(2,1)S(1)}, bf16[384,128]{1,0:T(8,128)(2,1)S(1)}, u32[]{:S(2)}, u32[]{:S(2)}) collective-permute-start(bf16[384,128]{1,0:T(8,128)(2,1)S(1)} %add_convert_fusion.3.refs_0_), channel_id=1, source_target_pairs={{0,8},{8,0},{16,24},{24,16},{1,9},{9,1},{17,25},{25,17},{2,10},{10... | collective-permute-start | bytes 294920 | tf_op jit(solution)/shard_map/ppermute | solution.py:55
  60.1 7.0 %collective-permute-start.22 = (bf16[768,128]{1,0:T(8,128)(2,1)S(1)}, bf16[768,128]{1,0:T(8,128)(2,1)S(1)}, u32[]{:S(2)}, u32[]{:S(2)}) collective-permute-start(bf16[768,128]{1,0:T(8,128)(2,1)S(1)} %shard_map.107.whole_ref.refs_0_), channel_id=1, source_target_pairs={{0,6},{1,7},{2,4},{3,5},{4,2},{5,3},{6,0},{7,1},{8,14},{9,15},{10,... | collective-permute-start | bytes 589832 | tf_op jit(solution)/shard_map/ppermute | solution.py:55
  62.1 7.0 %collective-permute-start.20 = (bf16[768,128]{1,0:T(8,128)(2,1)S(1)}, bf16[768,128]{1,0:T(8,128)(2,1)S(1)}, u32[]{:S(2)}, u32[]{:S(2)}) collective-permute-start(bf16[768,128]{1,0:T(8,128)(2,1)S(1)} %shard_map.107.whole_ref.refs_0_), channel_id=1, source_target_pairs={{0,4},{1,5},{2,6},{3,7},{4,0},{5,1},{6,2},{7,3},{8,12},{9,13},{10,... | collective-permute-start | bytes 589832 | tf_op jit(solution)/shard_map/ppermute | solution.py:55
  63.1 6.0 %collective-permute-start.18 = (bf16[768,128]{1,0:T(8,128)(2,1)S(1)}, bf16[768,128]{1,0:T(8,128)(2,1)S(1)}, u32[]{:S(2)}, u32[]{:S(2)}) collective-permute-start(bf16[768,128]{1,0:T(8,128)(2,1)S(1)} %shard_map.107.whole_ref.refs_0_), channel_id=1, source_target_pairs={{0,2},{1,3},{2,0},{3,1},{4,6},{5,7},{6,4},{7,5},{8,10},{9,11},{10,... | collective-permute-start | bytes 589832 | tf_op jit(solution)/shard_map/ppermute | solution.py:55
  63.8 5.8 %collective-permute-start.17 = (bf16[768,128]{1,0:T(8,128)(2,1)S(1)}, bf16[768,128]{1,0:T(8,128)(2,1)S(1)}, u32[]{:S(2)}, u32[]{:S(2)}) collective-permute-start(bf16[768,128]{1,0:T(8,128)(2,1)S(1)} %shard_map.107.whole_ref.refs_0_), channel_id=1, source_target_pairs={{0,1},{1,0},{2,3},{3,2},{4,5},{5,4},{6,7},{7,6},{8,9},{9,8},{10,11... | collective-permute-start | bytes 589832 | tf_op jit(solution)/shard_map/ppermute | solution.py:55
  67.1 2.5 %collective-permute-start.23 = (bf16[768,128]{1,0:T(8,128)(2,1)S(1)}, bf16[768,128]{1,0:T(8,128)(2,1)S(1)}, u32[]{:S(2)}, u32[]{:S(2)}) collective-permute-start(bf16[768,128]{1,0:T(8,128)(2,1)S(1)} %shard_map.111.refs_6_), channel_id=1, source_target_pairs={{0,1},{1,0},{2,3},{3,2},{4,5},{5,4},{6,7},{7,6},{8,9},{9,8},{10,11... | collective-permute-start | bytes 589832 | tf_op jit(solution)/shard_map/ppermute | solution.py:55
  69.1 1.4 %collective-permute-start.21 = (bf16[768,128]{1,0:T(8,128)(2,1)S(1)}, bf16[768,128]{1,0:T(8,128)(2,1)S(1)}, u32[]{:S(2)}, u32[]{:S(2)}) collective-permute-start(bf16[768,128]{1,0:T(8,128)(2,1)S(1)} %shard_map.110.refs_4_), channel_id=1, source_target_pairs={{0,1},{1,0},{2,3},{3,2},{4,5},{5,4},{6,7},{7,6},{8,9},{9,8},{10,11... | collective-permute-start | bytes 589832 | tf_op jit(solution)/shard_map/ppermute | solution.py:55
  69.2 1.7 %collective-permute-start.19 = (bf16[768,128]{1,0:T(8,128)(2,1)S(1)}, bf16[768,128]{1,0:T(8,128)(2,1)S(1)}, u32[]{:S(2)}, u32[]{:S(2)}) collective-permute-start(bf16[768,128]{1,0:T(8,128)(2,1)S(1)} %shard_map.109.refs_2_), channel_id=1, source_target_pairs={{0,1},{1,0},{2,3},{3,2},{4,5},{5,4},{6,7},{7,6},{8,9},{9,8},{10,11... | collective-permute-start | bytes 589832 | tf_op jit(solution)/shard_map/ppermute | solution.py:55
  (10 other events, 22.4 us)

commit v6 on v5

--- a/solution.py
+++ b/solution.py
@@ -55,17 +55,13 @@
     return lax.ppermute(value, axis, [(i, i ^ distance) for i in range(size)])
 
 
-def payload_kernel(num_hbm, den_hbm, rows_hbm, enc_hbm, proj_hbm, wanted_hbm, out_ref, enc_ref, proj_ref, wanted_ref, num_ref, den_ref, sems):
+def payload_kernel(num_hbm, den_hbm, rows_hbm, out_ref, num_ref, den_ref, sems):
     size, width = rows_hbm.shape
-    pairs = [
-        (num_hbm, num_ref),
-        (den_hbm, den_ref),
-        (rows_hbm, out_ref.at[pl.ds(0, size), :]),
-        (wanted_hbm, wanted_ref),
-        (proj_hbm, proj_ref),
-        (enc_hbm, enc_ref),
+    copies = [
+        pltpu.make_async_copy(num_hbm, num_ref, sems.at[0]),
+        pltpu.make_async_copy(den_hbm, den_ref, sems.at[1]),
+        pltpu.make_async_copy(rows_hbm, out_ref.at[pl.ds(0, size), :], sems.at[2]),
     ]
-    copies = [pltpu.make_async_copy(a, b, sems.at[i]) for i, (a, b) in enumerate(pairs)]
     for copy in copies:
         copy.start()
     out_ref[size:, size:] = jnp.zeros((TAIL, width - size), BF16)
@@ -74,28 +70,30 @@
     row = lax.broadcasted_iota(jnp.int32, (TAIL, size), 0)
     both = jnp.where(row == 0, num_ref[...], den_ref[...])
     out_ref[size:, :size] = both.astype(F32).astype(BF16)
-    for copy in copies[2:]:
-        copy.wait()
-
-
-def inputs_kernel(beam, block, enc_ref, proj_ref, wanted_ref, hidden_ref, enc_t_ref, target_ref):
-    samples = enc_ref.shape[0]
+    copies[2].wait()
+
+
+def target_kernel(beam, block, wanted_ref, target_ref):
+    samples = wanted_ref.shape[1]
     size = target_ref.shape[0] // beam
     label_iota = lax.broadcasted_iota(jnp.int32, (size, block), 0)
+    for low in range(0, samples, block):
+        for place in range(beam):
+            labels = label_iota + place * size
+            target = labels == wanted_ref[0:1, low : low + block]
+            for column in range(1, wanted_ref.shape[0]):
+                target = target | (labels == wanted_ref[column : column + 1, low : low + block])
+            target_ref[place * size : (place + 1) * size, low : low + block] = jnp.where(
+                target, 1.0, 0.0
+            ).astype(BF16)
+
+
+def inputs_kernel(enc_ref, proj_ref, after_ref, hidden_t_ref):
+    samples = enc_ref.shape[0]
     tile = min(256, samples)
     for start in range(0, samples, tile):
-        rows = enc_ref[start : start + tile, :]
-        enc_t_ref[:, start : start + tile] = rows.T
-        hidden_ref[start : start + tile, :] = dot(rows, proj_ref[...], NN).astype(BF16)
-        for low in range(start, start + tile, block):
-            for place in range(beam):
-                labels = label_iota + place * size
-                target = labels == wanted_ref[0:1, low : low + block]
-                for column in range(1, wanted_ref.shape[0]):
-                    target = target | (labels == wanted_ref[column : column + 1, low : low + block])
-                target_ref[place * size : (place + 1) * size, low : low + block] = jnp.where(
-                    target, 1.0, 0.0
-                ).astype(BF16)
+        hidden = dot(enc_ref[start : start + tile, :], proj_ref[...], NN).astype(BF16)
+        hidden_t_ref[:, start : start + tile] = hidden.T
 
 
 def logistic(value):
@@ -104,10 +102,10 @@
     return guess * (2.0 - bottom * guess)
 
 
-def score_kernel(group, block, count, list_ref, me_ref, z_ref, hidden_ref, target_ref, enc_t_ref, *refs):
+def score_kernel(group, block, count, list_ref, me_ref, z_ref, hidden_t_ref, target_ref, enc_ref, *refs):
     payloads, refs = refs[:2], refs[-8:]
     grads_ref, kept_ref, sent_ref, weights_ref, scale_ref, logits_ref = refs[-6:]
-    samples = hidden_ref.shape[0]
+    samples = enc_ref.shape[0]
     size = payloads[0].shape[0] - TAIL
     for core in range(2):
         rows = pl.ds(core * size, size)
@@ -115,7 +113,7 @@
         tail = payloads[core][size:, :size].astype(F32)
         ratio = tail[0:1, :] / tail[1:2, :]
         scale_ref[rows, :] = jnp.broadcast_to(ratio, (block, size)).T / block
-    logits_ref[...] = dot(weights_ref[...], hidden_ref[...], NT)
+    logits_ref[...] = dot(weights_ref[...], hidden_t_ref[...], NN)
     grads_ref[...] = jnp.zeros_like(grads_ref)
 
     def one_block(at, carried):
@@ -136,12 +134,12 @@
         return carried
 
     lax.fori_loop(0, samples // block, one_block, 0)
-    outer = dot(enc_t_ref[...], grads_ref[...], NT)
-    depth = enc_t_ref.shape[0] // count
+    outer = dot(grads_ref[...], enc_ref[...], NN)
+    depth = size // count
     for r in range(count):
         rows = pl.ds(pl.multiple_of((z_ref[0] ^ r) * depth, depth), depth)
-        kept_ref[rows, :] = outer[r * depth : (r + 1) * depth, :size]
-        sent_ref[rows, :] = outer[r * depth : (r + 1) * depth, size:].astype(BF16)
+        kept_ref[rows, :] = outer[r * depth : (r + 1) * depth, :]
+        sent_ref[rows, :] = outer[size + r * depth : size + (r + 1) * depth, :].astype(BF16)
 
 
 def hidden_kernel(owners, me_ref, *refs):
@@ -179,43 +177,35 @@
         out_ref[...] = total.astype(out_ref.dtype)
 
 
-def whole_kernel(*refs):
-    *parts, whole_ref = refs
+def whole_kernel(z_ref, *refs):
+    *parts, whole_ref, rows_ref = refs
     depth = parts[0].shape[0]
     for r, part in enumerate(parts):
-        whole_ref[r * depth : (r + 1) * depth, :] = part[...]
-
-
-def head_kernel(count, z_ref, rows_any, whole_ref, slice_ref, rows_ref, head_ref, sem):
+        rows_ref[pl.ds(pl.multiple_of((z_ref[0] ^ r) * depth, depth), depth), :] = part[...]
+    whole_ref[...] = rows_ref[...].T
+
+
+def head_kernel(rows_any, whole_ref, slice_ref, rows_ref, head_ref, sem):
     copy = pltpu.make_async_copy(rows_any, rows_ref, sem)
     copy.start()
-    depth = whole_ref.shape[0] // count
-    head = jnp.zeros(head_ref.shape, F32)
-    for r in range(count):
-        start = pl.multiple_of((z_ref[0] ^ r) * depth, depth)
-        head = head + dot(slice_ref[pl.ds(start, depth), :], whole_ref[r * depth : (r + 1) * depth, :], TN)
-    head_ref[...] = head
+    head_ref[...] = dot(slice_ref[...], whole_ref[...], TN)
     copy.wait()
 
 
-def proj_kernel(count, cuts, me_ref, z_ref, *refs):
+def proj_kernel(cuts, me_ref, *refs):
     *parts, rows_ref, out_hbm, outer_ref, done_ref, sems = refs
     width, size = parts[0].shape
     for distance, part in enumerate(parts):
         start = pl.multiple_of((me_ref[0] ^ distance) * size, size)
         outer_ref[:, pl.ds(start, size)] = part[...]
-    depth, height = width // count, width // count // cuts
+    height = width // cuts
     copies = []
-    for r in range(count):
-        for cut in range(cuts):
-            low = r * depth + cut * height
-            start = pl.multiple_of((z_ref[0] ^ r) * depth + cut * height, height)
-            done_ref[low : low + height, :] = dot(outer_ref[low : low + height, :], rows_ref[...], NN)
-            copy = pltpu.make_async_copy(
-                done_ref.at[pl.ds(low, height), :], out_hbm.at[pl.ds(start, height), :], sems.at[len(copies)]
-            )
-            copy.start()
-            copies.append(copy)
+    for cut in range(cuts):
+        rows = pl.ds(cut * height, height)
+        done_ref[rows, :] = dot(outer_ref[rows, :], rows_ref[...], NN)
+        copy = pltpu.make_async_copy(done_ref.at[rows, :], out_hbm.at[rows, :], sems.at[cut])
+        copy.start()
+        copies.append(copy)
     for copy in copies:
         copy.wait()
 
@@ -234,50 +224,49 @@
     block = samples // blocks
     size = head_weight.shape[0]
     labels = owners * size
-    depth = width // row_blocks
+    depth = size // row_blocks
     me_s, z_s = me.reshape(1), z_low.reshape(1)
     listed = shortlist.astype(jnp.int32).T
 
-    payload, enc_near, proj_near, wanted = pl.pallas_call(
+    payload = pl.pallas_call(
         payload_kernel,
-        out_shape=[
-            shape((size + TAIL, width), BF16),
-            shape((samples, width), BF16),
-            shape((width, width), BF16),
-            shape((positives.shape[1], samples), jnp.int32),
-        ],
-        in_specs=[ANY] * 6,
-        out_specs=[VMEM] * 4,
-        scratch_shapes=[pltpu.VMEM((1, size), jnp.int32)] * 2 + [pltpu.SemaphoreType.DMA((6,))],
-        compiler_params=pltpu.CompilerParams(vmem_limit_bytes=48 * MIB),
-    )(weight_num.reshape(1, size), weight_den.reshape(1, size), head_weight, enc, proj, positives.T)
+        out_shape=shape((size + TAIL, width), BF16),
+        in_specs=[ANY] * 3,
+        out_specs=VMEM,
+        scratch_shapes=[pltpu.VMEM((1, size), jnp.int32)] * 2 + [pltpu.SemaphoreType.DMA((3,))],
+        compiler_params=pltpu.CompilerParams(vmem_limit_bytes=56 * MIB),
+    )(weight_num.reshape(1, size), weight_den.reshape(1, size), head_weight)
     got = {0: payload}
     for g in far + near:
         got[2 * g] = swap(payload, "label", 2 * g)
     got[1] = swap(payload, "label", 1)
-    hidden, enc_t, target = call(
-        functools.partial(inputs_kernel, beam, block),
-        [shape((samples, width), BF16), shape((width, samples), BF16), shape((beam * size, samples), BF16)],
-        [enc_near, proj_near, wanted],
+    (target,) = call(
+        functools.partial(target_kernel, beam, block),
+        [shape((beam * size, samples), BF16)],
+        [positives.T],
+        vmem=2,
+        nbytes=8_000_000,
+    )
+    (hidden_t,) = call(
+        inputs_kernel,
+        [shape((width, samples), BF16)],
+        [enc, proj],
+        after=[target],
         flops=2 * samples * width * width,
         nbytes=6_000_000,
     )
     grads, kept, from_core, moved, received = {}, {}, {}, {}, {}
     order = [0] + far + near
     for at, g in enumerate(order):
-        if at + 1 < len(order):
-            ahead = order[at + 1]
-            got[2 * ahead] = gate(got[2 * ahead], hidden if at < 2 else grads[order[at - 2]])
-            got[2 * ahead + 1] = swap(got[2 * ahead], "label", 1)
         after = [] if at == 0 else [grads[order[at - 1]]]
-        if at + 1 < len(order) and at > 0:
+        if at and at + 1 < len(order):
             after.append(got[2 * order[at + 1]])
         if at >= 3:
             after.append(moved[order[at - 2]])
         grads[g], kept[g], sent = call(
             functools.partial(score_kernel, g, block, row_blocks),
-            [shape((2 * size, samples), BF16), shape((width, size), F32), shape((width, size), BF16)],
-            [hidden, target, enc_t, got[2 * g], got[2 * g + 1]],
+            [shape((2 * size, samples), BF16), shape((size, width), F32), shape((size, width), BF16)],
+            [hidden_t, target, enc, got[2 * g], got[2 * g + 1]],
             scalars=[listed, me_s, z_s],
             after=after,
             scratch=[
@@ -288,6 +277,9 @@
             flops=8 * samples * size * width,
             nbytes=5_000_000,
         )
+        for ahead in order[1:3] if at == 0 else order[at + 2 : at + 3]:
+            got[2 * ahead] = gate(got[2 * ahead], grads[g])
+            got[2 * ahead + 1] = swap(got[2 * ahead], "label", 1)
         from_core[g] = swap(sent, "label", 1)
         if g:
             moved[g] = (kept[g] + from_core[g].astype(F32)).astype(BF16)
@@ -329,10 +321,10 @@
         )(grad_hidden, proj, value)
 
     if row_blocks > 1:
-        cut = width // 2
+        cut = size // 2
         total, upper = call(
             combine_kernel,
-            [shape((cut, size), F32), shape((cut, size), BF16)],
+            [shape((cut, width), F32), shape((cut, width), BF16)],
             [own] + received,
             after=[grad_hidden],
             nbytes=2_000_000,
@@ -359,39 +351,46 @@
             parts[r + span] = swap(parts[r], "dp", span)
         span *= 2
     proj_slice = lax.dynamic_slice_in_dim(proj, z * (width // planes), width // planes, 1)
-    (whole,) = call(whole_kernel, [shape((width, size), BF16)], [parts[r] for r in range(row_blocks)], vmem=2)
+    (whole,) = call(
+        whole_kernel,
+        [shape((width, size), BF16)],
+        [parts[r] for r in range(row_blocks)],
+        scalars=[z_s],
+        scratch=[pltpu.VMEM((size, width), BF16)],
+        vmem=4,
+    )
     rows, grad_head = pl.pallas_call(
-        functools.partial(head_kernel, row_blocks),
+        head_kernel,
         out_shape=[shape((labels, width), BF16), shape((width // planes, size), F32)],
-        in_specs=[SMEM, ANY, VMEM, VMEM],
+        in_specs=[ANY, VMEM, VMEM],
         out_specs=[VMEM, VMEM],
         scratch_shapes=[pltpu.SemaphoreType.DMA],
         compiler_params=pltpu.CompilerParams(vmem_limit_bytes=4 * MIB),
         cost_estimate=pl.CostEstimate(
             flops=2 * size * width * width // planes, bytes_accessed=3_000_000, transcendentals=0
         ),
-    )(z_s, rows, whole, proj_slice)
+    )(rows, whole, proj_slice)
     have = {0: whole}
     for g in near + far:
         have[2 * g] = gate(swap(whole, "label", 2 * g), rows)
     for distance in list(have):
         have[distance + 1] = swap(have[distance], "label", 1)
-    cuts = 2
+    cuts = 4
     grad_proj = pl.pallas_call(
-        functools.partial(proj_kernel, row_blocks, cuts),
+        functools.partial(proj_kernel, cuts),
         out_shape=shape((width, width), F32),
-        in_specs=[SMEM] * 2 + [VMEM] * (owners + 1),
+        in_specs=[SMEM] + [VMEM] * (owners + 1),
         out_specs=ANY,
         scratch_shapes=[
             pltpu.VMEM((width, labels), BF16),
             pltpu.VMEM((width, width), F32),
-            pltpu.SemaphoreType.DMA((row_blocks * cuts,)),
+            pltpu.SemaphoreType.DMA((cuts,)),
         ],
         compiler_params=pltpu.CompilerParams(vmem_limit_bytes=16 * MIB),
         cost_estimate=pl.CostEstimate(
             flops=2 * labels * width * width, bytes_accessed=6_000_000, transcendentals=0
         ),
-    )(me_s, z_s, *[have[distance] for distance in range(owners)], rows)
+    )(me_s, *[have[distance] for distance in range(owners)], rows)
     return (grad_enc, grad_proj, grad_head.T)
 
 

time: 74.2 us -> 68.8 us (0.927)
  local copies, waits for them, and re-layouts: 6.82 us -> 3.76 us
  starting transfers between devices: 21.6 us -> 19.9 us
    unnamed x20 -> x16, local copies, waits for them, and re-layouts: 6.64 us -> 3.59 us
    ppermute x24, starting transfers between devices: 21.6 us -> 19.9 us  [swap(): return lax.ppermute(value, axis, [(i, i ^ distance) for i in range(size)])]
    pallas_call x8 -> x9, Pallas kernels: 16.5 us -> 15.8 us  [call(): pl.pallas_call(kernel, out_shape=outs, in_specs=[SMEM] * len(scalars) + [...]
  transfers between devices with their start and end apart: 24 -> 24, of which waited for: 11 -> 10; matrix products, arithmetic and copies ran while one was open for 0% -> 0% of each run, Pallas kernels for 28% -> 29%
where the time goes in v6:
time: 68.8 us; the launch traced here: 68.3 us
  Pallas kernels  24.7 us (36%)
  starting transfers between devices  19.9 us (29%)
  waiting for transfers between devices  18.6 us (27%)
  local copies, waits for them, and re-layouts  3.76 us (5%)
  between operations  1.08 us (2%)
    ppermute x24, starting transfers between devices, swap(): return lax.ppermute(value, axis, [(i, i ^ distance) for i in range(size)])  19.9 us
    ppermute x24, waiting for transfers between devices, swap(): return lax.ppermute(value, axis, [(i, i ^ distance) for i in range(size)])  18.6 us
    pallas_call x9, Pallas kernels, call(): pl.pallas_call(kernel, out_shape=outs, in_specs=[SMEM] * len(scalars) + [...  15.8 us
    unnamed x16, local copies, waits for them, and re-layouts  3.59 us
    pallas_call x1, Pallas kernels, grad_enc_after(): pl.pallas_call(enc_kernel, grid=(samples // tile,), out_shape=[shape((sam...  3.29 us
    pallas_call x1, Pallas kernels, shards(): pl.pallas_call(functools.partial(proj_kernel, cuts), out_shape=shape((wid...  2.76 us
    pallas_call x1, Pallas kernels, shards(): pl.pallas_call(payload_kernel, out_shape=shape((size + TAIL, width), BF16...  1.76 us
  transfers between devices with their start and end apart: 24, of which 10 were waited for; matrix products, arithmetic and copies ran while one was open for 0% of the time, Pallas kernels for 29%

profile of v6, /device:TPU:0, one launch (start us, length us, event | category | flops | bytes accessed | tf_op | source)
XLA Modules:
  0.0 68.3 jit_solution(9600082058376450268)
XLA Ops:
  0.6 1.8 %shard_map.96.refs_0_.refs_4_ = bf16[144,768]{1,0:T(8,128)(2,1)} custom-call(s32[1,128]{1,0:T(1,128)} %bitcast.12, s32[1,128]{1,0:T(1,128)} %bitcast.13, bf16[128,768]{1,0:T(8,128)(2,1)} %rows_hbm.1), custom_call_target="tpu_custom_call" | custom-call | tf_op jit(solution)/shard_map/pallas_call | solution.py:231
  2.9 3.5 %collective-permute-start.3 = (bf16[144,768]{1,0:T(8,128)(2,1)}, bf16[144,768]{1,0:T(8,128)(2,1)S(1)}, u32[]{:S(2)}, u32[]{:S(2)}) collective-permute-start(bf16[144,768]{1,0:T(8,128)(2,1)} %shard_map.96.refs_0_.refs_4_), channel_id=1, source_target_pairs={{0,6},{1,7},{2,4},{3,5},{4,2},{5,3},{6,0},{7,1},{8,14},{9,15},{10,... | collective-permute-start | bytes 663560 | tf_op jit(solution)/shard_map/ppermute | solution.py:55
  7.7 1.9 %shard_map.94.after_ref.target_ref = bf16[512,1024]{1,0:T(8,128)(2,1)S(1)} custom-call(s32[8,1024]{1,0:T(8,128)S(1)} %bitcast.11), custom_call_target="tpu_custom_call" | custom-call | bytes 8000000 | tf_op jit(solution)/shard_map/pallas_call | solution.py:31
  11.1 1.5 %shard_map.95.hidden_t_ref = bf16[768,1024]{1,0:T(8,128)(2,1)S(1)} custom-call(bf16[1024,768]{1,0:T(8,128)(2,1)S(1)} %copy-done, bf16[768,768]{1,0:T(8,128)(2,1)S(1)} %copy-done.2, bf16[512,1024]{1,0:T(8,128)(2,1)S(1)} %shard_map.94.after_ref.target_ref), custom_call_target="tpu_custom_call" | custom-call | flops 1207959552 | bytes 6000000 | tf_op jit(solution)/shard_map/pallas_call | solution.py:31
  12.6 2.8 %shard_map.97 = (bf16[256,1024]{1,0:T(8,128)(2,1)S(1)}, f32[128,768]{1,0:T(8,128)S(1)}, bf16[128,768]{1,0:T(8,128)(2,1)S(1)}) custom-call(s32[4,8]{1,0:T(4,128)S(1)} %bitcast.7, s32[1]{0:T(128)} %bitcast.me_ref, s32[1]{0:T(128)} %bitcast.2.z_ref, bf16[768,1024]{1,0:T(8,128)(2,1)S(1)} %shard_map.95.hidden_t_ref, ...), custom_call_target="tpu_custom_call" | custom-call | flops 805306368 | bytes 5000000 | tf_op jit(solution)/shard_map/pallas_call | solution.py:31
  15.8 1.9 %collective-permute-done.1.value_ref = bf16[144,768]{1,0:T(8,128)(2,1)S(1)} collective-permute-done((bf16[144,768]{1,0:T(8,128)(2,1)}, bf16[144,768]{1,0:T(8,128)(2,1)S(1)}, u32[]{:S(2)}, u32[]{:S(2)}) %collective-permute-start.1) | collective-permute-done | bytes 221216 | tf_op jit(solution)/shard_map/ppermute | solution.py:55
  17.7 2.4 %shard_map.100 = (bf16[256,1024]{1,0:T(8,128)(2,1)S(1)}, f32[128,768]{1,0:T(8,128)S(1)}, bf16[128,768]{1,0:T(8,128)(2,1)S(1)}) custom-call(s32[4,8]{1,0:T(4,128)S(1)} %bitcast.8, s32[1]{0:T(128)} %bitcast.me_ref, s32[1]{0:T(128)} %bitcast.2.z_ref, bf16[768,1024]{1,0:T(8,128)(2,1)S(1)} %shard_map.95.hidden_t_ref, ...), custom_call_target="tpu_custom_call" | custom-call | flops 805306368 | bytes 5000000 | tf_op jit(solution)/shard_map/pallas_call | solution.py:31
  20.7 2.6 %collective-permute-done.5.value_ref = bf16[144,768]{1,0:T(8,128)(2,1)S(1)} collective-permute-done((bf16[144,768]{1,0:T(8,128)(2,1)S(1)}, bf16[144,768]{1,0:T(8,128)(2,1)S(1)}, u32[]{:S(2)}, u32[]{:S(2)}) %collective-permute-start.5) | collective-permute-done | bytes 221216 | tf_op jit(solution)/shard_map/ppermute | solution.py:55
  23.3 2.5 %shard_map.102 = (bf16[256,1024]{1,0:T(8,128)(2,1)S(1)}, f32[128,768]{1,0:T(8,128)S(1)}, bf16[128,768]{1,0:T(8,128)(2,1)S(1)}) custom-call(s32[4,8]{1,0:T(4,128)S(1)} %bitcast.9, s32[1]{0:T(128)} %bitcast.me_ref, s32[1]{0:T(128)} %bitcast.2.z_ref, bf16[768,1024]{1,0:T(8,128)(2,1)S(1)} %shard_map.95.hidden_t_ref, ...), custom_call_target="tpu_custom_call" | custom-call | flops 805306368 | bytes 5000000 | tf_op jit(solution)/shard_map/pallas_call | solution.py:31
  26.5 1.4 %collective-permute-start.11 = (bf16[128,768]{1,0:T(8,128)(2,1)S(1)}, bf16[128,768]{1,0:T(8,128)(2,1)S(1)}, u32[]{:S(2)}, u32[]{:S(2)}) collective-permute-start(bf16[128,768]{1,0:T(8,128)(2,1)S(1)} %add_convert_fusion.2.refs_3_.refs_12_), channel_id=1, source_target_pairs={{0,6},{1,7},{2,4},{3,5},{4,2},{5,3},{6,0},{7,1},{8,14},{9,15},{10,... | collective-permute-start | bytes 589832 | tf_op jit(solution)/shard_map/ppermute | solution.py:55
  27.9 2.7 %shard_map.103 = (bf16[256,1024]{1,0:T(8,128)(2,1)S(1)}, f32[128,768]{1,0:T(8,128)S(1)}, bf16[128,768]{1,0:T(8,128)(2,1)S(1)}) custom-call(s32[4,8]{1,0:T(4,128)S(1)} %bitcast.10, s32[1]{0:T(128)} %bitcast.me_ref, s32[1]{0:T(128)} %bitcast.2.z_ref, bf16[768,1024]{1,0:T(8,128)(2,1)S(1)} %shard_map.95.hidden_t_ref, ...), custom_call_target="tpu_custom_call" | custom-call | flops 805306368 | bytes 5000000 | tf_op jit(solution)/shard_map/pallas_call | solution.py:31
  32.2 1.4 %collective-permute-start.13 = (bf16[128,768]{1,0:T(8,128)(2,1)S(1)}, bf16[128,768]{1,0:T(8,128)(2,1)S(1)}, u32[]{:S(2)}, u32[]{:S(2)}) collective-permute-start(bf16[128,768]{1,0:T(8,128)(2,1)S(1)} %add_convert_fusion.refs_14_), channel_id=1, source_target_pairs={{0,4},{1,5},{2,6},{3,7},{4,0},{5,1},{6,2},{7,3},{8,12},{9,13},{10,... | collective-permute-start | bytes 589832 | tf_op jit(solution)/shard_map/ppermute | solution.py:55
  33.7 1.9 %shard_map.104 = (bf16[1024,768]{1,0:T(8,128)(2,1)S(1)}, bf16[1024,768]{1,0:T(8,128)(2,1)S(1)}) custom-call(s32[1]{0:T(128)} %bitcast.me_ref, bf16[256,1024]{1,0:T(8,128)(2,1)S(1)} %get-tuple-element.23.refs_0_.refs_2_, bf16[256,1024]{1,0:T(8,128)(2,1)S(1)} %get-tuple-element.25.refs_2_.refs_1_, bf16[256,1024]{1,0:T(8,128)(2,1)S(1)} %get-tuple-element.28.refs_2_, ...), custom_call_target="tpu_custom_call" | custom-call | flops 1610612736 | bytes 5000000 | tf_op jit(solution)/shard_map/pallas_call | solution.py:31
  35.6 2.5 %collective-permute-done.12.refs_1_ = bf16[128,768]{1,0:T(8,128)(2,1)S(1)} collective-permute-done((bf16[128,768]{1,0:T(8,128)(2,1)S(1)}, bf16[128,768]{1,0:T(8,128)(2,1)S(1)}, u32[]{:S(2)}, u32[]{:S(2)}) %collective-permute-start.12) | collective-permute-done | bytes 196640 | tf_op jit(solution)/shard_map/ppermute | solution.py:55
  39.3 1.7 %collective-permute-start.14 = (bf16[64,768]{1,0:T(8,128)(2,1)S(1)}, bf16[64,768]{1,0:T(8,128)(2,1)S(1)}, u32[]{:S(2)}, u32[]{:S(2)}) collective-permute-start(bf16[64,768]{1,0:T(8,128)(2,1)S(1)} %get-tuple-element.37), channel_id=1, source_target_pairs={{0,8},{8,0},{16,24},{24,16},{1,9},{9,1},{17,25},{25,17},{2,10},{10... | collective-permute-start | bytes 294920 | tf_op jit(solution)/shard_map/ppermute | solution.py:55
  41.0 3.0 %collective-permute-done.14 = bf16[64,768]{1,0:T(8,128)(2,1)S(1)} collective-permute-done((bf16[64,768]{1,0:T(8,128)(2,1)S(1)}, bf16[64,768]{1,0:T(8,128)(2,1)S(1)}, u32[]{:S(2)}, u32[]{:S(2)}) %collective-permute-start.14) | collective-permute-done | bytes 98336 | tf_op jit(solution)/shard_map/ppermute | solution.py:55
  44.0 2.7 %collective-permute-start.15 = (bf16[64,768]{1,0:T(8,128)(2,1)S(1)}, bf16[64,768]{1,0:T(8,128)(2,1)S(1)}, u32[]{:S(2)}, u32[]{:S(2)}) collective-permute-start(bf16[64,768]{1,0:T(8,128)(2,1)S(1)} %add_convert_fusion.4.after_ref), channel_id=1, source_target_pairs={{0,16},{8,24},{16,0},{24,8},{1,17},{9,25},{17,1},{25,9},{2,18},{10... | collective-permute-start | bytes 294920 | tf_op jit(solution)/shard_map/ppermute | solution.py:55
  46.7 3.3 %shard_map.106 = (f32[1024,768]{1,0:T(8,128)}, f32[8,128]{1,0:T(8,128)S(1)}) custom-call(bf16[1024,768]{1,0:T(8,128)(2,1)S(1)} %get-tuple-element.33.refs_3_.grad_hidden_ref, bf16[768,768]{1,0:T(8,128)(2,1)S(1)} %copy-done.2, bf16[64,768]{1,0:T(8,128)(2,1)S(1)} %add_convert_fusion.4.after_ref), custom_call_target="tpu_custom_call" | custom-call | flops 1207959552 | bytes 6000000 | tf_op jit(solution)/shard_map/pallas_call | solution.py:304
  50.0 1.6 %collective-permute-start.16 = (bf16[64,768]{1,0:T(8,128)(2,1)S(1)}, bf16[64,768]{1,0:T(8,128)(2,1)S(1)}, u32[]{:S(2)}, u32[]{:S(2)}) collective-permute-start(bf16[64,768]{1,0:T(8,128)(2,1)S(1)} %add_convert_fusion.3.refs_0_), channel_id=1, source_target_pairs={{0,8},{8,0},{16,24},{24,16},{1,9},{9,1},{17,25},{25,17},{2,10},{10... | collective-permute-start | bytes 294920 | tf_op jit(solution)/shard_map/ppermute | solution.py:55
  51.6 3.1 %collective-permute-done.16.refs_1_ = bf16[64,768]{1,0:T(8,128)(2,1)S(1)} collective-permute-done((bf16[64,768]{1,0:T(8,128)(2,1)S(1)}, bf16[64,768]{1,0:T(8,128)(2,1)S(1)}, u32[]{:S(2)}, u32[]{:S(2)}) %collective-permute-start.16) | collective-permute-done | bytes 98336 | tf_op jit(solution)/shard_map/ppermute | solution.py:55
  56.9 1.5 %collective-permute-start.22 = (bf16[768,128]{1,0:T(8,128)(2,1)S(1)}, bf16[768,128]{1,0:T(8,128)(2,1)S(1)}, u32[]{:S(2)}, u32[]{:S(2)}) collective-permute-start(bf16[768,128]{1,0:T(8,128)(2,1)S(1)} %shard_map.108.whole_ref.refs_0_), channel_id=1, source_target_pairs={{0,6},{1,7},{2,4},{3,5},{4,2},{5,3},{6,0},{7,1},{8,14},{9,15},{10,... | collective-permute-start | bytes 589832 | tf_op jit(solution)/shard_map/ppermute | solution.py:55
  58.6 1.4 %copy-done.4 = bf16[1024,768]{1,0:T(8,128)(2,1)S(1)} copy-done((bf16[1024,768]{1,0:T(8,128)(2,1)S(1)}, bf16[1024,768]{1,0:T(8,128)(2,1)}, u32[]{:S(2)}) %copy-start.4) | copy-done | bytes 1572888
  61.7 1.9 %collective-permute-done.20.value_ref = bf16[768,128]{1,0:T(8,128)(2,1)S(1)} collective-permute-done((bf16[768,128]{1,0:T(8,128)(2,1)S(1)}, bf16[768,128]{1,0:T(8,128)(2,1)S(1)}, u32[]{:S(2)}, u32[]{:S(2)}) %collective-permute-start.20) | collective-permute-done | bytes 196640 | tf_op jit(solution)/shard_map/ppermute | solution.py:55
  65.3 2.8 %shard_map.113 = f32[768,768]{1,0:T(8,128)} custom-call(s32[1]{0:T(128)} %bitcast.me_ref, bf16[768,128]{1,0:T(8,128)(2,1)S(1)} %shard_map.108.whole_ref.refs_0_, bf16[768,128]{1,0:T(8,128)(2,1)S(1)} %collective-permute-done.17.refs_1_, bf16[768,128]{1,0:T(8,128)(2,1)S(1)} %shard_map.110.refs_2_, bf16[768,128]{1,0:T(8,128)(2,1)S(1)} %collective-permute-done.19.refs_3_, ...), custom_call_target="tpu_custom_call" | custom-call | flops 1207959552 | bytes 6000000 | tf_op jit(solution)/shard_map/pallas_call | solution.py:379
  (67 shorter events, 13.5 us)
Async XLA Ops:
  2.4 10.1 %collective-permute-start = (bf16[144,768]{1,0:T(8,128)(2,1)}, bf16[144,768]{1,0:T(8,128)(2,1)S(1)}, u32[]{:S(2)}, u32[]{:S(2)}) collective-permute-start(bf16[144,768]{1,0:T(8,128)(2,1)} %shard_map.96.refs_0_.refs_4_), channel_id=1, source_target_pairs={{0,1},{1,0},{2,3},{3,2},{4,5},{5,4},{6,7},{7,6},{8,9},{9,8},{10,11... | collective-permute-start | bytes 663560 | tf_op jit(solution)/shard_map/ppermute | solution.py:55
  2.9 12.4 %collective-permute-start.3 = (bf16[144,768]{1,0:T(8,128)(2,1)}, bf16[144,768]{1,0:T(8,128)(2,1)S(1)}, u32[]{:S(2)}, u32[]{:S(2)}) collective-permute-start(bf16[144,768]{1,0:T(8,128)(2,1)} %shard_map.96.refs_0_.refs_4_), channel_id=1, source_target_pairs={{0,6},{1,7},{2,4},{3,5},{4,2},{5,3},{6,0},{7,1},{8,14},{9,15},{10,... | collective-permute-start | bytes 663560 | tf_op jit(solution)/shard_map/ppermute | solution.py:55
  6.5 11.2 %collective-permute-start.1 = (bf16[144,768]{1,0:T(8,128)(2,1)}, bf16[144,768]{1,0:T(8,128)(2,1)S(1)}, u32[]{:S(2)}, u32[]{:S(2)}) collective-permute-start(bf16[144,768]{1,0:T(8,128)(2,1)} %shard_map.96.refs_0_.refs_4_), channel_id=1, source_target_pairs={{0,2},{1,3},{2,0},{3,1},{4,6},{5,7},{6,4},{7,5},{8,10},{9,11},{10,... | collective-permute-start | bytes 663560 | tf_op jit(solution)/shard_map/ppermute | solution.py:55
  15.4 2.3 %collective-permute-start.4 = (bf16[144,768]{1,0:T(8,128)(2,1)S(1)}, bf16[144,768]{1,0:T(8,128)(2,1)S(1)}, u32[]{:S(2)}, u32[]{:S(2)}) collective-permute-start(bf16[144,768]{1,0:T(8,128)(2,1)S(1)} %shard_map.99.refs_0_.refs_10_), channel_id=1, source_target_pairs={{0,1},{1,0},{2,3},{3,2},{4,5},{5,4},{6,7},{7,6},{8,9},{9,8},{10,11... | collective-permute-start | bytes 663560 | tf_op jit(solution)/shard_map/ppermute | solution.py:55
  15.5 7.8 %collective-permute-start.5 = (bf16[144,768]{1,0:T(8,128)(2,1)S(1)}, bf16[144,768]{1,0:T(8,128)(2,1)S(1)}, u32[]{:S(2)}, u32[]{:S(2)}) collective-permute-start(bf16[144,768]{1,0:T(8,128)(2,1)S(1)} %copy-done.5), channel_id=1, source_target_pairs={{0,4},{1,5},{2,6},{3,7},{4,0},{5,1},{6,2},{7,3},{8,12},{9,13},{10,... | collective-permute-start | bytes 663560 | tf_op jit(solution)/shard_map/ppermute | solution.py:55
  17.7 5.6 %collective-permute-start.2 = (bf16[144,768]{1,0:T(8,128)(2,1)S(1)}, bf16[144,768]{1,0:T(8,128)(2,1)S(1)}, u32[]{:S(2)}, u32[]{:S(2)}) collective-permute-start(bf16[144,768]{1,0:T(8,128)(2,1)S(1)} %shard_map.98.refs_3_.refs_0_.refs_6_), channel_id=1, source_target_pairs={{0,1},{1,0},{2,3},{3,2},{4,5},{5,4},{6,7},{7,6},{8,9},{9,8},{10,11... | collective-permute-start | bytes 663560 | tf_op jit(solution)/shard_map/ppermute | solution.py:55
  20.1 6.4 %collective-permute-start.7 = (bf16[128,768]{1,0:T(8,128)(2,1)S(1)}, bf16[128,768]{1,0:T(8,128)(2,1)S(1)}, u32[]{:S(2)}, u32[]{:S(2)}) collective-permute-start(bf16[128,768]{1,0:T(8,128)(2,1)S(1)} %get-tuple-element.27), channel_id=1, source_target_pairs={{0,1},{1,0},{2,3},{3,2},{4,5},{5,4},{6,7},{7,6},{8,9},{9,8},{10,11... | collective-permute-start | bytes 589832 | tf_op jit(solution)/shard_map/ppermute | solution.py:55
  20.7 13.0 %collective-permute-start.10 = (bf16[128,768]{1,0:T(8,128)(2,1)S(1)}, bf16[128,768]{1,0:T(8,128)(2,1)S(1)}, u32[]{:S(2)}, u32[]{:S(2)}) collective-permute-start(bf16[128,768]{1,0:T(8,128)(2,1)S(1)} %get-tuple-element.35), channel_id=1, source_target_pairs={{0,1},{1,0},{2,3},{3,2},{4,5},{5,4},{6,7},{7,6},{8,9},{9,8},{10,11... | collective-permute-start | bytes 589832 | tf_op jit(solution)/shard_map/ppermute | solution.py:55
  23.3 4.6 %collective-permute-start.6 = (bf16[144,768]{1,0:T(8,128)(2,1)S(1)}, bf16[144,768]{1,0:T(8,128)(2,1)S(1)}, u32[]{:S(2)}, u32[]{:S(2)}) collective-permute-start(bf16[144,768]{1,0:T(8,128)(2,1)S(1)} %shard_map.101.refs_3_.refs_0_.refs_8_), channel_id=1, source_target_pairs={{0,1},{1,0},{2,3},{3,2},{4,5},{5,4},{6,7},{7,6},{8,9},{9,8},{10,11... | collective-permute-start | bytes 663560 | tf_op jit(solution)/shard_map/ppermute | solution.py:55
  25.8 4.9 %collective-permute-start.8 = (bf16[128,768]{1,0:T(8,128)(2,1)S(1)}, bf16[128,768]{1,0:T(8,128)(2,1)S(1)}, u32[]{:S(2)}, u32[]{:S(2)}) collective-permute-start(bf16[128,768]{1,0:T(8,128)(2,1)S(1)} %get-tuple-element.30), channel_id=1, source_target_pairs={{0,1},{1,0},{2,3},{3,2},{4,5},{5,4},{6,7},{7,6},{8,9},{9,8},{10,11... | collective-permute-start | bytes 589832 | tf_op jit(solution)/shard_map/ppermute | solution.py:55
  26.5 9.1 %collective-permute-start.11 = (bf16[128,768]{1,0:T(8,128)(2,1)S(1)}, bf16[128,768]{1,0:T(8,128)(2,1)S(1)}, u32[]{:S(2)}, u32[]{:S(2)}) collective-permute-start(bf16[128,768]{1,0:T(8,128)(2,1)S(1)} %add_convert_fusion.2.refs_3_.refs_12_), channel_id=1, source_target_pairs={{0,6},{1,7},{2,4},{3,5},{4,2},{5,3},{6,0},{7,1},{8,14},{9,15},{10,... | collective-permute-start | bytes 589832 | tf_op jit(solution)/shard_map/ppermute | solution.py:55
  30.6 1.5 %collective-permute-start.9 = (bf16[128,768]{1,0:T(8,128)(2,1)S(1)}, bf16[128,768]{1,0:T(8,128)(2,1)S(1)}, u32[]{:S(2)}, u32[]{:S(2)}) collective-permute-start(bf16[128,768]{1,0:T(8,128)(2,1)S(1)} %get-tuple-element.32), channel_id=1, source_target_pairs={{0,1},{1,0},{2,3},{3,2},{4,5},{5,4},{6,7},{7,6},{8,9},{9,8},{10,11... | collective-permute-start | bytes 589832 | tf_op jit(solution)/shard_map/ppermute | solution.py:55
  30.8 7.4 %collective-permute-start.12 = (bf16[128,768]{1,0:T(8,128)(2,1)S(1)}, bf16[128,768]{1,0:T(8,128)(2,1)S(1)}, u32[]{:S(2)}, u32[]{:S(2)}) collective-permute-start(bf16[128,768]{1,0:T(8,128)(2,1)S(1)} %add_convert_fusion.1.refs_13_), channel_id=1, source_target_pairs={{0,2},{1,3},{2,0},{3,1},{4,6},{5,7},{6,4},{7,5},{8,10},{9,11},{10,... | collective-permute-start | bytes 589832 | tf_op jit(solution)/shard_map/ppermute | solution.py:55
  32.2 7.0 %collective-permute-start.13 = (bf16[128,768]{1,0:T(8,128)(2,1)S(1)}, bf16[128,768]{1,0:T(8,128)(2,1)S(1)}, u32[]{:S(2)}, u32[]{:S(2)}) collective-permute-start(bf16[128,768]{1,0:T(8,128)(2,1)S(1)} %add_convert_fusion.refs_14_), channel_id=1, source_target_pairs={{0,4},{1,5},{2,6},{3,7},{4,0},{5,1},{6,2},{7,3},{8,12},{9,13},{10,... | collective-permute-start | bytes 589832 | tf_op jit(solution)/shard_map/ppermute | solution.py:55
  39.3 4.7 %collective-permute-start.14 = (bf16[64,768]{1,0:T(8,128)(2,1)S(1)}, bf16[64,768]{1,0:T(8,128)(2,1)S(1)}, u32[]{:S(2)}, u32[]{:S(2)}) collective-permute-start(bf16[64,768]{1,0:T(8,128)(2,1)S(1)} %get-tuple-element.37), channel_id=1, source_target_pairs={{0,8},{8,0},{16,24},{24,16},{1,9},{9,1},{17,25},{25,17},{2,10},{10... | collective-permute-start | bytes 294920 | tf_op jit(solution)/shard_map/ppermute | solution.py:55
  44.0 6.0 %collective-permute-start.15 = (bf16[64,768]{1,0:T(8,128)(2,1)S(1)}, bf16[64,768]{1,0:T(8,128)(2,1)S(1)}, u32[]{:S(2)}, u32[]{:S(2)}) collective-permute-start(bf16[64,768]{1,0:T(8,128)(2,1)S(1)} %add_convert_fusion.4.after_ref), channel_id=1, source_target_pairs={{0,16},{8,24},{16,0},{24,8},{1,17},{9,25},{17,1},{25,9},{2,18},{10... | collective-permute-start | bytes 294920 | tf_op jit(solution)/shard_map/ppermute | solution.py:55
  50.0 4.7 %collective-permute-start.16 = (bf16[64,768]{1,0:T(8,128)(2,1)S(1)}, bf16[64,768]{1,0:T(8,128)(2,1)S(1)}, u32[]{:S(2)}, u32[]{:S(2)}) collective-permute-start(bf16[64,768]{1,0:T(8,128)(2,1)S(1)} %add_convert_fusion.3.refs_0_), channel_id=1, source_target_pairs={{0,8},{8,0},{16,24},{24,16},{1,9},{9,1},{17,25},{25,17},{2,10},{10... | collective-permute-start | bytes 294920 | tf_op jit(solution)/shard_map/ppermute | solution.py:55
  54.8 6.3 %collective-permute-start.18 = (bf16[768,128]{1,0:T(8,128)(2,1)S(1)}, bf16[768,128]{1,0:T(8,128)(2,1)S(1)}, u32[]{:S(2)}, u32[]{:S(2)}) collective-permute-start(bf16[768,128]{1,0:T(8,128)(2,1)S(1)} %shard_map.108.whole_ref.refs_0_), channel_id=1, source_target_pairs={{0,2},{1,3},{2,0},{3,1},{4,6},{5,7},{6,4},{7,5},{8,10},{9,11},{10,... | collective-permute-start | bytes 589832 | tf_op jit(solution)/shard_map/ppermute | solution.py:55
  55.8 7.8 %collective-permute-start.20 = (bf16[768,128]{1,0:T(8,128)(2,1)S(1)}, bf16[768,128]{1,0:T(8,128)(2,1)S(1)}, u32[]{:S(2)}, u32[]{:S(2)}) collective-permute-start(bf16[768,128]{1,0:T(8,128)(2,1)S(1)} %shard_map.108.whole_ref.refs_0_), channel_id=1, source_target_pairs={{0,4},{1,5},{2,6},{3,7},{4,0},{5,1},{6,2},{7,3},{8,12},{9,13},{10,... | collective-permute-start | bytes 589832 | tf_op jit(solution)/shard_map/ppermute | solution.py:55
  56.9 6.7 %collective-permute-start.22 = (bf16[768,128]{1,0:T(8,128)(2,1)S(1)}, bf16[768,128]{1,0:T(8,128)(2,1)S(1)}, u32[]{:S(2)}, u32[]{:S(2)}) collective-permute-start(bf16[768,128]{1,0:T(8,128)(2,1)S(1)} %shard_map.108.whole_ref.refs_0_), channel_id=1, source_target_pairs={{0,6},{1,7},{2,4},{3,5},{4,2},{5,3},{6,0},{7,1},{8,14},{9,15},{10,... | collective-permute-start | bytes 589832 | tf_op jit(solution)/shard_map/ppermute | solution.py:55
  58.6 5.6 %collective-permute-start.17 = (bf16[768,128]{1,0:T(8,128)(2,1)S(1)}, bf16[768,128]{1,0:T(8,128)(2,1)S(1)}, u32[]{:S(2)}, u32[]{:S(2)}) collective-permute-start(bf16[768,128]{1,0:T(8,128)(2,1)S(1)} %shard_map.108.whole_ref.refs_0_), channel_id=1, source_target_pairs={{0,1},{1,0},{2,3},{3,2},{4,5},{5,4},{6,7},{7,6},{8,9},{9,8},{10,11... | collective-permute-start | bytes 589832 | tf_op jit(solution)/shard_map/ppermute | solution.py:55
  61.1 3.0 %collective-permute-start.19 = (bf16[768,128]{1,0:T(8,128)(2,1)S(1)}, bf16[768,128]{1,0:T(8,128)(2,1)S(1)}, u32[]{:S(2)}, u32[]{:S(2)}) collective-permute-start(bf16[768,128]{1,0:T(8,128)(2,1)S(1)} %shard_map.110.refs_2_), channel_id=1, source_target_pairs={{0,1},{1,0},{2,3},{3,2},{4,5},{5,4},{6,7},{7,6},{8,9},{9,8},{10,11... | collective-permute-start | bytes 589832 | tf_op jit(solution)/shard_map/ppermute | solution.py:55
  63.6 1.4 %collective-permute-start.21 = (bf16[768,128]{1,0:T(8,128)(2,1)S(1)}, bf16[768,128]{1,0:T(8,128)(2,1)S(1)}, u32[]{:S(2)}, u32[]{:S(2)}) collective-permute-start(bf16[768,128]{1,0:T(8,128)(2,1)S(1)} %shard_map.111.refs_4_), channel_id=1, source_target_pairs={{0,1},{1,0},{2,3},{3,2},{4,5},{5,4},{6,7},{7,6},{8,9},{9,8},{10,11... | collective-permute-start | bytes 589832 | tf_op jit(solution)/shard_map/ppermute | solution.py:55
  63.6 1.7 %collective-permute-start.23 = (bf16[768,128]{1,0:T(8,128)(2,1)S(1)}, bf16[768,128]{1,0:T(8,128)(2,1)S(1)}, u32[]{:S(2)}, u32[]{:S(2)}) collective-permute-start(bf16[768,128]{1,0:T(8,128)(2,1)S(1)} %shard_map.112.refs_6_), channel_id=1, source_target_pairs={{0,1},{1,0},{2,3},{3,2},{4,5},{5,4},{6,7},{7,6},{8,9},{9,8},{10,11... | collective-permute-start | bytes 589832 | tf_op jit(solution)/shard_map/ppermute | solution.py:55
  (8 other events, 34.7 us)

commit v7 on v6

--- a/solution.py
+++ b/solution.py
@@ -73,7 +73,8 @@
     copies[2].wait()
 
 
-def target_kernel(beam, block, wanted_ref, target_ref):
+def target_kernel(beam, block, wanted_ref, payload_ref, target_ref, copy_ref):
+    copy_ref[...] = payload_ref[...]
     samples = wanted_ref.shape[1]
     size = target_ref.shape[0] // beam
     label_iota = lax.broadcasted_iota(jnp.int32, (size, block), 0)
@@ -102,38 +103,32 @@
     return guess * (2.0 - bottom * guess)
 
 
-def score_kernel(group, block, count, list_ref, me_ref, z_ref, hidden_t_ref, target_ref, enc_ref, *refs):
-    payloads, refs = refs[:2], refs[-8:]
-    grads_ref, kept_ref, sent_ref, weights_ref, scale_ref, logits_ref = refs[-6:]
+def score_kernel(group, block, count, places_ref, z_ref, hidden_t_ref, target_ref, enc_ref, *refs):
+    payloads, refs = refs[:2], refs[-6:]
+    grads_ref, kept_ref, sent_ref, weights_ref, scale_ref, logits_ref = refs
     samples = enc_ref.shape[0]
     size = payloads[0].shape[0] - TAIL
+    blocks = samples // block
     for core in range(2):
         rows = pl.ds(core * size, size)
         weights_ref[rows, :] = payloads[core][:size, :]
         tail = payloads[core][size:, :size].astype(F32)
         ratio = tail[0:1, :] / tail[1:2, :]
-        scale_ref[rows, :] = jnp.broadcast_to(ratio, (block, size)).T / block
-    logits_ref[...] = dot(weights_ref[...], hidden_t_ref[...], NN)
-    grads_ref[...] = jnp.zeros_like(grads_ref)
-
-    def one_block(at, carried):
-        low = pl.multiple_of(at * block, block)
-        for core in range(2):
-            cluster = me_ref[0] ^ (2 * group + core)
-            place = jnp.int32(-1)
-            for beam_slot in range(list_ref.shape[0]):
-                place = jnp.where(list_ref[beam_slot, at] == cluster, beam_slot, place)
-
-            @pl.when(place >= 0)
-            def _():
+        scale_ref[rows, :] = jnp.broadcast_to(ratio, (block, size)).T
+    tile = min(2 * block, samples)
+    for start in range(0, samples, tile):
+        logits_ref[:, start : start + tile] = dot(
+            weights_ref[...], hidden_t_ref[:, start : start + tile], NN
+        )
+        for low in range(start, start + tile, block):
+            for core in range(2):
+                place = places_ref[(2 * group + core) * blocks + low // block]
+                factor = jnp.where(place >= 0, 1.0 / block, 0.0)
+                first = pl.multiple_of(jnp.maximum(place, 0) * size, size)
                 rows = slice(core * size, (core + 1) * size)
-                target = target_ref[pl.ds(pl.multiple_of(place * size, size), size), pl.ds(low, block)]
-                share = logistic(logits_ref[rows, pl.ds(low, block)]) - target.astype(F32)
-                grads_ref[rows, pl.ds(low, block)] = (scale_ref[rows, :] * share).astype(BF16)
-
-        return carried
-
-    lax.fori_loop(0, samples // block, one_block, 0)
+                target = target_ref[pl.ds(first, size), low : low + block].astype(F32)
+                share = logistic(logits_ref[rows, low : low + block]) - target
+                grads_ref[rows, low : low + block] = (scale_ref[rows, :] * factor * share).astype(BF16)
     outer = dot(grads_ref[...], enc_ref[...], NN)
     depth = size // count
     for r in range(count):
@@ -226,8 +221,6 @@
     labels = owners * size
     depth = size // row_blocks
     me_s, z_s = me.reshape(1), z_low.reshape(1)
-    listed = shortlist.astype(jnp.int32).T
-
     payload = pl.pallas_call(
         payload_kernel,
         out_shape=shape((size + TAIL, width), BF16),
@@ -237,14 +230,14 @@
         compiler_params=pltpu.CompilerParams(vmem_limit_bytes=56 * MIB),
     )(weight_num.reshape(1, size), weight_den.reshape(1, size), head_weight)
     got = {0: payload}
-    for g in far + near:
+    for g in near:
         got[2 * g] = swap(payload, "label", 2 * g)
     got[1] = swap(payload, "label", 1)
-    (target,) = call(
+    target, late = call(
         functools.partial(target_kernel, beam, block),
-        [shape((beam * size, samples), BF16)],
-        [positives.T],
-        vmem=2,
+        [shape((beam * size, samples), BF16), shape(payload.shape, BF16)],
+        [positives.T, payload],
+        vmem=4,
         nbytes=8_000_000,
     )
     (hidden_t,) = call(
@@ -255,10 +248,18 @@
         flops=2 * samples * width * width,
         nbytes=6_000_000,
     )
+    for g in far:
+        got[2 * g] = swap(late, "label", 2 * g)
+    for g in near:
+        got[2 * g] = gate(got[2 * g], hidden_t)
+        got[2 * g + 1] = swap(got[2 * g], "label", 1)
+    clusters = me ^ jnp.arange(owners, dtype=jnp.int32)
+    listing = shortlist.astype(jnp.int32)[None, :, :] == clusters[:, None, None]
+    places = jnp.max(jnp.where(listing, jnp.arange(beam, dtype=jnp.int32), -1), axis=2).reshape(-1)
     grads, kept, from_core, moved, received = {}, {}, {}, {}, {}
-    order = [0] + far + near
+    order = [0] + near + far
     for at, g in enumerate(order):
-        after = [] if at == 0 else [grads[order[at - 1]]]
+        after = [got[2 * n] for n in near] if at == 0 else [grads[order[at - 1]]]
         if at and at + 1 < len(order):
             after.append(got[2 * order[at + 1]])
         if at >= 3:
@@ -267,7 +268,7 @@
             functools.partial(score_kernel, g, block, row_blocks),
             [shape((2 * size, samples), BF16), shape((size, width), F32), shape((size, width), BF16)],
             [hidden_t, target, enc, got[2 * g], got[2 * g + 1]],
-            scalars=[listed, me_s, z_s],
+            scalars=[places, z_s],
             after=after,
             scratch=[
                 pltpu.VMEM((2 * size, width), BF16),
@@ -277,7 +278,7 @@
             flops=8 * samples * size * width,
             nbytes=5_000_000,
         )
-        for ahead in order[1:3] if at == 0 else order[at + 2 : at + 3]:
+        for ahead in [n for n in order[at + 2 : at + 3] if n in far]:
             got[2 * ahead] = gate(got[2 * ahead], grads[g])
             got[2 * ahead + 1] = swap(got[2 * ahead], "label", 1)
         from_core[g] = swap(sent, "label", 1)
@@ -285,14 +286,14 @@
             moved[g] = (kept[g] + from_core[g].astype(F32)).astype(BF16)
             received[g] = swap(moved[g], "label", 2 * g)
     own = kept[0] + from_core[0].astype(F32)
-    received = [received[g] for g in far + near]
+    received = [received[g] for g in near + far]
 
     grad_hidden, rows = call(
         functools.partial(hidden_kernel, owners),
         [shape((samples, width), BF16), shape((labels, width), BF16)],
         [grads[g] for g in range(chips)] + [got[d] for d in range(owners)],
         scalars=[me_s],
-        after=[moved[g] for g in far + near],
+        after=[moved[g] for g in near + far],
         scratch=[pltpu.VMEM((labels, width), BF16)],
         vmem=12,
         flops=2 * samples * width * labels,
@@ -330,7 +331,8 @@
             nbytes=2_000_000,
         )
         span = row_blocks // 2
-        total = total + swap(upper, "dp", span).astype(F32)
+        grad_enc, enc_done = grad_enc_after(upper)
+        total = total + gate(swap(upper, "dp", span), enc_done).astype(F32)
         while span > 1:
             cut = span // 2 * depth
             total = total[:cut] + swap(total[cut:].astype(BF16), "dp", span // 2).astype(F32)
@@ -339,10 +341,10 @@
         total = own
         for value in received:
             total = total + value.astype(F32)
+        grad_enc, enc_done = grad_enc_after(total)
     total = total.astype(BF16)
-    grad_enc, enc_done = grad_enc_after(total)
     if planes > 1:
-        other = gate(swap(total, "dp", planes // 2), enc_done)
+        other = swap(total, "dp", planes // 2)
         total = (total.astype(F32) + other.astype(F32)).astype(BF16)
     parts = {0: total}
     span = 1

time: 68.8 us -> 75.9 us (1.10)
  local copies, waits for them, and re-layouts: 3.76 us -> 7.3 us
  waiting for transfers between devices: 18.6 us -> 21.4 us
  Pallas kernels: 24.7 us -> 26.4 us
  starting transfers between devices: 19.9 us -> 19.1 us
    unnamed x16 -> x20, local copies, waits for them, and re-layouts: 3.59 us -> 7.04 us
    ppermute x24, waiting for transfers between devices: 18.6 us -> 21.4 us  [swap(): return lax.ppermute(value, axis, [(i, i ^ distance) for i in range(size)])]
    pallas_call x1, Pallas kernels: 2.76 us -> 3.82 us  [shards(): pl.pallas_call(functools.partial(proj_kernel, cuts), out_shape=shape((wid...]
    ppermute x24, starting transfers between devices: 19.9 us -> 19.1 us  [swap(): return lax.ppermute(value, axis, [(i, i ^ distance) for i in range(size)])]
    pallas_call x9, Pallas kernels: 15.8 us -> 16.6 us  [call(): pl.pallas_call(kernel, out_shape=outs, in_specs=[SMEM] * len(scalars) + [...]
  transfers between devices with their start and end apart: 24 -> 24, of which waited for: 10 -> 7; matrix products, arithmetic and copies ran while one was open for 0% -> 1% of each run, Pallas kernels for 29% -> 27%
where the time goes in v7:
time: 75.9 us; the launch traced here: 75.5 us
  Pallas kernels  26.4 us (35%)
  waiting for transfers between devices  21.4 us (28%)
  starting transfers between devices  19.1 us (25%)
  local copies, waits for them, and re-layouts  7.3 us (10%)
  between operations  1.01 us (1%)
    ppermute x24, waiting for transfers between devices, swap(): return lax.ppermute(value, axis, [(i, i ^ distance) for i in range(size)])  21.4 us
    ppermute x24, starting transfers between devices, swap(): return lax.ppermute(value, axis, [(i, i ^ distance) for i in range(size)])  19.1 us
    pallas_call x9, Pallas kernels, call(): pl.pallas_call(kernel, out_shape=outs, in_specs=[SMEM] * len(scalars) + [...  16.6 us
    unnamed x20, local copies, waits for them, and re-layouts  7.04 us
    pallas_call x1, Pallas kernels, shards(): pl.pallas_call(functools.partial(proj_kernel, cuts), out_shape=shape((wid...  3.82 us
    pallas_call x1, Pallas kernels, grad_enc_after(): pl.pallas_call(enc_kernel, grid=(samples // tile,), out_shape=[shape((sam...  3.29 us
    pallas_call x1, Pallas kernels, shards(): pl.pallas_call(payload_kernel, out_shape=shape((size + TAIL, width), BF16...  1.67 us
  transfers between devices with their start and end apart: 24, of which 7 were waited for; matrix products, arithmetic and copies ran while one was open for 1% of the time, Pallas kernels for 27%

profile of v7, /device:TPU:0, one launch (start us, length us, event | category | flops | bytes accessed | tf_op | source)
XLA Modules:
  0.0 75.5 jit_solution(8358912512614347751)
XLA Ops:
  0.6 1.7 %shard_map.94.payload_ref.refs_0_.refs_4_ = bf16[144,768]{1,0:T(8,128)(2,1)} custom-call(s32[1,128]{1,0:T(1,128)} %bitcast.7, s32[1,128]{1,0:T(1,128)} %bitcast.8, bf16[128,768]{1,0:T(8,128)(2,1)} %rows_hbm.1), custom_call_target="tpu_custom_call" | custom-call | tf_op jit(solution)/shard_map/pallas_call | solution.py:224
  2.3 3.0 %collective-permute-start.1 = (bf16[144,768]{1,0:T(8,128)(2,1)}, bf16[144,768]{1,0:T(8,128)(2,1)}, u32[]{:S(2)}, u32[]{:S(2)}) collective-permute-start(bf16[144,768]{1,0:T(8,128)(2,1)} %shard_map.94.payload_ref.refs_0_.refs_4_), channel_id=1, source_target_pairs={{0,2},{1,3},{2,0},{3,1},{4,6},{5,7},{6,4},{7,5},{8,10},{9,11},{10,... | collective-permute-start | bytes 663560 | tf_op jit(solution)/shard_map/ppermute | solution.py:55
  5.3 1.5 %collective-permute-start.2 = (bf16[144,768]{1,0:T(8,128)(2,1)}, bf16[144,768]{1,0:T(8,128)(2,1)S(1)}, u32[]{:S(2)}, u32[]{:S(2)}) collective-permute-start(bf16[144,768]{1,0:T(8,128)(2,1)} %shard_map.94.payload_ref.refs_0_.refs_4_), channel_id=1, source_target_pairs={{0,4},{1,5},{2,6},{3,7},{4,0},{5,1},{6,2},{7,3},{8,12},{9,13},{10,... | collective-permute-start | bytes 663560 | tf_op jit(solution)/shard_map/ppermute | solution.py:55
  8.6 2.6 %shard_map.95 = (bf16[512,1024]{1,0:T(8,128)(2,1)S(1)}, bf16[144,768]{1,0:T(8,128)(2,1)}) custom-call(s32[8,1024]{1,0:T(8,128)S(1)} %bitcast.6, bf16[144,768]{1,0:T(8,128)(2,1)S(1)} %copy-done.6), custom_call_target="tpu_custom_call" | custom-call | bytes 8000000 | tf_op jit(solution)/shard_map/pallas_call | solution.py:31
  13.9 1.5 %shard_map.96.refs_0_.hidden_t_ref = bf16[768,1024]{1,0:T(8,128)(2,1)S(1)} custom-call(bf16[1024,768]{1,0:T(8,128)(2,1)S(1)} %copy-done, bf16[768,768]{1,0:T(8,128)(2,1)S(1)} %copy-done.4, bf16[512,1024]{1,0:T(8,128)(2,1)S(1)} %get-tuple-element.25.after_ref.target_ref), custom_call_target="tpu_custom_call" | custom-call | flops 1207959552 | bytes 6000000 | tf_op jit(solution)/shard_map/pallas_call | solution.py:31
  18.6 2.4 %shard_map.99 = (bf16[256,1024]{1,0:T(8,128)(2,1)S(1)}, f32[128,768]{1,0:T(8,128)S(1)}, bf16[128,768]{1,0:T(8,128)(2,1)S(1)}) custom-call(s32[64]{0:T(128)S(1)} %reshape.27.places_ref, s32[1]{0:T(128)} %bitcast.1.z_ref, bf16[768,1024]{1,0:T(8,128)(2,1)S(1)} %shard_map.96.refs_0_.hidden_t_ref, bf16[512,1024]{1,0:T(8,128)(2,1)S(1)} %copy-done.3, ...), custom_call_target="tpu_custom_call" | custom-call | flops 805306368 | bytes 5000000 | tf_op jit(solution)/shard_map/pallas_call | solution.py:31
  21.0 2.5 %shard_map.100 = (bf16[256,1024]{1,0:T(8,128)(2,1)S(1)}, f32[128,768]{1,0:T(8,128)S(1)}, bf16[128,768]{1,0:T(8,128)(2,1)S(1)}) custom-call(s32[64]{0:T(128)S(1)} %reshape.27.places_ref, s32[1]{0:T(128)} %bitcast.1.z_ref, bf16[768,1024]{1,0:T(8,128)(2,1)S(1)} %shard_map.96.refs_0_.hidden_t_ref, bf16[512,1024]{1,0:T(8,128)(2,1)S(1)} %copy-done.3, ...), custom_call_target="tpu_custom_call" | custom-call | flops 805306368 | bytes 5000000 | tf_op jit(solution)/shard_map/pallas_call | solution.py:31
  24.2 1.9 %shard_map.102 = (bf16[256,1024]{1,0:T(8,128)(2,1)S(1)}, f32[128,768]{1,0:T(8,128)S(1)}, bf16[128,768]{1,0:T(8,128)(2,1)S(1)}) custom-call(s32[64]{0:T(128)S(1)} %reshape.27.places_ref, s32[1]{0:T(128)} %bitcast.1.z_ref, bf16[768,1024]{1,0:T(8,128)(2,1)S(1)} %shard_map.96.refs_0_.hidden_t_ref, bf16[512,1024]{1,0:T(8,128)(2,1)S(1)} %copy-done.3, ...), custom_call_target="tpu_custom_call" | custom-call | flops 805306368 | bytes 5000000 | tf_op jit(solution)/shard_map/pallas_call | solution.py:31
  26.6 1.9 %collective-permute-start.11 = (bf16[128,768]{1,0:T(8,128)(2,1)S(1)}, bf16[128,768]{1,0:T(8,128)(2,1)S(1)}, u32[]{:S(2)}, u32[]{:S(2)}) collective-permute-start(bf16[128,768]{1,0:T(8,128)(2,1)S(1)} %add_convert_fusion.2.refs_3_.refs_12_), channel_id=1, source_target_pairs={{0,2},{1,3},{2,0},{3,1},{4,6},{5,7},{6,4},{7,5},{8,10},{9,11},{10,... | collective-permute-start | bytes 589832 | tf_op jit(solution)/shard_map/ppermute | solution.py:55
  28.5 2.4 %shard_map.103 = (bf16[256,1024]{1,0:T(8,128)(2,1)S(1)}, f32[128,768]{1,0:T(8,128)S(1)}, bf16[128,768]{1,0:T(8,128)(2,1)S(1)}) custom-call(s32[64]{0:T(128)S(1)} %reshape.27.places_ref, s32[1]{0:T(128)} %bitcast.1.z_ref, bf16[768,1024]{1,0:T(8,128)(2,1)S(1)} %shard_map.96.refs_0_.hidden_t_ref, bf16[512,1024]{1,0:T(8,128)(2,1)S(1)} %copy-done.3, ...), custom_call_target="tpu_custom_call" | custom-call | flops 805306368 | bytes 5000000 | tf_op jit(solution)/shard_map/pallas_call | solution.py:31
  31.0 1.6 %collective-permute-start.12 = (bf16[128,768]{1,0:T(8,128)(2,1)S(1)}, bf16[128,768]{1,0:T(8,128)(2,1)S(1)}, u32[]{:S(2)}, u32[]{:S(2)}) collective-permute-start(bf16[128,768]{1,0:T(8,128)(2,1)S(1)} %add_convert_fusion.1.refs_13_), channel_id=1, source_target_pairs={{0,4},{1,5},{2,6},{3,7},{4,0},{5,1},{6,2},{7,3},{8,12},{9,13},{10,... | collective-permute-start | bytes 589832 | tf_op jit(solution)/shard_map/ppermute | solution.py:55
  34.1 3.2 %shard_map.104 = (bf16[1024,768]{1,0:T(8,128)(2,1)S(1)}, bf16[1024,768]{1,0:T(8,128)(2,1)S(1)}) custom-call(s32[1]{0:T(128)} %bitcast.me_ref, bf16[256,1024]{1,0:T(8,128)(2,1)S(1)} %get-tuple-element.26.refs_2_.refs_0_, bf16[256,1024]{1,0:T(8,128)(2,1)S(1)} %get-tuple-element.27.refs_0_.refs_2_.refs_1_, bf16[256,1024]{1,0:T(8,128)(2,1)S(1)} %get-tuple-element.29.refs_2_, ...), custom_call_target="tpu_custom_call" | custom-call | flops 1610612736 | bytes 5000000 | tf_op jit(solution)/shard_map/pallas_call | solution.py:31
  37.3 5.3 %collective-permute-done.12.refs_1_ = bf16[128,768]{1,0:T(8,128)(2,1)S(1)} collective-permute-done((bf16[128,768]{1,0:T(8,128)(2,1)S(1)}, bf16[128,768]{1,0:T(8,128)(2,1)S(1)}, u32[]{:S(2)}, u32[]{:S(2)}) %collective-permute-start.12) | collective-permute-done | bytes 196640 | tf_op jit(solution)/shard_map/ppermute | solution.py:55
  42.7 1.7 %collective-permute-start.14 = (bf16[64,768]{1,0:T(8,128)(2,1)S(1)}, bf16[64,768]{1,0:T(8,128)(2,1)S(1)}, u32[]{:S(2)}, u32[]{:S(2)}) collective-permute-start(bf16[64,768]{1,0:T(8,128)(2,1)S(1)} %get-tuple-element.40.after_ref), channel_id=1, source_target_pairs={{0,8},{8,0},{16,24},{24,16},{1,9},{9,1},{17,25},{25,17},{2,10},{10... | collective-permute-start | bytes 294920 | tf_op jit(solution)/shard_map/ppermute | solution.py:55
  44.4 3.3 %shard_map.106 = (f32[1024,768]{1,0:T(8,128)}, f32[8,128]{1,0:T(8,128)S(1)}) custom-call(bf16[1024,768]{1,0:T(8,128)(2,1)S(1)} %get-tuple-element.37.refs_3_.grad_hidden_ref, bf16[768,768]{1,0:T(8,128)(2,1)S(1)} %copy-done.5, bf16[64,768]{1,0:T(8,128)(2,1)S(1)} %get-tuple-element.40.after_ref), custom_call_target="tpu_custom_call" | custom-call | flops 1207959552 | bytes 6000000 | tf_op jit(solution)/shard_map/pallas_call | solution.py:305
  47.7 2.6 %collective-permute-start.15 = (bf16[64,768]{1,0:T(8,128)(2,1)S(1)}, bf16[64,768]{1,0:T(8,128)(2,1)S(1)}, u32[]{:S(2)}, u32[]{:S(2)}) collective-permute-start(bf16[64,768]{1,0:T(8,128)(2,1)S(1)} %add_convert_fusion.4), channel_id=1, source_target_pairs={{0,16},{8,24},{16,0},{24,8},{1,17},{9,25},{17,1},{25,9},{2,18},{10... | collective-permute-start | bytes 294920 | tf_op jit(solution)/shard_map/ppermute | solution.py:55
  50.3 4.5 %collective-permute-done.15 = bf16[64,768]{1,0:T(8,128)(2,1)S(1)} collective-permute-done((bf16[64,768]{1,0:T(8,128)(2,1)S(1)}, bf16[64,768]{1,0:T(8,128)(2,1)S(1)}, u32[]{:S(2)}, u32[]{:S(2)}) %collective-permute-start.15) | collective-permute-done | bytes 98336 | tf_op jit(solution)/shard_map/ppermute | solution.py:55
  54.9 4.6 %collective-permute-done.16.refs_1_ = bf16[64,768]{1,0:T(8,128)(2,1)S(1)} collective-permute-done((bf16[64,768]{1,0:T(8,128)(2,1)S(1)}, bf16[64,768]{1,0:T(8,128)(2,1)S(1)}, u32[]{:S(2)}, u32[]{:S(2)}) %collective-permute-start.16) | collective-permute-done | bytes 98336 | tf_op jit(solution)/shard_map/ppermute | solution.py:55
  60.3 1.5 %collective-permute-start.20 = (bf16[768,128]{1,0:T(8,128)(2,1)S(1)}, bf16[768,128]{1,0:T(8,128)(2,1)}, u32[]{:S(2)}, u32[]{:S(2)}) collective-permute-start(bf16[768,128]{1,0:T(8,128)(2,1)S(1)} %shard_map.108.whole_ref.refs_0_), channel_id=1, source_target_pairs={{0,4},{1,5},{2,6},{3,7},{4,0},{5,1},{6,2},{7,3},{8,12},{9,13},{10,... | collective-permute-start | bytes 589832 | tf_op jit(solution)/shard_map/ppermute | solution.py:55
  61.8 1.4 %collective-permute-start.22 = (bf16[768,128]{1,0:T(8,128)(2,1)S(1)}, bf16[768,128]{1,0:T(8,128)(2,1)S(1)}, u32[]{:S(2)}, u32[]{:S(2)}) collective-permute-start(bf16[768,128]{1,0:T(8,128)(2,1)S(1)} %shard_map.108.whole_ref.refs_0_), channel_id=1, source_target_pairs={{0,6},{1,7},{2,4},{3,5},{4,2},{5,3},{6,0},{7,1},{8,14},{9,15},{10,... | collective-permute-start | bytes 589832 | tf_op jit(solution)/shard_map/ppermute | solution.py:55
  64.5 2.6 %collective-permute-done.18.value_ref = bf16[768,128]{1,0:T(8,128)(2,1)} collective-permute-done((bf16[768,128]{1,0:T(8,128)(2,1)S(1)}, bf16[768,128]{1,0:T(8,128)(2,1)}, u32[]{:S(2)}, u32[]{:S(2)}) %collective-permute-start.18) | collective-permute-done | bytes 196640 | tf_op jit(solution)/shard_map/ppermute | solution.py:55
  68.4 1.6 %collective-permute-done.22.value_ref = bf16[768,128]{1,0:T(8,128)(2,1)S(1)} collective-permute-done((bf16[768,128]{1,0:T(8,128)(2,1)S(1)}, bf16[768,128]{1,0:T(8,128)(2,1)S(1)}, u32[]{:S(2)}, u32[]{:S(2)}) %collective-permute-start.22) | collective-permute-done | bytes 196640 | tf_op jit(solution)/shard_map/ppermute | solution.py:55
  70.1 1.4 %collective-permute-done.23.refs_7_ = bf16[768,128]{1,0:T(8,128)(2,1)S(1)} collective-permute-done((bf16[768,128]{1,0:T(8,128)(2,1)S(1)}, bf16[768,128]{1,0:T(8,128)(2,1)S(1)}, u32[]{:S(2)}, u32[]{:S(2)}) %collective-permute-start.23) | collective-permute-done | bytes 196640 | tf_op jit(solution)/shard_map/ppermute | solution.py:55
  71.5 3.8 %shard_map.113 = f32[768,768]{1,0:T(8,128)} custom-call(s32[1]{0:T(128)} %bitcast.me_ref, bf16[768,128]{1,0:T(8,128)(2,1)S(1)} %shard_map.108.whole_ref.refs_0_, bf16[768,128]{1,0:T(8,128)(2,1)S(1)} %collective-permute-done.17.refs_1_, bf16[768,128]{1,0:T(8,128)(2,1)} %shard_map.110.refs_2_, bf16[768,128]{1,0:T(8,128)(2,1)S(1)} %collective-permute-done.19.refs_3_, ...), custom_call_target="tpu_custom_call" | custom-call | flops 1207959552 | bytes 6000000 | tf_op jit(solution)/shard_map/pallas_call | solution.py:381
  (74 shorter events, 14.0 us)
Async XLA Ops:
  2.3 14.1 %collective-permute-start.1 = (bf16[144,768]{1,0:T(8,128)(2,1)}, bf16[144,768]{1,0:T(8,128)(2,1)}, u32[]{:S(2)}, u32[]{:S(2)}) collective-permute-start(bf16[144,768]{1,0:T(8,128)(2,1)} %shard_map.94.payload_ref.refs_0_.refs_4_), channel_id=1, source_target_pairs={{0,2},{1,3},{2,0},{3,1},{4,6},{5,7},{6,4},{7,5},{8,10},{9,11},{10,... | collective-permute-start | bytes 663560 | tf_op jit(solution)/shard_map/ppermute | solution.py:55
  5.3 12.1 %collective-permute-start = (bf16[144,768]{1,0:T(8,128)(2,1)}, bf16[144,768]{1,0:T(8,128)(2,1)}, u32[]{:S(2)}, u32[]{:S(2)}) collective-permute-start(bf16[144,768]{1,0:T(8,128)(2,1)} %shard_map.94.payload_ref.refs_0_.refs_4_), channel_id=1, source_target_pairs={{0,1},{1,0},{2,3},{3,2},{4,5},{5,4},{6,7},{7,6},{8,9},{9,8},{10,11... | collective-permute-start | bytes 663560 | tf_op jit(solution)/shard_map/ppermute | solution.py:55
  5.3 11.9 %collective-permute-start.2 = (bf16[144,768]{1,0:T(8,128)(2,1)}, bf16[144,768]{1,0:T(8,128)(2,1)S(1)}, u32[]{:S(2)}, u32[]{:S(2)}) collective-permute-start(bf16[144,768]{1,0:T(8,128)(2,1)} %shard_map.94.payload_ref.refs_0_.refs_4_), channel_id=1, source_target_pairs={{0,4},{1,5},{2,6},{3,7},{4,0},{5,1},{6,2},{7,3},{8,12},{9,13},{10,... | collective-permute-start | bytes 663560 | tf_op jit(solution)/shard_map/ppermute | solution.py:55
  11.1 12.9 %collective-permute-start.5 = (bf16[144,768]{1,0:T(8,128)(2,1)}, bf16[144,768]{1,0:T(8,128)(2,1)}, u32[]{:S(2)}, u32[]{:S(2)}) collective-permute-start(bf16[144,768]{1,0:T(8,128)(2,1)} %get-tuple-element.28), channel_id=1, source_target_pairs={{0,6},{1,7},{2,4},{3,5},{4,2},{5,3},{6,0},{7,1},{8,14},{9,15},{10,... | collective-permute-start | bytes 663560 | tf_op jit(solution)/shard_map/ppermute | solution.py:55
  16.4 4.6 %collective-permute-start.3 = (bf16[144,768]{1,0:T(8,128)(2,1)}, bf16[144,768]{1,0:T(8,128)(2,1)}, u32[]{:S(2)}, u32[]{:S(2)}) collective-permute-start(bf16[144,768]{1,0:T(8,128)(2,1)} %shard_map.97.refs_2_.refs_0_.refs_6_), channel_id=1, source_target_pairs={{0,1},{1,0},{2,3},{3,2},{4,5},{5,4},{6,7},{7,6},{8,9},{9,8},{10,11... | collective-permute-start | bytes 663560 | tf_op jit(solution)/shard_map/ppermute | solution.py:55
  17.3 6.9 %collective-permute-start.4 = (bf16[144,768]{1,0:T(8,128)(2,1)S(1)}, bf16[144,768]{1,0:T(8,128)(2,1)S(1)}, u32[]{:S(2)}, u32[]{:S(2)}) collective-permute-start(bf16[144,768]{1,0:T(8,128)(2,1)S(1)} %shard_map.98.refs_3_.refs_0_.refs_8_), channel_id=1, source_target_pairs={{0,1},{1,0},{2,3},{3,2},{4,5},{5,4},{6,7},{7,6},{8,9},{9,8},{10,11... | collective-permute-start | bytes 663560 | tf_op jit(solution)/shard_map/ppermute | solution.py:55
  23.5 3.1 %collective-permute-start.7 = (bf16[128,768]{1,0:T(8,128)(2,1)S(1)}, bf16[128,768]{1,0:T(8,128)(2,1)S(1)}, u32[]{:S(2)}, u32[]{:S(2)}) collective-permute-start(bf16[128,768]{1,0:T(8,128)(2,1)S(1)} %get-tuple-element.31), channel_id=1, source_target_pairs={{0,1},{1,0},{2,3},{3,2},{4,5},{5,4},{6,7},{7,6},{8,9},{9,8},{10,11... | collective-permute-start | bytes 589832 | tf_op jit(solution)/shard_map/ppermute | solution.py:55
  23.6 10.4 %collective-permute-start.10 = (bf16[128,768]{1,0:T(8,128)(2,1)S(1)}, bf16[128,768]{1,0:T(8,128)(2,1)S(1)}, u32[]{:S(2)}, u32[]{:S(2)}) collective-permute-start(bf16[128,768]{1,0:T(8,128)(2,1)S(1)} %get-tuple-element.39), channel_id=1, source_target_pairs={{0,1},{1,0},{2,3},{3,2},{4,5},{5,4},{6,7},{7,6},{8,9},{9,8},{10,11... | collective-permute-start | bytes 589832 | tf_op jit(solution)/shard_map/ppermute | solution.py:55
  24.0 4.5 %collective-permute-start.6 = (bf16[144,768]{1,0:T(8,128)(2,1)}, bf16[144,768]{1,0:T(8,128)(2,1)S(1)}, u32[]{:S(2)}, u32[]{:S(2)}) collective-permute-start(bf16[144,768]{1,0:T(8,128)(2,1)} %shard_map.101.refs_3_.refs_0_.refs_10_), channel_id=1, source_target_pairs={{0,1},{1,0},{2,3},{3,2},{4,5},{5,4},{6,7},{7,6},{8,9},{9,8},{10,11... | collective-permute-start | bytes 663560 | tf_op jit(solution)/shard_map/ppermute | solution.py:55
  26.1 4.9 %collective-permute-start.8 = (bf16[128,768]{1,0:T(8,128)(2,1)S(1)}, bf16[128,768]{1,0:T(8,128)(2,1)S(1)}, u32[]{:S(2)}, u32[]{:S(2)}) collective-permute-start(bf16[128,768]{1,0:T(8,128)(2,1)S(1)} %get-tuple-element.34), channel_id=1, source_target_pairs={{0,1},{1,0},{2,3},{3,2},{4,5},{5,4},{6,7},{7,6},{8,9},{9,8},{10,11... | collective-permute-start | bytes 589832 | tf_op jit(solution)/shard_map/ppermute | solution.py:55
  26.6 10.7 %collective-permute-start.11 = (bf16[128,768]{1,0:T(8,128)(2,1)S(1)}, bf16[128,768]{1,0:T(8,128)(2,1)S(1)}, u32[]{:S(2)}, u32[]{:S(2)}) collective-permute-start(bf16[128,768]{1,0:T(8,128)(2,1)S(1)} %add_convert_fusion.2.refs_3_.refs_12_), channel_id=1, source_target_pairs={{0,2},{1,3},{2,0},{3,1},{4,6},{5,7},{6,4},{7,5},{8,10},{9,11},{10,... | collective-permute-start | bytes 589832 | tf_op jit(solution)/shard_map/ppermute | solution.py:55
  30.9 1.7 %collective-permute-start.9 = (bf16[128,768]{1,0:T(8,128)(2,1)S(1)}, bf16[128,768]{1,0:T(8,128)(2,1)S(1)}, u32[]{:S(2)}, u32[]{:S(2)}) collective-permute-start(bf16[128,768]{1,0:T(8,128)(2,1)S(1)} %get-tuple-element.36), channel_id=1, source_target_pairs={{0,1},{1,0},{2,3},{3,2},{4,5},{5,4},{6,7},{7,6},{8,9},{9,8},{10,11... | collective-permute-start | bytes 589832 | tf_op jit(solution)/shard_map/ppermute | solution.py:55
  31.0 11.6 %collective-permute-start.12 = (bf16[128,768]{1,0:T(8,128)(2,1)S(1)}, bf16[128,768]{1,0:T(8,128)(2,1)S(1)}, u32[]{:S(2)}, u32[]{:S(2)}) collective-permute-start(bf16[128,768]{1,0:T(8,128)(2,1)S(1)} %add_convert_fusion.1.refs_13_), channel_id=1, source_target_pairs={{0,4},{1,5},{2,6},{3,7},{4,0},{5,1},{6,2},{7,3},{8,12},{9,13},{10,... | collective-permute-start | bytes 589832 | tf_op jit(solution)/shard_map/ppermute | solution.py:55
  32.7 9.9 %collective-permute-start.13 = (bf16[128,768]{1,0:T(8,128)(2,1)S(1)}, bf16[128,768]{1,0:T(8,128)(2,1)S(1)}, u32[]{:S(2)}, u32[]{:S(2)}) collective-permute-start(bf16[128,768]{1,0:T(8,128)(2,1)S(1)} %add_convert_fusion.refs_14_), channel_id=1, source_target_pairs={{0,6},{1,7},{2,4},{3,5},{4,2},{5,3},{6,0},{7,1},{8,14},{9,15},{10,... | collective-permute-start | bytes 589832 | tf_op jit(solution)/shard_map/ppermute | solution.py:55
  42.7 5.0 %collective-permute-start.14 = (bf16[64,768]{1,0:T(8,128)(2,1)S(1)}, bf16[64,768]{1,0:T(8,128)(2,1)S(1)}, u32[]{:S(2)}, u32[]{:S(2)}) collective-permute-start(bf16[64,768]{1,0:T(8,128)(2,1)S(1)} %get-tuple-element.40.after_ref), channel_id=1, source_target_pairs={{0,8},{8,0},{16,24},{24,16},{1,9},{9,1},{17,25},{25,17},{2,10},{10... | collective-permute-start | bytes 294920 | tf_op jit(solution)/shard_map/ppermute | solution.py:55
  47.7 7.1 %collective-permute-start.15 = (bf16[64,768]{1,0:T(8,128)(2,1)S(1)}, bf16[64,768]{1,0:T(8,128)(2,1)S(1)}, u32[]{:S(2)}, u32[]{:S(2)}) collective-permute-start(bf16[64,768]{1,0:T(8,128)(2,1)S(1)} %add_convert_fusion.4), channel_id=1, source_target_pairs={{0,16},{8,24},{16,0},{24,8},{1,17},{9,25},{17,1},{25,9},{2,18},{10... | collective-permute-start | bytes 294920 | tf_op jit(solution)/shard_map/ppermute | solution.py:55
  54.9 4.7 %collective-permute-start.16 = (bf16[64,768]{1,0:T(8,128)(2,1)S(1)}, bf16[64,768]{1,0:T(8,128)(2,1)S(1)}, u32[]{:S(2)}, u32[]{:S(2)}) collective-permute-start(bf16[64,768]{1,0:T(8,128)(2,1)S(1)} %add_convert_fusion.3.refs_0_), channel_id=1, source_target_pairs={{0,8},{8,0},{16,24},{24,16},{1,9},{9,1},{17,25},{25,17},{2,10},{10... | collective-permute-start | bytes 294920 | tf_op jit(solution)/shard_map/ppermute | solution.py:55
  59.7 7.4 %collective-permute-start.18 = (bf16[768,128]{1,0:T(8,128)(2,1)S(1)}, bf16[768,128]{1,0:T(8,128)(2,1)}, u32[]{:S(2)}, u32[]{:S(2)}) collective-permute-start(bf16[768,128]{1,0:T(8,128)(2,1)S(1)} %shard_map.108.whole_ref.refs_0_), channel_id=1, source_target_pairs={{0,2},{1,3},{2,0},{3,1},{4,6},{5,7},{6,4},{7,5},{8,10},{9,11},{10,... | collective-permute-start | bytes 589832 | tf_op jit(solution)/shard_map/ppermute | solution.py:55
  60.3 8.2 %collective-permute-start.20 = (bf16[768,128]{1,0:T(8,128)(2,1)S(1)}, bf16[768,128]{1,0:T(8,128)(2,1)}, u32[]{:S(2)}, u32[]{:S(2)}) collective-permute-start(bf16[768,128]{1,0:T(8,128)(2,1)S(1)} %shard_map.108.whole_ref.refs_0_), channel_id=1, source_target_pairs={{0,4},{1,5},{2,6},{3,7},{4,0},{5,1},{6,2},{7,3},{8,12},{9,13},{10,... | collective-permute-start | bytes 589832 | tf_op jit(solution)/shard_map/ppermute | solution.py:55
  61.8 8.3 %collective-permute-start.22 = (bf16[768,128]{1,0:T(8,128)(2,1)S(1)}, bf16[768,128]{1,0:T(8,128)(2,1)S(1)}, u32[]{:S(2)}, u32[]{:S(2)}) collective-permute-start(bf16[768,128]{1,0:T(8,128)(2,1)S(1)} %shard_map.108.whole_ref.refs_0_), channel_id=1, source_target_pairs={{0,6},{1,7},{2,4},{3,5},{4,2},{5,3},{6,0},{7,1},{8,14},{9,15},{10,... | collective-permute-start | bytes 589832 | tf_op jit(solution)/shard_map/ppermute | solution.py:55
  63.4 6.6 %collective-permute-start.17 = (bf16[768,128]{1,0:T(8,128)(2,1)S(1)}, bf16[768,128]{1,0:T(8,128)(2,1)S(1)}, u32[]{:S(2)}, u32[]{:S(2)}) collective-permute-start(bf16[768,128]{1,0:T(8,128)(2,1)S(1)} %shard_map.108.whole_ref.refs_0_), channel_id=1, source_target_pairs={{0,1},{1,0},{2,3},{3,2},{4,5},{5,4},{6,7},{7,6},{8,9},{9,8},{10,11... | collective-permute-start | bytes 589832 | tf_op jit(solution)/shard_map/ppermute | solution.py:55
  67.1 3.0 %collective-permute-start.19 = (bf16[768,128]{1,0:T(8,128)(2,1)}, bf16[768,128]{1,0:T(8,128)(2,1)S(1)}, u32[]{:S(2)}, u32[]{:S(2)}) collective-permute-start(bf16[768,128]{1,0:T(8,128)(2,1)} %shard_map.110.refs_2_), channel_id=1, source_target_pairs={{0,1},{1,0},{2,3},{3,2},{4,5},{5,4},{6,7},{7,6},{8,9},{9,8},{10,11... | collective-permute-start | bytes 589832 | tf_op jit(solution)/shard_map/ppermute | solution.py:55
  68.4 1.7 %collective-permute-start.21 = (bf16[768,128]{1,0:T(8,128)(2,1)}, bf16[768,128]{1,0:T(8,128)(2,1)S(1)}, u32[]{:S(2)}, u32[]{:S(2)}) collective-permute-start(bf16[768,128]{1,0:T(8,128)(2,1)} %shard_map.111.refs_4_), channel_id=1, source_target_pairs={{0,1},{1,0},{2,3},{3,2},{4,5},{5,4},{6,7},{7,6},{8,9},{9,8},{10,11... | collective-permute-start | bytes 589832 | tf_op jit(solution)/shard_map/ppermute | solution.py:55
  70.0 1.4 %collective-permute-start.23 = (bf16[768,128]{1,0:T(8,128)(2,1)S(1)}, bf16[768,128]{1,0:T(8,128)(2,1)S(1)}, u32[]{:S(2)}, u32[]{:S(2)}) collective-permute-start(bf16[768,128]{1,0:T(8,128)(2,1)S(1)} %shard_map.112.refs_6_), channel_id=1, source_target_pairs={{0,1},{1,0},{2,3},{3,2},{4,5},{5,4},{6,7},{7,6},{8,9},{9,8},{10,11... | collective-permute-start | bytes 589832 | tf_op jit(solution)/shard_map/ppermute | solution.py:55
  (10 other events, 17.3 us)

commit v8 on v7

--- a/solution.py
+++ b/solution.py
@@ -73,8 +73,7 @@
     copies[2].wait()
 
 
-def target_kernel(beam, block, wanted_ref, payload_ref, target_ref, copy_ref):
-    copy_ref[...] = payload_ref[...]
+def target_kernel(beam, block, wanted_ref, target_ref):
     samples = wanted_ref.shape[1]
     size = target_ref.shape[0] // beam
     label_iota = lax.broadcasted_iota(jnp.int32, (size, block), 0)
@@ -103,12 +102,11 @@
     return guess * (2.0 - bottom * guess)
 
 
-def score_kernel(group, block, count, places_ref, z_ref, hidden_t_ref, target_ref, enc_ref, *refs):
+def score_kernel(group, block, count, list_ref, me_ref, z_ref, hidden_t_ref, target_ref, enc_ref, *refs):
     payloads, refs = refs[:2], refs[-6:]
     grads_ref, kept_ref, sent_ref, weights_ref, scale_ref, logits_ref = refs
     samples = enc_ref.shape[0]
     size = payloads[0].shape[0] - TAIL
-    blocks = samples // block
     for core in range(2):
         rows = pl.ds(core * size, size)
         weights_ref[rows, :] = payloads[core][:size, :]
@@ -122,7 +120,10 @@
         )
         for low in range(start, start + tile, block):
             for core in range(2):
-                place = places_ref[(2 * group + core) * blocks + low // block]
+                cluster = me_ref[0] ^ (2 * group + core)
+                place = jnp.int32(-1)
+                for beam_slot in range(list_ref.shape[0]):
+                    place = jnp.where(list_ref[beam_slot, low // block] == cluster, beam_slot, place)
                 factor = jnp.where(place >= 0, 1.0 / block, 0.0)
                 first = pl.multiple_of(jnp.maximum(place, 0) * size, size)
                 rows = slice(core * size, (core + 1) * size)
@@ -221,6 +222,8 @@
     labels = owners * size
     depth = size // row_blocks
     me_s, z_s = me.reshape(1), z_low.reshape(1)
+    listed = shortlist.astype(jnp.int32).T
+
     payload = pl.pallas_call(
         payload_kernel,
         out_shape=shape((size + TAIL, width), BF16),
@@ -230,14 +233,14 @@
         compiler_params=pltpu.CompilerParams(vmem_limit_bytes=56 * MIB),
     )(weight_num.reshape(1, size), weight_den.reshape(1, size), head_weight)
     got = {0: payload}
-    for g in near:
+    for g in near + far:
         got[2 * g] = swap(payload, "label", 2 * g)
     got[1] = swap(payload, "label", 1)
-    target, late = call(
+    (target,) = call(
         functools.partial(target_kernel, beam, block),
-        [shape((beam * size, samples), BF16), shape(payload.shape, BF16)],
-        [positives.T, payload],
-        vmem=4,
+        [shape((beam * size, samples), BF16)],
+        [positives.T],
+        vmem=2,
         nbytes=8_000_000,
     )
     (hidden_t,) = call(
@@ -248,14 +251,9 @@
         flops=2 * samples * width * width,
         nbytes=6_000_000,
     )
-    for g in far:
-        got[2 * g] = swap(late, "label", 2 * g)
     for g in near:
         got[2 * g] = gate(got[2 * g], hidden_t)
         got[2 * g + 1] = swap(got[2 * g], "label", 1)
-    clusters = me ^ jnp.arange(owners, dtype=jnp.int32)
-    listing = shortlist.astype(jnp.int32)[None, :, :] == clusters[:, None, None]
-    places = jnp.max(jnp.where(listing, jnp.arange(beam, dtype=jnp.int32), -1), axis=2).reshape(-1)
     grads, kept, from_core, moved, received = {}, {}, {}, {}, {}
     order = [0] + near + far
     for at, g in enumerate(order):
@@ -268,7 +266,7 @@
             functools.partial(score_kernel, g, block, row_blocks),
             [shape((2 * size, samples), BF16), shape((size, width), F32), shape((size, width), BF16)],
             [hidden_t, target, enc, got[2 * g], got[2 * g + 1]],
-            scalars=[places, z_s],
+            scalars=[listed, me_s, z_s],
             after=after,
             scratch=[
                 pltpu.VMEM((2 * size, width), BF16),
@@ -331,8 +329,7 @@
             nbytes=2_000_000,
         )
         span = row_blocks // 2
-        grad_enc, enc_done = grad_enc_after(upper)
-        total = total + gate(swap(upper, "dp", span), enc_done).astype(F32)
+        total = total + swap(upper, "dp", span).astype(F32)
         while span > 1:
             cut = span // 2 * depth
             total = total[:cut] + swap(total[cut:].astype(BF16), "dp", span // 2).astype(F32)
@@ -341,10 +338,10 @@
         total = own
         for value in received:
             total = total + value.astype(F32)
-        grad_enc, enc_done = grad_enc_after(total)
     total = total.astype(BF16)
+    grad_enc, enc_done = grad_enc_after(total)
     if planes > 1:
-        other = swap(total, "dp", planes // 2)
+        other = gate(swap(total, "dp", planes // 2), enc_done)
         total = (total.astype(F32) + other.astype(F32)).astype(BF16)
     parts = {0: total}
     span = 1

time: 75.9 us -> 68.9 us (0.908)
  local copies, waits for them, and re-layouts: 7.3 us -> 3.36 us
  waiting for transfers between devices: 21.4 us -> 18.1 us
  starting transfers between devices: 19.1 us -> 21 us
  Pallas kernels: 26.4 us -> 24.8 us
    unnamed x20 -> x16, local copies, waits for them, and re-layouts: 7.04 us -> 3.19 us
    ppermute x24, waiting for transfers between devices: 21.4 us -> 18.1 us  [swap(): return lax.ppermute(value, axis, [(i, i ^ distance) for i in range(size)])]
    ppermute x24, starting transfers between devices: 19.1 us -> 21 us  [swap(): return lax.ppermute(value, axis, [(i, i ^ distance) for i in range(size)])]
    pallas_call x1, Pallas kernels: 3.82 us -> 2.76 us  [shards(): pl.pallas_call(functools.partial(proj_kernel, cuts), out_shape=shape((wid...]
  transfers between devices with their start and end apart: 24 -> 24, of which waited for: 7 -> 8; matrix products, arithmetic and copies ran while one was open for 1% -> 0% of each run, Pallas kernels for 27% -> 29%
where the time goes in v8:
time: 68.9 us; the launch traced here: 68.5 us
  Pallas kernels  24.8 us (36%)
  starting transfers between devices  21 us (30%)
  waiting for transfers between devices  18.1 us (26%)
  local copies, waits for them, and re-layouts  3.36 us (5%)
  between operations  1.04 us (2%)
    ppermute x24, starting transfers between devices, swap(): return lax.ppermute(value, axis, [(i, i ^ distance) for i in range(size)])  21 us
    ppermute x24, waiting for transfers between devices, swap(): return lax.ppermute(value, axis, [(i, i ^ distance) for i in range(size)])  18.1 us
    pallas_call x9, Pallas kernels, call(): pl.pallas_call(kernel, out_shape=outs, in_specs=[SMEM] * len(scalars) + [...  15.9 us
    pallas_call x1, Pallas kernels, grad_enc_after(): pl.pallas_call(enc_kernel, grid=(samples // tile,), out_shape=[shape((sam...  3.29 us
    unnamed x16, local copies, waits for them, and re-layouts  3.19 us
    pallas_call x1, Pallas kernels, shards(): pl.pallas_call(functools.partial(proj_kernel, cuts), out_shape=shape((wid...  2.76 us
    pallas_call x1, Pallas kernels, shards(): pl.pallas_call(payload_kernel, out_shape=shape((size + TAIL, width), BF16...  1.76 us
  transfers between devices with their start and end apart: 24, of which 8 were waited for; matrix products, arithmetic and copies ran while one was open for 0% of the time, Pallas kernels for 29%

profile of v8, /device:TPU:0, one launch (start us, length us, event | category | flops | bytes accessed | tf_op | source)
XLA Modules:
  0.0 68.5 jit_solution(3904784879635128367)
XLA Ops:
  0.6 1.8 %shard_map.96.refs_0_.refs_4_ = bf16[144,768]{1,0:T(8,128)(2,1)} custom-call(s32[1,128]{1,0:T(1,128)} %bitcast.12, s32[1,128]{1,0:T(1,128)} %bitcast.13, bf16[128,768]{1,0:T(8,128)(2,1)} %rows_hbm.1), custom_call_target="tpu_custom_call" | custom-call | tf_op jit(solution)/shard_map/pallas_call | solution.py:227
  2.4 3.0 %collective-permute-start.1 = (bf16[144,768]{1,0:T(8,128)(2,1)}, bf16[144,768]{1,0:T(8,128)(2,1)}, u32[]{:S(2)}, u32[]{:S(2)}) collective-permute-start(bf16[144,768]{1,0:T(8,128)(2,1)} %shard_map.96.refs_0_.refs_4_), channel_id=1, source_target_pairs={{0,2},{1,3},{2,0},{3,1},{4,6},{5,7},{6,4},{7,5},{8,10},{9,11},{10,... | collective-permute-start | bytes 663560 | tf_op jit(solution)/shard_map/ppermute | solution.py:55
  5.4 1.5 %collective-permute-start.2 = (bf16[144,768]{1,0:T(8,128)(2,1)}, bf16[144,768]{1,0:T(8,128)(2,1)S(1)}, u32[]{:S(2)}, u32[]{:S(2)}) collective-permute-start(bf16[144,768]{1,0:T(8,128)(2,1)} %shard_map.96.refs_0_.refs_4_), channel_id=1, source_target_pairs={{0,4},{1,5},{2,6},{3,7},{4,0},{5,1},{6,2},{7,3},{8,12},{9,13},{10,... | collective-permute-start | bytes 663560 | tf_op jit(solution)/shard_map/ppermute | solution.py:55
  7.7 1.9 %shard_map.94.after_ref.target_ref = bf16[512,1024]{1,0:T(8,128)(2,1)S(1)} custom-call(s32[8,1024]{1,0:T(8,128)S(1)} %bitcast.11), custom_call_target="tpu_custom_call" | custom-call | bytes 8000000 | tf_op jit(solution)/shard_map/pallas_call | solution.py:31
  9.6 1.4 %copy-done = bf16[1024,768]{1,0:T(8,128)(2,1)S(1)} copy-done((bf16[1024,768]{1,0:T(8,128)(2,1)S(1)}, bf16[1024,768]{1,0:T(8,128)(2,1)}, u32[]{:S(2)}) %copy-start) | copy-done | bytes 1572888
  11.0 1.5 %shard_map.95.refs_0_.hidden_t_ref = bf16[768,1024]{1,0:T(8,128)(2,1)S(1)} custom-call(bf16[1024,768]{1,0:T(8,128)(2,1)S(1)} %copy-done, bf16[768,768]{1,0:T(8,128)(2,1)S(1)} %copy-done.4, bf16[512,1024]{1,0:T(8,128)(2,1)S(1)} %shard_map.94.after_ref.target_ref), custom_call_target="tpu_custom_call" | custom-call | flops 1207959552 | bytes 6000000 | tf_op jit(solution)/shard_map/pallas_call | solution.py:31
  15.1 2.4 %shard_map.99 = (bf16[256,1024]{1,0:T(8,128)(2,1)S(1)}, f32[128,768]{1,0:T(8,128)S(1)}, bf16[128,768]{1,0:T(8,128)(2,1)S(1)}) custom-call(s32[4,8]{1,0:T(4,128)S(1)} %bitcast.7, s32[1]{0:T(128)} %bitcast.me_ref, s32[1]{0:T(128)} %bitcast.2.z_ref, bf16[768,1024]{1,0:T(8,128)(2,1)S(1)} %shard_map.95.refs_0_.hidden_t_ref, bf16[512,1024]{1,0:T(8,128)(2,1)S(1)} %copy-done.3, ...), custom_call_target="tpu_custom_call" | custom-call | flops 805306368 | bytes 5000000 | tf_op jit(solution)/shard_map/pallas_call | solution.py:31
  17.5 2.4 %shard_map.100 = (bf16[256,1024]{1,0:T(8,128)(2,1)S(1)}, f32[128,768]{1,0:T(8,128)S(1)}, bf16[128,768]{1,0:T(8,128)(2,1)S(1)}) custom-call(s32[4,8]{1,0:T(4,128)S(1)} %bitcast.8, s32[1]{0:T(128)} %bitcast.me_ref, s32[1]{0:T(128)} %bitcast.2.z_ref, bf16[768,1024]{1,0:T(8,128)(2,1)S(1)} %shard_map.95.refs_0_.hidden_t_ref, bf16[512,1024]{1,0:T(8,128)(2,1)S(1)} %copy-done.3, ...), custom_call_target="tpu_custom_call" | custom-call | flops 805306368 | bytes 5000000 | tf_op jit(solution)/shard_map/pallas_call | solution.py:31
  21.7 1.9 %shard_map.102 = (bf16[256,1024]{1,0:T(8,128)(2,1)S(1)}, f32[128,768]{1,0:T(8,128)S(1)}, bf16[128,768]{1,0:T(8,128)(2,1)S(1)}) custom-call(s32[4,8]{1,0:T(4,128)S(1)} %bitcast.9, s32[1]{0:T(128)} %bitcast.me_ref, s32[1]{0:T(128)} %bitcast.2.z_ref, bf16[768,1024]{1,0:T(8,128)(2,1)S(1)} %shard_map.95.refs_0_.hidden_t_ref, bf16[512,1024]{1,0:T(8,128)(2,1)S(1)} %copy-done.3, ...), custom_call_target="tpu_custom_call" | custom-call | flops 805306368 | bytes 5000000 | tf_op jit(solution)/shard_map/pallas_call | solution.py:31
  24.9 2.3 %shard_map.103 = (bf16[256,1024]{1,0:T(8,128)(2,1)S(1)}, f32[128,768]{1,0:T(8,128)S(1)}, bf16[128,768]{1,0:T(8,128)(2,1)S(1)}) custom-call(s32[4,8]{1,0:T(4,128)S(1)} %bitcast.10, s32[1]{0:T(128)} %bitcast.me_ref, s32[1]{0:T(128)} %bitcast.2.z_ref, bf16[768,1024]{1,0:T(8,128)(2,1)S(1)} %shard_map.95.refs_0_.hidden_t_ref, bf16[512,1024]{1,0:T(8,128)(2,1)S(1)} %copy-done.3, ...), custom_call_target="tpu_custom_call" | custom-call | flops 805306368 | bytes 5000000 | tf_op jit(solution)/shard_map/pallas_call | solution.py:31
  28.7 1.7 %collective-permute-start.13 = (bf16[128,768]{1,0:T(8,128)(2,1)S(1)}, bf16[128,768]{1,0:T(8,128)(2,1)S(1)}, u32[]{:S(2)}, u32[]{:S(2)}) collective-permute-start(bf16[128,768]{1,0:T(8,128)(2,1)S(1)} %add_convert_fusion.refs_14_), channel_id=1, source_target_pairs={{0,6},{1,7},{2,4},{3,5},{4,2},{5,3},{6,0},{7,1},{8,14},{9,15},{10,... | collective-permute-start | bytes 589832 | tf_op jit(solution)/shard_map/ppermute | solution.py:55
  30.5 3.3 %shard_map.104 = (bf16[1024,768]{1,0:T(8,128)(2,1)S(1)}, bf16[1024,768]{1,0:T(8,128)(2,1)S(1)}) custom-call(s32[1]{0:T(128)} %bitcast.me_ref, bf16[256,1024]{1,0:T(8,128)(2,1)S(1)} %get-tuple-element.23.refs_2_.refs_0_, bf16[256,1024]{1,0:T(8,128)(2,1)S(1)} %get-tuple-element.24.refs_0_.refs_2_.refs_1_, bf16[256,1024]{1,0:T(8,128)(2,1)S(1)} %get-tuple-element.25.refs_2_, ...), custom_call_target="tpu_custom_call" | custom-call | flops 1610612736 | bytes 5000000 | tf_op jit(solution)/shard_map/pallas_call | solution.py:31
  33.8 5.1 %collective-permute-done.12.refs_1_ = bf16[128,768]{1,0:T(8,128)(2,1)S(1)} collective-permute-done((bf16[128,768]{1,0:T(8,128)(2,1)S(1)}, bf16[128,768]{1,0:T(8,128)(2,1)S(1)}, u32[]{:S(2)}, u32[]{:S(2)}) %collective-permute-start.12) | collective-permute-done | bytes 196640 | tf_op jit(solution)/shard_map/ppermute | solution.py:55
  39.0 1.6 %collective-permute-start.14 = (bf16[64,768]{1,0:T(8,128)(2,1)S(1)}, bf16[64,768]{1,0:T(8,128)(2,1)S(1)}, u32[]{:S(2)}, u32[]{:S(2)}) collective-permute-start(bf16[64,768]{1,0:T(8,128)(2,1)S(1)} %get-tuple-element.37), channel_id=1, source_target_pairs={{0,8},{8,0},{16,24},{24,16},{1,9},{9,1},{17,25},{25,17},{2,10},{10... | collective-permute-start | bytes 294920 | tf_op jit(solution)/shard_map/ppermute | solution.py:55
  40.6 3.0 %collective-permute-done.14 = bf16[64,768]{1,0:T(8,128)(2,1)S(1)} collective-permute-done((bf16[64,768]{1,0:T(8,128)(2,1)S(1)}, bf16[64,768]{1,0:T(8,128)(2,1)S(1)}, u32[]{:S(2)}, u32[]{:S(2)}) %collective-permute-start.14) | collective-permute-done | bytes 98336 | tf_op jit(solution)/shard_map/ppermute | solution.py:55
  43.7 2.7 %collective-permute-start.15 = (bf16[64,768]{1,0:T(8,128)(2,1)S(1)}, bf16[64,768]{1,0:T(8,128)(2,1)S(1)}, u32[]{:S(2)}, u32[]{:S(2)}) collective-permute-start(bf16[64,768]{1,0:T(8,128)(2,1)S(1)} %add_convert_fusion.4.after_ref), channel_id=1, source_target_pairs={{0,16},{8,24},{16,0},{24,8},{1,17},{9,25},{17,1},{25,9},{2,18},{10... | collective-permute-start | bytes 294920 | tf_op jit(solution)/shard_map/ppermute | solution.py:55
  46.3 3.3 %shard_map.106 = (f32[1024,768]{1,0:T(8,128)}, f32[8,128]{1,0:T(8,128)S(1)}) custom-call(bf16[1024,768]{1,0:T(8,128)(2,1)S(1)} %get-tuple-element.33.refs_3_.grad_hidden_ref, bf16[768,768]{1,0:T(8,128)(2,1)S(1)} %copy-done.5, bf16[64,768]{1,0:T(8,128)(2,1)S(1)} %add_convert_fusion.4.after_ref), custom_call_target="tpu_custom_call" | custom-call | flops 1207959552 | bytes 6000000 | tf_op jit(solution)/shard_map/pallas_call | solution.py:303
  49.7 1.6 %collective-permute-start.16 = (bf16[64,768]{1,0:T(8,128)(2,1)S(1)}, bf16[64,768]{1,0:T(8,128)(2,1)S(1)}, u32[]{:S(2)}, u32[]{:S(2)}) collective-permute-start(bf16[64,768]{1,0:T(8,128)(2,1)S(1)} %add_convert_fusion.3.refs_0_), channel_id=1, source_target_pairs={{0,8},{8,0},{16,24},{24,16},{1,9},{9,1},{17,25},{25,17},{2,10},{10... | collective-permute-start | bytes 294920 | tf_op jit(solution)/shard_map/ppermute | solution.py:55
  51.3 3.1 %collective-permute-done.16.refs_1_ = bf16[64,768]{1,0:T(8,128)(2,1)S(1)} collective-permute-done((bf16[64,768]{1,0:T(8,128)(2,1)S(1)}, bf16[64,768]{1,0:T(8,128)(2,1)S(1)}, u32[]{:S(2)}, u32[]{:S(2)}) %collective-permute-start.16) | collective-permute-done | bytes 98336 | tf_op jit(solution)/shard_map/ppermute | solution.py:55
  54.5 1.5 %collective-permute-start.18 = (bf16[768,128]{1,0:T(8,128)(2,1)S(1)}, bf16[768,128]{1,0:T(8,128)(2,1)S(1)}, u32[]{:S(2)}, u32[]{:S(2)}) collective-permute-start(bf16[768,128]{1,0:T(8,128)(2,1)S(1)} %shard_map.108.whole_ref.refs_0_), channel_id=1, source_target_pairs={{0,2},{1,3},{2,0},{3,1},{4,6},{5,7},{6,4},{7,5},{8,10},{9,11},{10,... | collective-permute-start | bytes 589832 | tf_op jit(solution)/shard_map/ppermute | solution.py:55
  56.5 1.5 %collective-permute-start.22 = (bf16[768,128]{1,0:T(8,128)(2,1)S(1)}, bf16[768,128]{1,0:T(8,128)(2,1)S(1)}, u32[]{:S(2)}, u32[]{:S(2)}) collective-permute-start(bf16[768,128]{1,0:T(8,128)(2,1)S(1)} %shard_map.108.whole_ref.refs_0_), channel_id=1, source_target_pairs={{0,6},{1,7},{2,4},{3,5},{4,2},{5,3},{6,0},{7,1},{8,14},{9,15},{10,... | collective-permute-start | bytes 589832 | tf_op jit(solution)/shard_map/ppermute | solution.py:55
  59.3 1.5 %collective-permute-done.18.value_ref = bf16[768,128]{1,0:T(8,128)(2,1)S(1)} collective-permute-done((bf16[768,128]{1,0:T(8,128)(2,1)S(1)}, bf16[768,128]{1,0:T(8,128)(2,1)S(1)}, u32[]{:S(2)}, u32[]{:S(2)}) %collective-permute-start.18) | collective-permute-done | bytes 196640 | tf_op jit(solution)/shard_map/ppermute | solution.py:55
  60.9 3.0 %collective-permute-done.20.value_ref = bf16[768,128]{1,0:T(8,128)(2,1)S(1)} collective-permute-done((bf16[768,128]{1,0:T(8,128)(2,1)S(1)}, bf16[768,128]{1,0:T(8,128)(2,1)S(1)}, u32[]{:S(2)}, u32[]{:S(2)}) %collective-permute-start.20) | collective-permute-done | bytes 196640 | tf_op jit(solution)/shard_map/ppermute | solution.py:55
  65.6 2.8 %shard_map.113 = f32[768,768]{1,0:T(8,128)} custom-call(s32[1]{0:T(128)} %bitcast.me_ref, bf16[768,128]{1,0:T(8,128)(2,1)S(1)} %shard_map.108.whole_ref.refs_0_, bf16[768,128]{1,0:T(8,128)(2,1)S(1)} %collective-permute-done.17.refs_1_, bf16[768,128]{1,0:T(8,128)(2,1)S(1)} %shard_map.110.refs_2_, bf16[768,128]{1,0:T(8,128)(2,1)S(1)} %collective-permute-done.19.refs_3_, ...), custom_call_target="tpu_custom_call" | custom-call | flops 1207959552 | bytes 6000000 | tf_op jit(solution)/shard_map/pallas_call | solution.py:378
  (67 shorter events, 11.6 us)
Async XLA Ops:
  2.4 10.1 %collective-permute-start.1 = (bf16[144,768]{1,0:T(8,128)(2,1)}, bf16[144,768]{1,0:T(8,128)(2,1)}, u32[]{:S(2)}, u32[]{:S(2)}) collective-permute-start(bf16[144,768]{1,0:T(8,128)(2,1)} %shard_map.96.refs_0_.refs_4_), channel_id=1, source_target_pairs={{0,2},{1,3},{2,0},{3,1},{4,6},{5,7},{6,4},{7,5},{8,10},{9,11},{10,... | collective-permute-start | bytes 663560 | tf_op jit(solution)/shard_map/ppermute | solution.py:55
  5.4 8.7 %collective-permute-start = (bf16[144,768]{1,0:T(8,128)(2,1)}, bf16[144,768]{1,0:T(8,128)(2,1)}, u32[]{:S(2)}, u32[]{:S(2)}) collective-permute-start(bf16[144,768]{1,0:T(8,128)(2,1)} %shard_map.96.refs_0_.refs_4_), channel_id=1, source_target_pairs={{0,1},{1,0},{2,3},{3,2},{4,5},{5,4},{6,7},{7,6},{8,9},{9,8},{10,11... | collective-permute-start | bytes 663560 | tf_op jit(solution)/shard_map/ppermute | solution.py:55
  5.4 8.4 %collective-permute-start.2 = (bf16[144,768]{1,0:T(8,128)(2,1)}, bf16[144,768]{1,0:T(8,128)(2,1)S(1)}, u32[]{:S(2)}, u32[]{:S(2)}) collective-permute-start(bf16[144,768]{1,0:T(8,128)(2,1)} %shard_map.96.refs_0_.refs_4_), channel_id=1, source_target_pairs={{0,4},{1,5},{2,6},{3,7},{4,0},{5,1},{6,2},{7,3},{8,12},{9,13},{10,... | collective-permute-start | bytes 663560 | tf_op jit(solution)/shard_map/ppermute | solution.py:55
  12.6 5.0 %collective-permute-start.3 = (bf16[144,768]{1,0:T(8,128)(2,1)}, bf16[144,768]{1,0:T(8,128)(2,1)}, u32[]{:S(2)}, u32[]{:S(2)}) collective-permute-start(bf16[144,768]{1,0:T(8,128)(2,1)} %shard_map.97.refs_2_.refs_0_.refs_6_), channel_id=1, source_target_pairs={{0,1},{1,0},{2,3},{3,2},{4,5},{5,4},{6,7},{7,6},{8,9},{9,8},{10,11... | collective-permute-start | bytes 663560 | tf_op jit(solution)/shard_map/ppermute | solution.py:55
  12.9 8.8 %collective-permute-start.5 = (bf16[144,768]{1,0:T(8,128)(2,1)}, bf16[144,768]{1,0:T(8,128)(2,1)}, u32[]{:S(2)}, u32[]{:S(2)}) collective-permute-start(bf16[144,768]{1,0:T(8,128)(2,1)} %shard_map.96.refs_0_.refs_4_), channel_id=1, source_target_pairs={{0,6},{1,7},{2,4},{3,5},{4,2},{5,3},{6,0},{7,1},{8,14},{9,15},{10,... | collective-permute-start | bytes 663560 | tf_op jit(solution)/shard_map/ppermute | solution.py:55
  13.9 7.8 %collective-permute-start.4 = (bf16[144,768]{1,0:T(8,128)(2,1)S(1)}, bf16[144,768]{1,0:T(8,128)(2,1)S(1)}, u32[]{:S(2)}, u32[]{:S(2)}) collective-permute-start(bf16[144,768]{1,0:T(8,128)(2,1)S(1)} %shard_map.98.refs_3_.refs_0_.refs_8_), channel_id=1, source_target_pairs={{0,1},{1,0},{2,3},{3,2},{4,5},{5,4},{6,7},{7,6},{8,9},{9,8},{10,11... | collective-permute-start | bytes 663560 | tf_op jit(solution)/shard_map/ppermute | solution.py:55
  20.0 4.3 %collective-permute-start.7 = (bf16[128,768]{1,0:T(8,128)(2,1)S(1)}, bf16[128,768]{1,0:T(8,128)(2,1)S(1)}, u32[]{:S(2)}, u32[]{:S(2)}) collective-permute-start(bf16[128,768]{1,0:T(8,128)(2,1)S(1)} %get-tuple-element.27), channel_id=1, source_target_pairs={{0,1},{1,0},{2,3},{3,2},{4,5},{5,4},{6,7},{7,6},{8,9},{9,8},{10,11... | collective-permute-start | bytes 589832 | tf_op jit(solution)/shard_map/ppermute | solution.py:55
  20.2 10.2 %collective-permute-start.10 = (bf16[128,768]{1,0:T(8,128)(2,1)S(1)}, bf16[128,768]{1,0:T(8,128)(2,1)S(1)}, u32[]{:S(2)}, u32[]{:S(2)}) collective-permute-start(bf16[128,768]{1,0:T(8,128)(2,1)S(1)} %get-tuple-element.35), channel_id=1, source_target_pairs={{0,1},{1,0},{2,3},{3,2},{4,5},{5,4},{6,7},{7,6},{8,9},{9,8},{10,11... | collective-permute-start | bytes 589832 | tf_op jit(solution)/shard_map/ppermute | solution.py:55
  21.7 3.2 %collective-permute-start.6 = (bf16[144,768]{1,0:T(8,128)(2,1)}, bf16[144,768]{1,0:T(8,128)(2,1)S(1)}, u32[]{:S(2)}, u32[]{:S(2)}) collective-permute-start(bf16[144,768]{1,0:T(8,128)(2,1)} %shard_map.101.refs_3_.refs_0_.refs_10_), channel_id=1, source_target_pairs={{0,1},{1,0},{2,3},{3,2},{4,5},{5,4},{6,7},{7,6},{8,9},{9,8},{10,11... | collective-permute-start | bytes 663560 | tf_op jit(solution)/shard_map/ppermute | solution.py:55
  23.6 3.6 %collective-permute-start.8 = (bf16[128,768]{1,0:T(8,128)(2,1)S(1)}, bf16[128,768]{1,0:T(8,128)(2,1)S(1)}, u32[]{:S(2)}, u32[]{:S(2)}) collective-permute-start(bf16[128,768]{1,0:T(8,128)(2,1)S(1)} %get-tuple-element.30), channel_id=1, source_target_pairs={{0,1},{1,0},{2,3},{3,2},{4,5},{5,4},{6,7},{7,6},{8,9},{9,8},{10,11... | collective-permute-start | bytes 589832 | tf_op jit(solution)/shard_map/ppermute | solution.py:55
  24.3 9.5 %collective-permute-start.11 = (bf16[128,768]{1,0:T(8,128)(2,1)S(1)}, bf16[128,768]{1,0:T(8,128)(2,1)S(1)}, u32[]{:S(2)}, u32[]{:S(2)}) collective-permute-start(bf16[128,768]{1,0:T(8,128)(2,1)S(1)} %add_convert_fusion.2.refs_3_.refs_12_), channel_id=1, source_target_pairs={{0,2},{1,3},{2,0},{3,1},{4,6},{5,7},{6,4},{7,5},{8,10},{9,11},{10,... | collective-permute-start | bytes 589832 | tf_op jit(solution)/shard_map/ppermute | solution.py:55
  27.2 1.5 %collective-permute-start.9 = (bf16[128,768]{1,0:T(8,128)(2,1)S(1)}, bf16[128,768]{1,0:T(8,128)(2,1)S(1)}, u32[]{:S(2)}, u32[]{:S(2)}) collective-permute-start(bf16[128,768]{1,0:T(8,128)(2,1)S(1)} %get-tuple-element.32), channel_id=1, source_target_pairs={{0,1},{1,0},{2,3},{3,2},{4,5},{5,4},{6,7},{7,6},{8,9},{9,8},{10,11... | collective-permute-start | bytes 589832 | tf_op jit(solution)/shard_map/ppermute | solution.py:55
  27.3 11.6 %collective-permute-start.12 = (bf16[128,768]{1,0:T(8,128)(2,1)S(1)}, bf16[128,768]{1,0:T(8,128)(2,1)S(1)}, u32[]{:S(2)}, u32[]{:S(2)}) collective-permute-start(bf16[128,768]{1,0:T(8,128)(2,1)S(1)} %add_convert_fusion.1.refs_13_), channel_id=1, source_target_pairs={{0,4},{1,5},{2,6},{3,7},{4,0},{5,1},{6,2},{7,3},{8,12},{9,13},{10,... | collective-permute-start | bytes 589832 | tf_op jit(solution)/shard_map/ppermute | solution.py:55
  28.7 10.2 %collective-permute-start.13 = (bf16[128,768]{1,0:T(8,128)(2,1)S(1)}, bf16[128,768]{1,0:T(8,128)(2,1)S(1)}, u32[]{:S(2)}, u32[]{:S(2)}) collective-permute-start(bf16[128,768]{1,0:T(8,128)(2,1)S(1)} %add_convert_fusion.refs_14_), channel_id=1, source_target_pairs={{0,6},{1,7},{2,4},{3,5},{4,2},{5,3},{6,0},{7,1},{8,14},{9,15},{10,... | collective-permute-start | bytes 589832 | tf_op jit(solution)/shard_map/ppermute | solution.py:55
  39.0 4.7 %collective-permute-start.14 = (bf16[64,768]{1,0:T(8,128)(2,1)S(1)}, bf16[64,768]{1,0:T(8,128)(2,1)S(1)}, u32[]{:S(2)}, u32[]{:S(2)}) collective-permute-start(bf16[64,768]{1,0:T(8,128)(2,1)S(1)} %get-tuple-element.37), channel_id=1, source_target_pairs={{0,8},{8,0},{16,24},{24,16},{1,9},{9,1},{17,25},{25,17},{2,10},{10... | collective-permute-start | bytes 294920 | tf_op jit(solution)/shard_map/ppermute | solution.py:55
  43.7 6.0 %collective-permute-start.15 = (bf16[64,768]{1,0:T(8,128)(2,1)S(1)}, bf16[64,768]{1,0:T(8,128)(2,1)S(1)}, u32[]{:S(2)}, u32[]{:S(2)}) collective-permute-start(bf16[64,768]{1,0:T(8,128)(2,1)S(1)} %add_convert_fusion.4.after_ref), channel_id=1, source_target_pairs={{0,16},{8,24},{16,0},{24,8},{1,17},{9,25},{17,1},{25,9},{2,18},{10... | collective-permute-start | bytes 294920 | tf_op jit(solution)/shard_map/ppermute | solution.py:55
  49.7 4.7 %collective-permute-start.16 = (bf16[64,768]{1,0:T(8,128)(2,1)S(1)}, bf16[64,768]{1,0:T(8,128)(2,1)S(1)}, u32[]{:S(2)}, u32[]{:S(2)}) collective-permute-start(bf16[64,768]{1,0:T(8,128)(2,1)S(1)} %add_convert_fusion.3.refs_0_), channel_id=1, source_target_pairs={{0,8},{8,0},{16,24},{24,16},{1,9},{9,1},{17,25},{25,17},{2,10},{10... | collective-permute-start | bytes 294920 | tf_op jit(solution)/shard_map/ppermute | solution.py:55
  54.5 6.4 %collective-permute-start.18 = (bf16[768,128]{1,0:T(8,128)(2,1)S(1)}, bf16[768,128]{1,0:T(8,128)(2,1)S(1)}, u32[]{:S(2)}, u32[]{:S(2)}) collective-permute-start(bf16[768,128]{1,0:T(8,128)(2,1)S(1)} %shard_map.108.whole_ref.refs_0_), channel_id=1, source_target_pairs={{0,2},{1,3},{2,0},{3,1},{4,6},{5,7},{6,4},{7,5},{8,10},{9,11},{10,... | collective-permute-start | bytes 589832 | tf_op jit(solution)/shard_map/ppermute | solution.py:55
  56.0 7.9 %collective-permute-start.20 = (bf16[768,128]{1,0:T(8,128)(2,1)S(1)}, bf16[768,128]{1,0:T(8,128)(2,1)S(1)}, u32[]{:S(2)}, u32[]{:S(2)}) collective-permute-start(bf16[768,128]{1,0:T(8,128)(2,1)S(1)} %shard_map.108.whole_ref.refs_0_), channel_id=1, source_target_pairs={{0,4},{1,5},{2,6},{3,7},{4,0},{5,1},{6,2},{7,3},{8,12},{9,13},{10,... | collective-permute-start | bytes 589832 | tf_op jit(solution)/shard_map/ppermute | solution.py:55
  56.5 7.4 %collective-permute-start.22 = (bf16[768,128]{1,0:T(8,128)(2,1)S(1)}, bf16[768,128]{1,0:T(8,128)(2,1)S(1)}, u32[]{:S(2)}, u32[]{:S(2)}) collective-permute-start(bf16[768,128]{1,0:T(8,128)(2,1)S(1)} %shard_map.108.whole_ref.refs_0_), channel_id=1, source_target_pairs={{0,6},{1,7},{2,4},{3,5},{4,2},{5,3},{6,0},{7,1},{8,14},{9,15},{10,... | collective-permute-start | bytes 589832 | tf_op jit(solution)/shard_map/ppermute | solution.py:55
  58.2 6.2 %collective-permute-start.17 = (bf16[768,128]{1,0:T(8,128)(2,1)S(1)}, bf16[768,128]{1,0:T(8,128)(2,1)S(1)}, u32[]{:S(2)}, u32[]{:S(2)}) collective-permute-start(bf16[768,128]{1,0:T(8,128)(2,1)S(1)} %shard_map.108.whole_ref.refs_0_), channel_id=1, source_target_pairs={{0,1},{1,0},{2,3},{3,2},{4,5},{5,4},{6,7},{7,6},{8,9},{9,8},{10,11... | collective-permute-start | bytes 589832 | tf_op jit(solution)/shard_map/ppermute | solution.py:55
  60.9 3.6 %collective-permute-start.19 = (bf16[768,128]{1,0:T(8,128)(2,1)S(1)}, bf16[768,128]{1,0:T(8,128)(2,1)S(1)}, u32[]{:S(2)}, u32[]{:S(2)}) collective-permute-start(bf16[768,128]{1,0:T(8,128)(2,1)S(1)} %shard_map.110.refs_2_), channel_id=1, source_target_pairs={{0,1},{1,0},{2,3},{3,2},{4,5},{5,4},{6,7},{7,6},{8,9},{9,8},{10,11... | collective-permute-start | bytes 589832 | tf_op jit(solution)/shard_map/ppermute | solution.py:55
  63.9 1.4 %collective-permute-start.21 = (bf16[768,128]{1,0:T(8,128)(2,1)S(1)}, bf16[768,128]{1,0:T(8,128)(2,1)S(1)}, u32[]{:S(2)}, u32[]{:S(2)}) collective-permute-start(bf16[768,128]{1,0:T(8,128)(2,1)S(1)} %shard_map.111.refs_4_), channel_id=1, source_target_pairs={{0,1},{1,0},{2,3},{3,2},{4,5},{5,4},{6,7},{7,6},{8,9},{9,8},{10,11... | collective-permute-start | bytes 589832 | tf_op jit(solution)/shard_map/ppermute | solution.py:55
  63.9 1.7 %collective-permute-start.23 = (bf16[768,128]{1,0:T(8,128)(2,1)S(1)}, bf16[768,128]{1,0:T(8,128)(2,1)S(1)}, u32[]{:S(2)}, u32[]{:S(2)}) collective-permute-start(bf16[768,128]{1,0:T(8,128)(2,1)S(1)} %shard_map.112.refs_6_), channel_id=1, source_target_pairs={{0,1},{1,0},{2,3},{3,2},{4,5},{5,4},{6,7},{7,6},{8,9},{9,8},{10,11... | collective-permute-start | bytes 589832 | tf_op jit(solution)/shard_map/ppermute | solution.py:55
  (8 other events, 29.6 us)

commit v9 on v8

--- a/solution.py
+++ b/solution.py
@@ -233,7 +233,7 @@
         compiler_params=pltpu.CompilerParams(vmem_limit_bytes=56 * MIB),
     )(weight_num.reshape(1, size), weight_den.reshape(1, size), head_weight)
     got = {0: payload}
-    for g in near + far:
+    for g in far + near:
         got[2 * g] = swap(payload, "label", 2 * g)
     got[1] = swap(payload, "label", 1)
     (target,) = call(
@@ -251,15 +251,15 @@
         flops=2 * samples * width * width,
         nbytes=6_000_000,
     )
-    for g in near:
-        got[2 * g] = gate(got[2 * g], hidden_t)
-        got[2 * g + 1] = swap(got[2 * g], "label", 1)
     grads, kept, from_core, moved, received = {}, {}, {}, {}, {}
-    order = [0] + near + far
+    order = [0] + far + near
     for at, g in enumerate(order):
-        after = [got[2 * n] for n in near] if at == 0 else [grads[order[at - 1]]]
-        if at and at + 1 < len(order):
-            after.append(got[2 * order[at + 1]])
+        after = [grads[order[at - 1]]] if at else []
+        if at + 1 < len(order):
+            ahead = 2 * order[at + 1]
+            got[ahead] = gate(got[ahead], grads[order[at - 1]] if at else hidden_t)
+            got[ahead + 1] = swap(got[ahead], "label", 1)
+            after.append(got[ahead])
         if at >= 3:
             after.append(moved[order[at - 2]])
         grads[g], kept[g], sent = call(
@@ -276,22 +276,19 @@
             flops=8 * samples * size * width,
             nbytes=5_000_000,
         )
-        for ahead in [n for n in order[at + 2 : at + 3] if n in far]:
-            got[2 * ahead] = gate(got[2 * ahead], grads[g])
-            got[2 * ahead + 1] = swap(got[2 * ahead], "label", 1)
         from_core[g] = swap(sent, "label", 1)
         if g:
             moved[g] = (kept[g] + from_core[g].astype(F32)).astype(BF16)
             received[g] = swap(moved[g], "label", 2 * g)
     own = kept[0] + from_core[0].astype(F32)
-    received = [received[g] for g in near + far]
+    received = [received[g] for g in far + near]
 
     grad_hidden, rows = call(
         functools.partial(hidden_kernel, owners),
         [shape((samples, width), BF16), shape((labels, width), BF16)],
         [grads[g] for g in range(chips)] + [got[d] for d in range(owners)],
         scalars=[me_s],
-        after=[moved[g] for g in near + far],
+        after=[moved[g] for g in far + near],
         scratch=[pltpu.VMEM((labels, width), BF16)],
         vmem=12,
         flops=2 * samples * width * labels,

time: 68.9 us -> 67.4 us (0.978)
  waiting for transfers between devices: 18.1 us -> 15.6 us
  starting transfers between devices: 21 us -> 21.9 us
    ppermute x24, waiting for transfers between devices: 18.1 us -> 15.6 us  [swap(): return lax.ppermute(value, axis, [(i, i ^ distance) for i in range(size)])]
    ppermute x24, starting transfers between devices: 21 us -> 21.9 us  [swap(): return lax.ppermute(value, axis, [(i, i ^ distance) for i in range(size)])]
    unnamed x16 -> x18, local copies, waits for them, and re-layouts: 3.19 us -> 3.41 us
  transfers between devices with their start and end apart: 24 -> 24, of which waited for: 8 -> 10; matrix products, arithmetic and copies ran while one was open for 0% -> 0% of each run, Pallas kernels for 29% -> 30%
where the time goes in v9:
time: 67.4 us; the launch traced here: 67.1 us
  Pallas kernels  24.8 us (37%)
  starting transfers between devices  21.9 us (32%)
  waiting for transfers between devices  15.6 us (23%)
  local copies, waits for them, and re-layouts  3.59 us (5%)
  between operations  1.04 us (2%)
    ppermute x24, starting transfers between devices, swap(): return lax.ppermute(value, axis, [(i, i ^ distance) for i in range(size)])  21.9 us
    pallas_call x9, Pallas kernels, call(): pl.pallas_call(kernel, out_shape=outs, in_specs=[SMEM] * len(scalars) + [...  15.9 us
    ppermute x24, waiting for transfers between devices, swap(): return lax.ppermute(value, axis, [(i, i ^ distance) for i in range(size)])  15.6 us
    unnamed x18, local copies, waits for them, and re-layouts  3.41 us
    pallas_call x1, Pallas kernels, grad_enc_after(): pl.pallas_call(enc_kernel, grid=(samples // tile,), out_shape=[shape((sam...  3.29 us
    pallas_call x1, Pallas kernels, shards(): pl.pallas_call(functools.partial(proj_kernel, cuts), out_shape=shape((wid...  2.77 us
    pallas_call x1, Pallas kernels, shards(): pl.pallas_call(payload_kernel, out_shape=shape((size + TAIL, width), BF16...  1.76 us
  transfers between devices with their start and end apart: 24, of which 10 were waited for; matrix products, arithmetic and copies ran while one was open for 0% of the time, Pallas kernels for 30%

profile of v9, /device:TPU:0, one launch (start us, length us, event | category | flops | bytes accessed | tf_op | source)
XLA Modules:
  0.0 67.1 jit_solution(10096227759924111404)
XLA Ops:
  0.6 1.8 %shard_map.96.refs_0_.refs_4_ = bf16[144,768]{1,0:T(8,128)(2,1)} custom-call(s32[1,128]{1,0:T(1,128)} %bitcast.12, s32[1,128]{1,0:T(1,128)} %bitcast.13, bf16[128,768]{1,0:T(8,128)(2,1)} %rows_hbm.1), custom_call_target="tpu_custom_call" | custom-call | tf_op jit(solution)/shard_map/pallas_call | solution.py:227
  2.4 4.0 %collective-permute-start.1 = (bf16[144,768]{1,0:T(8,128)(2,1)}, bf16[144,768]{1,0:T(8,128)(2,1)}, u32[]{:S(2)}, u32[]{:S(2)}) collective-permute-start(bf16[144,768]{1,0:T(8,128)(2,1)} %shard_map.96.refs_0_.refs_4_), channel_id=1, source_target_pairs={{0,6},{1,7},{2,4},{3,5},{4,2},{5,3},{6,0},{7,1},{8,14},{9,15},{10,... | collective-permute-start | bytes 663560 | tf_op jit(solution)/shard_map/ppermute | solution.py:55
  7.7 1.9 %shard_map.94.after_ref.target_ref = bf16[512,1024]{1,0:T(8,128)(2,1)S(1)} custom-call(s32[8,1024]{1,0:T(8,128)S(1)} %bitcast.11), custom_call_target="tpu_custom_call" | custom-call | bytes 8000000 | tf_op jit(solution)/shard_map/pallas_call | solution.py:31
  9.6 1.4 %copy-done = bf16[1024,768]{1,0:T(8,128)(2,1)S(1)} copy-done((bf16[1024,768]{1,0:T(8,128)(2,1)S(1)}, bf16[1024,768]{1,0:T(8,128)(2,1)}, u32[]{:S(2)}) %copy-start) | copy-done | bytes 1572888
  11.0 1.5 %shard_map.95.refs_0_.hidden_t_ref = bf16[768,1024]{1,0:T(8,128)(2,1)S(1)} custom-call(bf16[1024,768]{1,0:T(8,128)(2,1)S(1)} %copy-done, bf16[768,768]{1,0:T(8,128)(2,1)S(1)} %copy-done.5, bf16[512,1024]{1,0:T(8,128)(2,1)S(1)} %shard_map.94.after_ref.target_ref), custom_call_target="tpu_custom_call" | custom-call | flops 1207959552 | bytes 6000000 | tf_op jit(solution)/shard_map/pallas_call | solution.py:31
  13.0 2.0 %collective-permute-start.5 = (bf16[144,768]{1,0:T(8,128)(2,1)}, bf16[144,768]{1,0:T(8,128)(2,1)S(1)}, u32[]{:S(2)}, u32[]{:S(2)}) collective-permute-start(bf16[144,768]{1,0:T(8,128)(2,1)} %shard_map.96.refs_0_.refs_4_), channel_id=1, source_target_pairs={{0,4},{1,5},{2,6},{3,7},{4,0},{5,1},{6,2},{7,3},{8,12},{9,13},{10,... | collective-permute-start | bytes 663560 | tf_op jit(solution)/shard_map/ppermute | solution.py:55
  15.0 1.2 %copy-done.3 = bf16[512,1024]{1,0:T(8,128)(2,1)S(1)} copy-done((bf16[512,1024]{1,0:T(8,128)(2,1)S(1)}, bf16[512,1024]{1,0:T(8,128)(2,1)}, u32[]{:S(2)}) %copy-start.3) | copy-done | bytes 1048600
  16.2 2.4 %shard_map.98 = (bf16[256,1024]{1,0:T(8,128)(2,1)S(1)}, f32[128,768]{1,0:T(8,128)S(1)}, bf16[128,768]{1,0:T(8,128)(2,1)S(1)}) custom-call(s32[4,8]{1,0:T(4,128)S(1)} %bitcast.7, s32[1]{0:T(128)} %bitcast.me_ref, s32[1]{0:T(128)} %bitcast.2.z_ref, bf16[768,1024]{1,0:T(8,128)(2,1)S(1)} %shard_map.95.refs_0_.hidden_t_ref, bf16[512,1024]{1,0:T(8,128)(2,1)S(1)} %copy-done.3, ...), custom_call_target="tpu_custom_call" | custom-call | flops 805306368 | bytes 5000000 | tf_op jit(solution)/shard_map/pallas_call | solution.py:31
  18.9 2.4 %shard_map.100 = (bf16[256,1024]{1,0:T(8,128)(2,1)S(1)}, f32[128,768]{1,0:T(8,128)S(1)}, bf16[128,768]{1,0:T(8,128)(2,1)S(1)}) custom-call(s32[4,8]{1,0:T(4,128)S(1)} %bitcast.8, s32[1]{0:T(128)} %bitcast.me_ref, s32[1]{0:T(128)} %bitcast.2.z_ref, bf16[768,1024]{1,0:T(8,128)(2,1)S(1)} %shard_map.95.refs_0_.hidden_t_ref, bf16[512,1024]{1,0:T(8,128)(2,1)S(1)} %copy-done.3, ...), custom_call_target="tpu_custom_call" | custom-call | flops 805306368 | bytes 5000000 | tf_op jit(solution)/shard_map/pallas_call | solution.py:31
  22.2 2.3 %shard_map.102 = (bf16[256,1024]{1,0:T(8,128)(2,1)S(1)}, f32[128,768]{1,0:T(8,128)S(1)}, bf16[128,768]{1,0:T(8,128)(2,1)S(1)}) custom-call(s32[4,8]{1,0:T(4,128)S(1)} %bitcast.9, s32[1]{0:T(128)} %bitcast.me_ref, s32[1]{0:T(128)} %bitcast.2.z_ref, bf16[768,1024]{1,0:T(8,128)(2,1)S(1)} %shard_map.95.refs_0_.hidden_t_ref, bf16[512,1024]{1,0:T(8,128)(2,1)S(1)} %copy-done.3, ...), custom_call_target="tpu_custom_call" | custom-call | flops 805306368 | bytes 5000000 | tf_op jit(solution)/shard_map/pallas_call | solution.py:31
  24.9 2.0 %collective-permute-start.11 = (bf16[128,768]{1,0:T(8,128)(2,1)S(1)}, bf16[128,768]{1,0:T(8,128)(2,1)S(1)}, u32[]{:S(2)}, u32[]{:S(2)}) collective-permute-start(bf16[128,768]{1,0:T(8,128)(2,1)S(1)} %add_convert_fusion.2.refs_3_.refs_12_), channel_id=1, source_target_pairs={{0,6},{1,7},{2,4},{3,5},{4,2},{5,3},{6,0},{7,1},{8,14},{9,15},{10,... | collective-permute-start | bytes 589832 | tf_op jit(solution)/shard_map/ppermute | solution.py:55
  27.0 1.9 %shard_map.103 = (bf16[256,1024]{1,0:T(8,128)(2,1)S(1)}, f32[128,768]{1,0:T(8,128)S(1)}, bf16[128,768]{1,0:T(8,128)(2,1)S(1)}) custom-call(s32[4,8]{1,0:T(4,128)S(1)} %bitcast.10, s32[1]{0:T(128)} %bitcast.me_ref, s32[1]{0:T(128)} %bitcast.2.z_ref, bf16[768,1024]{1,0:T(8,128)(2,1)S(1)} %shard_map.95.refs_0_.hidden_t_ref, bf16[512,1024]{1,0:T(8,128)(2,1)S(1)} %copy-done.4, ...), custom_call_target="tpu_custom_call" | custom-call | flops 805306368 | bytes 5000000 | tf_op jit(solution)/shard_map/pallas_call | solution.py:31
  31.6 3.3 %shard_map.104 = (bf16[1024,768]{1,0:T(8,128)(2,1)S(1)}, bf16[1024,768]{1,0:T(8,128)(2,1)S(1)}) custom-call(s32[1]{0:T(128)} %bitcast.me_ref, bf16[256,1024]{1,0:T(8,128)(2,1)S(1)} %get-tuple-element.23.refs_0_.refs_2_, bf16[256,1024]{1,0:T(8,128)(2,1)S(1)} %get-tuple-element.25.refs_2_.refs_1_, bf16[256,1024]{1,0:T(8,128)(2,1)S(1)} %get-tuple-element.28.refs_2_, ...), custom_call_target="tpu_custom_call" | custom-call | flops 1610612736 | bytes 5000000 | tf_op jit(solution)/shard_map/pallas_call | solution.py:31
  34.9 1.7 %collective-permute-done.12.refs_1_ = bf16[128,768]{1,0:T(8,128)(2,1)S(1)} collective-permute-done((bf16[128,768]{1,0:T(8,128)(2,1)S(1)}, bf16[128,768]{1,0:T(8,128)(2,1)S(1)}, u32[]{:S(2)}, u32[]{:S(2)}) %collective-permute-start.12) | collective-permute-done | bytes 196640 | tf_op jit(solution)/shard_map/ppermute | solution.py:55
  37.6 1.6 %collective-permute-start.14 = (bf16[64,768]{1,0:T(8,128)(2,1)S(1)}, bf16[64,768]{1,0:T(8,128)(2,1)S(1)}, u32[]{:S(2)}, u32[]{:S(2)}) collective-permute-start(bf16[64,768]{1,0:T(8,128)(2,1)S(1)} %get-tuple-element.37), channel_id=1, source_target_pairs={{0,8},{8,0},{16,24},{24,16},{1,9},{9,1},{17,25},{25,17},{2,10},{10... | collective-permute-start | bytes 294920 | tf_op jit(solution)/shard_map/ppermute | solution.py:55
  39.2 3.0 %collective-permute-done.14 = bf16[64,768]{1,0:T(8,128)(2,1)S(1)} collective-permute-done((bf16[64,768]{1,0:T(8,128)(2,1)S(1)}, bf16[64,768]{1,0:T(8,128)(2,1)S(1)}, u32[]{:S(2)}, u32[]{:S(2)}) %collective-permute-start.14) | collective-permute-done | bytes 98336 | tf_op jit(solution)/shard_map/ppermute | solution.py:55
  42.3 2.7 %collective-permute-start.15 = (bf16[64,768]{1,0:T(8,128)(2,1)S(1)}, bf16[64,768]{1,0:T(8,128)(2,1)S(1)}, u32[]{:S(2)}, u32[]{:S(2)}) collective-permute-start(bf16[64,768]{1,0:T(8,128)(2,1)S(1)} %add_convert_fusion.4.after_ref), channel_id=1, source_target_pairs={{0,16},{8,24},{16,0},{24,8},{1,17},{9,25},{17,1},{25,9},{2,18},{10... | collective-permute-start | bytes 294920 | tf_op jit(solution)/shard_map/ppermute | solution.py:55
  45.0 3.3 %shard_map.106 = (f32[1024,768]{1,0:T(8,128)}, f32[8,128]{1,0:T(8,128)S(1)}) custom-call(bf16[1024,768]{1,0:T(8,128)(2,1)S(1)} %get-tuple-element.33.refs_3_.grad_hidden_ref, bf16[768,768]{1,0:T(8,128)(2,1)S(1)} %copy-done.6, bf16[64,768]{1,0:T(8,128)(2,1)S(1)} %add_convert_fusion.4.after_ref), custom_call_target="tpu_custom_call" | custom-call | flops 1207959552 | bytes 6000000 | tf_op jit(solution)/shard_map/pallas_call | solution.py:300
  48.3 1.6 %collective-permute-start.16 = (bf16[64,768]{1,0:T(8,128)(2,1)S(1)}, bf16[64,768]{1,0:T(8,128)(2,1)S(1)}, u32[]{:S(2)}, u32[]{:S(2)}) collective-permute-start(bf16[64,768]{1,0:T(8,128)(2,1)S(1)} %add_convert_fusion.3.refs_0_), channel_id=1, source_target_pairs={{0,8},{8,0},{16,24},{24,16},{1,9},{9,1},{17,25},{25,17},{2,10},{10... | collective-permute-start | bytes 294920 | tf_op jit(solution)/shard_map/ppermute | solution.py:55
  49.9 3.1 %collective-permute-done.16.refs_1_ = bf16[64,768]{1,0:T(8,128)(2,1)S(1)} collective-permute-done((bf16[64,768]{1,0:T(8,128)(2,1)S(1)}, bf16[64,768]{1,0:T(8,128)(2,1)S(1)}, u32[]{:S(2)}, u32[]{:S(2)}) %collective-permute-start.16) | collective-permute-done | bytes 98336 | tf_op jit(solution)/shard_map/ppermute | solution.py:55
  53.1 1.4 %collective-permute-start.18 = (bf16[768,128]{1,0:T(8,128)(2,1)S(1)}, bf16[768,128]{1,0:T(8,128)(2,1)S(1)}, u32[]{:S(2)}, u32[]{:S(2)}) collective-permute-start(bf16[768,128]{1,0:T(8,128)(2,1)S(1)} %shard_map.108.whole_ref.refs_0_), channel_id=1, source_target_pairs={{0,2},{1,3},{2,0},{3,1},{4,6},{5,7},{6,4},{7,5},{8,10},{9,11},{10,... | collective-permute-start | bytes 589832 | tf_op jit(solution)/shard_map/ppermute | solution.py:55
  57.9 1.5 %collective-permute-done.18.value_ref = bf16[768,128]{1,0:T(8,128)(2,1)S(1)} collective-permute-done((bf16[768,128]{1,0:T(8,128)(2,1)S(1)}, bf16[768,128]{1,0:T(8,128)(2,1)S(1)}, u32[]{:S(2)}, u32[]{:S(2)}) %collective-permute-start.18) | collective-permute-done | bytes 196640 | tf_op jit(solution)/shard_map/ppermute | solution.py:55
  59.4 3.0 %collective-permute-done.20.value_ref = bf16[768,128]{1,0:T(8,128)(2,1)S(1)} collective-permute-done((bf16[768,128]{1,0:T(8,128)(2,1)S(1)}, bf16[768,128]{1,0:T(8,128)(2,1)S(1)}, u32[]{:S(2)}, u32[]{:S(2)}) %collective-permute-start.20) | collective-permute-done | bytes 196640 | tf_op jit(solution)/shard_map/ppermute | solution.py:55
  64.1 2.8 %shard_map.113 = f32[768,768]{1,0:T(8,128)} custom-call(s32[1]{0:T(128)} %bitcast.me_ref, bf16[768,128]{1,0:T(8,128)(2,1)S(1)} %shard_map.108.whole_ref.refs_0_, bf16[768,128]{1,0:T(8,128)(2,1)S(1)} %collective-permute-done.17.refs_1_, bf16[768,128]{1,0:T(8,128)(2,1)S(1)} %shard_map.110.refs_2_, bf16[768,128]{1,0:T(8,128)(2,1)S(1)} %collective-permute-done.19.refs_3_, ...), custom_call_target="tpu_custom_call" | custom-call | flops 1207959552 | bytes 6000000 | tf_op jit(solution)/shard_map/pallas_call | solution.py:375
  (69 shorter events, 12.3 us)
Async XLA Ops:
  2.4 10.5 %collective-permute-start.1 = (bf16[144,768]{1,0:T(8,128)(2,1)}, bf16[144,768]{1,0:T(8,128)(2,1)}, u32[]{:S(2)}, u32[]{:S(2)}) collective-permute-start(bf16[144,768]{1,0:T(8,128)(2,1)} %shard_map.96.refs_0_.refs_4_), channel_id=1, source_target_pairs={{0,6},{1,7},{2,4},{3,5},{4,2},{5,3},{6,0},{7,1},{8,14},{9,15},{10,... | collective-permute-start | bytes 663560 | tf_op jit(solution)/shard_map/ppermute | solution.py:55
  6.4 8.6 %collective-permute-start = (bf16[144,768]{1,0:T(8,128)(2,1)}, bf16[144,768]{1,0:T(8,128)(2,1)}, u32[]{:S(2)}, u32[]{:S(2)}) collective-permute-start(bf16[144,768]{1,0:T(8,128)(2,1)} %shard_map.96.refs_0_.refs_4_), channel_id=1, source_target_pairs={{0,1},{1,0},{2,3},{3,2},{4,5},{5,4},{6,7},{7,6},{8,9},{9,8},{10,11... | collective-permute-start | bytes 663560 | tf_op jit(solution)/shard_map/ppermute | solution.py:55
  6.4 12.2 %collective-permute-start.2 = (bf16[144,768]{1,0:T(8,128)(2,1)}, bf16[144,768]{1,0:T(8,128)(2,1)}, u32[]{:S(2)}, u32[]{:S(2)}) collective-permute-start(bf16[144,768]{1,0:T(8,128)(2,1)} %shard_map.96.refs_0_.refs_4_), channel_id=1, source_target_pairs={{0,2},{1,3},{2,0},{3,1},{4,6},{5,7},{6,4},{7,5},{8,10},{9,11},{10,... | collective-permute-start | bytes 663560 | tf_op jit(solution)/shard_map/ppermute | solution.py:55
  12.9 6.0 %collective-permute-start.4 = (bf16[144,768]{1,0:T(8,128)(2,1)}, bf16[144,768]{1,0:T(8,128)(2,1)}, u32[]{:S(2)}, u32[]{:S(2)}) collective-permute-start(bf16[144,768]{1,0:T(8,128)(2,1)} %shard_map.97.refs_2_.refs_0_.refs_10_), channel_id=1, source_target_pairs={{0,1},{1,0},{2,3},{3,2},{4,5},{5,4},{6,7},{7,6},{8,9},{9,8},{10,11... | collective-permute-start | bytes 663560 | tf_op jit(solution)/shard_map/ppermute | solution.py:55
  13.0 9.0 %collective-permute-start.5 = (bf16[144,768]{1,0:T(8,128)(2,1)}, bf16[144,768]{1,0:T(8,128)(2,1)S(1)}, u32[]{:S(2)}, u32[]{:S(2)}) collective-permute-start(bf16[144,768]{1,0:T(8,128)(2,1)} %shard_map.96.refs_0_.refs_4_), channel_id=1, source_target_pairs={{0,4},{1,5},{2,6},{3,7},{4,0},{5,1},{6,2},{7,3},{8,12},{9,13},{10,... | collective-permute-start | bytes 663560 | tf_op jit(solution)/shard_map/ppermute | solution.py:55
  18.6 3.6 %collective-permute-start.3 = (bf16[144,768]{1,0:T(8,128)(2,1)}, bf16[144,768]{1,0:T(8,128)(2,1)S(1)}, u32[]{:S(2)}, u32[]{:S(2)}) collective-permute-start(bf16[144,768]{1,0:T(8,128)(2,1)} %shard_map.99.refs_3_.refs_0_.refs_6_), channel_id=1, source_target_pairs={{0,1},{1,0},{2,3},{3,2},{4,5},{5,4},{6,7},{7,6},{8,9},{9,8},{10,11... | collective-permute-start | bytes 663560 | tf_op jit(solution)/shard_map/ppermute | solution.py:55
  21.3 3.6 %collective-permute-start.7 = (bf16[128,768]{1,0:T(8,128)(2,1)S(1)}, bf16[128,768]{1,0:T(8,128)(2,1)S(1)}, u32[]{:S(2)}, u32[]{:S(2)}) collective-permute-start(bf16[128,768]{1,0:T(8,128)(2,1)S(1)} %get-tuple-element.27), channel_id=1, source_target_pairs={{0,1},{1,0},{2,3},{3,2},{4,5},{5,4},{6,7},{7,6},{8,9},{9,8},{10,11... | collective-permute-start | bytes 589832 | tf_op jit(solution)/shard_map/ppermute | solution.py:55
  21.7 9.8 %collective-permute-start.10 = (bf16[128,768]{1,0:T(8,128)(2,1)S(1)}, bf16[128,768]{1,0:T(8,128)(2,1)S(1)}, u32[]{:S(2)}, u32[]{:S(2)}) collective-permute-start(bf16[128,768]{1,0:T(8,128)(2,1)S(1)} %get-tuple-element.35), channel_id=1, source_target_pairs={{0,1},{1,0},{2,3},{3,2},{4,5},{5,4},{6,7},{7,6},{8,9},{9,8},{10,11... | collective-permute-start | bytes 589832 | tf_op jit(solution)/shard_map/ppermute | solution.py:55
  21.9 5.0 %collective-permute-start.6 = (bf16[144,768]{1,0:T(8,128)(2,1)S(1)}, bf16[144,768]{1,0:T(8,128)(2,1)S(1)}, u32[]{:S(2)}, u32[]{:S(2)}) collective-permute-start(bf16[144,768]{1,0:T(8,128)(2,1)S(1)} %shard_map.101.refs_3_.refs_0_.refs_8_), channel_id=1, source_target_pairs={{0,1},{1,0},{2,3},{3,2},{4,5},{5,4},{6,7},{7,6},{8,9},{9,8},{10,11... | collective-permute-start | bytes 663560 | tf_op jit(solution)/shard_map/ppermute | solution.py:55
  24.5 4.4 %collective-permute-start.8 = (bf16[128,768]{1,0:T(8,128)(2,1)S(1)}, bf16[128,768]{1,0:T(8,128)(2,1)S(1)}, u32[]{:S(2)}, u32[]{:S(2)}) collective-permute-start(bf16[128,768]{1,0:T(8,128)(2,1)S(1)} %get-tuple-element.30), channel_id=1, source_target_pairs={{0,1},{1,0},{2,3},{3,2},{4,5},{5,4},{6,7},{7,6},{8,9},{9,8},{10,11... | collective-permute-start | bytes 589832 | tf_op jit(solution)/shard_map/ppermute | solution.py:55
  24.9 9.9 %collective-permute-start.11 = (bf16[128,768]{1,0:T(8,128)(2,1)S(1)}, bf16[128,768]{1,0:T(8,128)(2,1)S(1)}, u32[]{:S(2)}, u32[]{:S(2)}) collective-permute-start(bf16[128,768]{1,0:T(8,128)(2,1)S(1)} %add_convert_fusion.2.refs_3_.refs_12_), channel_id=1, source_target_pairs={{0,6},{1,7},{2,4},{3,5},{4,2},{5,3},{6,0},{7,1},{8,14},{9,15},{10,... | collective-permute-start | bytes 589832 | tf_op jit(solution)/shard_map/ppermute | solution.py:55
  28.9 1.5 %collective-permute-start.9 = (bf16[128,768]{1,0:T(8,128)(2,1)S(1)}, bf16[128,768]{1,0:T(8,128)(2,1)S(1)}, u32[]{:S(2)}, u32[]{:S(2)}) collective-permute-start(bf16[128,768]{1,0:T(8,128)(2,1)S(1)} %get-tuple-element.32), channel_id=1, source_target_pairs={{0,1},{1,0},{2,3},{3,2},{4,5},{5,4},{6,7},{7,6},{8,9},{9,8},{10,11... | collective-permute-start | bytes 589832 | tf_op jit(solution)/shard_map/ppermute | solution.py:55
  29.0 7.5 %collective-permute-start.12 = (bf16[128,768]{1,0:T(8,128)(2,1)S(1)}, bf16[128,768]{1,0:T(8,128)(2,1)S(1)}, u32[]{:S(2)}, u32[]{:S(2)}) collective-permute-start(bf16[128,768]{1,0:T(8,128)(2,1)S(1)} %add_convert_fusion.1.refs_13_), channel_id=1, source_target_pairs={{0,2},{1,3},{2,0},{3,1},{4,6},{5,7},{6,4},{7,5},{8,10},{9,11},{10,... | collective-permute-start | bytes 589832 | tf_op jit(solution)/shard_map/ppermute | solution.py:55
  30.5 7.0 %collective-permute-start.13 = (bf16[128,768]{1,0:T(8,128)(2,1)S(1)}, bf16[128,768]{1,0:T(8,128)(2,1)S(1)}, u32[]{:S(2)}, u32[]{:S(2)}) collective-permute-start(bf16[128,768]{1,0:T(8,128)(2,1)S(1)} %add_convert_fusion.refs_14_), channel_id=1, source_target_pairs={{0,4},{1,5},{2,6},{3,7},{4,0},{5,1},{6,2},{7,3},{8,12},{9,13},{10,... | collective-permute-start | bytes 589832 | tf_op jit(solution)/shard_map/ppermute | solution.py:55
  37.6 4.7 %collective-permute-start.14 = (bf16[64,768]{1,0:T(8,128)(2,1)S(1)}, bf16[64,768]{1,0:T(8,128)(2,1)S(1)}, u32[]{:S(2)}, u32[]{:S(2)}) collective-permute-start(bf16[64,768]{1,0:T(8,128)(2,1)S(1)} %get-tuple-element.37), channel_id=1, source_target_pairs={{0,8},{8,0},{16,24},{24,16},{1,9},{9,1},{17,25},{25,17},{2,10},{10... | collective-permute-start | bytes 294920 | tf_op jit(solution)/shard_map/ppermute | solution.py:55
  42.3 6.0 %collective-permute-start.15 = (bf16[64,768]{1,0:T(8,128)(2,1)S(1)}, bf16[64,768]{1,0:T(8,128)(2,1)S(1)}, u32[]{:S(2)}, u32[]{:S(2)}) collective-permute-start(bf16[64,768]{1,0:T(8,128)(2,1)S(1)} %add_convert_fusion.4.after_ref), channel_id=1, source_target_pairs={{0,16},{8,24},{16,0},{24,8},{1,17},{9,25},{17,1},{25,9},{2,18},{10... | collective-permute-start | bytes 294920 | tf_op jit(solution)/shard_map/ppermute | solution.py:55
  48.3 4.7 %collective-permute-start.16 = (bf16[64,768]{1,0:T(8,128)(2,1)S(1)}, bf16[64,768]{1,0:T(8,128)(2,1)S(1)}, u32[]{:S(2)}, u32[]{:S(2)}) collective-permute-start(bf16[64,768]{1,0:T(8,128)(2,1)S(1)} %add_convert_fusion.3.refs_0_), channel_id=1, source_target_pairs={{0,8},{8,0},{16,24},{24,16},{1,9},{9,1},{17,25},{25,17},{2,10},{10... | collective-permute-start | bytes 294920 | tf_op jit(solution)/shard_map/ppermute | solution.py:55
  53.1 6.3 %collective-permute-start.18 = (bf16[768,128]{1,0:T(8,128)(2,1)S(1)}, bf16[768,128]{1,0:T(8,128)(2,1)S(1)}, u32[]{:S(2)}, u32[]{:S(2)}) collective-permute-start(bf16[768,128]{1,0:T(8,128)(2,1)S(1)} %shard_map.108.whole_ref.refs_0_), channel_id=1, source_target_pairs={{0,2},{1,3},{2,0},{3,1},{4,6},{5,7},{6,4},{7,5},{8,10},{9,11},{10,... | collective-permute-start | bytes 589832 | tf_op jit(solution)/shard_map/ppermute | solution.py:55
  54.5 7.9 %collective-permute-start.20 = (bf16[768,128]{1,0:T(8,128)(2,1)S(1)}, bf16[768,128]{1,0:T(8,128)(2,1)S(1)}, u32[]{:S(2)}, u32[]{:S(2)}) collective-permute-start(bf16[768,128]{1,0:T(8,128)(2,1)S(1)} %shard_map.108.whole_ref.refs_0_), channel_id=1, source_target_pairs={{0,4},{1,5},{2,6},{3,7},{4,0},{5,1},{6,2},{7,3},{8,12},{9,13},{10,... | collective-permute-start | bytes 589832 | tf_op jit(solution)/shard_map/ppermute | solution.py:55
  55.5 6.9 %collective-permute-start.22 = (bf16[768,128]{1,0:T(8,128)(2,1)S(1)}, bf16[768,128]{1,0:T(8,128)(2,1)S(1)}, u32[]{:S(2)}, u32[]{:S(2)}) collective-permute-start(bf16[768,128]{1,0:T(8,128)(2,1)S(1)} %shard_map.108.whole_ref.refs_0_), channel_id=1, source_target_pairs={{0,6},{1,7},{2,4},{3,5},{4,2},{5,3},{6,0},{7,1},{8,14},{9,15},{10,... | collective-permute-start | bytes 589832 | tf_op jit(solution)/shard_map/ppermute | solution.py:55
  56.8 6.1 %collective-permute-start.17 = (bf16[768,128]{1,0:T(8,128)(2,1)S(1)}, bf16[768,128]{1,0:T(8,128)(2,1)S(1)}, u32[]{:S(2)}, u32[]{:S(2)}) collective-permute-start(bf16[768,128]{1,0:T(8,128)(2,1)S(1)} %shard_map.108.whole_ref.refs_0_), channel_id=1, source_target_pairs={{0,1},{1,0},{2,3},{3,2},{4,5},{5,4},{6,7},{7,6},{8,9},{9,8},{10,11... | collective-permute-start | bytes 589832 | tf_op jit(solution)/shard_map/ppermute | solution.py:55
  59.4 3.5 %collective-permute-start.19 = (bf16[768,128]{1,0:T(8,128)(2,1)S(1)}, bf16[768,128]{1,0:T(8,128)(2,1)S(1)}, u32[]{:S(2)}, u32[]{:S(2)}) collective-permute-start(bf16[768,128]{1,0:T(8,128)(2,1)S(1)} %shard_map.110.refs_2_), channel_id=1, source_target_pairs={{0,1},{1,0},{2,3},{3,2},{4,5},{5,4},{6,7},{7,6},{8,9},{9,8},{10,11... | collective-permute-start | bytes 589832 | tf_op jit(solution)/shard_map/ppermute | solution.py:55
  62.4 1.4 %collective-permute-start.21 = (bf16[768,128]{1,0:T(8,128)(2,1)S(1)}, bf16[768,128]{1,0:T(8,128)(2,1)S(1)}, u32[]{:S(2)}, u32[]{:S(2)}) collective-permute-start(bf16[768,128]{1,0:T(8,128)(2,1)S(1)} %shard_map.111.refs_4_), channel_id=1, source_target_pairs={{0,1},{1,0},{2,3},{3,2},{4,5},{5,4},{6,7},{7,6},{8,9},{9,8},{10,11... | collective-permute-start | bytes 589832 | tf_op jit(solution)/shard_map/ppermute | solution.py:55
  62.4 1.7 %collective-permute-start.23 = (bf16[768,128]{1,0:T(8,128)(2,1)S(1)}, bf16[768,128]{1,0:T(8,128)(2,1)S(1)}, u32[]{:S(2)}, u32[]{:S(2)}) collective-permute-start(bf16[768,128]{1,0:T(8,128)(2,1)S(1)} %shard_map.112.refs_6_), channel_id=1, source_target_pairs={{0,1},{1,0},{2,3},{3,2},{4,5},{5,4},{6,7},{7,6},{8,9},{9,8},{10,11... | collective-permute-start | bytes 589832 | tf_op jit(solution)/shard_map/ppermute | solution.py:55
  (9 other events, 34.0 us)

commit v10 on v9

--- a/solution.py
+++ b/solution.py
@@ -73,7 +73,7 @@
     copies[2].wait()
 
 
-def target_kernel(beam, block, wanted_ref, target_ref):
+def target_kernel(beam, block, wanted_ref, after_ref, target_ref):
     samples = wanted_ref.shape[1]
     size = target_ref.shape[0] // beam
     label_iota = lax.broadcasted_iota(jnp.int32, (size, block), 0)
@@ -88,7 +88,7 @@
             ).astype(BF16)
 
 
-def inputs_kernel(enc_ref, proj_ref, after_ref, hidden_t_ref):
+def inputs_kernel(enc_ref, proj_ref, hidden_t_ref):
     samples = enc_ref.shape[0]
     tile = min(256, samples)
     for start in range(0, samples, tile):
@@ -236,30 +236,27 @@
     for g in far + near:
         got[2 * g] = swap(payload, "label", 2 * g)
     got[1] = swap(payload, "label", 1)
+    (hidden_t,) = call(
+        inputs_kernel,
+        [shape((width, samples), BF16)],
+        [enc, proj],
+        flops=2 * samples * width * width,
+        nbytes=6_000_000,
+    )
     (target,) = call(
         functools.partial(target_kernel, beam, block),
         [shape((beam * size, samples), BF16)],
         [positives.T],
+        after=[hidden_t],
         vmem=2,
         nbytes=8_000_000,
-    )
-    (hidden_t,) = call(
-        inputs_kernel,
-        [shape((width, samples), BF16)],
-        [enc, proj],
-        after=[target],
-        flops=2 * samples * width * width,
-        nbytes=6_000_000,
     )
     grads, kept, from_core, moved, received = {}, {}, {}, {}, {}
     order = [0] + far + near
     for at, g in enumerate(order):
         after = [grads[order[at - 1]]] if at else []
-        if at + 1 < len(order):
-            ahead = 2 * order[at + 1]
-            got[ahead] = gate(got[ahead], grads[order[at - 1]] if at else hidden_t)
-            got[ahead + 1] = swap(got[ahead], "label", 1)
-            after.append(got[ahead])
+        if at == 1 and len(order) > 2:
+            after.append(got[2 * order[2]])
         if at >= 3:
             after.append(moved[order[at - 2]])
         grads[g], kept[g], sent = call(
@@ -276,6 +273,9 @@
             flops=8 * samples * size * width,
             nbytes=5_000_000,
         )
+        for ahead in order[1:3] if at == 0 else order[at + 1 : at + 2] if at > 1 else []:
+            got[2 * ahead] = gate(got[2 * ahead], grads[g])
+            got[2 * ahead + 1] = swap(got[2 * ahead], "label", 1)
         from_core[g] = swap(sent, "label", 1)
         if g:
             moved[g] = (kept[g] + from_core[g].astype(F32)).astype(BF16)

time: 67.4 us -> 68.2 us (1.012)
  local copies, waits for them, and re-layouts: 3.59 us -> 5.56 us
  waiting for transfers between devices: 15.6 us -> 17.2 us
  starting transfers between devices: 21.9 us -> 20.3 us
  Pallas kernels: 24.8 us -> 23.5 us
    ppermute x24, waiting for transfers between devices: 15.6 us -> 17.2 us  [swap(): return lax.ppermute(value, axis, [(i, i ^ distance) for i in range(size)])]
    ppermute x24, starting transfers between devices: 21.9 us -> 20.3 us  [swap(): return lax.ppermute(value, axis, [(i, i ^ distance) for i in range(size)])]
    pallas_call x9, Pallas kernels: 15.9 us -> 14.7 us  [call(): pl.pallas_call(kernel, out_shape=outs, in_specs=[SMEM] * len(scalars) + [...]
    dynamic_slice x1, local copies, waits for them, and re-layouts: 0.17 us -> 1.24 us  [shards(): lax.dynamic_slice_in_dim(proj, z * (width // planes), width // planes, 1)]
    unnamed x18 -> x20, local copies, waits for them, and re-layouts: 3.41 us -> 4.33 us
  transfers between devices with their start and end apart: 24 -> 24, of which waited for: 10 -> 12; matrix products, arithmetic and copies ran while one was open for 0% -> 2% of each run, Pallas kernels for 30% -> 28%
where the time goes in v10:
time: 68.2 us; the launch traced here: 67.9 us
  Pallas kernels  23.5 us (34%)
  starting transfers between devices  20.3 us (30%)
  waiting for transfers between devices  17.2 us (25%)
  local copies, waits for them, and re-layouts  5.56 us (8%)
  between operations  1.06 us (2%)
    ppermute x24, starting transfers between devices, swap(): return lax.ppermute(value, axis, [(i, i ^ distance) for i in range(size)])  20.3 us
    ppermute x24, waiting for transfers between devices, swap(): return lax.ppermute(value, axis, [(i, i ^ distance) for i in range(size)])  17.2 us
    pallas_call x9, Pallas kernels, call(): pl.pallas_call(kernel, out_shape=outs, in_specs=[SMEM] * len(scalars) + [...  14.7 us
    unnamed x20, local copies, waits for them, and re-layouts  4.33 us
    pallas_call x1, Pallas kernels, grad_enc_after(): pl.pallas_call(enc_kernel, grid=(samples // tile,), out_shape=[shape((sam...  3.28 us
    pallas_call x1, Pallas kernels, shards(): pl.pallas_call(functools.partial(proj_kernel, cuts), out_shape=shape((wid...  2.79 us
    pallas_call x1, Pallas kernels, shards(): pl.pallas_call(payload_kernel, out_shape=shape((size + TAIL, width), BF16...  1.67 us
  transfers between devices with their start and end apart: 24, of which 12 were waited for; matrix products, arithmetic and copies ran while one was open for 2% of the time, Pallas kernels for 28%

profile of v10, /device:TPU:0, one launch (start us, length us, event | category | flops | bytes accessed | tf_op | source)
XLA Modules:
  0.0 67.9 jit_solution(6515847895033842)
XLA Ops:
  0.6 1.7 %shard_map.96.refs_0_.refs_4_ = bf16[144,768]{1,0:T(8,128)(2,1)} custom-call(s32[1,128]{1,0:T(1,128)} %bitcast.12, s32[1,128]{1,0:T(1,128)} %bitcast.13, bf16[128,768]{1,0:T(8,128)(2,1)} %rows_hbm.1), custom_call_target="tpu_custom_call" | custom-call | tf_op jit(solution)/shard_map/pallas_call | solution.py:227
  2.8 3.5 %collective-permute-start.3 = (bf16[144,768]{1,0:T(8,128)(2,1)}, bf16[144,768]{1,0:T(8,128)(2,1)}, u32[]{:S(2)}, u32[]{:S(2)}) collective-permute-start(bf16[144,768]{1,0:T(8,128)(2,1)} %shard_map.96.refs_0_.refs_4_), channel_id=1, source_target_pairs={{0,6},{1,7},{2,4},{3,5},{4,2},{5,3},{6,0},{7,1},{8,14},{9,15},{10,... | collective-permute-start | bytes 663560 | tf_op jit(solution)/shard_map/ppermute | solution.py:55
  6.9 1.4 %copy-done = bf16[1024,768]{1,0:T(8,128)(2,1)S(1)} copy-done((bf16[1024,768]{1,0:T(8,128)(2,1)S(1)}, bf16[1024,768]{1,0:T(8,128)(2,1)}, u32[]{:S(2)}) %copy-start) | copy-done | bytes 1572888
  8.3 1.3 %copy-done.6 = bf16[768,768]{1,0:T(8,128)(2,1)S(1)} copy-done((bf16[768,768]{1,0:T(8,128)(2,1)S(1)}, bf16[768,768]{1,0:T(8,128)(2,1)}, u32[]{:S(2)}) %copy-start.6) | copy-done | bytes 1179672
  9.6 1.5 %shard_map.94.after_ref.hidden_t_ref = bf16[768,1024]{1,0:T(8,128)(2,1)S(1)} custom-call(bf16[1024,768]{1,0:T(8,128)(2,1)S(1)} %copy-done, bf16[768,768]{1,0:T(8,128)(2,1)S(1)} %copy-done.6), custom_call_target="tpu_custom_call" | custom-call | flops 1207959552 | bytes 6000000 | tf_op jit(solution)/shard_map/pallas_call | solution.py:31
  11.1 1.9 %shard_map.95.target_ref = bf16[512,1024]{1,0:T(8,128)(2,1)S(1)} custom-call(s32[8,1024]{1,0:T(8,128)S(1)} %bitcast.11, bf16[768,1024]{1,0:T(8,128)(2,1)S(1)} %shard_map.94.after_ref.hidden_t_ref), custom_call_target="tpu_custom_call" | custom-call | bytes 8000000 | tf_op jit(solution)/shard_map/pallas_call | solution.py:31
  14.6 2.0 %shard_map.97 = (bf16[256,1024]{1,0:T(8,128)(2,1)S(1)}, f32[128,768]{1,0:T(8,128)S(1)}, bf16[128,768]{1,0:T(8,128)(2,1)S(1)}) custom-call(s32[4,8]{1,0:T(4,128)S(1)} %bitcast.7, s32[1]{0:T(128)} %bitcast.me_ref, s32[1]{0:T(128)} %bitcast.2.z_ref, bf16[768,1024]{1,0:T(8,128)(2,1)S(1)} %shard_map.94.after_ref.hidden_t_ref, ...), custom_call_target="tpu_custom_call" | custom-call | flops 805306368 | bytes 5000000 | tf_op jit(solution)/shard_map/pallas_call | solution.py:31
  18.4 2.3 %shard_map.100 = (bf16[256,1024]{1,0:T(8,128)(2,1)S(1)}, f32[128,768]{1,0:T(8,128)S(1)}, bf16[128,768]{1,0:T(8,128)(2,1)S(1)}) custom-call(s32[4,8]{1,0:T(4,128)S(1)} %bitcast.8, s32[1]{0:T(128)} %bitcast.me_ref, s32[1]{0:T(128)} %bitcast.2.z_ref, bf16[768,1024]{1,0:T(8,128)(2,1)S(1)} %shard_map.94.after_ref.hidden_t_ref, ...), custom_call_target="tpu_custom_call" | custom-call | flops 805306368 | bytes 5000000 | tf_op jit(solution)/shard_map/pallas_call | solution.py:31
  21.3 2.0 %shard_map.101 = (bf16[256,1024]{1,0:T(8,128)(2,1)S(1)}, f32[128,768]{1,0:T(8,128)S(1)}, bf16[128,768]{1,0:T(8,128)(2,1)S(1)}) custom-call(s32[4,8]{1,0:T(4,128)S(1)} %bitcast.9, s32[1]{0:T(128)} %bitcast.me_ref, s32[1]{0:T(128)} %bitcast.2.z_ref, bf16[768,1024]{1,0:T(8,128)(2,1)S(1)} %shard_map.94.after_ref.hidden_t_ref, ...), custom_call_target="tpu_custom_call" | custom-call | flops 805306368 | bytes 5000000 | tf_op jit(solution)/shard_map/pallas_call | solution.py:31
  23.3 2.1 %collective-permute-done.5.value_ref = bf16[144,768]{1,0:T(8,128)(2,1)S(1)} collective-permute-done((bf16[144,768]{1,0:T(8,128)(2,1)S(1)}, bf16[144,768]{1,0:T(8,128)(2,1)S(1)}, u32[]{:S(2)}, u32[]{:S(2)}) %collective-permute-start.5) | collective-permute-done | bytes 221216 | tf_op jit(solution)/shard_map/ppermute | solution.py:55
  26.0 1.5 %collective-permute-start.11 = (bf16[128,768]{1,0:T(8,128)(2,1)S(1)}, bf16[128,768]{1,0:T(8,128)(2,1)S(1)}, u32[]{:S(2)}, u32[]{:S(2)}) collective-permute-start(bf16[128,768]{1,0:T(8,128)(2,1)S(1)} %add_convert_fusion.2.refs_3_.refs_12_), channel_id=1, source_target_pairs={{0,6},{1,7},{2,4},{3,5},{4,2},{5,3},{6,0},{7,1},{8,14},{9,15},{10,... | collective-permute-start | bytes 589832 | tf_op jit(solution)/shard_map/ppermute | solution.py:55
  27.5 2.0 %shard_map.103 = (bf16[256,1024]{1,0:T(8,128)(2,1)S(1)}, f32[128,768]{1,0:T(8,128)S(1)}, bf16[128,768]{1,0:T(8,128)(2,1)S(1)}) custom-call(s32[4,8]{1,0:T(4,128)S(1)} %bitcast.10, s32[1]{0:T(128)} %bitcast.me_ref, s32[1]{0:T(128)} %bitcast.2.z_ref, bf16[768,1024]{1,0:T(8,128)(2,1)S(1)} %shard_map.94.after_ref.hidden_t_ref, ...), custom_call_target="tpu_custom_call" | custom-call | flops 805306368 | bytes 5000000 | tf_op jit(solution)/shard_map/pallas_call | solution.py:31
  31.0 1.6 %collective-permute-start.13 = (bf16[128,768]{1,0:T(8,128)(2,1)S(1)}, bf16[128,768]{1,0:T(8,128)(2,1)S(1)}, u32[]{:S(2)}, u32[]{:S(2)}) collective-permute-start(bf16[128,768]{1,0:T(8,128)(2,1)S(1)} %add_convert_fusion.refs_14_), channel_id=1, source_target_pairs={{0,4},{1,5},{2,6},{3,7},{4,0},{5,1},{6,2},{7,3},{8,12},{9,13},{10,... | collective-permute-start | bytes 589832 | tf_op jit(solution)/shard_map/ppermute | solution.py:55
  32.7 2.9 %shard_map.104 = (bf16[1024,768]{1,0:T(8,128)(2,1)S(1)}, bf16[1024,768]{1,0:T(8,128)(2,1)S(1)}) custom-call(s32[1]{0:T(128)} %bitcast.me_ref, bf16[256,1024]{1,0:T(8,128)(2,1)S(1)} %get-tuple-element.23.refs_0_.refs_2_, bf16[256,1024]{1,0:T(8,128)(2,1)S(1)} %get-tuple-element.25.refs_0_.refs_2_.refs_1_, bf16[256,1024]{1,0:T(8,128)(2,1)S(1)} %get-tuple-element.28.refs_2_, ...), custom_call_target="tpu_custom_call" | custom-call | flops 1610612736 | bytes 5000000 | tf_op jit(solution)/shard_map/pallas_call | solution.py:31
  35.6 1.4 %collective-permute-done.12.refs_1_ = bf16[128,768]{1,0:T(8,128)(2,1)S(1)} collective-permute-done((bf16[128,768]{1,0:T(8,128)(2,1)S(1)}, bf16[128,768]{1,0:T(8,128)(2,1)S(1)}, u32[]{:S(2)}, u32[]{:S(2)}) %collective-permute-start.12) | collective-permute-done | bytes 196640 | tf_op jit(solution)/shard_map/ppermute | solution.py:55
  38.1 1.6 %collective-permute-start.14 = (bf16[64,768]{1,0:T(8,128)(2,1)S(1)}, bf16[64,768]{1,0:T(8,128)(2,1)S(1)}, u32[]{:S(2)}, u32[]{:S(2)}) collective-permute-start(bf16[64,768]{1,0:T(8,128)(2,1)S(1)} %get-tuple-element.37), channel_id=1, source_target_pairs={{0,8},{8,0},{16,24},{24,16},{1,9},{9,1},{17,25},{25,17},{2,10},{10... | collective-permute-start | bytes 294920 | tf_op jit(solution)/shard_map/ppermute | solution.py:55
  39.8 3.0 %collective-permute-done.14 = bf16[64,768]{1,0:T(8,128)(2,1)S(1)} collective-permute-done((bf16[64,768]{1,0:T(8,128)(2,1)S(1)}, bf16[64,768]{1,0:T(8,128)(2,1)S(1)}, u32[]{:S(2)}, u32[]{:S(2)}) %collective-permute-start.14) | collective-permute-done | bytes 98336 | tf_op jit(solution)/shard_map/ppermute | solution.py:55
  42.8 2.7 %collective-permute-start.15 = (bf16[64,768]{1,0:T(8,128)(2,1)S(1)}, bf16[64,768]{1,0:T(8,128)(2,1)S(1)}, u32[]{:S(2)}, u32[]{:S(2)}) collective-permute-start(bf16[64,768]{1,0:T(8,128)(2,1)S(1)} %add_convert_fusion.4.after_ref), channel_id=1, source_target_pairs={{0,16},{8,24},{16,0},{24,8},{1,17},{9,25},{17,1},{25,9},{2,18},{10... | collective-permute-start | bytes 294920 | tf_op jit(solution)/shard_map/ppermute | solution.py:55
  45.5 3.3 %shard_map.106 = (f32[1024,768]{1,0:T(8,128)}, f32[8,128]{1,0:T(8,128)S(1)}) custom-call(bf16[1024,768]{1,0:T(8,128)(2,1)S(1)} %get-tuple-element.33.refs_3_.grad_hidden_ref, bf16[768,768]{1,0:T(8,128)(2,1)S(1)} %copy-done.7, bf16[64,768]{1,0:T(8,128)(2,1)S(1)} %add_convert_fusion.4.after_ref), custom_call_target="tpu_custom_call" | custom-call | flops 1207959552 | bytes 6000000 | tf_op jit(solution)/shard_map/pallas_call | solution.py:300
  48.8 1.6 %collective-permute-start.16 = (bf16[64,768]{1,0:T(8,128)(2,1)S(1)}, bf16[64,768]{1,0:T(8,128)(2,1)S(1)}, u32[]{:S(2)}, u32[]{:S(2)}) collective-permute-start(bf16[64,768]{1,0:T(8,128)(2,1)S(1)} %add_convert_fusion.3.refs_0_), channel_id=1, source_target_pairs={{0,8},{8,0},{16,24},{24,16},{1,9},{9,1},{17,25},{25,17},{2,10},{10... | collective-permute-start | bytes 294920 | tf_op jit(solution)/shard_map/ppermute | solution.py:55
  50.5 3.0 %collective-permute-done.16.refs_1_ = bf16[64,768]{1,0:T(8,128)(2,1)S(1)} collective-permute-done((bf16[64,768]{1,0:T(8,128)(2,1)S(1)}, bf16[64,768]{1,0:T(8,128)(2,1)S(1)}, u32[]{:S(2)}, u32[]{:S(2)}) %collective-permute-start.16) | collective-permute-done | bytes 98336 | tf_op jit(solution)/shard_map/ppermute | solution.py:55
  53.6 1.7 %collective-permute-start.18 = (bf16[768,128]{1,0:T(8,128)(2,1)S(1)}, bf16[768,128]{1,0:T(8,128)(2,1)S(1)}, u32[]{:S(2)}, u32[]{:S(2)}) collective-permute-start(bf16[768,128]{1,0:T(8,128)(2,1)S(1)} %shard_map.108.whole_ref.refs_0_), channel_id=1, source_target_pairs={{0,2},{1,3},{2,0},{3,1},{4,6},{5,7},{6,4},{7,5},{8,10},{9,11},{10,... | collective-permute-start | bytes 589832 | tf_op jit(solution)/shard_map/ppermute | solution.py:55
  60.2 3.0 %collective-permute-done.20.value_ref = bf16[768,128]{1,0:T(8,128)(2,1)S(1)} collective-permute-done((bf16[768,128]{1,0:T(8,128)(2,1)S(1)}, bf16[768,128]{1,0:T(8,128)(2,1)S(1)}, u32[]{:S(2)}, u32[]{:S(2)}) %collective-permute-start.20) | collective-permute-done | bytes 196640 | tf_op jit(solution)/shard_map/ppermute | solution.py:55
  65.0 2.8 %shard_map.113 = f32[768,768]{1,0:T(8,128)} custom-call(s32[1]{0:T(128)} %bitcast.me_ref, bf16[768,128]{1,0:T(8,128)(2,1)S(1)} %shard_map.108.whole_ref.refs_0_, bf16[768,128]{1,0:T(8,128)(2,1)S(1)} %collective-permute-done.17.refs_1_, bf16[768,128]{1,0:T(8,128)(2,1)S(1)} %shard_map.110.refs_2_, bf16[768,128]{1,0:T(8,128)(2,1)S(1)} %collective-permute-done.19.refs_3_, ...), custom_call_target="tpu_custom_call" | custom-call | flops 1207959552 | bytes 6000000 | tf_op jit(solution)/shard_map/pallas_call | solution.py:375
  (71 shorter events, 15.1 us)
Async XLA Ops:
  2.3 10.7 %collective-permute-start = (bf16[144,768]{1,0:T(8,128)(2,1)}, bf16[144,768]{1,0:T(8,128)(2,1)S(1)}, u32[]{:S(2)}, u32[]{:S(2)}) collective-permute-start(bf16[144,768]{1,0:T(8,128)(2,1)} %shard_map.96.refs_0_.refs_4_), channel_id=1, source_target_pairs={{0,1},{1,0},{2,3},{3,2},{4,5},{5,4},{6,7},{7,6},{8,9},{9,8},{10,11... | collective-permute-start | bytes 663560 | tf_op jit(solution)/shard_map/ppermute | solution.py:55
  2.8 13.8 %collective-permute-start.3 = (bf16[144,768]{1,0:T(8,128)(2,1)}, bf16[144,768]{1,0:T(8,128)(2,1)}, u32[]{:S(2)}, u32[]{:S(2)}) collective-permute-start(bf16[144,768]{1,0:T(8,128)(2,1)} %shard_map.96.refs_0_.refs_4_), channel_id=1, source_target_pairs={{0,6},{1,7},{2,4},{3,5},{4,2},{5,3},{6,0},{7,1},{8,14},{9,15},{10,... | collective-permute-start | bytes 663560 | tf_op jit(solution)/shard_map/ppermute | solution.py:55
  6.3 11.2 %collective-permute-start.1 = (bf16[144,768]{1,0:T(8,128)(2,1)}, bf16[144,768]{1,0:T(8,128)(2,1)S(1)}, u32[]{:S(2)}, u32[]{:S(2)}) collective-permute-start(bf16[144,768]{1,0:T(8,128)(2,1)} %shard_map.96.refs_0_.refs_4_), channel_id=1, source_target_pairs={{0,2},{1,3},{2,0},{3,1},{4,6},{5,7},{6,4},{7,5},{8,10},{9,11},{10,... | collective-permute-start | bytes 663560 | tf_op jit(solution)/shard_map/ppermute | solution.py:55
  16.6 1.8 %collective-permute-start.4 = (bf16[144,768]{1,0:T(8,128)(2,1)}, bf16[144,768]{1,0:T(8,128)(2,1)S(1)}, u32[]{:S(2)}, u32[]{:S(2)}) collective-permute-start(bf16[144,768]{1,0:T(8,128)(2,1)} %shard_map.99.refs_0_.refs_10_), channel_id=1, source_target_pairs={{0,1},{1,0},{2,3},{3,2},{4,5},{5,4},{6,7},{7,6},{8,9},{9,8},{10,11... | collective-permute-start | bytes 663560 | tf_op jit(solution)/shard_map/ppermute | solution.py:55
  17.6 3.7 %collective-permute-start.2 = (bf16[144,768]{1,0:T(8,128)(2,1)S(1)}, bf16[144,768]{1,0:T(8,128)(2,1)S(1)}, u32[]{:S(2)}, u32[]{:S(2)}) collective-permute-start(bf16[144,768]{1,0:T(8,128)(2,1)S(1)} %shard_map.98.refs_3_.refs_0_.refs_6_), channel_id=1, source_target_pairs={{0,1},{1,0},{2,3},{3,2},{4,5},{5,4},{6,7},{7,6},{8,9},{9,8},{10,11... | collective-permute-start | bytes 663560 | tf_op jit(solution)/shard_map/ppermute | solution.py:55
  17.6 7.8 %collective-permute-start.5 = (bf16[144,768]{1,0:T(8,128)(2,1)S(1)}, bf16[144,768]{1,0:T(8,128)(2,1)S(1)}, u32[]{:S(2)}, u32[]{:S(2)}) collective-permute-start(bf16[144,768]{1,0:T(8,128)(2,1)S(1)} %copy-done.2), channel_id=1, source_target_pairs={{0,4},{1,5},{2,6},{3,7},{4,0},{5,1},{6,2},{7,3},{8,12},{9,13},{10,... | collective-permute-start | bytes 663560 | tf_op jit(solution)/shard_map/ppermute | solution.py:55
  20.7 5.2 %collective-permute-start.7 = (bf16[128,768]{1,0:T(8,128)(2,1)S(1)}, bf16[128,768]{1,0:T(8,128)(2,1)S(1)}, u32[]{:S(2)}, u32[]{:S(2)}) collective-permute-start(bf16[128,768]{1,0:T(8,128)(2,1)S(1)} %get-tuple-element.27), channel_id=1, source_target_pairs={{0,1},{1,0},{2,3},{3,2},{4,5},{5,4},{6,7},{7,6},{8,9},{9,8},{10,11... | collective-permute-start | bytes 589832 | tf_op jit(solution)/shard_map/ppermute | solution.py:55
  20.9 11.7 %collective-permute-start.10 = (bf16[128,768]{1,0:T(8,128)(2,1)S(1)}, bf16[128,768]{1,0:T(8,128)(2,1)S(1)}, u32[]{:S(2)}, u32[]{:S(2)}) collective-permute-start(bf16[128,768]{1,0:T(8,128)(2,1)S(1)} %get-tuple-element.35), channel_id=1, source_target_pairs={{0,1},{1,0},{2,3},{3,2},{4,5},{5,4},{6,7},{7,6},{8,9},{9,8},{10,11... | collective-permute-start | bytes 589832 | tf_op jit(solution)/shard_map/ppermute | solution.py:55
  25.4 2.1 %collective-permute-start.6 = (bf16[144,768]{1,0:T(8,128)(2,1)S(1)}, bf16[144,768]{1,0:T(8,128)(2,1)S(1)}, u32[]{:S(2)}, u32[]{:S(2)}) collective-permute-start(bf16[144,768]{1,0:T(8,128)(2,1)S(1)} %shard_map.102.refs_0_.refs_8_), channel_id=1, source_target_pairs={{0,1},{1,0},{2,3},{3,2},{4,5},{5,4},{6,7},{7,6},{8,9},{9,8},{10,11... | collective-permute-start | bytes 663560 | tf_op jit(solution)/shard_map/ppermute | solution.py:55
  25.4 4.1 %collective-permute-start.8 = (bf16[128,768]{1,0:T(8,128)(2,1)S(1)}, bf16[128,768]{1,0:T(8,128)(2,1)S(1)}, u32[]{:S(2)}, u32[]{:S(2)}) collective-permute-start(bf16[128,768]{1,0:T(8,128)(2,1)S(1)} %get-tuple-element.30), channel_id=1, source_target_pairs={{0,1},{1,0},{2,3},{3,2},{4,5},{5,4},{6,7},{7,6},{8,9},{9,8},{10,11... | collective-permute-start | bytes 589832 | tf_op jit(solution)/shard_map/ppermute | solution.py:55
  26.0 9.6 %collective-permute-start.11 = (bf16[128,768]{1,0:T(8,128)(2,1)S(1)}, bf16[128,768]{1,0:T(8,128)(2,1)S(1)}, u32[]{:S(2)}, u32[]{:S(2)}) collective-permute-start(bf16[128,768]{1,0:T(8,128)(2,1)S(1)} %add_convert_fusion.2.refs_3_.refs_12_), channel_id=1, source_target_pairs={{0,6},{1,7},{2,4},{3,5},{4,2},{5,3},{6,0},{7,1},{8,14},{9,15},{10,... | collective-permute-start | bytes 589832 | tf_op jit(solution)/shard_map/ppermute | solution.py:55
  29.5 1.5 %collective-permute-start.9 = (bf16[128,768]{1,0:T(8,128)(2,1)S(1)}, bf16[128,768]{1,0:T(8,128)(2,1)S(1)}, u32[]{:S(2)}, u32[]{:S(2)}) collective-permute-start(bf16[128,768]{1,0:T(8,128)(2,1)S(1)} %get-tuple-element.32), channel_id=1, source_target_pairs={{0,1},{1,0},{2,3},{3,2},{4,5},{5,4},{6,7},{7,6},{8,9},{9,8},{10,11... | collective-permute-start | bytes 589832 | tf_op jit(solution)/shard_map/ppermute | solution.py:55
  29.6 7.4 %collective-permute-start.12 = (bf16[128,768]{1,0:T(8,128)(2,1)S(1)}, bf16[128,768]{1,0:T(8,128)(2,1)S(1)}, u32[]{:S(2)}, u32[]{:S(2)}) collective-permute-start(bf16[128,768]{1,0:T(8,128)(2,1)S(1)} %add_convert_fusion.1.refs_13_), channel_id=1, source_target_pairs={{0,2},{1,3},{2,0},{3,1},{4,6},{5,7},{6,4},{7,5},{8,10},{9,11},{10,... | collective-permute-start | bytes 589832 | tf_op jit(solution)/shard_map/ppermute | solution.py:55
  31.0 7.0 %collective-permute-start.13 = (bf16[128,768]{1,0:T(8,128)(2,1)S(1)}, bf16[128,768]{1,0:T(8,128)(2,1)S(1)}, u32[]{:S(2)}, u32[]{:S(2)}) collective-permute-start(bf16[128,768]{1,0:T(8,128)(2,1)S(1)} %add_convert_fusion.refs_14_), channel_id=1, source_target_pairs={{0,4},{1,5},{2,6},{3,7},{4,0},{5,1},{6,2},{7,3},{8,12},{9,13},{10,... | collective-permute-start | bytes 589832 | tf_op jit(solution)/shard_map/ppermute | solution.py:55
  38.1 4.7 %collective-permute-start.14 = (bf16[64,768]{1,0:T(8,128)(2,1)S(1)}, bf16[64,768]{1,0:T(8,128)(2,1)S(1)}, u32[]{:S(2)}, u32[]{:S(2)}) collective-permute-start(bf16[64,768]{1,0:T(8,128)(2,1)S(1)} %get-tuple-element.37), channel_id=1, source_target_pairs={{0,8},{8,0},{16,24},{24,16},{1,9},{9,1},{17,25},{25,17},{2,10},{10... | collective-permute-start | bytes 294920 | tf_op jit(solution)/shard_map/ppermute | solution.py:55
  42.8 5.9 %collective-permute-start.15 = (bf16[64,768]{1,0:T(8,128)(2,1)S(1)}, bf16[64,768]{1,0:T(8,128)(2,1)S(1)}, u32[]{:S(2)}, u32[]{:S(2)}) collective-permute-start(bf16[64,768]{1,0:T(8,128)(2,1)S(1)} %add_convert_fusion.4.after_ref), channel_id=1, source_target_pairs={{0,16},{8,24},{16,0},{24,8},{1,17},{9,25},{17,1},{25,9},{2,18},{10... | collective-permute-start | bytes 294920 | tf_op jit(solution)/shard_map/ppermute | solution.py:55
  48.8 4.7 %collective-permute-start.16 = (bf16[64,768]{1,0:T(8,128)(2,1)S(1)}, bf16[64,768]{1,0:T(8,128)(2,1)S(1)}, u32[]{:S(2)}, u32[]{:S(2)}) collective-permute-start(bf16[64,768]{1,0:T(8,128)(2,1)S(1)} %add_convert_fusion.3.refs_0_), channel_id=1, source_target_pairs={{0,8},{8,0},{16,24},{24,16},{1,9},{9,1},{17,25},{25,17},{2,10},{10... | collective-permute-start | bytes 294920 | tf_op jit(solution)/shard_map/ppermute | solution.py:55
  53.6 6.6 %collective-permute-start.18 = (bf16[768,128]{1,0:T(8,128)(2,1)S(1)}, bf16[768,128]{1,0:T(8,128)(2,1)S(1)}, u32[]{:S(2)}, u32[]{:S(2)}) collective-permute-start(bf16[768,128]{1,0:T(8,128)(2,1)S(1)} %shard_map.108.whole_ref.refs_0_), channel_id=1, source_target_pairs={{0,2},{1,3},{2,0},{3,1},{4,6},{5,7},{6,4},{7,5},{8,10},{9,11},{10,... | collective-permute-start | bytes 589832 | tf_op jit(solution)/shard_map/ppermute | solution.py:55
  55.3 7.9 %collective-permute-start.20 = (bf16[768,128]{1,0:T(8,128)(2,1)S(1)}, bf16[768,128]{1,0:T(8,128)(2,1)S(1)}, u32[]{:S(2)}, u32[]{:S(2)}) collective-permute-start(bf16[768,128]{1,0:T(8,128)(2,1)S(1)} %shard_map.108.whole_ref.refs_0_), channel_id=1, source_target_pairs={{0,4},{1,5},{2,6},{3,7},{4,0},{5,1},{6,2},{7,3},{8,12},{9,13},{10,... | collective-permute-start | bytes 589832 | tf_op jit(solution)/shard_map/ppermute | solution.py:55
  56.1 7.1 %collective-permute-start.22 = (bf16[768,128]{1,0:T(8,128)(2,1)S(1)}, bf16[768,128]{1,0:T(8,128)(2,1)S(1)}, u32[]{:S(2)}, u32[]{:S(2)}) collective-permute-start(bf16[768,128]{1,0:T(8,128)(2,1)S(1)} %shard_map.108.whole_ref.refs_0_), channel_id=1, source_target_pairs={{0,6},{1,7},{2,4},{3,5},{4,2},{5,3},{6,0},{7,1},{8,14},{9,15},{10,... | collective-permute-start | bytes 589832 | tf_op jit(solution)/shard_map/ppermute | solution.py:55
  58.4 5.3 %collective-permute-start.17 = (bf16[768,128]{1,0:T(8,128)(2,1)S(1)}, bf16[768,128]{1,0:T(8,128)(2,1)S(1)}, u32[]{:S(2)}, u32[]{:S(2)}) collective-permute-start(bf16[768,128]{1,0:T(8,128)(2,1)S(1)} %shard_map.108.whole_ref.refs_0_), channel_id=1, source_target_pairs={{0,1},{1,0},{2,3},{3,2},{4,5},{5,4},{6,7},{7,6},{8,9},{9,8},{10,11... | collective-permute-start | bytes 589832 | tf_op jit(solution)/shard_map/ppermute | solution.py:55
  60.2 3.6 %collective-permute-start.19 = (bf16[768,128]{1,0:T(8,128)(2,1)S(1)}, bf16[768,128]{1,0:T(8,128)(2,1)S(1)}, u32[]{:S(2)}, u32[]{:S(2)}) collective-permute-start(bf16[768,128]{1,0:T(8,128)(2,1)S(1)} %shard_map.110.refs_2_), channel_id=1, source_target_pairs={{0,1},{1,0},{2,3},{3,2},{4,5},{5,4},{6,7},{7,6},{8,9},{9,8},{10,11... | collective-permute-start | bytes 589832 | tf_op jit(solution)/shard_map/ppermute | solution.py:55
  63.2 1.4 %collective-permute-start.21 = (bf16[768,128]{1,0:T(8,128)(2,1)S(1)}, bf16[768,128]{1,0:T(8,128)(2,1)S(1)}, u32[]{:S(2)}, u32[]{:S(2)}) collective-permute-start(bf16[768,128]{1,0:T(8,128)(2,1)S(1)} %shard_map.111.refs_4_), channel_id=1, source_target_pairs={{0,1},{1,0},{2,3},{3,2},{4,5},{5,4},{6,7},{7,6},{8,9},{9,8},{10,11... | collective-permute-start | bytes 589832 | tf_op jit(solution)/shard_map/ppermute | solution.py:55
  63.2 1.7 %collective-permute-start.23 = (bf16[768,128]{1,0:T(8,128)(2,1)S(1)}, bf16[768,128]{1,0:T(8,128)(2,1)S(1)}, u32[]{:S(2)}, u32[]{:S(2)}) collective-permute-start(bf16[768,128]{1,0:T(8,128)(2,1)S(1)} %shard_map.112.refs_6_), channel_id=1, source_target_pairs={{0,1},{1,0},{2,3},{3,2},{4,5},{5,4},{6,7},{7,6},{8,9},{9,8},{10,11... | collective-permute-start | bytes 589832 | tf_op jit(solution)/shard_map/ppermute | solution.py:55
  (10 other events, 28.4 us)

commit v11 on v9

--- a/solution.py
+++ b/solution.py
@@ -255,11 +255,8 @@
     order = [0] + far + near
     for at, g in enumerate(order):
         after = [grads[order[at - 1]]] if at else []
-        if at + 1 < len(order):
-            ahead = 2 * order[at + 1]
-            got[ahead] = gate(got[ahead], grads[order[at - 1]] if at else hidden_t)
-            got[ahead + 1] = swap(got[ahead], "label", 1)
-            after.append(got[ahead])
+        if at == 1:
+            after.extend(got[2 * ahead] for ahead in order[2:])
         if at >= 3:
             after.append(moved[order[at - 2]])
         grads[g], kept[g], sent = call(
@@ -276,6 +273,9 @@
             flops=8 * samples * size * width,
             nbytes=5_000_000,
         )
+        for ahead in order[1:] if at == 0 else []:
+            got[2 * ahead] = gate(got[2 * ahead], grads[g])
+            got[2 * ahead + 1] = swap(got[2 * ahead], "label", 1)
         from_core[g] = swap(sent, "label", 1)
         if g:
             moved[g] = (kept[g] + from_core[g].astype(F32)).astype(BF16)

time: 67.4 us -> 65.4 us (0.970)
  Pallas kernels: 24.8 us -> 22.1 us
  waiting for transfers between devices: 15.6 us -> 17.6 us
  starting transfers between devices: 21.9 us -> 20.3 us
    pallas_call x9, Pallas kernels: 15.9 us -> 13.3 us  [call(): pl.pallas_call(kernel, out_shape=outs, in_specs=[SMEM] * len(scalars) + [...]
    ppermute x24, waiting for transfers between devices: 15.6 us -> 17.6 us  [swap(): return lax.ppermute(value, axis, [(i, i ^ distance) for i in range(size)])]
    ppermute x24, starting transfers between devices: 21.9 us -> 20.3 us  [swap(): return lax.ppermute(value, axis, [(i, i ^ distance) for i in range(size)])]
    unnamed x18 -> x16, local copies, waits for them, and re-layouts: 3.41 us -> 3.59 us
  transfers between devices with their start and end apart: 24 -> 24, of which waited for: 10 -> 10; matrix products, arithmetic and copies ran while one was open for 0% -> 1% of each run, Pallas kernels for 30% -> 27%
where the time goes in v11:
time: 65.4 us; the launch traced here: 65.1 us
  Pallas kernels  22.1 us (34%)
  starting transfers between devices  20.3 us (31%)
  waiting for transfers between devices  17.6 us (27%)
  local copies, waits for them, and re-layouts  3.76 us (6%)
  between operations  1.07 us (2%)
    ppermute x24, starting transfers between devices, swap(): return lax.ppermute(value, axis, [(i, i ^ distance) for i in range(size)])  20.3 us
    ppermute x24, waiting for transfers between devices, swap(): return lax.ppermute(value, axis, [(i, i ^ distance) for i in range(size)])  17.6 us
    pallas_call x9, Pallas kernels, call(): pl.pallas_call(kernel, out_shape=outs, in_specs=[SMEM] * len(scalars) + [...  13.3 us
    unnamed x16, local copies, waits for them, and re-layouts  3.59 us
    pallas_call x1, Pallas kernels, grad_enc_after(): pl.pallas_call(enc_kernel, grid=(samples // tile,), out_shape=[shape((sam...  3.28 us
    pallas_call x1, Pallas kernels, shards(): pl.pallas_call(functools.partial(proj_kernel, cuts), out_shape=shape((wid...  2.76 us
    pallas_call x1, Pallas kernels, shards(): pl.pallas_call(payload_kernel, out_shape=shape((size + TAIL, width), BF16...  1.76 us
  transfers between devices with their start and end apart: 24, of which 10 were waited for; matrix products, arithmetic and copies ran while one was open for 1% of the time, Pallas kernels for 27%

profile of v11, /device:TPU:0, one launch (start us, length us, event | category | flops | bytes accessed | tf_op | source)
XLA Modules:
  0.0 65.1 jit_solution(11887085085347260858)
XLA Ops:
  0.6 1.8 %shard_map.96.refs_0_.refs_4_ = bf16[144,768]{1,0:T(8,128)(2,1)} custom-call(s32[1,128]{1,0:T(1,128)} %bitcast.12, s32[1,128]{1,0:T(1,128)} %bitcast.13, bf16[128,768]{1,0:T(8,128)(2,1)} %rows_hbm.1), custom_call_target="tpu_custom_call" | custom-call | tf_op jit(solution)/shard_map/pallas_call | solution.py:227
  2.9 3.5 %collective-permute-start.3 = (bf16[144,768]{1,0:T(8,128)(2,1)}, bf16[144,768]{1,0:T(8,128)(2,1)S(1)}, u32[]{:S(2)}, u32[]{:S(2)}) collective-permute-start(bf16[144,768]{1,0:T(8,128)(2,1)} %shard_map.96.refs_0_.refs_4_), channel_id=1, source_target_pairs={{0,6},{1,7},{2,4},{3,5},{4,2},{5,3},{6,0},{7,1},{8,14},{9,15},{10,... | collective-permute-start | bytes 663560 | tf_op jit(solution)/shard_map/ppermute | solution.py:55
  7.9 1.9 %shard_map.94.after_ref.target_ref = bf16[512,1024]{1,0:T(8,128)(2,1)S(1)} custom-call(s32[8,1024]{1,0:T(8,128)S(1)} %bitcast.11), custom_call_target="tpu_custom_call" | custom-call | bytes 8000000 | tf_op jit(solution)/shard_map/pallas_call | solution.py:31
  9.8 1.4 %copy-done = bf16[1024,768]{1,0:T(8,128)(2,1)S(1)} copy-done((bf16[1024,768]{1,0:T(8,128)(2,1)S(1)}, bf16[1024,768]{1,0:T(8,128)(2,1)}, u32[]{:S(2)}) %copy-start) | copy-done | bytes 1572888
  11.2 1.5 %shard_map.95.hidden_t_ref = bf16[768,1024]{1,0:T(8,128)(2,1)S(1)} custom-call(bf16[1024,768]{1,0:T(8,128)(2,1)S(1)} %copy-done, bf16[768,768]{1,0:T(8,128)(2,1)S(1)} %copy-done.2, bf16[512,1024]{1,0:T(8,128)(2,1)S(1)} %shard_map.94.after_ref.target_ref), custom_call_target="tpu_custom_call" | custom-call | flops 1207959552 | bytes 6000000 | tf_op jit(solution)/shard_map/pallas_call | solution.py:31
  12.7 1.9 %shard_map.97 = (bf16[256,1024]{1,0:T(8,128)(2,1)S(1)}, f32[128,768]{1,0:T(8,128)S(1)}, bf16[128,768]{1,0:T(8,128)(2,1)S(1)}) custom-call(s32[4,8]{1,0:T(4,128)S(1)} %bitcast.7, s32[1]{0:T(128)} %bitcast.me_ref, s32[1]{0:T(128)} %bitcast.2.z_ref, bf16[768,1024]{1,0:T(8,128)(2,1)S(1)} %shard_map.95.hidden_t_ref, ...), custom_call_target="tpu_custom_call" | custom-call | flops 805306368 | bytes 5000000 | tf_op jit(solution)/shard_map/pallas_call | solution.py:31
  14.8 3.0 %collective-permute-done.1.value_ref = bf16[144,768]{1,0:T(8,128)(2,1)S(1)} collective-permute-done((bf16[144,768]{1,0:T(8,128)(2,1)}, bf16[144,768]{1,0:T(8,128)(2,1)S(1)}, u32[]{:S(2)}, u32[]{:S(2)}) %collective-permute-start.1) | collective-permute-done | bytes 221216 | tf_op jit(solution)/shard_map/ppermute | solution.py:55
  17.8 1.9 %shard_map.101 = (bf16[256,1024]{1,0:T(8,128)(2,1)S(1)}, f32[128,768]{1,0:T(8,128)S(1)}, bf16[128,768]{1,0:T(8,128)(2,1)S(1)}) custom-call(s32[4,8]{1,0:T(4,128)S(1)} %bitcast.8, s32[1]{0:T(128)} %bitcast.me_ref, s32[1]{0:T(128)} %bitcast.2.z_ref, bf16[768,1024]{1,0:T(8,128)(2,1)S(1)} %shard_map.95.hidden_t_ref, ...), custom_call_target="tpu_custom_call" | custom-call | flops 805306368 | bytes 5000000 | tf_op jit(solution)/shard_map/pallas_call | solution.py:31
  20.8 1.9 %shard_map.102 = (bf16[256,1024]{1,0:T(8,128)(2,1)S(1)}, f32[128,768]{1,0:T(8,128)S(1)}, bf16[128,768]{1,0:T(8,128)(2,1)S(1)}) custom-call(s32[4,8]{1,0:T(4,128)S(1)} %bitcast.9, s32[1]{0:T(128)} %bitcast.me_ref, s32[1]{0:T(128)} %bitcast.2.z_ref, bf16[768,1024]{1,0:T(8,128)(2,1)S(1)} %shard_map.95.hidden_t_ref, ...), custom_call_target="tpu_custom_call" | custom-call | flops 805306368 | bytes 5000000 | tf_op jit(solution)/shard_map/pallas_call | solution.py:31
  22.9 2.3 %collective-permute-start.11 = (bf16[128,768]{1,0:T(8,128)(2,1)S(1)}, bf16[128,768]{1,0:T(8,128)(2,1)S(1)}, u32[]{:S(2)}, u32[]{:S(2)}) collective-permute-start(bf16[128,768]{1,0:T(8,128)(2,1)S(1)} %add_convert_fusion.2.refs_3_.refs_12_), channel_id=1, source_target_pairs={{0,6},{1,7},{2,4},{3,5},{4,2},{5,3},{6,0},{7,1},{8,14},{9,15},{10,... | collective-permute-start | bytes 589832 | tf_op jit(solution)/shard_map/ppermute | solution.py:55
  25.2 2.0 %shard_map.103 = (bf16[256,1024]{1,0:T(8,128)(2,1)S(1)}, f32[128,768]{1,0:T(8,128)S(1)}, bf16[128,768]{1,0:T(8,128)(2,1)S(1)}) custom-call(s32[4,8]{1,0:T(4,128)S(1)} %bitcast.10, s32[1]{0:T(128)} %bitcast.me_ref, s32[1]{0:T(128)} %bitcast.2.z_ref, bf16[768,1024]{1,0:T(8,128)(2,1)S(1)} %shard_map.95.hidden_t_ref, ...), custom_call_target="tpu_custom_call" | custom-call | flops 805306368 | bytes 5000000 | tf_op jit(solution)/shard_map/pallas_call | solution.py:31
  29.6 1.9 %shard_map.104 = (bf16[1024,768]{1,0:T(8,128)(2,1)S(1)}, bf16[1024,768]{1,0:T(8,128)(2,1)S(1)}) custom-call(s32[1]{0:T(128)} %bitcast.me_ref, bf16[256,1024]{1,0:T(8,128)(2,1)S(1)} %get-tuple-element.23.refs_0_.refs_2_, bf16[256,1024]{1,0:T(8,128)(2,1)S(1)} %get-tuple-element.25.refs_2_.refs_1_, bf16[256,1024]{1,0:T(8,128)(2,1)S(1)} %get-tuple-element.28.refs_2_, ...), custom_call_target="tpu_custom_call" | custom-call | flops 1610612736 | bytes 5000000 | tf_op jit(solution)/shard_map/pallas_call | solution.py:31
  31.6 3.3 %collective-permute-done.12.refs_1_ = bf16[128,768]{1,0:T(8,128)(2,1)S(1)} collective-permute-done((bf16[128,768]{1,0:T(8,128)(2,1)S(1)}, bf16[128,768]{1,0:T(8,128)(2,1)S(1)}, u32[]{:S(2)}, u32[]{:S(2)}) %collective-permute-start.12) | collective-permute-done | bytes 196640 | tf_op jit(solution)/shard_map/ppermute | solution.py:55
  35.9 1.6 %collective-permute-start.14 = (bf16[64,768]{1,0:T(8,128)(2,1)S(1)}, bf16[64,768]{1,0:T(8,128)(2,1)S(1)}, u32[]{:S(2)}, u32[]{:S(2)}) collective-permute-start(bf16[64,768]{1,0:T(8,128)(2,1)S(1)} %get-tuple-element.37), channel_id=1, source_target_pairs={{0,8},{8,0},{16,24},{24,16},{1,9},{9,1},{17,25},{25,17},{2,10},{10... | collective-permute-start | bytes 294920 | tf_op jit(solution)/shard_map/ppermute | solution.py:55
  37.5 3.0 %collective-permute-done.14 = bf16[64,768]{1,0:T(8,128)(2,1)S(1)} collective-permute-done((bf16[64,768]{1,0:T(8,128)(2,1)S(1)}, bf16[64,768]{1,0:T(8,128)(2,1)S(1)}, u32[]{:S(2)}, u32[]{:S(2)}) %collective-permute-start.14) | collective-permute-done | bytes 98336 | tf_op jit(solution)/shard_map/ppermute | solution.py:55
  40.6 2.7 %collective-permute-start.15 = (bf16[64,768]{1,0:T(8,128)(2,1)S(1)}, bf16[64,768]{1,0:T(8,128)(2,1)S(1)}, u32[]{:S(2)}, u32[]{:S(2)}) collective-permute-start(bf16[64,768]{1,0:T(8,128)(2,1)S(1)} %add_convert_fusion.4.after_ref), channel_id=1, source_target_pairs={{0,16},{8,24},{16,0},{24,8},{1,17},{9,25},{17,1},{25,9},{2,18},{10... | collective-permute-start | bytes 294920 | tf_op jit(solution)/shard_map/ppermute | solution.py:55
  43.2 3.3 %shard_map.106 = (f32[1024,768]{1,0:T(8,128)}, f32[8,128]{1,0:T(8,128)S(1)}) custom-call(bf16[1024,768]{1,0:T(8,128)(2,1)S(1)} %get-tuple-element.33.refs_3_.grad_hidden_ref, bf16[768,768]{1,0:T(8,128)(2,1)S(1)} %copy-done.2, bf16[64,768]{1,0:T(8,128)(2,1)S(1)} %add_convert_fusion.4.after_ref), custom_call_target="tpu_custom_call" | custom-call | flops 1207959552 | bytes 6000000 | tf_op jit(solution)/shard_map/pallas_call | solution.py:300
  46.6 1.6 %collective-permute-start.16 = (bf16[64,768]{1,0:T(8,128)(2,1)S(1)}, bf16[64,768]{1,0:T(8,128)(2,1)S(1)}, u32[]{:S(2)}, u32[]{:S(2)}) collective-permute-start(bf16[64,768]{1,0:T(8,128)(2,1)S(1)} %add_convert_fusion.3.refs_0_), channel_id=1, source_target_pairs={{0,8},{8,0},{16,24},{24,16},{1,9},{9,1},{17,25},{25,17},{2,10},{10... | collective-permute-start | bytes 294920 | tf_op jit(solution)/shard_map/ppermute | solution.py:55
  48.2 3.0 %collective-permute-done.16.refs_1_ = bf16[64,768]{1,0:T(8,128)(2,1)S(1)} collective-permute-done((bf16[64,768]{1,0:T(8,128)(2,1)S(1)}, bf16[64,768]{1,0:T(8,128)(2,1)S(1)}, u32[]{:S(2)}, u32[]{:S(2)}) %collective-permute-start.16) | collective-permute-done | bytes 98336 | tf_op jit(solution)/shard_map/ppermute | solution.py:55
  51.4 1.2 %collective-permute-start.18 = (bf16[768,128]{1,0:T(8,128)(2,1)S(1)}, bf16[768,128]{1,0:T(8,128)(2,1)S(1)}, u32[]{:S(2)}, u32[]{:S(2)}) collective-permute-start(bf16[768,128]{1,0:T(8,128)(2,1)S(1)} %shard_map.108.whole_ref.refs_0_), channel_id=1, source_target_pairs={{0,2},{1,3},{2,0},{3,1},{4,6},{5,7},{6,4},{7,5},{8,10},{9,11},{10,... | collective-permute-start | bytes 589832 | tf_op jit(solution)/shard_map/ppermute | solution.py:55
  53.6 1.3 %collective-permute-start.22 = (bf16[768,128]{1,0:T(8,128)(2,1)S(1)}, bf16[768,128]{1,0:T(8,128)(2,1)S(1)}, u32[]{:S(2)}, u32[]{:S(2)}) collective-permute-start(bf16[768,128]{1,0:T(8,128)(2,1)S(1)} %shard_map.108.whole_ref.refs_0_), channel_id=1, source_target_pairs={{0,6},{1,7},{2,4},{3,5},{4,2},{5,3},{6,0},{7,1},{8,14},{9,15},{10,... | collective-permute-start | bytes 589832 | tf_op jit(solution)/shard_map/ppermute | solution.py:55
  55.2 1.4 %copy-done.4 = bf16[1024,768]{1,0:T(8,128)(2,1)S(1)} copy-done((bf16[1024,768]{1,0:T(8,128)(2,1)S(1)}, bf16[1024,768]{1,0:T(8,128)(2,1)}, u32[]{:S(2)}) %copy-start.4) | copy-done | bytes 1572888
  58.2 2.3 %collective-permute-done.20.value_ref = bf16[768,128]{1,0:T(8,128)(2,1)S(1)} collective-permute-done((bf16[768,128]{1,0:T(8,128)(2,1)S(1)}, bf16[768,128]{1,0:T(8,128)(2,1)S(1)}, u32[]{:S(2)}, u32[]{:S(2)}) %collective-permute-start.20) | collective-permute-done | bytes 196640 | tf_op jit(solution)/shard_map/ppermute | solution.py:55
  62.2 2.8 %shard_map.113 = f32[768,768]{1,0:T(8,128)} custom-call(s32[1]{0:T(128)} %bitcast.me_ref, bf16[768,128]{1,0:T(8,128)(2,1)S(1)} %shard_map.108.whole_ref.refs_0_, bf16[768,128]{1,0:T(8,128)(2,1)S(1)} %collective-permute-done.17.refs_1_, bf16[768,128]{1,0:T(8,128)(2,1)S(1)} %shard_map.110.refs_2_, bf16[768,128]{1,0:T(8,128)(2,1)S(1)} %collective-permute-done.19.refs_3_, ...), custom_call_target="tpu_custom_call" | custom-call | flops 1207959552 | bytes 6000000 | tf_op jit(solution)/shard_map/pallas_call | solution.py:375
  (67 shorter events, 11.5 us)
Async XLA Ops:
  2.4 10.3 %collective-permute-start = (bf16[144,768]{1,0:T(8,128)(2,1)}, bf16[144,768]{1,0:T(8,128)(2,1)S(1)}, u32[]{:S(2)}, u32[]{:S(2)}) collective-permute-start(bf16[144,768]{1,0:T(8,128)(2,1)} %shard_map.96.refs_0_.refs_4_), channel_id=1, source_target_pairs={{0,1},{1,0},{2,3},{3,2},{4,5},{5,4},{6,7},{7,6},{8,9},{9,8},{10,11... | collective-permute-start | bytes 663560 | tf_op jit(solution)/shard_map/ppermute | solution.py:55
  2.9 11.7 %collective-permute-start.3 = (bf16[144,768]{1,0:T(8,128)(2,1)}, bf16[144,768]{1,0:T(8,128)(2,1)S(1)}, u32[]{:S(2)}, u32[]{:S(2)}) collective-permute-start(bf16[144,768]{1,0:T(8,128)(2,1)} %shard_map.96.refs_0_.refs_4_), channel_id=1, source_target_pairs={{0,6},{1,7},{2,4},{3,5},{4,2},{5,3},{6,0},{7,1},{8,14},{9,15},{10,... | collective-permute-start | bytes 663560 | tf_op jit(solution)/shard_map/ppermute | solution.py:55
  6.5 11.3 %collective-permute-start.1 = (bf16[144,768]{1,0:T(8,128)(2,1)}, bf16[144,768]{1,0:T(8,128)(2,1)S(1)}, u32[]{:S(2)}, u32[]{:S(2)}) collective-permute-start(bf16[144,768]{1,0:T(8,128)(2,1)} %shard_map.96.refs_0_.refs_4_), channel_id=1, source_target_pairs={{0,2},{1,3},{2,0},{3,1},{4,6},{5,7},{6,4},{7,5},{8,10},{9,11},{10,... | collective-permute-start | bytes 663560 | tf_op jit(solution)/shard_map/ppermute | solution.py:55
  7.0 10.8 %collective-permute-start.5 = (bf16[144,768]{1,0:T(8,128)(2,1)}, bf16[144,768]{1,0:T(8,128)(2,1)S(1)}, u32[]{:S(2)}, u32[]{:S(2)}) collective-permute-start(bf16[144,768]{1,0:T(8,128)(2,1)} %shard_map.96.refs_0_.refs_4_), channel_id=1, source_target_pairs={{0,4},{1,5},{2,6},{3,7},{4,0},{5,1},{6,2},{7,3},{8,12},{9,13},{10,... | collective-permute-start | bytes 663560 | tf_op jit(solution)/shard_map/ppermute | solution.py:55
  14.7 3.1 %collective-permute-start.4 = (bf16[144,768]{1,0:T(8,128)(2,1)S(1)}, bf16[144,768]{1,0:T(8,128)(2,1)S(1)}, u32[]{:S(2)}, u32[]{:S(2)}) collective-permute-start(bf16[144,768]{1,0:T(8,128)(2,1)S(1)} %shard_map.99.refs_0_.refs_10_), channel_id=1, source_target_pairs={{0,1},{1,0},{2,3},{3,2},{4,5},{5,4},{6,7},{7,6},{8,9},{9,8},{10,11... | collective-permute-start | bytes 663560 | tf_op jit(solution)/shard_map/ppermute | solution.py:55
  17.7 3.0 %collective-permute-start.2 = (bf16[144,768]{1,0:T(8,128)(2,1)S(1)}, bf16[144,768]{1,0:T(8,128)(2,1)S(1)}, u32[]{:S(2)}, u32[]{:S(2)}) collective-permute-start(bf16[144,768]{1,0:T(8,128)(2,1)S(1)} %shard_map.98.refs_3_.refs_0_.refs_6_), channel_id=1, source_target_pairs={{0,1},{1,0},{2,3},{3,2},{4,5},{5,4},{6,7},{7,6},{8,9},{9,8},{10,11... | collective-permute-start | bytes 663560 | tf_op jit(solution)/shard_map/ppermute | solution.py:55
  19.7 3.2 %collective-permute-start.7 = (bf16[128,768]{1,0:T(8,128)(2,1)S(1)}, bf16[128,768]{1,0:T(8,128)(2,1)S(1)}, u32[]{:S(2)}, u32[]{:S(2)}) collective-permute-start(bf16[128,768]{1,0:T(8,128)(2,1)S(1)} %get-tuple-element.27), channel_id=1, source_target_pairs={{0,1},{1,0},{2,3},{3,2},{4,5},{5,4},{6,7},{7,6},{8,9},{9,8},{10,11... | collective-permute-start | bytes 589832 | tf_op jit(solution)/shard_map/ppermute | solution.py:55
  20.3 5.0 %collective-permute-start.6 = (bf16[144,768]{1,0:T(8,128)(2,1)S(1)}, bf16[144,768]{1,0:T(8,128)(2,1)S(1)}, u32[]{:S(2)}, u32[]{:S(2)}) collective-permute-start(bf16[144,768]{1,0:T(8,128)(2,1)S(1)} %shard_map.100.refs_4_.refs_0_.refs_8_), channel_id=1, source_target_pairs={{0,1},{1,0},{2,3},{3,2},{4,5},{5,4},{6,7},{7,6},{8,9},{9,8},{10,11... | collective-permute-start | bytes 663560 | tf_op jit(solution)/shard_map/ppermute | solution.py:55
  20.3 9.2 %collective-permute-start.10 = (bf16[128,768]{1,0:T(8,128)(2,1)S(1)}, bf16[128,768]{1,0:T(8,128)(2,1)S(1)}, u32[]{:S(2)}, u32[]{:S(2)}) collective-permute-start(bf16[128,768]{1,0:T(8,128)(2,1)S(1)} %get-tuple-element.35), channel_id=1, source_target_pairs={{0,1},{1,0},{2,3},{3,2},{4,5},{5,4},{6,7},{7,6},{8,9},{9,8},{10,11... | collective-permute-start | bytes 589832 | tf_op jit(solution)/shard_map/ppermute | solution.py:55
  22.7 4.6 %collective-permute-start.8 = (bf16[128,768]{1,0:T(8,128)(2,1)S(1)}, bf16[128,768]{1,0:T(8,128)(2,1)S(1)}, u32[]{:S(2)}, u32[]{:S(2)}) collective-permute-start(bf16[128,768]{1,0:T(8,128)(2,1)S(1)} %get-tuple-element.30), channel_id=1, source_target_pairs={{0,1},{1,0},{2,3},{3,2},{4,5},{5,4},{6,7},{7,6},{8,9},{9,8},{10,11... | collective-permute-start | bytes 589832 | tf_op jit(solution)/shard_map/ppermute | solution.py:55
  22.9 8.7 %collective-permute-start.11 = (bf16[128,768]{1,0:T(8,128)(2,1)S(1)}, bf16[128,768]{1,0:T(8,128)(2,1)S(1)}, u32[]{:S(2)}, u32[]{:S(2)}) collective-permute-start(bf16[128,768]{1,0:T(8,128)(2,1)S(1)} %add_convert_fusion.2.refs_3_.refs_12_), channel_id=1, source_target_pairs={{0,6},{1,7},{2,4},{3,5},{4,2},{5,3},{6,0},{7,1},{8,14},{9,15},{10,... | collective-permute-start | bytes 589832 | tf_op jit(solution)/shard_map/ppermute | solution.py:55
  27.2 1.5 %collective-permute-start.9 = (bf16[128,768]{1,0:T(8,128)(2,1)S(1)}, bf16[128,768]{1,0:T(8,128)(2,1)S(1)}, u32[]{:S(2)}, u32[]{:S(2)}) collective-permute-start(bf16[128,768]{1,0:T(8,128)(2,1)S(1)} %get-tuple-element.32), channel_id=1, source_target_pairs={{0,1},{1,0},{2,3},{3,2},{4,5},{5,4},{6,7},{7,6},{8,9},{9,8},{10,11... | collective-permute-start | bytes 589832 | tf_op jit(solution)/shard_map/ppermute | solution.py:55
  27.4 7.5 %collective-permute-start.12 = (bf16[128,768]{1,0:T(8,128)(2,1)S(1)}, bf16[128,768]{1,0:T(8,128)(2,1)S(1)}, u32[]{:S(2)}, u32[]{:S(2)}) collective-permute-start(bf16[128,768]{1,0:T(8,128)(2,1)S(1)} %add_convert_fusion.1.refs_13_), channel_id=1, source_target_pairs={{0,2},{1,3},{2,0},{3,1},{4,6},{5,7},{6,4},{7,5},{8,10},{9,11},{10,... | collective-permute-start | bytes 589832 | tf_op jit(solution)/shard_map/ppermute | solution.py:55
  28.8 7.0 %collective-permute-start.13 = (bf16[128,768]{1,0:T(8,128)(2,1)S(1)}, bf16[128,768]{1,0:T(8,128)(2,1)S(1)}, u32[]{:S(2)}, u32[]{:S(2)}) collective-permute-start(bf16[128,768]{1,0:T(8,128)(2,1)S(1)} %add_convert_fusion.refs_14_), channel_id=1, source_target_pairs={{0,4},{1,5},{2,6},{3,7},{4,0},{5,1},{6,2},{7,3},{8,12},{9,13},{10,... | collective-permute-start | bytes 589832 | tf_op jit(solution)/shard_map/ppermute | solution.py:55
  35.9 4.7 %collective-permute-start.14 = (bf16[64,768]{1,0:T(8,128)(2,1)S(1)}, bf16[64,768]{1,0:T(8,128)(2,1)S(1)}, u32[]{:S(2)}, u32[]{:S(2)}) collective-permute-start(bf16[64,768]{1,0:T(8,128)(2,1)S(1)} %get-tuple-element.37), channel_id=1, source_target_pairs={{0,8},{8,0},{16,24},{24,16},{1,9},{9,1},{17,25},{25,17},{2,10},{10... | collective-permute-start | bytes 294920 | tf_op jit(solution)/shard_map/ppermute | solution.py:55
  40.6 5.9 %collective-permute-start.15 = (bf16[64,768]{1,0:T(8,128)(2,1)S(1)}, bf16[64,768]{1,0:T(8,128)(2,1)S(1)}, u32[]{:S(2)}, u32[]{:S(2)}) collective-permute-start(bf16[64,768]{1,0:T(8,128)(2,1)S(1)} %add_convert_fusion.4.after_ref), channel_id=1, source_target_pairs={{0,16},{8,24},{16,0},{24,8},{1,17},{9,25},{17,1},{25,9},{2,18},{10... | collective-permute-start | bytes 294920 | tf_op jit(solution)/shard_map/ppermute | solution.py:55
  46.6 4.7 %collective-permute-start.16 = (bf16[64,768]{1,0:T(8,128)(2,1)S(1)}, bf16[64,768]{1,0:T(8,128)(2,1)S(1)}, u32[]{:S(2)}, u32[]{:S(2)}) collective-permute-start(bf16[64,768]{1,0:T(8,128)(2,1)S(1)} %add_convert_fusion.3.refs_0_), channel_id=1, source_target_pairs={{0,8},{8,0},{16,24},{24,16},{1,9},{9,1},{17,25},{25,17},{2,10},{10... | collective-permute-start | bytes 294920 | tf_op jit(solution)/shard_map/ppermute | solution.py:55
  51.4 6.3 %collective-permute-start.18 = (bf16[768,128]{1,0:T(8,128)(2,1)S(1)}, bf16[768,128]{1,0:T(8,128)(2,1)S(1)}, u32[]{:S(2)}, u32[]{:S(2)}) collective-permute-start(bf16[768,128]{1,0:T(8,128)(2,1)S(1)} %shard_map.108.whole_ref.refs_0_), channel_id=1, source_target_pairs={{0,2},{1,3},{2,0},{3,1},{4,6},{5,7},{6,4},{7,5},{8,10},{9,11},{10,... | collective-permute-start | bytes 589832 | tf_op jit(solution)/shard_map/ppermute | solution.py:55
  52.6 7.9 %collective-permute-start.20 = (bf16[768,128]{1,0:T(8,128)(2,1)S(1)}, bf16[768,128]{1,0:T(8,128)(2,1)S(1)}, u32[]{:S(2)}, u32[]{:S(2)}) collective-permute-start(bf16[768,128]{1,0:T(8,128)(2,1)S(1)} %shard_map.108.whole_ref.refs_0_), channel_id=1, source_target_pairs={{0,4},{1,5},{2,6},{3,7},{4,0},{5,1},{6,2},{7,3},{8,12},{9,13},{10,... | collective-permute-start | bytes 589832 | tf_op jit(solution)/shard_map/ppermute | solution.py:55
  53.6 6.9 %collective-permute-start.22 = (bf16[768,128]{1,0:T(8,128)(2,1)S(1)}, bf16[768,128]{1,0:T(8,128)(2,1)S(1)}, u32[]{:S(2)}, u32[]{:S(2)}) collective-permute-start(bf16[768,128]{1,0:T(8,128)(2,1)S(1)} %shard_map.108.whole_ref.refs_0_), channel_id=1, source_target_pairs={{0,6},{1,7},{2,4},{3,5},{4,2},{5,3},{6,0},{7,1},{8,14},{9,15},{10,... | collective-permute-start | bytes 589832 | tf_op jit(solution)/shard_map/ppermute | solution.py:55
  55.1 5.9 %collective-permute-start.17 = (bf16[768,128]{1,0:T(8,128)(2,1)S(1)}, bf16[768,128]{1,0:T(8,128)(2,1)S(1)}, u32[]{:S(2)}, u32[]{:S(2)}) collective-permute-start(bf16[768,128]{1,0:T(8,128)(2,1)S(1)} %shard_map.108.whole_ref.refs_0_), channel_id=1, source_target_pairs={{0,1},{1,0},{2,3},{3,2},{4,5},{5,4},{6,7},{7,6},{8,9},{9,8},{10,11... | collective-permute-start | bytes 589832 | tf_op jit(solution)/shard_map/ppermute | solution.py:55
  57.7 3.4 %collective-permute-start.19 = (bf16[768,128]{1,0:T(8,128)(2,1)S(1)}, bf16[768,128]{1,0:T(8,128)(2,1)S(1)}, u32[]{:S(2)}, u32[]{:S(2)}) collective-permute-start(bf16[768,128]{1,0:T(8,128)(2,1)S(1)} %shard_map.110.refs_2_), channel_id=1, source_target_pairs={{0,1},{1,0},{2,3},{3,2},{4,5},{5,4},{6,7},{7,6},{8,9},{9,8},{10,11... | collective-permute-start | bytes 589832 | tf_op jit(solution)/shard_map/ppermute | solution.py:55
  60.5 1.4 %collective-permute-start.21 = (bf16[768,128]{1,0:T(8,128)(2,1)S(1)}, bf16[768,128]{1,0:T(8,128)(2,1)S(1)}, u32[]{:S(2)}, u32[]{:S(2)}) collective-permute-start(bf16[768,128]{1,0:T(8,128)(2,1)S(1)} %shard_map.111.refs_4_), channel_id=1, source_target_pairs={{0,1},{1,0},{2,3},{3,2},{4,5},{5,4},{6,7},{7,6},{8,9},{9,8},{10,11... | collective-permute-start | bytes 589832 | tf_op jit(solution)/shard_map/ppermute | solution.py:55
  60.5 1.7 %collective-permute-start.23 = (bf16[768,128]{1,0:T(8,128)(2,1)S(1)}, bf16[768,128]{1,0:T(8,128)(2,1)S(1)}, u32[]{:S(2)}, u32[]{:S(2)}) collective-permute-start(bf16[768,128]{1,0:T(8,128)(2,1)S(1)} %shard_map.112.refs_6_), channel_id=1, source_target_pairs={{0,1},{1,0},{2,3},{3,2},{4,5},{5,4},{6,7},{7,6},{8,9},{9,8},{10,11... | collective-permute-start | bytes 589832 | tf_op jit(solution)/shard_map/ppermute | solution.py:55
  (8 other events, 35.3 us)

commit v12 on v11

--- a/solution.py
+++ b/solution.py
@@ -173,32 +173,28 @@
         out_ref[...] = total.astype(out_ref.dtype)
 
 
-def whole_kernel(z_ref, *refs):
-    *parts, whole_ref, rows_ref = refs
+def head_kernel(count, z_ref, *refs):
+    parts, (slice_ref, rows_any, rows_ref, head_ref, whole_ref, sem) = refs[:count], refs[count:]
+    copy = pltpu.make_async_copy(rows_any, rows_ref, sem)
+    copy.start()
     depth = parts[0].shape[0]
     for r, part in enumerate(parts):
-        rows_ref[pl.ds(pl.multiple_of((z_ref[0] ^ r) * depth, depth), depth), :] = part[...]
-    whole_ref[...] = rows_ref[...].T
-
-
-def head_kernel(rows_any, whole_ref, slice_ref, rows_ref, head_ref, sem):
-    copy = pltpu.make_async_copy(rows_any, rows_ref, sem)
-    copy.start()
-    head_ref[...] = dot(slice_ref[...], whole_ref[...], TN)
+        whole_ref[pl.ds(pl.multiple_of((z_ref[0] ^ r) * depth, depth), depth), :] = part[...]
+    head_ref[...] = dot(whole_ref[...], slice_ref[...], NN).T
     copy.wait()
 
 
-def proj_kernel(cuts, me_ref, *refs):
+def proj_kernel(count, cuts, me_ref, z_ref, *refs):
     *parts, rows_ref, out_hbm, outer_ref, done_ref, sems = refs
-    width, size = parts[0].shape
-    for distance, part in enumerate(parts):
-        start = pl.multiple_of((me_ref[0] ^ distance) * size, size)
-        outer_ref[:, pl.ds(start, size)] = part[...]
+    depth, width = parts[0].shape
+    for at, part in enumerate(parts):
+        start = (me_ref[0] ^ (at // count)) * (depth * count) + (z_ref[0] ^ (at % count)) * depth
+        outer_ref[pl.ds(pl.multiple_of(start, depth), depth), :] = part[...]
     height = width // cuts
     copies = []
     for cut in range(cuts):
         rows = pl.ds(cut * height, height)
-        done_ref[rows, :] = dot(outer_ref[rows, :], rows_ref[...], NN)
+        done_ref[rows, :] = dot(outer_ref[:, rows], rows_ref[...], TN)
         copy = pltpu.make_async_copy(done_ref.at[rows, :], out_hbm.at[rows, :], sems.at[cut])
         copy.start()
         copies.append(copy)
@@ -347,38 +343,34 @@
             parts[r + span] = swap(parts[r], "dp", span)
         span *= 2
     proj_slice = lax.dynamic_slice_in_dim(proj, z * (width // planes), width // planes, 1)
-    (whole,) = call(
-        whole_kernel,
-        [shape((width, size), BF16)],
-        [parts[r] for r in range(row_blocks)],
-        scalars=[z_s],
-        scratch=[pltpu.VMEM((size, width), BF16)],
-        vmem=4,
-    )
     rows, grad_head = pl.pallas_call(
-        head_kernel,
+        functools.partial(head_kernel, row_blocks),
         out_shape=[shape((labels, width), BF16), shape((width // planes, size), F32)],
-        in_specs=[ANY, VMEM, VMEM],
+        in_specs=[SMEM] + [VMEM] * (row_blocks + 1) + [ANY],
         out_specs=[VMEM, VMEM],
-        scratch_shapes=[pltpu.SemaphoreType.DMA],
+        scratch_shapes=[pltpu.VMEM((size, width), BF16), pltpu.SemaphoreType.DMA],
         compiler_params=pltpu.CompilerParams(vmem_limit_bytes=4 * MIB),
         cost_estimate=pl.CostEstimate(
             flops=2 * size * width * width // planes, bytes_accessed=3_000_000, transcendentals=0
         ),
-    )(rows, whole, proj_slice)
-    have = {0: whole}
-    for g in near + far:
-        have[2 * g] = gate(swap(whole, "label", 2 * g), rows)
-    for distance in list(have):
-        have[distance + 1] = swap(have[distance], "label", 1)
-    cuts = 4
+    )(z_s, *[parts[r] for r in range(row_blocks)], proj_slice, rows)
+    have = {(0, r): parts[r] for r in range(row_blocks)}
+    for r in range(row_blocks):
+        for g in near + far:
+            have[2 * g, r] = swap(parts[r], "label", 2 * g)
+    if near:
+        last = (2 * near[0], row_blocks - 1)
+        have[last] = gate(have[last], rows)
+    for distance, r in list(have):
+        have[distance + 1, r] = swap(have[distance, r], "label", 1)
+    cuts = 3
     grad_proj = pl.pallas_call(
-        functools.partial(proj_kernel, cuts),
+        functools.partial(proj_kernel, row_blocks, cuts),
         out_shape=shape((width, width), F32),
-        in_specs=[SMEM] + [VMEM] * (owners + 1),
+        in_specs=[SMEM] * 2 + [VMEM] * (owners * row_blocks + 1),
         out_specs=ANY,
         scratch_shapes=[
-            pltpu.VMEM((width, labels), BF16),
+            pltpu.VMEM((labels, width), BF16),
             pltpu.VMEM((width, width), F32),
             pltpu.SemaphoreType.DMA((cuts,)),
         ],
@@ -386,7 +378,7 @@
         cost_estimate=pl.CostEstimate(
             flops=2 * labels * width * width, bytes_accessed=6_000_000, transcendentals=0
         ),
-    )(me_s, *[have[distance] for distance in range(owners)], rows)
+    )(me_s, z_s, *[have[distance, r] for distance in range(owners) for r in range(row_blocks)], rows)
     return (grad_enc, grad_proj, grad_head.T)
 
 

time: 65.4 us -> 66.1 us (1.011)
  starting transfers between devices: 20.3 us -> 24.2 us
  waiting for transfers between devices: 17.6 us -> 14.9 us
    ppermute x24 -> x31, starting transfers between devices: 20.3 us -> 24.2 us  [swap(): return lax.ppermute(value, axis, [(i, i ^ distance) for i in range(size)])]
    ppermute x24 -> x31, waiting for transfers between devices: 17.6 us -> 14.9 us  [swap(): return lax.ppermute(value, axis, [(i, i ^ distance) for i in range(size)])]
    pallas_call x9 -> x8, Pallas kernels: 13.3 us -> 13.1 us  [call(): pl.pallas_call(kernel, out_shape=outs, in_specs=[SMEM] * len(scalars) + [...]
  transfers between devices with their start and end apart: 24 -> 31, of which waited for: 10 -> 12; matrix products, arithmetic and copies ran while one was open for 1% -> 1% of each run, Pallas kernels for 27% -> 26%
where the time goes in v12:
time: 66.1 us; the launch traced here: 65.9 us
  starting transfers between devices  24.2 us (37%)
  Pallas kernels  21.7 us (33%)
  waiting for transfers between devices  14.9 us (23%)
  local copies, waits for them, and re-layouts  3.76 us (6%)
  between operations  1.06 us (2%)
    ppermute x31, starting transfers between devices, swap(): return lax.ppermute(value, axis, [(i, i ^ distance) for i in range(size)])  24.2 us
    ppermute x31, waiting for transfers between devices, swap(): return lax.ppermute(value, axis, [(i, i ^ distance) for i in range(size)])  14.9 us
    pallas_call x8, Pallas kernels, call(): pl.pallas_call(kernel, out_shape=outs, in_specs=[SMEM] * len(scalars) + [...  13.1 us
    unnamed x16, local copies, waits for them, and re-layouts  3.59 us
    pallas_call x1, Pallas kernels, grad_enc_after(): pl.pallas_call(enc_kernel, grid=(samples // tile,), out_shape=[shape((sam...  3.28 us
    pallas_call x1, Pallas kernels, shards(): pl.pallas_call(functools.partial(proj_kernel, row_blocks, cuts), out_shap...  2.47 us
    pallas_call x1, Pallas kernels, shards(): pl.pallas_call(payload_kernel, out_shape=shape((size + TAIL, width), BF16...  1.76 us
  transfers between devices with their start and end apart: 31, of which 12 were waited for; matrix products, arithmetic and copies ran while one was open for 1% of the time, Pallas kernels for 26%

profile of v12, /device:TPU:0, one launch (start us, length us, event | category | flops | bytes accessed | tf_op | source)
XLA Modules:
  0.0 65.9 jit_solution(14770331142634324646)
XLA Ops:
  0.6 1.8 %shard_map.96.refs_0_.refs_4_ = bf16[144,768]{1,0:T(8,128)(2,1)} custom-call(s32[1,128]{1,0:T(1,128)} %bitcast.12, s32[1,128]{1,0:T(1,128)} %bitcast.13, bf16[128,768]{1,0:T(8,128)(2,1)} %rows_hbm.1), custom_call_target="tpu_custom_call" | custom-call | tf_op jit(solution)/shard_map/pallas_call | solution.py:223
  2.9 3.5 %collective-permute-start.3 = (bf16[144,768]{1,0:T(8,128)(2,1)}, bf16[144,768]{1,0:T(8,128)(2,1)S(1)}, u32[]{:S(2)}, u32[]{:S(2)}) collective-permute-start(bf16[144,768]{1,0:T(8,128)(2,1)} %shard_map.96.refs_0_.refs_4_), channel_id=1, source_target_pairs={{0,6},{1,7},{2,4},{3,5},{4,2},{5,3},{6,0},{7,1},{8,14},{9,15},{10,... | collective-permute-start | bytes 663560 | tf_op jit(solution)/shard_map/ppermute | solution.py:55
  7.9 1.9 %shard_map.94.after_ref.target_ref = bf16[512,1024]{1,0:T(8,128)(2,1)S(1)} custom-call(s32[8,1024]{1,0:T(8,128)S(1)} %bitcast.11), custom_call_target="tpu_custom_call" | custom-call | bytes 8000000 | tf_op jit(solution)/shard_map/pallas_call | solution.py:31
  9.8 1.4 %copy-done = bf16[1024,768]{1,0:T(8,128)(2,1)S(1)} copy-done((bf16[1024,768]{1,0:T(8,128)(2,1)S(1)}, bf16[1024,768]{1,0:T(8,128)(2,1)}, u32[]{:S(2)}) %copy-start) | copy-done | bytes 1572888
  11.2 1.5 %shard_map.95.hidden_t_ref = bf16[768,1024]{1,0:T(8,128)(2,1)S(1)} custom-call(bf16[1024,768]{1,0:T(8,128)(2,1)S(1)} %copy-done, bf16[768,768]{1,0:T(8,128)(2,1)S(1)} %copy-done.2, bf16[512,1024]{1,0:T(8,128)(2,1)S(1)} %shard_map.94.after_ref.target_ref), custom_call_target="tpu_custom_call" | custom-call | flops 1207959552 | bytes 6000000 | tf_op jit(solution)/shard_map/pallas_call | solution.py:31
  12.7 1.9 %shard_map.97 = (bf16[256,1024]{1,0:T(8,128)(2,1)S(1)}, f32[128,768]{1,0:T(8,128)S(1)}, bf16[128,768]{1,0:T(8,128)(2,1)S(1)}) custom-call(s32[4,8]{1,0:T(4,128)S(1)} %bitcast.7, s32[1]{0:T(128)} %bitcast.me_ref, s32[1]{0:T(128)} %bitcast.2.z_ref, bf16[768,1024]{1,0:T(8,128)(2,1)S(1)} %shard_map.95.hidden_t_ref, ...), custom_call_target="tpu_custom_call" | custom-call | flops 805306368 | bytes 5000000 | tf_op jit(solution)/shard_map/pallas_call | solution.py:31
  14.7 3.0 %collective-permute-done.1.value_ref = bf16[144,768]{1,0:T(8,128)(2,1)S(1)} collective-permute-done((bf16[144,768]{1,0:T(8,128)(2,1)}, bf16[144,768]{1,0:T(8,128)(2,1)S(1)}, u32[]{:S(2)}, u32[]{:S(2)}) %collective-permute-start.1) | collective-permute-done | bytes 221216 | tf_op jit(solution)/shard_map/ppermute | solution.py:55
  17.8 1.9 %shard_map.101 = (bf16[256,1024]{1,0:T(8,128)(2,1)S(1)}, f32[128,768]{1,0:T(8,128)S(1)}, bf16[128,768]{1,0:T(8,128)(2,1)S(1)}) custom-call(s32[4,8]{1,0:T(4,128)S(1)} %bitcast.8, s32[1]{0:T(128)} %bitcast.me_ref, s32[1]{0:T(128)} %bitcast.2.z_ref, bf16[768,1024]{1,0:T(8,128)(2,1)S(1)} %shard_map.95.hidden_t_ref, ...), custom_call_target="tpu_custom_call" | custom-call | flops 805306368 | bytes 5000000 | tf_op jit(solution)/shard_map/pallas_call | solution.py:31
  20.8 1.9 %shard_map.102 = (bf16[256,1024]{1,0:T(8,128)(2,1)S(1)}, f32[128,768]{1,0:T(8,128)S(1)}, bf16[128,768]{1,0:T(8,128)(2,1)S(1)}) custom-call(s32[4,8]{1,0:T(4,128)S(1)} %bitcast.9, s32[1]{0:T(128)} %bitcast.me_ref, s32[1]{0:T(128)} %bitcast.2.z_ref, bf16[768,1024]{1,0:T(8,128)(2,1)S(1)} %shard_map.95.hidden_t_ref, ...), custom_call_target="tpu_custom_call" | custom-call | flops 805306368 | bytes 5000000 | tf_op jit(solution)/shard_map/pallas_call | solution.py:31
  22.9 2.3 %collective-permute-start.11 = (bf16[128,768]{1,0:T(8,128)(2,1)S(1)}, bf16[128,768]{1,0:T(8,128)(2,1)S(1)}, u32[]{:S(2)}, u32[]{:S(2)}) collective-permute-start(bf16[128,768]{1,0:T(8,128)(2,1)S(1)} %add_convert_fusion.2.refs_3_.refs_12_), channel_id=1, source_target_pairs={{0,6},{1,7},{2,4},{3,5},{4,2},{5,3},{6,0},{7,1},{8,14},{9,15},{10,... | collective-permute-start | bytes 589832 | tf_op jit(solution)/shard_map/ppermute | solution.py:55
  25.2 2.0 %shard_map.103 = (bf16[256,1024]{1,0:T(8,128)(2,1)S(1)}, f32[128,768]{1,0:T(8,128)S(1)}, bf16[128,768]{1,0:T(8,128)(2,1)S(1)}) custom-call(s32[4,8]{1,0:T(4,128)S(1)} %bitcast.10, s32[1]{0:T(128)} %bitcast.me_ref, s32[1]{0:T(128)} %bitcast.2.z_ref, bf16[768,1024]{1,0:T(8,128)(2,1)S(1)} %shard_map.95.hidden_t_ref, ...), custom_call_target="tpu_custom_call" | custom-call | flops 805306368 | bytes 5000000 | tf_op jit(solution)/shard_map/pallas_call | solution.py:31
  29.6 1.9 %shard_map.104 = (bf16[1024,768]{1,0:T(8,128)(2,1)S(1)}, bf16[1024,768]{1,0:T(8,128)(2,1)S(1)}) custom-call(s32[1]{0:T(128)} %bitcast.me_ref, bf16[256,1024]{1,0:T(8,128)(2,1)S(1)} %get-tuple-element.23.refs_0_.refs_2_, bf16[256,1024]{1,0:T(8,128)(2,1)S(1)} %get-tuple-element.25.refs_2_.refs_1_, bf16[256,1024]{1,0:T(8,128)(2,1)S(1)} %get-tuple-element.28.refs_2_, ...), custom_call_target="tpu_custom_call" | custom-call | flops 1610612736 | bytes 5000000 | tf_op jit(solution)/shard_map/pallas_call | solution.py:31
  31.6 3.3 %collective-permute-done.12.refs_1_ = bf16[128,768]{1,0:T(8,128)(2,1)S(1)} collective-permute-done((bf16[128,768]{1,0:T(8,128)(2,1)S(1)}, bf16[128,768]{1,0:T(8,128)(2,1)S(1)}, u32[]{:S(2)}, u32[]{:S(2)}) %collective-permute-start.12) | collective-permute-done | bytes 196640 | tf_op jit(solution)/shard_map/ppermute | solution.py:55
  35.9 1.6 %collective-permute-start.14 = (bf16[64,768]{1,0:T(8,128)(2,1)S(1)}, bf16[64,768]{1,0:T(8,128)(2,1)S(1)}, u32[]{:S(2)}, u32[]{:S(2)}) collective-permute-start(bf16[64,768]{1,0:T(8,128)(2,1)S(1)} %get-tuple-element.37), channel_id=1, source_target_pairs={{0,8},{8,0},{16,24},{24,16},{1,9},{9,1},{17,25},{25,17},{2,10},{10... | collective-permute-start | bytes 294920 | tf_op jit(solution)/shard_map/ppermute | solution.py:55
  37.5 3.0 %collective-permute-done.14 = bf16[64,768]{1,0:T(8,128)(2,1)S(1)} collective-permute-done((bf16[64,768]{1,0:T(8,128)(2,1)S(1)}, bf16[64,768]{1,0:T(8,128)(2,1)S(1)}, u32[]{:S(2)}, u32[]{:S(2)}) %collective-permute-start.14) | collective-permute-done | bytes 98336 | tf_op jit(solution)/shard_map/ppermute | solution.py:55
  40.6 2.7 %collective-permute-start.15 = (bf16[64,768]{1,0:T(8,128)(2,1)S(1)}, bf16[64,768]{1,0:T(8,128)(2,1)S(1)}, u32[]{:S(2)}, u32[]{:S(2)}) collective-permute-start(bf16[64,768]{1,0:T(8,128)(2,1)S(1)} %add_convert_fusion.4.after_ref), channel_id=1, source_target_pairs={{0,16},{8,24},{16,0},{24,8},{1,17},{9,25},{17,1},{25,9},{2,18},{10... | collective-permute-start | bytes 294920 | tf_op jit(solution)/shard_map/ppermute | solution.py:55
  43.2 3.3 %shard_map.106 = (f32[1024,768]{1,0:T(8,128)}, f32[8,128]{1,0:T(8,128)S(1)}) custom-call(bf16[1024,768]{1,0:T(8,128)(2,1)S(1)} %get-tuple-element.33.refs_3_.grad_hidden_ref, bf16[768,768]{1,0:T(8,128)(2,1)S(1)} %copy-done.2, bf16[64,768]{1,0:T(8,128)(2,1)S(1)} %add_convert_fusion.4.after_ref), custom_call_target="tpu_custom_call" | custom-call | flops 1207959552 | bytes 6000000 | tf_op jit(solution)/shard_map/pallas_call | solution.py:296
  46.5 1.6 %collective-permute-start.16 = (bf16[64,768]{1,0:T(8,128)(2,1)S(1)}, bf16[64,768]{1,0:T(8,128)(2,1)S(1)}, u32[]{:S(2)}, u32[]{:S(2)}) collective-permute-start(bf16[64,768]{1,0:T(8,128)(2,1)S(1)} %add_convert_fusion.3.refs_0_), channel_id=1, source_target_pairs={{0,8},{8,0},{16,24},{24,16},{1,9},{9,1},{17,25},{25,17},{2,10},{10... | collective-permute-start | bytes 294920 | tf_op jit(solution)/shard_map/ppermute | solution.py:55
  48.2 1.1 %collective-permute-start.19 = (bf16[64,768]{1,0:T(8,128)(2,1)S(1)}, bf16[64,768]{1,0:T(8,128)(2,1)S(1)}, u32[]{:S(2)}, u32[]{:S(2)}) collective-permute-start(bf16[64,768]{1,0:T(8,128)(2,1)S(1)} %add_convert_fusion.3.refs_0_), channel_id=1, source_target_pairs={{0,2},{1,3},{2,0},{3,1},{4,6},{5,7},{6,4},{7,5},{8,10},{9,11},{10,... | collective-permute-start | bytes 294920 | tf_op jit(solution)/shard_map/ppermute | solution.py:55
  51.2 1.1 %collective-permute-start.20 = (bf16[64,768]{1,0:T(8,128)(2,1)S(1)}, bf16[64,768]{1,0:T(8,128)(2,1)S(1)}, u32[]{:S(2)}, u32[]{:S(2)}) collective-permute-start(bf16[64,768]{1,0:T(8,128)(2,1)S(1)} %collective-permute-done.16.refs_1_), channel_id=1, source_target_pairs={{0,2},{1,3},{2,0},{3,1},{4,6},{5,7},{6,4},{7,5},{8,10},{9,11},{10,... | collective-permute-start | bytes 294920 | tf_op jit(solution)/shard_map/ppermute | solution.py:55
  54.8 1.6 %collective-permute-start.28 = (bf16[64,768]{1,0:T(8,128)(2,1)S(1)}, bf16[64,768]{1,0:T(8,128)(2,1)S(1)}, u32[]{:S(2)}, u32[]{:S(2)}) collective-permute-start(bf16[64,768]{1,0:T(8,128)(2,1)S(1)} %collective-permute-done.16.refs_1_), channel_id=1, source_target_pairs={{0,6},{1,7},{2,4},{3,5},{4,2},{5,3},{6,0},{7,1},{8,14},{9,15},{10,... | collective-permute-start | bytes 294920 | tf_op jit(solution)/shard_map/ppermute | solution.py:55
  56.8 1.4 %copy-done.4 = bf16[1024,768]{1,0:T(8,128)(2,1)S(1)} copy-done((bf16[1024,768]{1,0:T(8,128)(2,1)S(1)}, bf16[1024,768]{1,0:T(8,128)(2,1)}, u32[]{:S(2)}) %copy-start.4) | copy-done | bytes 1572888
  60.3 1.4 %collective-permute-done.24.refs_9_ = bf16[64,768]{1,0:T(8,128)(2,1)S(1)} collective-permute-done((bf16[64,768]{1,0:T(8,128)(2,1)S(1)}, bf16[64,768]{1,0:T(8,128)(2,1)S(1)}, u32[]{:S(2)}, u32[]{:S(2)}) %collective-permute-start.24) | collective-permute-done | bytes 98336 | tf_op jit(solution)/shard_map/ppermute | solution.py:55
  63.2 2.5 %shard_map.110 = f32[768,768]{1,0:T(8,128)} custom-call(s32[1]{0:T(128)} %bitcast.me_ref, s32[1]{0:T(128)} %bitcast.2.z_ref, bf16[64,768]{1,0:T(8,128)(2,1)S(1)} %add_convert_fusion.3.refs_0_, bf16[64,768]{1,0:T(8,128)(2,1)S(1)} %collective-permute-done.16.refs_1_, bf16[64,768]{1,0:T(8,128)(2,1)S(1)} %collective-permute-done.17.refs_2_, ...), custom_call_target="tpu_custom_call" | custom-call | flops 1207959552 | bytes 6000000 | tf_op jit(solution)/shard_map/pallas_call | solution.py:367
  (78 shorter events, 15.0 us)
Async XLA Ops:
  2.4 10.3 %collective-permute-start = (bf16[144,768]{1,0:T(8,128)(2,1)}, bf16[144,768]{1,0:T(8,128)(2,1)S(1)}, u32[]{:S(2)}, u32[]{:S(2)}) collective-permute-start(bf16[144,768]{1,0:T(8,128)(2,1)} %shard_map.96.refs_0_.refs_4_), channel_id=1, source_target_pairs={{0,1},{1,0},{2,3},{3,2},{4,5},{5,4},{6,7},{7,6},{8,9},{9,8},{10,11... | collective-permute-start | bytes 663560 | tf_op jit(solution)/shard_map/ppermute | solution.py:55
  2.9 11.7 %collective-permute-start.3 = (bf16[144,768]{1,0:T(8,128)(2,1)}, bf16[144,768]{1,0:T(8,128)(2,1)S(1)}, u32[]{:S(2)}, u32[]{:S(2)}) collective-permute-start(bf16[144,768]{1,0:T(8,128)(2,1)} %shard_map.96.refs_0_.refs_4_), channel_id=1, source_target_pairs={{0,6},{1,7},{2,4},{3,5},{4,2},{5,3},{6,0},{7,1},{8,14},{9,15},{10,... | collective-permute-start | bytes 663560 | tf_op jit(solution)/shard_map/ppermute | solution.py:55
  6.5 11.3 %collective-permute-start.1 = (bf16[144,768]{1,0:T(8,128)(2,1)}, bf16[144,768]{1,0:T(8,128)(2,1)S(1)}, u32[]{:S(2)}, u32[]{:S(2)}) collective-permute-start(bf16[144,768]{1,0:T(8,128)(2,1)} %shard_map.96.refs_0_.refs_4_), channel_id=1, source_target_pairs={{0,2},{1,3},{2,0},{3,1},{4,6},{5,7},{6,4},{7,5},{8,10},{9,11},{10,... | collective-permute-start | bytes 663560 | tf_op jit(solution)/shard_map/ppermute | solution.py:55
  7.0 10.8 %collective-permute-start.5 = (bf16[144,768]{1,0:T(8,128)(2,1)}, bf16[144,768]{1,0:T(8,128)(2,1)S(1)}, u32[]{:S(2)}, u32[]{:S(2)}) collective-permute-start(bf16[144,768]{1,0:T(8,128)(2,1)} %shard_map.96.refs_0_.refs_4_), channel_id=1, source_target_pairs={{0,4},{1,5},{2,6},{3,7},{4,0},{5,1},{6,2},{7,3},{8,12},{9,13},{10,... | collective-permute-start | bytes 663560 | tf_op jit(solution)/shard_map/ppermute | solution.py:55
  14.7 3.1 %collective-permute-start.4 = (bf16[144,768]{1,0:T(8,128)(2,1)S(1)}, bf16[144,768]{1,0:T(8,128)(2,1)S(1)}, u32[]{:S(2)}, u32[]{:S(2)}) collective-permute-start(bf16[144,768]{1,0:T(8,128)(2,1)S(1)} %shard_map.99.refs_0_.refs_10_), channel_id=1, source_target_pairs={{0,1},{1,0},{2,3},{3,2},{4,5},{5,4},{6,7},{7,6},{8,9},{9,8},{10,11... | collective-permute-start | bytes 663560 | tf_op jit(solution)/shard_map/ppermute | solution.py:55
  19.7 3.2 %collective-permute-start.7 = (bf16[128,768]{1,0:T(8,128)(2,1)S(1)}, bf16[128,768]{1,0:T(8,128)(2,1)S(1)}, u32[]{:S(2)}, u32[]{:S(2)}) collective-permute-start(bf16[128,768]{1,0:T(8,128)(2,1)S(1)} %get-tuple-element.27), channel_id=1, source_target_pairs={{0,1},{1,0},{2,3},{3,2},{4,5},{5,4},{6,7},{7,6},{8,9},{9,8},{10,11... | collective-permute-start | bytes 589832 | tf_op jit(solution)/shard_map/ppermute | solution.py:55
  20.2 5.0 %collective-permute-start.6 = (bf16[144,768]{1,0:T(8,128)(2,1)S(1)}, bf16[144,768]{1,0:T(8,128)(2,1)S(1)}, u32[]{:S(2)}, u32[]{:S(2)}) collective-permute-start(bf16[144,768]{1,0:T(8,128)(2,1)S(1)} %shard_map.100.refs_4_.refs_0_.refs_8_), channel_id=1, source_target_pairs={{0,1},{1,0},{2,3},{3,2},{4,5},{5,4},{6,7},{7,6},{8,9},{9,8},{10,11... | collective-permute-start | bytes 663560 | tf_op jit(solution)/shard_map/ppermute | solution.py:55
  20.3 9.2 %collective-permute-start.10 = (bf16[128,768]{1,0:T(8,128)(2,1)S(1)}, bf16[128,768]{1,0:T(8,128)(2,1)S(1)}, u32[]{:S(2)}, u32[]{:S(2)}) collective-permute-start(bf16[128,768]{1,0:T(8,128)(2,1)S(1)} %get-tuple-element.35), channel_id=1, source_target_pairs={{0,1},{1,0},{2,3},{3,2},{4,5},{5,4},{6,7},{7,6},{8,9},{9,8},{10,11... | collective-permute-start | bytes 589832 | tf_op jit(solution)/shard_map/ppermute | solution.py:55
  22.7 4.6 %collective-permute-start.8 = (bf16[128,768]{1,0:T(8,128)(2,1)S(1)}, bf16[128,768]{1,0:T(8,128)(2,1)S(1)}, u32[]{:S(2)}, u32[]{:S(2)}) collective-permute-start(bf16[128,768]{1,0:T(8,128)(2,1)S(1)} %get-tuple-element.30), channel_id=1, source_target_pairs={{0,1},{1,0},{2,3},{3,2},{4,5},{5,4},{6,7},{7,6},{8,9},{9,8},{10,11... | collective-permute-start | bytes 589832 | tf_op jit(solution)/shard_map/ppermute | solution.py:55
  22.9 8.7 %collective-permute-start.11 = (bf16[128,768]{1,0:T(8,128)(2,1)S(1)}, bf16[128,768]{1,0:T(8,128)(2,1)S(1)}, u32[]{:S(2)}, u32[]{:S(2)}) collective-permute-start(bf16[128,768]{1,0:T(8,128)(2,1)S(1)} %add_convert_fusion.2.refs_3_.refs_12_), channel_id=1, source_target_pairs={{0,6},{1,7},{2,4},{3,5},{4,2},{5,3},{6,0},{7,1},{8,14},{9,15},{10,... | collective-permute-start | bytes 589832 | tf_op jit(solution)/shard_map/ppermute | solution.py:55
  27.3 7.5 %collective-permute-start.12 = (bf16[128,768]{1,0:T(8,128)(2,1)S(1)}, bf16[128,768]{1,0:T(8,128)(2,1)S(1)}, u32[]{:S(2)}, u32[]{:S(2)}) collective-permute-start(bf16[128,768]{1,0:T(8,128)(2,1)S(1)} %add_convert_fusion.1.refs_13_), channel_id=1, source_target_pairs={{0,2},{1,3},{2,0},{3,1},{4,6},{5,7},{6,4},{7,5},{8,10},{9,11},{10,... | collective-permute-start | bytes 589832 | tf_op jit(solution)/shard_map/ppermute | solution.py:55
  28.7 7.0 %collective-permute-start.13 = (bf16[128,768]{1,0:T(8,128)(2,1)S(1)}, bf16[128,768]{1,0:T(8,128)(2,1)S(1)}, u32[]{:S(2)}, u32[]{:S(2)}) collective-permute-start(bf16[128,768]{1,0:T(8,128)(2,1)S(1)} %add_convert_fusion.refs_14_), channel_id=1, source_target_pairs={{0,4},{1,5},{2,6},{3,7},{4,0},{5,1},{6,2},{7,3},{8,12},{9,13},{10,... | collective-permute-start | bytes 589832 | tf_op jit(solution)/shard_map/ppermute | solution.py:55
  35.9 4.7 %collective-permute-start.14 = (bf16[64,768]{1,0:T(8,128)(2,1)S(1)}, bf16[64,768]{1,0:T(8,128)(2,1)S(1)}, u32[]{:S(2)}, u32[]{:S(2)}) collective-permute-start(bf16[64,768]{1,0:T(8,128)(2,1)S(1)} %get-tuple-element.37), channel_id=1, source_target_pairs={{0,8},{8,0},{16,24},{24,16},{1,9},{9,1},{17,25},{25,17},{2,10},{10... | collective-permute-start | bytes 294920 | tf_op jit(solution)/shard_map/ppermute | solution.py:55
  40.6 5.9 %collective-permute-start.15 = (bf16[64,768]{1,0:T(8,128)(2,1)S(1)}, bf16[64,768]{1,0:T(8,128)(2,1)S(1)}, u32[]{:S(2)}, u32[]{:S(2)}) collective-permute-start(bf16[64,768]{1,0:T(8,128)(2,1)S(1)} %add_convert_fusion.4.after_ref), channel_id=1, source_target_pairs={{0,16},{8,24},{16,0},{24,8},{1,17},{9,25},{17,1},{25,9},{2,18},{10... | collective-permute-start | bytes 294920 | tf_op jit(solution)/shard_map/ppermute | solution.py:55
  46.5 4.7 %collective-permute-start.16 = (bf16[64,768]{1,0:T(8,128)(2,1)S(1)}, bf16[64,768]{1,0:T(8,128)(2,1)S(1)}, u32[]{:S(2)}, u32[]{:S(2)}) collective-permute-start(bf16[64,768]{1,0:T(8,128)(2,1)S(1)} %add_convert_fusion.3.refs_0_), channel_id=1, source_target_pairs={{0,8},{8,0},{16,24},{24,16},{1,9},{9,1},{17,25},{25,17},{2,10},{10... | collective-permute-start | bytes 294920 | tf_op jit(solution)/shard_map/ppermute | solution.py:55
  48.2 5.2 %collective-permute-start.17 = (bf16[64,768]{1,0:T(8,128)(2,1)S(1)}, bf16[64,768]{1,0:T(8,128)(2,1)S(1)}, u32[]{:S(2)}, u32[]{:S(2)}) collective-permute-start(bf16[64,768]{1,0:T(8,128)(2,1)S(1)} %add_convert_fusion.3.refs_0_), channel_id=1, source_target_pairs={{0,1},{1,0},{2,3},{3,2},{4,5},{5,4},{6,7},{7,6},{8,9},{9,8},{10,11... | collective-permute-start | bytes 294920 | tf_op jit(solution)/shard_map/ppermute | solution.py:55
  48.2 5.6 %collective-permute-start.19 = (bf16[64,768]{1,0:T(8,128)(2,1)S(1)}, bf16[64,768]{1,0:T(8,128)(2,1)S(1)}, u32[]{:S(2)}, u32[]{:S(2)}) collective-permute-start(bf16[64,768]{1,0:T(8,128)(2,1)S(1)} %add_convert_fusion.3.refs_0_), channel_id=1, source_target_pairs={{0,2},{1,3},{2,0},{3,1},{4,6},{5,7},{6,4},{7,5},{8,10},{9,11},{10,... | collective-permute-start | bytes 294920 | tf_op jit(solution)/shard_map/ppermute | solution.py:55
  49.3 5.5 %collective-permute-start.23 = (bf16[64,768]{1,0:T(8,128)(2,1)S(1)}, bf16[64,768]{1,0:T(8,128)(2,1)S(1)}, u32[]{:S(2)}, u32[]{:S(2)}) collective-permute-start(bf16[64,768]{1,0:T(8,128)(2,1)S(1)} %add_convert_fusion.3.refs_0_), channel_id=1, source_target_pairs={{0,4},{1,5},{2,6},{3,7},{4,0},{5,1},{6,2},{7,3},{8,12},{9,13},{10,... | collective-permute-start | bytes 294920 | tf_op jit(solution)/shard_map/ppermute | solution.py:55
  51.2 5.3 %collective-permute-start.20 = (bf16[64,768]{1,0:T(8,128)(2,1)S(1)}, bf16[64,768]{1,0:T(8,128)(2,1)S(1)}, u32[]{:S(2)}, u32[]{:S(2)}) collective-permute-start(bf16[64,768]{1,0:T(8,128)(2,1)S(1)} %collective-permute-done.16.refs_1_), channel_id=1, source_target_pairs={{0,2},{1,3},{2,0},{3,1},{4,6},{5,7},{6,4},{7,5},{8,10},{9,11},{10,... | collective-permute-start | bytes 294920 | tf_op jit(solution)/shard_map/ppermute | solution.py:55
  52.4 6.9 %collective-permute-start.27 = (bf16[64,768]{1,0:T(8,128)(2,1)S(1)}, bf16[64,768]{1,0:T(8,128)(2,1)S(1)}, u32[]{:S(2)}, u32[]{:S(2)}) collective-permute-start(bf16[64,768]{1,0:T(8,128)(2,1)S(1)} %add_convert_fusion.3.refs_0_), channel_id=1, source_target_pairs={{0,6},{1,7},{2,4},{3,5},{4,2},{5,3},{6,0},{7,1},{8,14},{9,15},{10,... | collective-permute-start | bytes 294920 | tf_op jit(solution)/shard_map/ppermute | solution.py:55
  53.4 6.4 %collective-permute-start.18 = (bf16[64,768]{1,0:T(8,128)(2,1)S(1)}, bf16[64,768]{1,0:T(8,128)(2,1)S(1)}, u32[]{:S(2)}, u32[]{:S(2)}) collective-permute-start(bf16[64,768]{1,0:T(8,128)(2,1)S(1)} %collective-permute-done.16.refs_1_), channel_id=1, source_target_pairs={{0,1},{1,0},{2,3},{3,2},{4,5},{5,4},{6,7},{7,6},{8,9},{9,8},{10,11... | collective-permute-start | bytes 294920 | tf_op jit(solution)/shard_map/ppermute | solution.py:55
  53.8 8.0 %collective-permute-start.24 = (bf16[64,768]{1,0:T(8,128)(2,1)S(1)}, bf16[64,768]{1,0:T(8,128)(2,1)S(1)}, u32[]{:S(2)}, u32[]{:S(2)}) collective-permute-start(bf16[64,768]{1,0:T(8,128)(2,1)S(1)} %collective-permute-done.16.refs_1_), channel_id=1, source_target_pairs={{0,4},{1,5},{2,6},{3,7},{4,0},{5,1},{6,2},{7,3},{8,12},{9,13},{10,... | collective-permute-start | bytes 294920 | tf_op jit(solution)/shard_map/ppermute | solution.py:55
  54.8 7.0 %collective-permute-start.28 = (bf16[64,768]{1,0:T(8,128)(2,1)S(1)}, bf16[64,768]{1,0:T(8,128)(2,1)S(1)}, u32[]{:S(2)}, u32[]{:S(2)}) collective-permute-start(bf16[64,768]{1,0:T(8,128)(2,1)S(1)} %collective-permute-done.16.refs_1_), channel_id=1, source_target_pairs={{0,6},{1,7},{2,4},{3,5},{4,2},{5,3},{6,0},{7,1},{8,14},{9,15},{10,... | collective-permute-start | bytes 294920 | tf_op jit(solution)/shard_map/ppermute | solution.py:55
  56.6 3.4 %collective-permute-start.21 = (bf16[64,768]{1,0:T(8,128)(2,1)S(1)}, bf16[64,768]{1,0:T(8,128)(2,1)S(1)}, u32[]{:S(2)}, u32[]{:S(2)}) collective-permute-start(bf16[64,768]{1,0:T(8,128)(2,1)S(1)} %collective-permute-done.19.refs_4_), channel_id=1, source_target_pairs={{0,1},{1,0},{2,3},{3,2},{4,5},{5,4},{6,7},{7,6},{8,9},{9,8},{10,11... | collective-permute-start | bytes 294920 | tf_op jit(solution)/shard_map/ppermute | solution.py:55
  (15 other events, 50.5 us)

commit v13 on v11

--- a/solution.py
+++ b/solution.py
@@ -316,13 +316,14 @@
             ),
         )(grad_hidden, proj, value)
 
+    grad_enc, enc_done = grad_enc_after(own)
     if row_blocks > 1:
         cut = size // 2
         total, upper = call(
             combine_kernel,
             [shape((cut, width), F32), shape((cut, width), BF16)],
             [own] + received,
-            after=[grad_hidden],
+            after=[enc_done],
             nbytes=2_000_000,
         )
         span = row_blocks // 2
@@ -336,9 +337,8 @@
         for value in received:
             total = total + value.astype(F32)
     total = total.astype(BF16)
-    grad_enc, enc_done = grad_enc_after(total)
     if planes > 1:
-        other = gate(swap(total, "dp", planes // 2), enc_done)
+        other = swap(total, "dp", planes // 2)
         total = (total.astype(F32) + other.astype(F32)).astype(BF16)
     parts = {0: total}
     span = 1
@@ -371,7 +371,7 @@
         have[2 * g] = gate(swap(whole, "label", 2 * g), rows)
     for distance in list(have):
         have[distance + 1] = swap(have[distance], "label", 1)
-    cuts = 4
+    cuts = max(1, width // 256)
     grad_proj = pl.pallas_call(
         functools.partial(proj_kernel, cuts),
         out_shape=shape((width, width), F32),

time: 65.4 us -> 64.9 us (level)
  waiting for transfers between devices: 17.6 us -> 15.9 us
  starting transfers between devices: 20.3 us -> 21.1 us
    ppermute x24, waiting for transfers between devices: 17.6 us -> 15.9 us  [swap(): return lax.ppermute(value, axis, [(i, i ^ distance) for i in range(size)])]
    ppermute x24, starting transfers between devices: 20.3 us -> 21.1 us  [swap(): return lax.ppermute(value, axis, [(i, i ^ distance) for i in range(size)])]
  transfers between devices with their start and end apart: 24 -> 24, of which waited for: 10 -> 9; matrix products, arithmetic and copies ran while one was open for 1% -> 1% of each run, Pallas kernels for 27% -> 27%
where the time goes in v13:
time: 64.9 us; the launch traced here: 64.6 us
  Pallas kernels  22.5 us (35%)
  starting transfers between devices  21.1 us (33%)
  waiting for transfers between devices  15.9 us (24%)
  local copies, waits for them, and re-layouts  3.76 us (6%)
  between operations  1.06 us (2%)
    ppermute x24, starting transfers between devices, swap(): return lax.ppermute(value, axis, [(i, i ^ distance) for i in range(size)])  21.1 us
    ppermute x24, waiting for transfers between devices, swap(): return lax.ppermute(value, axis, [(i, i ^ distance) for i in range(size)])  15.9 us
    pallas_call x9, Pallas kernels, call(): pl.pallas_call(kernel, out_shape=outs, in_specs=[SMEM] * len(scalars) + [...  13.3 us
    unnamed x16, local copies, waits for them, and re-layouts  3.59 us
    pallas_call x1, Pallas kernels, grad_enc_after(): pl.pallas_call(enc_kernel, grid=(samples // tile,), out_shape=[shape((sam...  3.49 us
    pallas_call x1, Pallas kernels, shards(): pl.pallas_call(functools.partial(proj_kernel, cuts), out_shape=shape((wid...  2.85 us
    pallas_call x1, Pallas kernels, shards(): pl.pallas_call(payload_kernel, out_shape=shape((size + TAIL, width), BF16...  1.76 us
  transfers between devices with their start and end apart: 24, of which 9 were waited for; matrix products, arithmetic and copies ran while one was open for 1% of the time, Pallas kernels for 27%

profile of v13, /device:TPU:0, one launch (start us, length us, event | category | flops | bytes accessed | tf_op | source)
XLA Modules:
  0.0 64.6 jit_solution(4492705578718489983)
XLA Ops:
  0.6 1.8 %shard_map.96.refs_0_.refs_4_ = bf16[144,768]{1,0:T(8,128)(2,1)} custom-call(s32[1,128]{1,0:T(1,128)} %bitcast.12, s32[1,128]{1,0:T(1,128)} %bitcast.13, bf16[128,768]{1,0:T(8,128)(2,1)} %rows_hbm.1), custom_call_target="tpu_custom_call" | custom-call | tf_op jit(solution)/shard_map/pallas_call | solution.py:227
  2.9 3.5 %collective-permute-start.3 = (bf16[144,768]{1,0:T(8,128)(2,1)}, bf16[144,768]{1,0:T(8,128)(2,1)S(1)}, u32[]{:S(2)}, u32[]{:S(2)}) collective-permute-start(bf16[144,768]{1,0:T(8,128)(2,1)} %shard_map.96.refs_0_.refs_4_), channel_id=1, source_target_pairs={{0,6},{1,7},{2,4},{3,5},{4,2},{5,3},{6,0},{7,1},{8,14},{9,15},{10,... | collective-permute-start | bytes 663560 | tf_op jit(solution)/shard_map/ppermute | solution.py:55
  7.9 1.9 %shard_map.94.after_ref.target_ref = bf16[512,1024]{1,0:T(8,128)(2,1)S(1)} custom-call(s32[8,1024]{1,0:T(8,128)S(1)} %bitcast.11), custom_call_target="tpu_custom_call" | custom-call | bytes 8000000 | tf_op jit(solution)/shard_map/pallas_call | solution.py:31
  9.8 1.4 %copy-done = bf16[1024,768]{1,0:T(8,128)(2,1)S(1)} copy-done((bf16[1024,768]{1,0:T(8,128)(2,1)S(1)}, bf16[1024,768]{1,0:T(8,128)(2,1)}, u32[]{:S(2)}) %copy-start) | copy-done | bytes 1572888
  11.2 1.5 %shard_map.95.hidden_t_ref = bf16[768,1024]{1,0:T(8,128)(2,1)S(1)} custom-call(bf16[1024,768]{1,0:T(8,128)(2,1)S(1)} %copy-done, bf16[768,768]{1,0:T(8,128)(2,1)S(1)} %copy-done.2, bf16[512,1024]{1,0:T(8,128)(2,1)S(1)} %shard_map.94.after_ref.target_ref), custom_call_target="tpu_custom_call" | custom-call | flops 1207959552 | bytes 6000000 | tf_op jit(solution)/shard_map/pallas_call | solution.py:31
  12.7 2.0 %shard_map.97 = (bf16[256,1024]{1,0:T(8,128)(2,1)S(1)}, f32[128,768]{1,0:T(8,128)S(1)}, bf16[128,768]{1,0:T(8,128)(2,1)S(1)}) custom-call(s32[4,8]{1,0:T(4,128)S(1)} %bitcast.7, s32[1]{0:T(128)} %bitcast.me_ref, s32[1]{0:T(128)} %bitcast.2.z_ref, bf16[768,1024]{1,0:T(8,128)(2,1)S(1)} %shard_map.95.hidden_t_ref, ...), custom_call_target="tpu_custom_call" | custom-call | flops 805306368 | bytes 5000000 | tf_op jit(solution)/shard_map/pallas_call | solution.py:31
  15.3 2.4 %collective-permute-done.1.value_ref = bf16[144,768]{1,0:T(8,128)(2,1)S(1)} collective-permute-done((bf16[144,768]{1,0:T(8,128)(2,1)}, bf16[144,768]{1,0:T(8,128)(2,1)S(1)}, u32[]{:S(2)}, u32[]{:S(2)}) %collective-permute-start.1) | collective-permute-done | bytes 221216 | tf_op jit(solution)/shard_map/ppermute | solution.py:55
  18.3 2.0 %shard_map.101 = (bf16[256,1024]{1,0:T(8,128)(2,1)S(1)}, f32[128,768]{1,0:T(8,128)S(1)}, bf16[128,768]{1,0:T(8,128)(2,1)S(1)}) custom-call(s32[4,8]{1,0:T(4,128)S(1)} %bitcast.8, s32[1]{0:T(128)} %bitcast.me_ref, s32[1]{0:T(128)} %bitcast.2.z_ref, bf16[768,1024]{1,0:T(8,128)(2,1)S(1)} %shard_map.95.hidden_t_ref, ...), custom_call_target="tpu_custom_call" | custom-call | flops 805306368 | bytes 5000000 | tf_op jit(solution)/shard_map/pallas_call | solution.py:31
  20.4 2.0 %shard_map.102 = (bf16[256,1024]{1,0:T(8,128)(2,1)S(1)}, f32[128,768]{1,0:T(8,128)S(1)}, bf16[128,768]{1,0:T(8,128)(2,1)S(1)}) custom-call(s32[4,8]{1,0:T(4,128)S(1)} %bitcast.9, s32[1]{0:T(128)} %bitcast.me_ref, s32[1]{0:T(128)} %bitcast.2.z_ref, bf16[768,1024]{1,0:T(8,128)(2,1)S(1)} %shard_map.95.hidden_t_ref, ...), custom_call_target="tpu_custom_call" | custom-call | flops 805306368 | bytes 5000000 | tf_op jit(solution)/shard_map/pallas_call | solution.py:31
  22.9 1.9 %collective-permute-start.11 = (bf16[128,768]{1,0:T(8,128)(2,1)S(1)}, bf16[128,768]{1,0:T(8,128)(2,1)S(1)}, u32[]{:S(2)}, u32[]{:S(2)}) collective-permute-start(bf16[128,768]{1,0:T(8,128)(2,1)S(1)} %add_convert_fusion.2.refs_3_.refs_12_), channel_id=1, source_target_pairs={{0,6},{1,7},{2,4},{3,5},{4,2},{5,3},{6,0},{7,1},{8,14},{9,15},{10,... | collective-permute-start | bytes 589832 | tf_op jit(solution)/shard_map/ppermute | solution.py:55
  24.9 2.0 %shard_map.103 = (bf16[256,1024]{1,0:T(8,128)(2,1)S(1)}, f32[128,768]{1,0:T(8,128)S(1)}, bf16[128,768]{1,0:T(8,128)(2,1)S(1)}) custom-call(s32[4,8]{1,0:T(4,128)S(1)} %bitcast.10, s32[1]{0:T(128)} %bitcast.me_ref, s32[1]{0:T(128)} %bitcast.2.z_ref, bf16[768,1024]{1,0:T(8,128)(2,1)S(1)} %shard_map.95.hidden_t_ref, ...), custom_call_target="tpu_custom_call" | custom-call | flops 805306368 | bytes 5000000 | tf_op jit(solution)/shard_map/pallas_call | solution.py:31
  28.4 1.2 %collective-permute-start.13 = (bf16[128,768]{1,0:T(8,128)(2,1)S(1)}, bf16[128,768]{1,0:T(8,128)(2,1)S(1)}, u32[]{:S(2)}, u32[]{:S(2)}) collective-permute-start(bf16[128,768]{1,0:T(8,128)(2,1)S(1)} %add_convert_fusion.refs_14_), channel_id=1, source_target_pairs={{0,4},{1,5},{2,6},{3,7},{4,0},{5,1},{6,2},{7,3},{8,12},{9,13},{10,... | collective-permute-start | bytes 589832 | tf_op jit(solution)/shard_map/ppermute | solution.py:55
  29.6 1.9 %shard_map.104 = (bf16[1024,768]{1,0:T(8,128)(2,1)S(1)}, bf16[1024,768]{1,0:T(8,128)(2,1)S(1)}) custom-call(s32[1]{0:T(128)} %bitcast.me_ref, bf16[256,1024]{1,0:T(8,128)(2,1)S(1)} %get-tuple-element.23.refs_0_.refs_2_, bf16[256,1024]{1,0:T(8,128)(2,1)S(1)} %get-tuple-element.25.refs_2_.refs_1_, bf16[256,1024]{1,0:T(8,128)(2,1)S(1)} %get-tuple-element.28.refs_2_, ...), custom_call_target="tpu_custom_call" | custom-call | flops 1610612736 | bytes 5000000 | tf_op jit(solution)/shard_map/pallas_call | solution.py:31
  31.5 3.5 %shard_map.105 = (f32[1024,768]{1,0:T(8,128)}, f32[8,128]{1,0:T(8,128)S(1)}) custom-call(bf16[1024,768]{1,0:T(8,128)(2,1)S(1)} %get-tuple-element.33.grad_hidden_ref, bf16[768,768]{1,0:T(8,128)(2,1)S(1)} %copy-done.2, f32[128,768]{1,0:T(8,128)S(1)} %convert_add_fusion.after_ref.own_ref), custom_call_target="tpu_custom_call" | custom-call | flops 1207959552 | bytes 6000000 | tf_op jit(solution)/shard_map/pallas_call | solution.py:300
  35.6 1.6 %collective-permute-start.14 = (bf16[64,768]{1,0:T(8,128)(2,1)S(1)}, bf16[64,768]{1,0:T(8,128)(2,1)S(1)}, u32[]{:S(2)}, u32[]{:S(2)}) collective-permute-start(bf16[64,768]{1,0:T(8,128)(2,1)S(1)} %get-tuple-element.39), channel_id=1, source_target_pairs={{0,8},{8,0},{16,24},{24,16},{1,9},{9,1},{17,25},{25,17},{2,10},{10... | collective-permute-start | bytes 294920 | tf_op jit(solution)/shard_map/ppermute | solution.py:55
  37.2 3.0 %collective-permute-done.14 = bf16[64,768]{1,0:T(8,128)(2,1)S(1)} collective-permute-done((bf16[64,768]{1,0:T(8,128)(2,1)S(1)}, bf16[64,768]{1,0:T(8,128)(2,1)S(1)}, u32[]{:S(2)}, u32[]{:S(2)}) %collective-permute-start.14) | collective-permute-done | bytes 98336 | tf_op jit(solution)/shard_map/ppermute | solution.py:55
  40.3 2.7 %collective-permute-start.15 = (bf16[64,768]{1,0:T(8,128)(2,1)S(1)}, bf16[64,768]{1,0:T(8,128)(2,1)S(1)}, u32[]{:S(2)}, u32[]{:S(2)}) collective-permute-start(bf16[64,768]{1,0:T(8,128)(2,1)S(1)} %add_convert_fusion.4), channel_id=1, source_target_pairs={{0,16},{8,24},{16,0},{24,8},{1,17},{9,25},{17,1},{25,9},{2,18},{10... | collective-permute-start | bytes 294920 | tf_op jit(solution)/shard_map/ppermute | solution.py:55
  42.9 2.9 %collective-permute-done.15 = bf16[64,768]{1,0:T(8,128)(2,1)S(1)} collective-permute-done((bf16[64,768]{1,0:T(8,128)(2,1)S(1)}, bf16[64,768]{1,0:T(8,128)(2,1)S(1)}, u32[]{:S(2)}, u32[]{:S(2)}) %collective-permute-start.15) | collective-permute-done | bytes 98336 | tf_op jit(solution)/shard_map/ppermute | solution.py:55
  45.9 1.8 %collective-permute-start.16 = (bf16[64,768]{1,0:T(8,128)(2,1)S(1)}, bf16[64,768]{1,0:T(8,128)(2,1)S(1)}, u32[]{:S(2)}, u32[]{:S(2)}) collective-permute-start(bf16[64,768]{1,0:T(8,128)(2,1)S(1)} %add_convert_fusion.3.refs_0_), channel_id=1, source_target_pairs={{0,8},{8,0},{16,24},{24,16},{1,9},{9,1},{17,25},{25,17},{2,10},{10... | collective-permute-start | bytes 294920 | tf_op jit(solution)/shard_map/ppermute | solution.py:55
  47.7 2.9 %collective-permute-done.16.refs_1_ = bf16[64,768]{1,0:T(8,128)(2,1)S(1)} collective-permute-done((bf16[64,768]{1,0:T(8,128)(2,1)S(1)}, bf16[64,768]{1,0:T(8,128)(2,1)S(1)}, u32[]{:S(2)}, u32[]{:S(2)}) %collective-permute-start.16) | collective-permute-done | bytes 98336 | tf_op jit(solution)/shard_map/ppermute | solution.py:55
  50.7 1.4 %collective-permute-start.18 = (bf16[768,128]{1,0:T(8,128)(2,1)S(1)}, bf16[768,128]{1,0:T(8,128)(2,1)S(1)}, u32[]{:S(2)}, u32[]{:S(2)}) collective-permute-start(bf16[768,128]{1,0:T(8,128)(2,1)S(1)} %shard_map.107.whole_ref.refs_0_), channel_id=1, source_target_pairs={{0,2},{1,3},{2,0},{3,1},{4,6},{5,7},{6,4},{7,5},{8,10},{9,11},{10,... | collective-permute-start | bytes 589832 | tf_op jit(solution)/shard_map/ppermute | solution.py:55
  54.5 1.4 %copy-done.4 = bf16[1024,768]{1,0:T(8,128)(2,1)S(1)} copy-done((bf16[1024,768]{1,0:T(8,128)(2,1)S(1)}, bf16[1024,768]{1,0:T(8,128)(2,1)}, u32[]{:S(2)}) %copy-start.4) | copy-done | bytes 1572888
  57.6 2.3 %collective-permute-done.20.value_ref = bf16[768,128]{1,0:T(8,128)(2,1)S(1)} collective-permute-done((bf16[768,128]{1,0:T(8,128)(2,1)S(1)}, bf16[768,128]{1,0:T(8,128)(2,1)S(1)}, u32[]{:S(2)}, u32[]{:S(2)}) %collective-permute-start.20) | collective-permute-done | bytes 196640 | tf_op jit(solution)/shard_map/ppermute | solution.py:55
  61.6 2.9 %shard_map.112 = f32[768,768]{1,0:T(8,128)} custom-call(s32[1]{0:T(128)} %bitcast.me_ref, bf16[768,128]{1,0:T(8,128)(2,1)S(1)} %shard_map.107.whole_ref.refs_0_, bf16[768,128]{1,0:T(8,128)(2,1)S(1)} %collective-permute-done.17.refs_1_, bf16[768,128]{1,0:T(8,128)(2,1)S(1)} %shard_map.109.refs_2_, bf16[768,128]{1,0:T(8,128)(2,1)S(1)} %collective-permute-done.19.refs_3_, ...), custom_call_target="tpu_custom_call" | custom-call | flops 1207959552 | bytes 6000000 | tf_op jit(solution)/shard_map/pallas_call | solution.py:375
  (66 shorter events, 11.9 us)
Async XLA Ops:
  2.4 10.3 %collective-permute-start = (bf16[144,768]{1,0:T(8,128)(2,1)}, bf16[144,768]{1,0:T(8,128)(2,1)S(1)}, u32[]{:S(2)}, u32[]{:S(2)}) collective-permute-start(bf16[144,768]{1,0:T(8,128)(2,1)} %shard_map.96.refs_0_.refs_4_), channel_id=1, source_target_pairs={{0,1},{1,0},{2,3},{3,2},{4,5},{5,4},{6,7},{7,6},{8,9},{9,8},{10,11... | collective-permute-start | bytes 663560 | tf_op jit(solution)/shard_map/ppermute | solution.py:55
  2.9 11.8 %collective-permute-start.3 = (bf16[144,768]{1,0:T(8,128)(2,1)}, bf16[144,768]{1,0:T(8,128)(2,1)S(1)}, u32[]{:S(2)}, u32[]{:S(2)}) collective-permute-start(bf16[144,768]{1,0:T(8,128)(2,1)} %shard_map.96.refs_0_.refs_4_), channel_id=1, source_target_pairs={{0,6},{1,7},{2,4},{3,5},{4,2},{5,3},{6,0},{7,1},{8,14},{9,15},{10,... | collective-permute-start | bytes 663560 | tf_op jit(solution)/shard_map/ppermute | solution.py:55
  6.5 11.3 %collective-permute-start.1 = (bf16[144,768]{1,0:T(8,128)(2,1)}, bf16[144,768]{1,0:T(8,128)(2,1)S(1)}, u32[]{:S(2)}, u32[]{:S(2)}) collective-permute-start(bf16[144,768]{1,0:T(8,128)(2,1)} %shard_map.96.refs_0_.refs_4_), channel_id=1, source_target_pairs={{0,2},{1,3},{2,0},{3,1},{4,6},{5,7},{6,4},{7,5},{8,10},{9,11},{10,... | collective-permute-start | bytes 663560 | tf_op jit(solution)/shard_map/ppermute | solution.py:55
  7.0 10.8 %collective-permute-start.5 = (bf16[144,768]{1,0:T(8,128)(2,1)}, bf16[144,768]{1,0:T(8,128)(2,1)S(1)}, u32[]{:S(2)}, u32[]{:S(2)}) collective-permute-start(bf16[144,768]{1,0:T(8,128)(2,1)} %shard_map.96.refs_0_.refs_4_), channel_id=1, source_target_pairs={{0,4},{1,5},{2,6},{3,7},{4,0},{5,1},{6,2},{7,3},{8,12},{9,13},{10,... | collective-permute-start | bytes 663560 | tf_op jit(solution)/shard_map/ppermute | solution.py:55
  14.7 3.5 %collective-permute-start.4 = (bf16[144,768]{1,0:T(8,128)(2,1)S(1)}, bf16[144,768]{1,0:T(8,128)(2,1)S(1)}, u32[]{:S(2)}, u32[]{:S(2)}) collective-permute-start(bf16[144,768]{1,0:T(8,128)(2,1)S(1)} %shard_map.99.refs_0_.refs_10_), channel_id=1, source_target_pairs={{0,1},{1,0},{2,3},{3,2},{4,5},{5,4},{6,7},{7,6},{8,9},{9,8},{10,11... | collective-permute-start | bytes 663560 | tf_op jit(solution)/shard_map/ppermute | solution.py:55
  14.8 5.6 %collective-permute-start.10 = (bf16[128,768]{1,0:T(8,128)(2,1)S(1)}, bf16[128,768]{1,0:T(8,128)(2,1)S(1)}, u32[]{:S(2)}, u32[]{:S(2)}) collective-permute-start(bf16[128,768]{1,0:T(8,128)(2,1)S(1)} %get-tuple-element.35), channel_id=1, source_target_pairs={{0,1},{1,0},{2,3},{3,2},{4,5},{5,4},{6,7},{7,6},{8,9},{9,8},{10,11... | collective-permute-start | bytes 589832 | tf_op jit(solution)/shard_map/ppermute | solution.py:55
  17.7 2.7 %collective-permute-start.2 = (bf16[144,768]{1,0:T(8,128)(2,1)S(1)}, bf16[144,768]{1,0:T(8,128)(2,1)S(1)}, u32[]{:S(2)}, u32[]{:S(2)}) collective-permute-start(bf16[144,768]{1,0:T(8,128)(2,1)S(1)} %shard_map.98.refs_3_.refs_0_.refs_6_), channel_id=1, source_target_pairs={{0,1},{1,0},{2,3},{3,2},{4,5},{5,4},{6,7},{7,6},{8,9},{9,8},{10,11... | collective-permute-start | bytes 663560 | tf_op jit(solution)/shard_map/ppermute | solution.py:55
  17.7 7.1 %collective-permute-start.6 = (bf16[144,768]{1,0:T(8,128)(2,1)S(1)}, bf16[144,768]{1,0:T(8,128)(2,1)S(1)}, u32[]{:S(2)}, u32[]{:S(2)}) collective-permute-start(bf16[144,768]{1,0:T(8,128)(2,1)S(1)} %shard_map.100.refs_4_.refs_0_.refs_8_), channel_id=1, source_target_pairs={{0,1},{1,0},{2,3},{3,2},{4,5},{5,4},{6,7},{7,6},{8,9},{9,8},{10,11... | collective-permute-start | bytes 663560 | tf_op jit(solution)/shard_map/ppermute | solution.py:55
  20.2 2.7 %collective-permute-start.7 = (bf16[128,768]{1,0:T(8,128)(2,1)S(1)}, bf16[128,768]{1,0:T(8,128)(2,1)S(1)}, u32[]{:S(2)}, u32[]{:S(2)}) collective-permute-start(bf16[128,768]{1,0:T(8,128)(2,1)S(1)} %get-tuple-element.27), channel_id=1, source_target_pairs={{0,1},{1,0},{2,3},{3,2},{4,5},{5,4},{6,7},{7,6},{8,9},{9,8},{10,11... | collective-permute-start | bytes 589832 | tf_op jit(solution)/shard_map/ppermute | solution.py:55
  22.4 4.7 %collective-permute-start.8 = (bf16[128,768]{1,0:T(8,128)(2,1)S(1)}, bf16[128,768]{1,0:T(8,128)(2,1)S(1)}, u32[]{:S(2)}, u32[]{:S(2)}) collective-permute-start(bf16[128,768]{1,0:T(8,128)(2,1)S(1)} %get-tuple-element.30), channel_id=1, source_target_pairs={{0,1},{1,0},{2,3},{3,2},{4,5},{5,4},{6,7},{7,6},{8,9},{9,8},{10,11... | collective-permute-start | bytes 589832 | tf_op jit(solution)/shard_map/ppermute | solution.py:55
  22.9 12.0 %collective-permute-start.11 = (bf16[128,768]{1,0:T(8,128)(2,1)S(1)}, bf16[128,768]{1,0:T(8,128)(2,1)S(1)}, u32[]{:S(2)}, u32[]{:S(2)}) collective-permute-start(bf16[128,768]{1,0:T(8,128)(2,1)S(1)} %add_convert_fusion.2.refs_3_.refs_12_), channel_id=1, source_target_pairs={{0,6},{1,7},{2,4},{3,5},{4,2},{5,3},{6,0},{7,1},{8,14},{9,15},{10,... | collective-permute-start | bytes 589832 | tf_op jit(solution)/shard_map/ppermute | solution.py:55
  26.8 1.5 %collective-permute-start.9 = (bf16[128,768]{1,0:T(8,128)(2,1)S(1)}, bf16[128,768]{1,0:T(8,128)(2,1)S(1)}, u32[]{:S(2)}, u32[]{:S(2)}) collective-permute-start(bf16[128,768]{1,0:T(8,128)(2,1)S(1)} %get-tuple-element.32), channel_id=1, source_target_pairs={{0,1},{1,0},{2,3},{3,2},{4,5},{5,4},{6,7},{7,6},{8,9},{9,8},{10,11... | collective-permute-start | bytes 589832 | tf_op jit(solution)/shard_map/ppermute | solution.py:55
  27.2 7.8 %collective-permute-start.12 = (bf16[128,768]{1,0:T(8,128)(2,1)S(1)}, bf16[128,768]{1,0:T(8,128)(2,1)S(1)}, u32[]{:S(2)}, u32[]{:S(2)}) collective-permute-start(bf16[128,768]{1,0:T(8,128)(2,1)S(1)} %add_convert_fusion.1.refs_13_), channel_id=1, source_target_pairs={{0,2},{1,3},{2,0},{3,1},{4,6},{5,7},{6,4},{7,5},{8,10},{9,11},{10,... | collective-permute-start | bytes 589832 | tf_op jit(solution)/shard_map/ppermute | solution.py:55
  28.4 7.1 %collective-permute-start.13 = (bf16[128,768]{1,0:T(8,128)(2,1)S(1)}, bf16[128,768]{1,0:T(8,128)(2,1)S(1)}, u32[]{:S(2)}, u32[]{:S(2)}) collective-permute-start(bf16[128,768]{1,0:T(8,128)(2,1)S(1)} %add_convert_fusion.refs_14_), channel_id=1, source_target_pairs={{0,4},{1,5},{2,6},{3,7},{4,0},{5,1},{6,2},{7,3},{8,12},{9,13},{10,... | collective-permute-start | bytes 589832 | tf_op jit(solution)/shard_map/ppermute | solution.py:55
  35.6 4.7 %collective-permute-start.14 = (bf16[64,768]{1,0:T(8,128)(2,1)S(1)}, bf16[64,768]{1,0:T(8,128)(2,1)S(1)}, u32[]{:S(2)}, u32[]{:S(2)}) collective-permute-start(bf16[64,768]{1,0:T(8,128)(2,1)S(1)} %get-tuple-element.39), channel_id=1, source_target_pairs={{0,8},{8,0},{16,24},{24,16},{1,9},{9,1},{17,25},{25,17},{2,10},{10... | collective-permute-start | bytes 294920 | tf_op jit(solution)/shard_map/ppermute | solution.py:55
  40.3 5.6 %collective-permute-start.15 = (bf16[64,768]{1,0:T(8,128)(2,1)S(1)}, bf16[64,768]{1,0:T(8,128)(2,1)S(1)}, u32[]{:S(2)}, u32[]{:S(2)}) collective-permute-start(bf16[64,768]{1,0:T(8,128)(2,1)S(1)} %add_convert_fusion.4), channel_id=1, source_target_pairs={{0,16},{8,24},{16,0},{24,8},{1,17},{9,25},{17,1},{25,9},{2,18},{10... | collective-permute-start | bytes 294920 | tf_op jit(solution)/shard_map/ppermute | solution.py:55
  45.9 4.7 %collective-permute-start.16 = (bf16[64,768]{1,0:T(8,128)(2,1)S(1)}, bf16[64,768]{1,0:T(8,128)(2,1)S(1)}, u32[]{:S(2)}, u32[]{:S(2)}) collective-permute-start(bf16[64,768]{1,0:T(8,128)(2,1)S(1)} %add_convert_fusion.3.refs_0_), channel_id=1, source_target_pairs={{0,8},{8,0},{16,24},{24,16},{1,9},{9,1},{17,25},{25,17},{2,10},{10... | collective-permute-start | bytes 294920 | tf_op jit(solution)/shard_map/ppermute | solution.py:55
  50.7 6.3 %collective-permute-start.18 = (bf16[768,128]{1,0:T(8,128)(2,1)S(1)}, bf16[768,128]{1,0:T(8,128)(2,1)S(1)}, u32[]{:S(2)}, u32[]{:S(2)}) collective-permute-start(bf16[768,128]{1,0:T(8,128)(2,1)S(1)} %shard_map.107.whole_ref.refs_0_), channel_id=1, source_target_pairs={{0,2},{1,3},{2,0},{3,1},{4,6},{5,7},{6,4},{7,5},{8,10},{9,11},{10,... | collective-permute-start | bytes 589832 | tf_op jit(solution)/shard_map/ppermute | solution.py:55
  52.1 7.8 %collective-permute-start.20 = (bf16[768,128]{1,0:T(8,128)(2,1)S(1)}, bf16[768,128]{1,0:T(8,128)(2,1)S(1)}, u32[]{:S(2)}, u32[]{:S(2)}) collective-permute-start(bf16[768,128]{1,0:T(8,128)(2,1)S(1)} %shard_map.107.whole_ref.refs_0_), channel_id=1, source_target_pairs={{0,4},{1,5},{2,6},{3,7},{4,0},{5,1},{6,2},{7,3},{8,12},{9,13},{10,... | collective-permute-start | bytes 589832 | tf_op jit(solution)/shard_map/ppermute | solution.py:55
  53.1 6.7 %collective-permute-start.22 = (bf16[768,128]{1,0:T(8,128)(2,1)S(1)}, bf16[768,128]{1,0:T(8,128)(2,1)S(1)}, u32[]{:S(2)}, u32[]{:S(2)}) collective-permute-start(bf16[768,128]{1,0:T(8,128)(2,1)S(1)} %shard_map.107.whole_ref.refs_0_), channel_id=1, source_target_pairs={{0,6},{1,7},{2,4},{3,5},{4,2},{5,3},{6,0},{7,1},{8,14},{9,15},{10,... | collective-permute-start | bytes 589832 | tf_op jit(solution)/shard_map/ppermute | solution.py:55
  54.5 5.9 %collective-permute-start.17 = (bf16[768,128]{1,0:T(8,128)(2,1)S(1)}, bf16[768,128]{1,0:T(8,128)(2,1)S(1)}, u32[]{:S(2)}, u32[]{:S(2)}) collective-permute-start(bf16[768,128]{1,0:T(8,128)(2,1)S(1)} %shard_map.107.whole_ref.refs_0_), channel_id=1, source_target_pairs={{0,1},{1,0},{2,3},{3,2},{4,5},{5,4},{6,7},{7,6},{8,9},{9,8},{10,11... | collective-permute-start | bytes 589832 | tf_op jit(solution)/shard_map/ppermute | solution.py:55
  57.0 3.4 %collective-permute-start.19 = (bf16[768,128]{1,0:T(8,128)(2,1)S(1)}, bf16[768,128]{1,0:T(8,128)(2,1)S(1)}, u32[]{:S(2)}, u32[]{:S(2)}) collective-permute-start(bf16[768,128]{1,0:T(8,128)(2,1)S(1)} %shard_map.109.refs_2_), channel_id=1, source_target_pairs={{0,1},{1,0},{2,3},{3,2},{4,5},{5,4},{6,7},{7,6},{8,9},{9,8},{10,11... | collective-permute-start | bytes 589832 | tf_op jit(solution)/shard_map/ppermute | solution.py:55
  59.9 1.4 %collective-permute-start.21 = (bf16[768,128]{1,0:T(8,128)(2,1)S(1)}, bf16[768,128]{1,0:T(8,128)(2,1)S(1)}, u32[]{:S(2)}, u32[]{:S(2)}) collective-permute-start(bf16[768,128]{1,0:T(8,128)(2,1)S(1)} %shard_map.110.refs_4_), channel_id=1, source_target_pairs={{0,1},{1,0},{2,3},{3,2},{4,5},{5,4},{6,7},{7,6},{8,9},{9,8},{10,11... | collective-permute-start | bytes 589832 | tf_op jit(solution)/shard_map/ppermute | solution.py:55
  59.9 1.7 %collective-permute-start.23 = (bf16[768,128]{1,0:T(8,128)(2,1)S(1)}, bf16[768,128]{1,0:T(8,128)(2,1)S(1)}, u32[]{:S(2)}, u32[]{:S(2)}) collective-permute-start(bf16[768,128]{1,0:T(8,128)(2,1)S(1)} %shard_map.111.refs_6_), channel_id=1, source_target_pairs={{0,1},{1,0},{2,3},{3,2},{4,5},{5,4},{6,7},{7,6},{8,9},{9,8},{10,11... | collective-permute-start | bytes 589832 | tf_op jit(solution)/shard_map/ppermute | solution.py:55
  (8 other events, 21.4 us)

commit v14 on v13

--- a/solution.py
+++ b/solution.py
@@ -88,7 +88,8 @@
             ).astype(BF16)
 
 
-def inputs_kernel(enc_ref, proj_ref, after_ref, hidden_t_ref):
+def inputs_kernel(enc_ref, proj_ref, *refs):
+    hidden_t_ref = refs[-1]
     samples = enc_ref.shape[0]
     tile = min(256, samples)
     for start in range(0, samples, tile):
@@ -102,8 +103,8 @@
     return guess * (2.0 - bottom * guess)
 
 
-def score_kernel(group, block, count, list_ref, me_ref, z_ref, hidden_t_ref, target_ref, enc_ref, *refs):
-    payloads, refs = refs[:2], refs[-6:]
+def score_kernel(group, block, count, halves, list_ref, me_ref, z_ref, hidden_t_ref, enc_ref, *refs):
+    targets, payloads, refs = refs[:halves], refs[halves : halves + 2], refs[-6:]
     grads_ref, kept_ref, sent_ref, weights_ref, scale_ref, logits_ref = refs
     samples = enc_ref.shape[0]
     size = payloads[0].shape[0] - TAIL
@@ -127,7 +128,8 @@
                 factor = jnp.where(place >= 0, 1.0 / block, 0.0)
                 first = pl.multiple_of(jnp.maximum(place, 0) * size, size)
                 rows = slice(core * size, (core + 1) * size)
-                target = target_ref[pl.ds(first, size), low : low + block].astype(F32)
+                half, column = divmod(low, samples // halves)
+                target = targets[half][pl.ds(first, size), column : column + block].astype(F32)
                 share = logistic(logits_ref[rows, low : low + block]) - target
                 grads_ref[rows, low : low + block] = (scale_ref[rows, :] * factor * share).astype(BF16)
     outer = dot(grads_ref[...], enc_ref[...], NN)
@@ -236,18 +238,22 @@
     for g in far + near:
         got[2 * g] = swap(payload, "label", 2 * g)
     got[1] = swap(payload, "label", 1)
-    (target,) = call(
-        functools.partial(target_kernel, beam, block),
-        [shape((beam * size, samples), BF16)],
-        [positives.T],
-        vmem=2,
-        nbytes=8_000_000,
-    )
+    halves = 2 if blocks % 2 == 0 else 1
+    targets = [
+        call(
+            functools.partial(target_kernel, beam, block),
+            [shape((beam * size, samples // halves), BF16)],
+            [part],
+            vmem=2,
+            nbytes=8_000_000 // halves,
+        )[0]
+        for part in jnp.split(positives.T, halves, axis=1)
+    ]
     (hidden_t,) = call(
         inputs_kernel,
         [shape((width, samples), BF16)],
         [enc, proj],
-        after=[target],
+        after=targets,
         flops=2 * samples * width * width,
         nbytes=6_000_000,
     )
@@ -260,9 +266,9 @@
         if at >= 3:
             after.append(moved[order[at - 2]])
         grads[g], kept[g], sent = call(
-            functools.partial(score_kernel, g, block, row_blocks),
+            functools.partial(score_kernel, g, block, row_blocks, halves),
             [shape((2 * size, samples), BF16), shape((size, width), F32), shape((size, width), BF16)],
-            [hidden_t, target, enc, got[2 * g], got[2 * g + 1]],
+            [hidden_t, enc, *targets, got[2 * g], got[2 * g + 1]],
             scalars=[listed, me_s, z_s],
             after=after,
             scratch=[

time: 64.9 us -> 68.3 us (1.052)
  waiting for transfers between devices: 15.9 us -> 20.7 us
  local copies, waits for them, and re-layouts: 3.76 us -> 2.2 us
  Pallas kernels: 22.5 us -> 23.3 us
    ppermute x24, waiting for transfers between devices: 15.9 us -> 20.7 us  [swap(): return lax.ppermute(value, axis, [(i, i ^ distance) for i in range(size)])]
    unnamed x16 -> x14, local copies, waits for them, and re-layouts: 3.59 us -> 1.29 us
    pallas_call x1, Pallas kernels: 2.85 us -> 3.82 us  [shards(): pl.pallas_call(functools.partial(proj_kernel, cuts), out_shape=shape((wid...]
    split x0 -> x1, local copies, waits for them, and re-layouts: none -> 0.74 us  [shards(): jnp.split(positives.T, halves, axis=1)]
    pallas_call x9 -> x10, Pallas kernels: 13.3 us -> 13.2 us  [call(): pl.pallas_call(kernel, out_shape=outs, in_specs=[SMEM] * len(scalars) + [...]
  transfers between devices with their start and end apart: 24 -> 24, of which waited for: 9 -> 12; matrix products, arithmetic and copies ran while one was open for 1% -> 2% of each run, Pallas kernels for 27% -> 26%
where the time goes in v14:
time: 68.3 us; the launch traced here: 68 us
  Pallas kernels  23.3 us (34%)
  waiting for transfers between devices  20.7 us (30%)
  starting transfers between devices  20.5 us (30%)
  local copies, waits for them, and re-layouts  2.2 us (3%)
  between operations  1.04 us (2%)
    ppermute x24, waiting for transfers between devices, swap(): return lax.ppermute(value, axis, [(i, i ^ distance) for i in range(size)])  20.7 us
    ppermute x24, starting transfers between devices, swap(): return lax.ppermute(value, axis, [(i, i ^ distance) for i in range(size)])  20.5 us
    pallas_call x10, Pallas kernels, call(): pl.pallas_call(kernel, out_shape=outs, in_specs=[SMEM] * len(scalars) + [...  13.2 us
    pallas_call x1, Pallas kernels, shards(): pl.pallas_call(functools.partial(proj_kernel, cuts), out_shape=shape((wid...  3.82 us
    pallas_call x1, Pallas kernels, grad_enc_after(): pl.pallas_call(enc_kernel, grid=(samples // tile,), out_shape=[shape((sam...  3.49 us
    pallas_call x1, Pallas kernels, shards(): pl.pallas_call(payload_kernel, out_shape=shape((size + TAIL, width), BF16...  1.79 us
  transfers between devices with their start and end apart: 24, of which 12 were waited for; matrix products, arithmetic and copies ran while one was open for 2% of the time, Pallas kernels for 26%

profile of v14, /device:TPU:0, one launch (start us, length us, event | category | flops | bytes accessed | tf_op | source)
XLA Modules:
  0.0 68.0 jit_solution(11187957824767751004)
XLA Ops:
  0.6 1.8 %shard_map.97.refs_2_.refs_4_ = bf16[144,768]{1,0:T(8,128)(2,1)} custom-call(s32[1,128]{1,0:T(1,128)} %bitcast.12, s32[1,128]{1,0:T(1,128)} %bitcast.13, bf16[128,768]{1,0:T(8,128)(2,1)} %rows_hbm.1), custom_call_target="tpu_custom_call" | custom-call | tf_op jit(solution)/shard_map/pallas_call | solution.py:229
  3.0 2.6 %collective-permute-start.1 = (bf16[144,768]{1,0:T(8,128)(2,1)}, bf16[144,768]{1,0:T(8,128)(2,1)S(1)}, u32[]{:S(2)}, u32[]{:S(2)}) collective-permute-start(bf16[144,768]{1,0:T(8,128)(2,1)} %shard_map.97.refs_2_.refs_4_), channel_id=1, source_target_pairs={{0,2},{1,3},{2,0},{3,1},{4,6},{5,7},{6,4},{7,5},{8,10},{9,11},{10,... | collective-permute-start | bytes 663560 | tf_op jit(solution)/shard_map/ppermute | solution.py:55
  5.5 1.5 %collective-permute-start.3 = (bf16[144,768]{1,0:T(8,128)(2,1)}, bf16[144,768]{1,0:T(8,128)(2,1)S(1)}, u32[]{:S(2)}, u32[]{:S(2)}) collective-permute-start(bf16[144,768]{1,0:T(8,128)(2,1)} %shard_map.97.refs_2_.refs_4_), channel_id=1, source_target_pairs={{0,6},{1,7},{2,4},{3,5},{4,2},{5,3},{6,0},{7,1},{8,14},{9,15},{10,... | collective-permute-start | bytes 663560 | tf_op jit(solution)/shard_map/ppermute | solution.py:55
  11.0 1.5 %shard_map.96.hidden_t_ref = bf16[768,1024]{1,0:T(8,128)(2,1)S(1)} custom-call(bf16[1024,768]{1,0:T(8,128)(2,1)S(1)} %copy-done, bf16[768,768]{1,0:T(8,128)(2,1)S(1)} %copy-done.1, bf16[512,512]{1,0:T(8,128)(2,1)S(1)} %shard_map.94.refs_0_, bf16[512,512]{1,0:T(8,128)(2,1)S(1)} %shard_map.95.refs_1_), custom_call_target="tpu_custom_call" | custom-call | flops 1207959552 | bytes 6000000 | tf_op jit(solution)/shard_map/pallas_call | solution.py:31
  12.5 1.9 %shard_map.98 = (bf16[256,1024]{1,0:T(8,128)(2,1)S(1)}, f32[128,768]{1,0:T(8,128)S(1)}, bf16[128,768]{1,0:T(8,128)(2,1)S(1)}) custom-call(s32[4,8]{1,0:T(4,128)S(1)} %bitcast.7, s32[1]{0:T(128)} %bitcast.me_ref, s32[1]{0:T(128)} %bitcast.2.z_ref, bf16[768,1024]{1,0:T(8,128)(2,1)S(1)} %shard_map.96.hidden_t_ref, bf16[1024,768]{1,0:T(8,128)(2,1)S(1)} %copy-done, ...), custom_call_target="tpu_custom_call" | custom-call | flops 805306368 | bytes 5000000 | tf_op jit(solution)/shard_map/pallas_call | solution.py:31
  14.5 3.4 %collective-permute-done.3.value_ref = bf16[144,768]{1,0:T(8,128)(2,1)S(1)} collective-permute-done((bf16[144,768]{1,0:T(8,128)(2,1)}, bf16[144,768]{1,0:T(8,128)(2,1)S(1)}, u32[]{:S(2)}, u32[]{:S(2)}) %collective-permute-start.3) | collective-permute-done | bytes 221216 | tf_op jit(solution)/shard_map/ppermute | solution.py:55
  19.3 1.9 %shard_map.102 = (bf16[256,1024]{1,0:T(8,128)(2,1)S(1)}, f32[128,768]{1,0:T(8,128)S(1)}, bf16[128,768]{1,0:T(8,128)(2,1)S(1)}) custom-call(s32[4,8]{1,0:T(4,128)S(1)} %bitcast.8, s32[1]{0:T(128)} %bitcast.me_ref, s32[1]{0:T(128)} %bitcast.2.z_ref, bf16[768,1024]{1,0:T(8,128)(2,1)S(1)} %shard_map.96.hidden_t_ref, bf16[1024,768]{1,0:T(8,128)(2,1)S(1)} %copy-done, ...), custom_call_target="tpu_custom_call" | custom-call | flops 805306368 | bytes 5000000 | tf_op jit(solution)/shard_map/pallas_call | solution.py:31
  21.7 1.9 %shard_map.103 = (bf16[256,1024]{1,0:T(8,128)(2,1)S(1)}, f32[128,768]{1,0:T(8,128)S(1)}, bf16[128,768]{1,0:T(8,128)(2,1)S(1)}) custom-call(s32[4,8]{1,0:T(4,128)S(1)} %bitcast.9, s32[1]{0:T(128)} %bitcast.me_ref, s32[1]{0:T(128)} %bitcast.2.z_ref, bf16[768,1024]{1,0:T(8,128)(2,1)S(1)} %shard_map.96.hidden_t_ref, bf16[1024,768]{1,0:T(8,128)(2,1)S(1)} %copy-done, ...), custom_call_target="tpu_custom_call" | custom-call | flops 805306368 | bytes 5000000 | tf_op jit(solution)/shard_map/pallas_call | solution.py:31
  23.9 1.5 %collective-permute-start.11 = (bf16[128,768]{1,0:T(8,128)(2,1)S(1)}, bf16[128,768]{1,0:T(8,128)(2,1)S(1)}, u32[]{:S(2)}, u32[]{:S(2)}) collective-permute-start(bf16[128,768]{1,0:T(8,128)(2,1)S(1)} %add_convert_fusion.2.refs_5_.refs_12_), channel_id=1, source_target_pairs={{0,6},{1,7},{2,4},{3,5},{4,2},{5,3},{6,0},{7,1},{8,14},{9,15},{10,... | collective-permute-start | bytes 589832 | tf_op jit(solution)/shard_map/ppermute | solution.py:55
  25.4 1.9 %shard_map.104 = (bf16[256,1024]{1,0:T(8,128)(2,1)S(1)}, f32[128,768]{1,0:T(8,128)S(1)}, bf16[128,768]{1,0:T(8,128)(2,1)S(1)}) custom-call(s32[4,8]{1,0:T(4,128)S(1)} %bitcast.10, s32[1]{0:T(128)} %bitcast.me_ref, s32[1]{0:T(128)} %bitcast.2.z_ref, bf16[768,1024]{1,0:T(8,128)(2,1)S(1)} %shard_map.96.hidden_t_ref, bf16[1024,768]{1,0:T(8,128)(2,1)S(1)} %copy-done, ...), custom_call_target="tpu_custom_call" | custom-call | flops 805306368 | bytes 5000000 | tf_op jit(solution)/shard_map/pallas_call | solution.py:31
  28.9 1.6 %collective-permute-start.13 = (bf16[128,768]{1,0:T(8,128)(2,1)S(1)}, bf16[128,768]{1,0:T(8,128)(2,1)S(1)}, u32[]{:S(2)}, u32[]{:S(2)}) collective-permute-start(bf16[128,768]{1,0:T(8,128)(2,1)S(1)} %add_convert_fusion.refs_14_), channel_id=1, source_target_pairs={{0,4},{1,5},{2,6},{3,7},{4,0},{5,1},{6,2},{7,3},{8,12},{9,13},{10,... | collective-permute-start | bytes 589832 | tf_op jit(solution)/shard_map/ppermute | solution.py:55
  30.5 1.9 %shard_map.105 = (bf16[1024,768]{1,0:T(8,128)(2,1)S(1)}, bf16[1024,768]{1,0:T(8,128)(2,1)S(1)}) custom-call(s32[1]{0:T(128)} %bitcast.me_ref, bf16[256,1024]{1,0:T(8,128)(2,1)S(1)} %get-tuple-element.23.refs_0_.refs_4_, bf16[256,1024]{1,0:T(8,128)(2,1)S(1)} %get-tuple-element.25.refs_4_.refs_1_, bf16[256,1024]{1,0:T(8,128)(2,1)S(1)} %get-tuple-element.28.refs_2_, ...), custom_call_target="tpu_custom_call" | custom-call | flops 1610612736 | bytes 5000000 | tf_op jit(solution)/shard_map/pallas_call | solution.py:31
  32.4 3.5 %shard_map.106 = (f32[1024,768]{1,0:T(8,128)}, f32[8,128]{1,0:T(8,128)S(1)}) custom-call(bf16[1024,768]{1,0:T(8,128)(2,1)S(1)} %get-tuple-element.33.grad_hidden_ref, bf16[768,768]{1,0:T(8,128)(2,1)S(1)} %copy-done.2, f32[128,768]{1,0:T(8,128)S(1)} %convert_add_fusion.after_ref.own_ref), custom_call_target="tpu_custom_call" | custom-call | flops 1207959552 | bytes 6000000 | tf_op jit(solution)/shard_map/pallas_call | solution.py:306
  36.4 1.6 %collective-permute-start.14 = (bf16[64,768]{1,0:T(8,128)(2,1)S(1)}, bf16[64,768]{1,0:T(8,128)(2,1)S(1)}, u32[]{:S(2)}, u32[]{:S(2)}) collective-permute-start(bf16[64,768]{1,0:T(8,128)(2,1)S(1)} %get-tuple-element.39), channel_id=1, source_target_pairs={{0,8},{8,0},{16,24},{24,16},{1,9},{9,1},{17,25},{25,17},{2,10},{10... | collective-permute-start | bytes 294920 | tf_op jit(solution)/shard_map/ppermute | solution.py:55
  38.1 3.0 %collective-permute-done.14 = bf16[64,768]{1,0:T(8,128)(2,1)S(1)} collective-permute-done((bf16[64,768]{1,0:T(8,128)(2,1)S(1)}, bf16[64,768]{1,0:T(8,128)(2,1)S(1)}, u32[]{:S(2)}, u32[]{:S(2)}) %collective-permute-start.14) | collective-permute-done | bytes 98336 | tf_op jit(solution)/shard_map/ppermute | solution.py:55
  41.1 2.6 %collective-permute-start.15 = (bf16[64,768]{1,0:T(8,128)(2,1)S(1)}, bf16[64,768]{1,0:T(8,128)(2,1)S(1)}, u32[]{:S(2)}, u32[]{:S(2)}) collective-permute-start(bf16[64,768]{1,0:T(8,128)(2,1)S(1)} %add_convert_fusion.4), channel_id=1, source_target_pairs={{0,16},{8,24},{16,0},{24,8},{1,17},{9,25},{17,1},{25,9},{2,18},{10... | collective-permute-start | bytes 294920 | tf_op jit(solution)/shard_map/ppermute | solution.py:55
  43.8 2.9 %collective-permute-done.15 = bf16[64,768]{1,0:T(8,128)(2,1)S(1)} collective-permute-done((bf16[64,768]{1,0:T(8,128)(2,1)S(1)}, bf16[64,768]{1,0:T(8,128)(2,1)S(1)}, u32[]{:S(2)}, u32[]{:S(2)}) %collective-permute-start.15) | collective-permute-done | bytes 98336 | tf_op jit(solution)/shard_map/ppermute | solution.py:55
  46.7 1.8 %collective-permute-start.16 = (bf16[64,768]{1,0:T(8,128)(2,1)S(1)}, bf16[64,768]{1,0:T(8,128)(2,1)S(1)}, u32[]{:S(2)}, u32[]{:S(2)}) collective-permute-start(bf16[64,768]{1,0:T(8,128)(2,1)S(1)} %add_convert_fusion.3.refs_0_), channel_id=1, source_target_pairs={{0,8},{8,0},{16,24},{24,16},{1,9},{9,1},{17,25},{25,17},{2,10},{10... | collective-permute-start | bytes 294920 | tf_op jit(solution)/shard_map/ppermute | solution.py:55
  48.5 2.9 %collective-permute-done.16.refs_1_ = bf16[64,768]{1,0:T(8,128)(2,1)S(1)} collective-permute-done((bf16[64,768]{1,0:T(8,128)(2,1)S(1)}, bf16[64,768]{1,0:T(8,128)(2,1)S(1)}, u32[]{:S(2)}, u32[]{:S(2)}) %collective-permute-start.16) | collective-permute-done | bytes 98336 | tf_op jit(solution)/shard_map/ppermute | solution.py:55
  51.6 2.8 %collective-permute-start.18 = (bf16[768,128]{1,0:T(8,128)(2,1)S(1)}, bf16[768,128]{1,0:T(8,128)(2,1)}, u32[]{:S(2)}, u32[]{:S(2)}) collective-permute-start(bf16[768,128]{1,0:T(8,128)(2,1)S(1)} %shard_map.108.whole_ref.refs_0_), channel_id=1, source_target_pairs={{0,2},{1,3},{2,0},{3,1},{4,6},{5,7},{6,4},{7,5},{8,10},{9,11},{10,... | collective-permute-start | bytes 589832 | tf_op jit(solution)/shard_map/ppermute | solution.py:55
  54.4 1.5 %collective-permute-start.22 = (bf16[768,128]{1,0:T(8,128)(2,1)S(1)}, bf16[768,128]{1,0:T(8,128)(2,1)S(1)}, u32[]{:S(2)}, u32[]{:S(2)}) collective-permute-start(bf16[768,128]{1,0:T(8,128)(2,1)S(1)} %shard_map.108.whole_ref.refs_0_), channel_id=1, source_target_pairs={{0,6},{1,7},{2,4},{3,5},{4,2},{5,3},{6,0},{7,1},{8,14},{9,15},{10,... | collective-permute-start | bytes 589832 | tf_op jit(solution)/shard_map/ppermute | solution.py:55
  57.3 2.0 %collective-permute-done.18.value_ref = bf16[768,128]{1,0:T(8,128)(2,1)} collective-permute-done((bf16[768,128]{1,0:T(8,128)(2,1)S(1)}, bf16[768,128]{1,0:T(8,128)(2,1)}, u32[]{:S(2)}, u32[]{:S(2)}) %collective-permute-start.18) | collective-permute-done | bytes 196640 | tf_op jit(solution)/shard_map/ppermute | solution.py:55
  59.2 3.0 %collective-permute-done.20.value_ref = bf16[768,128]{1,0:T(8,128)(2,1)} collective-permute-done((bf16[768,128]{1,0:T(8,128)(2,1)S(1)}, bf16[768,128]{1,0:T(8,128)(2,1)}, u32[]{:S(2)}, u32[]{:S(2)}) %collective-permute-start.20) | collective-permute-done | bytes 196640 | tf_op jit(solution)/shard_map/ppermute | solution.py:55
  64.0 3.8 %shard_map.113 = f32[768,768]{1,0:T(8,128)} custom-call(s32[1]{0:T(128)} %bitcast.me_ref, bf16[768,128]{1,0:T(8,128)(2,1)S(1)} %shard_map.108.whole_ref.refs_0_, bf16[768,128]{1,0:T(8,128)(2,1)S(1)} %collective-permute-done.17.refs_1_, bf16[768,128]{1,0:T(8,128)(2,1)} %shard_map.110.refs_2_, bf16[768,128]{1,0:T(8,128)(2,1)S(1)} %collective-permute-done.19.refs_3_, ...), custom_call_target="tpu_custom_call" | custom-call | flops 1207959552 | bytes 6000000 | tf_op jit(solution)/shard_map/pallas_call | solution.py:381
  (66 shorter events, 11.9 us)
Async XLA Ops:
  2.4 10.1 %collective-permute-start = (bf16[144,768]{1,0:T(8,128)(2,1)}, bf16[144,768]{1,0:T(8,128)(2,1)S(1)}, u32[]{:S(2)}, u32[]{:S(2)}) collective-permute-start(bf16[144,768]{1,0:T(8,128)(2,1)} %shard_map.97.refs_2_.refs_4_), channel_id=1, source_target_pairs={{0,1},{1,0},{2,3},{3,2},{4,5},{5,4},{6,7},{7,6},{8,9},{9,8},{10,11... | collective-permute-start | bytes 663560 | tf_op jit(solution)/shard_map/ppermute | solution.py:55
  3.0 15.4 %collective-permute-start.1 = (bf16[144,768]{1,0:T(8,128)(2,1)}, bf16[144,768]{1,0:T(8,128)(2,1)S(1)}, u32[]{:S(2)}, u32[]{:S(2)}) collective-permute-start(bf16[144,768]{1,0:T(8,128)(2,1)} %shard_map.97.refs_2_.refs_4_), channel_id=1, source_target_pairs={{0,2},{1,3},{2,0},{3,1},{4,6},{5,7},{6,4},{7,5},{8,10},{9,11},{10,... | collective-permute-start | bytes 663560 | tf_op jit(solution)/shard_map/ppermute | solution.py:55
  5.5 12.3 %collective-permute-start.3 = (bf16[144,768]{1,0:T(8,128)(2,1)}, bf16[144,768]{1,0:T(8,128)(2,1)S(1)}, u32[]{:S(2)}, u32[]{:S(2)}) collective-permute-start(bf16[144,768]{1,0:T(8,128)(2,1)} %shard_map.97.refs_2_.refs_4_), channel_id=1, source_target_pairs={{0,6},{1,7},{2,4},{3,5},{4,2},{5,3},{6,0},{7,1},{8,14},{9,15},{10,... | collective-permute-start | bytes 663560 | tf_op jit(solution)/shard_map/ppermute | solution.py:55
  7.0 12.2 %collective-permute-start.5 = (bf16[144,768]{1,0:T(8,128)(2,1)}, bf16[144,768]{1,0:T(8,128)(2,1)S(1)}, u32[]{:S(2)}, u32[]{:S(2)}) collective-permute-start(bf16[144,768]{1,0:T(8,128)(2,1)} %shard_map.97.refs_2_.refs_4_), channel_id=1, source_target_pairs={{0,4},{1,5},{2,6},{3,7},{4,0},{5,1},{6,2},{7,3},{8,12},{9,13},{10,... | collective-permute-start | bytes 663560 | tf_op jit(solution)/shard_map/ppermute | solution.py:55
  17.8 1.5 %collective-permute-start.4 = (bf16[144,768]{1,0:T(8,128)(2,1)S(1)}, bf16[144,768]{1,0:T(8,128)(2,1)S(1)}, u32[]{:S(2)}, u32[]{:S(2)}) collective-permute-start(bf16[144,768]{1,0:T(8,128)(2,1)S(1)} %shard_map.100.refs_2_.refs_10_), channel_id=1, source_target_pairs={{0,1},{1,0},{2,3},{3,2},{4,5},{5,4},{6,7},{7,6},{8,9},{9,8},{10,11... | collective-permute-start | bytes 663560 | tf_op jit(solution)/shard_map/ppermute | solution.py:55
  17.8 3.9 %collective-permute-start.10 = (bf16[128,768]{1,0:T(8,128)(2,1)S(1)}, bf16[128,768]{1,0:T(8,128)(2,1)S(1)}, u32[]{:S(2)}, u32[]{:S(2)}) collective-permute-start(bf16[128,768]{1,0:T(8,128)(2,1)S(1)} %get-tuple-element.35), channel_id=1, source_target_pairs={{0,1},{1,0},{2,3},{3,2},{4,5},{5,4},{6,7},{7,6},{8,9},{9,8},{10,11... | collective-permute-start | bytes 589832 | tf_op jit(solution)/shard_map/ppermute | solution.py:55
  18.3 3.4 %collective-permute-start.2 = (bf16[144,768]{1,0:T(8,128)(2,1)S(1)}, bf16[144,768]{1,0:T(8,128)(2,1)S(1)}, u32[]{:S(2)}, u32[]{:S(2)}) collective-permute-start(bf16[144,768]{1,0:T(8,128)(2,1)S(1)} %shard_map.99.refs_5_.refs_2_.refs_6_), channel_id=1, source_target_pairs={{0,1},{1,0},{2,3},{3,2},{4,5},{5,4},{6,7},{7,6},{8,9},{9,8},{10,11... | collective-permute-start | bytes 663560 | tf_op jit(solution)/shard_map/ppermute | solution.py:55
  19.2 6.3 %collective-permute-start.6 = (bf16[144,768]{1,0:T(8,128)(2,1)S(1)}, bf16[144,768]{1,0:T(8,128)(2,1)S(1)}, u32[]{:S(2)}, u32[]{:S(2)}) collective-permute-start(bf16[144,768]{1,0:T(8,128)(2,1)S(1)} %shard_map.101.refs_6_.refs_2_.refs_8_), channel_id=1, source_target_pairs={{0,1},{1,0},{2,3},{3,2},{4,5},{5,4},{6,7},{7,6},{8,9},{9,8},{10,11... | collective-permute-start | bytes 663560 | tf_op jit(solution)/shard_map/ppermute | solution.py:55
  21.2 2.6 %collective-permute-start.7 = (bf16[128,768]{1,0:T(8,128)(2,1)S(1)}, bf16[128,768]{1,0:T(8,128)(2,1)S(1)}, u32[]{:S(2)}, u32[]{:S(2)}) collective-permute-start(bf16[128,768]{1,0:T(8,128)(2,1)S(1)} %get-tuple-element.27), channel_id=1, source_target_pairs={{0,1},{1,0},{2,3},{3,2},{4,5},{5,4},{6,7},{7,6},{8,9},{9,8},{10,11... | collective-permute-start | bytes 589832 | tf_op jit(solution)/shard_map/ppermute | solution.py:55
  23.7 3.8 %collective-permute-start.8 = (bf16[128,768]{1,0:T(8,128)(2,1)S(1)}, bf16[128,768]{1,0:T(8,128)(2,1)S(1)}, u32[]{:S(2)}, u32[]{:S(2)}) collective-permute-start(bf16[128,768]{1,0:T(8,128)(2,1)S(1)} %get-tuple-element.30), channel_id=1, source_target_pairs={{0,1},{1,0},{2,3},{3,2},{4,5},{5,4},{6,7},{7,6},{8,9},{9,8},{10,11... | collective-permute-start | bytes 589832 | tf_op jit(solution)/shard_map/ppermute | solution.py:55
  23.9 12.0 %collective-permute-start.11 = (bf16[128,768]{1,0:T(8,128)(2,1)S(1)}, bf16[128,768]{1,0:T(8,128)(2,1)S(1)}, u32[]{:S(2)}, u32[]{:S(2)}) collective-permute-start(bf16[128,768]{1,0:T(8,128)(2,1)S(1)} %add_convert_fusion.2.refs_5_.refs_12_), channel_id=1, source_target_pairs={{0,6},{1,7},{2,4},{3,5},{4,2},{5,3},{6,0},{7,1},{8,14},{9,15},{10,... | collective-permute-start | bytes 589832 | tf_op jit(solution)/shard_map/ppermute | solution.py:55
  27.4 1.5 %collective-permute-start.9 = (bf16[128,768]{1,0:T(8,128)(2,1)S(1)}, bf16[128,768]{1,0:T(8,128)(2,1)S(1)}, u32[]{:S(2)}, u32[]{:S(2)}) collective-permute-start(bf16[128,768]{1,0:T(8,128)(2,1)S(1)} %get-tuple-element.32), channel_id=1, source_target_pairs={{0,1},{1,0},{2,3},{3,2},{4,5},{5,4},{6,7},{7,6},{8,9},{9,8},{10,11... | collective-permute-start | bytes 589832 | tf_op jit(solution)/shard_map/ppermute | solution.py:55
  27.6 8.4 %collective-permute-start.12 = (bf16[128,768]{1,0:T(8,128)(2,1)S(1)}, bf16[128,768]{1,0:T(8,128)(2,1)S(1)}, u32[]{:S(2)}, u32[]{:S(2)}) collective-permute-start(bf16[128,768]{1,0:T(8,128)(2,1)S(1)} %add_convert_fusion.1.refs_13_), channel_id=1, source_target_pairs={{0,2},{1,3},{2,0},{3,1},{4,6},{5,7},{6,4},{7,5},{8,10},{9,11},{10,... | collective-permute-start | bytes 589832 | tf_op jit(solution)/shard_map/ppermute | solution.py:55
  28.9 7.4 %collective-permute-start.13 = (bf16[128,768]{1,0:T(8,128)(2,1)S(1)}, bf16[128,768]{1,0:T(8,128)(2,1)S(1)}, u32[]{:S(2)}, u32[]{:S(2)}) collective-permute-start(bf16[128,768]{1,0:T(8,128)(2,1)S(1)} %add_convert_fusion.refs_14_), channel_id=1, source_target_pairs={{0,4},{1,5},{2,6},{3,7},{4,0},{5,1},{6,2},{7,3},{8,12},{9,13},{10,... | collective-permute-start | bytes 589832 | tf_op jit(solution)/shard_map/ppermute | solution.py:55
  36.4 4.7 %collective-permute-start.14 = (bf16[64,768]{1,0:T(8,128)(2,1)S(1)}, bf16[64,768]{1,0:T(8,128)(2,1)S(1)}, u32[]{:S(2)}, u32[]{:S(2)}) collective-permute-start(bf16[64,768]{1,0:T(8,128)(2,1)S(1)} %get-tuple-element.39), channel_id=1, source_target_pairs={{0,8},{8,0},{16,24},{24,16},{1,9},{9,1},{17,25},{25,17},{2,10},{10... | collective-permute-start | bytes 294920 | tf_op jit(solution)/shard_map/ppermute | solution.py:55
  41.1 5.6 %collective-permute-start.15 = (bf16[64,768]{1,0:T(8,128)(2,1)S(1)}, bf16[64,768]{1,0:T(8,128)(2,1)S(1)}, u32[]{:S(2)}, u32[]{:S(2)}) collective-permute-start(bf16[64,768]{1,0:T(8,128)(2,1)S(1)} %add_convert_fusion.4), channel_id=1, source_target_pairs={{0,16},{8,24},{16,0},{24,8},{1,17},{9,25},{17,1},{25,9},{2,18},{10... | collective-permute-start | bytes 294920 | tf_op jit(solution)/shard_map/ppermute | solution.py:55
  46.7 4.7 %collective-permute-start.16 = (bf16[64,768]{1,0:T(8,128)(2,1)S(1)}, bf16[64,768]{1,0:T(8,128)(2,1)S(1)}, u32[]{:S(2)}, u32[]{:S(2)}) collective-permute-start(bf16[64,768]{1,0:T(8,128)(2,1)S(1)} %add_convert_fusion.3.refs_0_), channel_id=1, source_target_pairs={{0,8},{8,0},{16,24},{24,16},{1,9},{9,1},{17,25},{25,17},{2,10},{10... | collective-permute-start | bytes 294920 | tf_op jit(solution)/shard_map/ppermute | solution.py:55
  51.6 7.7 %collective-permute-start.18 = (bf16[768,128]{1,0:T(8,128)(2,1)S(1)}, bf16[768,128]{1,0:T(8,128)(2,1)}, u32[]{:S(2)}, u32[]{:S(2)}) collective-permute-start(bf16[768,128]{1,0:T(8,128)(2,1)S(1)} %shard_map.108.whole_ref.refs_0_), channel_id=1, source_target_pairs={{0,2},{1,3},{2,0},{3,1},{4,6},{5,7},{6,4},{7,5},{8,10},{9,11},{10,... | collective-permute-start | bytes 589832 | tf_op jit(solution)/shard_map/ppermute | solution.py:55
  54.4 7.9 %collective-permute-start.20 = (bf16[768,128]{1,0:T(8,128)(2,1)S(1)}, bf16[768,128]{1,0:T(8,128)(2,1)}, u32[]{:S(2)}, u32[]{:S(2)}) collective-permute-start(bf16[768,128]{1,0:T(8,128)(2,1)S(1)} %shard_map.108.whole_ref.refs_0_), channel_id=1, source_target_pairs={{0,4},{1,5},{2,6},{3,7},{4,0},{5,1},{6,2},{7,3},{8,12},{9,13},{10,... | collective-permute-start | bytes 589832 | tf_op jit(solution)/shard_map/ppermute | solution.py:55
  54.4 7.9 %collective-permute-start.22 = (bf16[768,128]{1,0:T(8,128)(2,1)S(1)}, bf16[768,128]{1,0:T(8,128)(2,1)S(1)}, u32[]{:S(2)}, u32[]{:S(2)}) collective-permute-start(bf16[768,128]{1,0:T(8,128)(2,1)S(1)} %shard_map.108.whole_ref.refs_0_), channel_id=1, source_target_pairs={{0,6},{1,7},{2,4},{3,5},{4,2},{5,3},{6,0},{7,1},{8,14},{9,15},{10,... | collective-permute-start | bytes 589832 | tf_op jit(solution)/shard_map/ppermute | solution.py:55
  56.1 6.7 %collective-permute-start.17 = (bf16[768,128]{1,0:T(8,128)(2,1)S(1)}, bf16[768,128]{1,0:T(8,128)(2,1)S(1)}, u32[]{:S(2)}, u32[]{:S(2)}) collective-permute-start(bf16[768,128]{1,0:T(8,128)(2,1)S(1)} %shard_map.108.whole_ref.refs_0_), channel_id=1, source_target_pairs={{0,1},{1,0},{2,3},{3,2},{4,5},{5,4},{6,7},{7,6},{8,9},{9,8},{10,11... | collective-permute-start | bytes 589832 | tf_op jit(solution)/shard_map/ppermute | solution.py:55
  59.2 3.6 %collective-permute-start.19 = (bf16[768,128]{1,0:T(8,128)(2,1)}, bf16[768,128]{1,0:T(8,128)(2,1)S(1)}, u32[]{:S(2)}, u32[]{:S(2)}) collective-permute-start(bf16[768,128]{1,0:T(8,128)(2,1)} %shard_map.110.refs_2_), channel_id=1, source_target_pairs={{0,1},{1,0},{2,3},{3,2},{4,5},{5,4},{6,7},{7,6},{8,9},{9,8},{10,11... | collective-permute-start | bytes 589832 | tf_op jit(solution)/shard_map/ppermute | solution.py:55
  62.3 1.7 %collective-permute-start.21 = (bf16[768,128]{1,0:T(8,128)(2,1)}, bf16[768,128]{1,0:T(8,128)(2,1)S(1)}, u32[]{:S(2)}, u32[]{:S(2)}) collective-permute-start(bf16[768,128]{1,0:T(8,128)(2,1)} %shard_map.111.refs_4_), channel_id=1, source_target_pairs={{0,1},{1,0},{2,3},{3,2},{4,5},{5,4},{6,7},{7,6},{8,9},{9,8},{10,11... | collective-permute-start | bytes 589832 | tf_op jit(solution)/shard_map/ppermute | solution.py:55
  62.3 1.7 %collective-permute-start.23 = (bf16[768,128]{1,0:T(8,128)(2,1)S(1)}, bf16[768,128]{1,0:T(8,128)(2,1)S(1)}, u32[]{:S(2)}, u32[]{:S(2)}) collective-permute-start(bf16[768,128]{1,0:T(8,128)(2,1)S(1)} %shard_map.112.refs_6_), channel_id=1, source_target_pairs={{0,1},{1,0},{2,3},{3,2},{4,5},{5,4},{6,7},{7,6},{8,9},{9,8},{10,11... | collective-permute-start | bytes 589832 | tf_op jit(solution)/shard_map/ppermute | solution.py:55
  (7 other events, 39.1 us)
